TPU v7x, 32 devices: a whole 2x2x4 slice. The times are simulated.
32 devices in a mesh: seq: 8 (over z, x), fsdp: 4 (over y, core).
Axes of the slice: x: 2, y: 2, z: 4, core: 2. Of those that a mesh axis runs over, the one named last changes fastest.
Arguments:
- tokens: bfloat16 [4, 1024, 2048], P('fsdp', 'seq'), may hold values from -6 to 6
- query_key_value_weight: bfloat16 [2048, 5120], P(('seq', 'fsdp')), may hold values from -0.125 to 0.125
- w_out_t: bfloat16 [2048, 4096], P(('seq', 'fsdp')), may hold values from -0.5 to 0.5
- w_router: bfloat16 [2048, 32], P(('seq', 'fsdp')), may hold values from -0.0625 to 0.0625
- w_in: bfloat16 [32, 2048, 1536], P(('seq', 'fsdp')), may hold values from -0.125 to 0.125
- w_down: bfloat16 [32, 768, 2048], P(('seq', 'fsdp')), may hold values from -0.625 to 0.625
- attn_gain: float32 [2048], replicated, may hold values from 0.1 to 1.9
- ffn_gain: float32 [2048], replicated, may hold values from 0.1 to 1.9
- q_gain: float32 [128], replicated, may hold values from 0.5 to 2
- k_gain: float32 [128], replicated, may hold values from 0.5 to 2
- routes: int32 [4, 1024, 8], P('fsdp', 'seq'), may hold values from 0 to 31, as said below
- cotangent: bfloat16 [4, 1024, 2048], P('fsdp', 'seq'), may hold values from -6 to 6
Outputs:
- output: bfloat16 [4, 1024, 2048], P('fsdp', 'seq')
- d_tokens: bfloat16 [4, 1024, 2048], P('fsdp', 'seq')
- d_w_qkv: float32 [2048, 5120], P(('seq', 'fsdp'))
- d_w_out_t: float32 [2048, 4096], P(('seq', 'fsdp'))
- d_w_router: float32 [2048, 32], P(('seq', 'fsdp'))
- d_w_in: float32 [32, 2048, 1536], P(('seq', 'fsdp'))
- d_w_down: float32 [32, 768, 2048], P(('seq', 'fsdp'))
- d_attn_gain: float32 [2048], replicated
- d_ffn_gain: float32 [2048], replicated
- d_q_gain: float32 [128], replicated
- d_k_gain: float32 [128], replicated
Inputs may be any that keep to these rules, and one draw needn't show every extreme that they name: `routes`: each token names 8 different experts. In each aligned block of 128 tokens of one sequence, 16 experts are named exactly 64 times each and the others not at all.
All inputs are finite; a program needn't handle non-finite values.
Results may differ from a plain program's by a relative error of at most 0.02.
Values may be sent and summed in bfloat16 or wider, within the bound.
A program may use at most 256 MiB of HBM per device.

v0:
```python
from functools import partial
import math

import jax
import jax.numpy as jnp
from jax import lax
from jax.sharding import PartitionSpec as P

QUERY_HEADS = 32
KEY_VALUE_HEADS = 4
HEAD_DIMENSION = 128
FF = 768
TOPK = 8


EPS = 1e-06
ROPE_BASE = 1000000.0


def rms_scale(values, gain):
    return values * lax.rsqrt(jnp.mean(values * values, axis=-1, keepdims=True) + EPS) * gain


def rotate(values, positions):
    half_dim = values.shape[-1] // 2
    frequency = ROPE_BASE ** (-2.0 * jnp.arange(half_dim, dtype=jnp.float32) / values.shape[-1])
    angles = positions.astype(jnp.float32)[:, None] * frequency[None, :]
    cosine = jnp.cos(angles)[:, None, :]
    sine_part = jnp.sin(angles)[:, None, :]
    first_half = values[..., :half_dim]
    second = values[..., half_dim:]
    return jnp.concatenate(
        [first_half * cosine - second * sine_part, second * cosine + first_half * sine_part],
        axis=-1,
    )


def head_prepare(raw_heads, gain, positions):
    return rotate(rms_scale(raw_heads, gain), positions)


def route_slots(route_flat, experts):
    onehot = (route_flat[:, None] == jnp.arange(experts, dtype=jnp.int32)[None, :]).astype(
        jnp.int32
    )
    earlier = jnp.cumsum(onehot, axis=0) - onehot
    return (onehot, jnp.sum(earlier * onehot, axis=1))


def pack_slots(row_values, expert_ids, slot_index, slot_shape):
    buffer = jnp.zeros(slot_shape, row_values.dtype)
    return buffer.at[expert_ids // slot_shape[1], expert_ids % slot_shape[1], slot_index].set(
        row_values
    )


def unpack_slots(buffer, expert_ids, slot_index):
    return buffer[expert_ids // buffer.shape[1], expert_ids % buffer.shape[1], slot_index]


def causal_scores(query_part, key_full, row_start):
    block_rows = query_part.shape[0]
    score_scale = 1.0 / math.sqrt(query_part.shape[2])
    scores = (
        jnp.einsum("qhd,khd->hqk", query_part, key_full, preferred_element_type=jnp.float32)
        * score_scale
    )
    key_pos = jnp.arange(key_full.shape[0], dtype=jnp.int32)
    row_pos = row_start + jnp.arange(block_rows, dtype=jnp.int32)
    allowed = key_pos[None, :] <= row_pos[:, None]
    return jnp.where(allowed[None], scores, -1e30)


def attend_forward(query_rows_all, key_full, value_full):
    sequence_length = query_rows_all.shape[0]
    block_rows = min(512, sequence_length)

    def one_block(block_index):
        row_start = block_index * block_rows
        query_part = lax.dynamic_slice_in_dim(query_rows_all, row_start, block_rows, 0)
        scores = causal_scores(query_part, key_full, row_start)
        row_max = jnp.max(scores, axis=-1, keepdims=True)
        weights = jnp.exp(scores - row_max)
        row_total = jnp.sum(weights, axis=-1, keepdims=True)
        prob_low = (weights / row_total).astype(jnp.bfloat16)
        mixed_out = jnp.einsum(
            "hqk,khd->qhd", prob_low, value_full, preferred_element_type=jnp.float32
        )
        return (mixed_out.astype(jnp.bfloat16), (row_max + jnp.log(row_total))[..., 0])

    mixed_out, log_total = lax.map(
        one_block, jnp.arange(sequence_length // block_rows, dtype=jnp.int32)
    )
    return (mixed_out.reshape(query_rows_all.shape), log_total)


def attend_backward(query_rows_all, key_full, value_full, log_total, d_mixed):
    sequence_length = query_rows_all.shape[0]
    block_rows = min(512, sequence_length)
    score_scale = 1.0 / math.sqrt(query_rows_all.shape[2])

    def one_block(running, block_index):
        d_key_sum, d_value_sum = running
        row_start = block_index * block_rows
        query_part = lax.dynamic_slice_in_dim(query_rows_all, row_start, block_rows, 0)
        d_part = lax.dynamic_slice_in_dim(d_mixed, row_start, block_rows, 0)
        scores = causal_scores(query_part, key_full, row_start)
        prob_full = jnp.exp(scores - log_total[block_index][..., None])
        prob_low = prob_full.astype(jnp.bfloat16)
        d_probs = jnp.einsum("qhd,khd->hqk", d_part, value_full, preferred_element_type=jnp.float32)
        row_delta = jnp.sum(prob_full * d_probs, axis=-1, keepdims=True)
        d_scores = (prob_full * (d_probs - row_delta)).astype(jnp.bfloat16)
        d_query_part = (
            jnp.einsum("hqk,khd->qhd", d_scores, key_full, preferred_element_type=jnp.float32)
            * score_scale
        )
        d_key_sum = (
            d_key_sum
            + jnp.einsum("hqk,qhd->khd", d_scores, query_part, preferred_element_type=jnp.float32)
            * score_scale
        )
        d_value_sum = d_value_sum + jnp.einsum(
            "hqk,qhd->khd", prob_low, d_part, preferred_element_type=jnp.float32
        )
        return ((d_key_sum, d_value_sum), d_query_part)

    zero_grad = jnp.zeros(key_full.shape, jnp.float32)
    (d_key_sum, d_value_sum), d_query = lax.scan(
        one_block,
        (zero_grad, zero_grad),
        jnp.arange(sequence_length // block_rows, dtype=jnp.int32),
    )
    return (d_query.reshape(query_rows_all.shape), d_key_sum, d_value_sum)


def body(
    tokens,
    query_key_value_weight,
    w_out_t,
    w_router,
    w_in,
    w_down,
    attn_gain,
    ffn_gain,
    q_gain,
    k_gain,
    routes,
    cotangent,
):
    sequence_count = lax.axis_size("seq")
    shard_count = lax.axis_size("fsdp")
    experts = sequence_count * shard_count
    token_row_count = tokens.shape[1]
    model_width = tokens.shape[2]
    query_group_width = QUERY_HEADS // KEY_VALUE_HEADS
    capacity = 2 * token_row_count * TOPK // experts
    slot_shape = (sequence_count, shard_count, capacity, model_width)
    positions = lax.axis_index("seq") * token_row_count + jnp.arange(
        token_row_count, dtype=jnp.int32
    )
    full_qkv, full_out, full_router = (
        lax.all_gather(query_key_value_weight, ("seq", "fsdp"), axis=0, tiled=True),
        lax.all_gather(w_out_t, ("seq", "fsdp"), axis=0, tiled=True),
        lax.all_gather(w_router, ("seq", "fsdp"), axis=0, tiled=True),
    )
    resid_in = tokens[0].astype(jnp.float32)
    normed_one = rms_scale(resid_in, attn_gain).astype(jnp.bfloat16)
    projection_output = jnp.dot(normed_one, full_qkv, preferred_element_type=jnp.float32)
    q_raw = projection_output[:, : QUERY_HEADS * HEAD_DIMENSION].reshape(
        token_row_count, QUERY_HEADS, HEAD_DIMENSION
    )
    key_unnormed = projection_output[
        :, QUERY_HEADS * HEAD_DIMENSION : (QUERY_HEADS + KEY_VALUE_HEADS) * HEAD_DIMENSION
    ].reshape(token_row_count, KEY_VALUE_HEADS, HEAD_DIMENSION)
    value_per_head = (
        projection_output[:, (QUERY_HEADS + KEY_VALUE_HEADS) * HEAD_DIMENSION :]
        .reshape(token_row_count, KEY_VALUE_HEADS, HEAD_DIMENSION)
        .astype(jnp.bfloat16)
    )
    prepare = partial(head_prepare, positions=positions)
    query_rows_all = prepare(q_raw, q_gain).astype(jnp.bfloat16)
    key_per_head = prepare(key_unnormed, k_gain).astype(jnp.bfloat16)
    send_keys = jnp.repeat(key_per_head, query_group_width, axis=1)
    send_values = jnp.repeat(value_per_head, query_group_width, axis=1)
    head_queries, head_keys, head_values = (
        lax.all_to_all(query_rows_all, "seq", split_axis=1, concat_axis=0, tiled=True),
        lax.all_to_all(send_keys, "seq", split_axis=1, concat_axis=0, tiled=True),
        lax.all_to_all(send_values, "seq", split_axis=1, concat_axis=0, tiled=True),
    )
    mixed_heads, log_total = attend_forward(head_queries, head_keys, head_values)
    mixed_tok = lax.all_to_all(mixed_heads, "seq", split_axis=0, concat_axis=1, tiled=True)
    attention_result = mixed_tok.reshape(token_row_count, QUERY_HEADS * HEAD_DIMENSION)
    attn_out = jnp.einsum(
        "tj,dj->td", attention_result, full_out, preferred_element_type=jnp.float32
    )
    hidden = resid_in + attn_out
    normed_two = rms_scale(hidden, ffn_gain).astype(jnp.bfloat16)
    logits = jnp.dot(normed_two, full_router, preferred_element_type=jnp.float32)
    route_flat = routes[0].reshape(-1)
    onehot, slot_index = route_slots(route_flat, experts)
    onehot_float = onehot.reshape(token_row_count, TOPK, experts).astype(jnp.float32)
    chosen = jnp.sum(onehot_float * logits[:, None, :], axis=-1)
    row_max = jnp.max(chosen, axis=-1, keepdims=True)
    exp_part = jnp.exp(chosen - row_max)
    gate_probs = exp_part / jnp.sum(exp_part, axis=-1, keepdims=True)
    send_rows = pack_slots(jnp.repeat(normed_two, TOPK, axis=0), route_flat, slot_index, slot_shape)
    arrived = lax.all_to_all(
        lax.all_to_all(send_rows, "seq", split_axis=0, concat_axis=0, tiled=True),
        "fsdp",
        split_axis=1,
        concat_axis=1,
        tiled=True,
    )
    rows_in = arrived.reshape(-1, model_width)
    gate_weight = w_in[0]
    down_weight = w_down[0]
    gate_up = jnp.dot(rows_in, gate_weight, preferred_element_type=jnp.float32)
    gate_half = gate_up[:, :FF]
    up_half = gate_up[:, FF:]
    gate_sig = jax.nn.sigmoid(gate_half)
    silu_gate = gate_half * gate_sig
    inner_act = (silu_gate * up_half).astype(jnp.bfloat16)
    expert_out = jnp.dot(inner_act, down_weight, preferred_element_type=jnp.float32).astype(
        jnp.bfloat16
    )
    returned = lax.all_to_all(
        lax.all_to_all(
            expert_out.reshape(slot_shape), "seq", split_axis=0, concat_axis=0, tiled=True
        ),
        "fsdp",
        split_axis=1,
        concat_axis=1,
        tiled=True,
    )
    picked = (
        unpack_slots(returned, route_flat, slot_index)
        .astype(jnp.float32)
        .reshape(token_row_count, TOPK, model_width)
    )
    mixture = jnp.sum(gate_probs[..., None] * picked, axis=1)
    output = (hidden + mixture).astype(jnp.bfloat16)
    full_qkv, full_out, full_router = (
        lax.all_gather(query_key_value_weight, ("seq", "fsdp"), axis=0, tiled=True),
        lax.all_gather(w_out_t, ("seq", "fsdp"), axis=0, tiled=True),
        lax.all_gather(w_router, ("seq", "fsdp"), axis=0, tiled=True),
    )
    out_grad = cotangent[0].astype(jnp.float32)
    d_picked = (
        (gate_probs[..., None] * out_grad[:, None, :]).astype(jnp.bfloat16).reshape(-1, model_width)
    )
    d_gates = jnp.sum(picked * out_grad[:, None, :], axis=-1)
    d_send = pack_slots(d_picked, route_flat, slot_index, slot_shape)
    d_arrived = lax.all_to_all(
        lax.all_to_all(d_send, "seq", split_axis=0, concat_axis=0, tiled=True),
        "fsdp",
        split_axis=1,
        concat_axis=1,
        tiled=True,
    ).reshape(-1, model_width)
    d_inner = jnp.einsum("rd,fd->rf", d_arrived, down_weight, preferred_element_type=jnp.float32)
    d_gate_half = d_inner * up_half * gate_sig * (1.0 + gate_half * (1.0 - gate_sig))
    d_up_half = d_inner * silu_gate
    d_gate_up = jnp.concatenate([d_gate_half, d_up_half], axis=1).astype(jnp.bfloat16)
    d_w_down = jnp.einsum("rf,rd->fd", inner_act, d_arrived, preferred_element_type=jnp.float32)[
        None
    ]
    d_w_in = jnp.einsum("rd,rf->df", rows_in, d_gate_up, preferred_element_type=jnp.float32)[None]
    d_rows = jnp.einsum(
        "rf,df->rd", d_gate_up, gate_weight, preferred_element_type=jnp.float32
    ).astype(jnp.bfloat16)
    d_back = lax.all_to_all(
        lax.all_to_all(d_rows.reshape(slot_shape), "seq", split_axis=0, concat_axis=0, tiled=True),
        "fsdp",
        split_axis=1,
        concat_axis=1,
        tiled=True,
    )
    d_routed = jnp.sum(
        unpack_slots(d_back, route_flat, slot_index)
        .astype(jnp.float32)
        .reshape(token_row_count, TOPK, model_width),
        axis=1,
    )
    d_chosen = gate_probs * (d_gates - jnp.sum(gate_probs * d_gates, axis=-1, keepdims=True))
    d_logits = jnp.einsum("tk,tke->te", d_chosen, onehot_float).astype(jnp.bfloat16)
    d_normed_two = d_routed + jnp.einsum(
        "te,de->td", d_logits, full_router, preferred_element_type=jnp.float32
    )
    unused_two, pull_two = jax.vjp(rms_scale, hidden, ffn_gain)
    d_hidden_norm, d_ffn_gain = pull_two(d_normed_two)
    d_hidden = out_grad + d_hidden_norm
    d_attn = d_hidden.astype(jnp.bfloat16)
    d_attended = jnp.einsum(
        "td,dj->tj", d_attn, full_out, preferred_element_type=jnp.float32
    ).astype(jnp.bfloat16)
    d_heads = lax.all_to_all(
        d_attended.reshape(token_row_count, QUERY_HEADS, HEAD_DIMENSION),
        "seq",
        split_axis=1,
        concat_axis=0,
        tiled=True,
    )
    d_query, d_key_sum, d_value_sum = attend_backward(
        head_queries, head_keys, head_values, log_total, d_heads
    )
    seq_rows = head_queries.shape[0]
    local_cols = head_queries.shape[1] * HEAD_DIMENSION
    normed_all, d_attn_all = (
        lax.all_gather(normed_one, "seq", axis=0, tiled=True),
        lax.all_gather(d_attn, "seq", axis=0, tiled=True),
    )
    query_cols = lax.dynamic_slice_in_dim(
        full_qkv, lax.axis_index("seq") * local_cols, local_cols, 1
    )
    q_head_raw = jnp.dot(normed_all, query_cols, preferred_element_type=jnp.float32).reshape(
        head_queries.shape
    )
    seq_positions = jnp.arange(seq_rows, dtype=jnp.int32)
    unused_head, pull_head = jax.vjp(
        partial(head_prepare, positions=seq_positions), q_head_raw, q_gain
    )
    send_d_query, d_q_gain = pull_head(d_query)
    d_query_tok, grad_key_token_rows, grad_value_token_rows = (
        lax.all_to_all(
            send_d_query.astype(jnp.bfloat16), "seq", split_axis=0, concat_axis=1, tiled=True
        ).astype(send_d_query.dtype),
        lax.all_to_all(
            d_key_sum.astype(jnp.bfloat16), "seq", split_axis=0, concat_axis=1, tiled=True
        ).astype(d_key_sum.dtype),
        lax.all_to_all(
            d_value_sum.astype(jnp.bfloat16), "seq", split_axis=0, concat_axis=1, tiled=True
        ).astype(d_value_sum.dtype),
    )
    grad_key_per_head = jnp.sum(
        grad_key_token_rows.reshape(token_row_count, KEY_VALUE_HEADS, -1, HEAD_DIMENSION), axis=2
    )
    grad_value_per_head = jnp.sum(
        grad_value_token_rows.reshape(token_row_count, KEY_VALUE_HEADS, -1, HEAD_DIMENSION), axis=2
    )
    unused_k, pull_k = jax.vjp(prepare, key_unnormed, k_gain)
    grad_key_unnormed, d_k_gain = pull_k(grad_key_per_head)
    d_projected = jnp.concatenate(
        [
            d_query_tok.reshape(token_row_count, QUERY_HEADS * HEAD_DIMENSION),
            grad_key_unnormed.reshape(token_row_count, KEY_VALUE_HEADS * HEAD_DIMENSION),
            grad_value_per_head.reshape(token_row_count, KEY_VALUE_HEADS * HEAD_DIMENSION),
        ],
        axis=1,
    ).astype(jnp.bfloat16)
    d_normed_one = jnp.einsum(
        "tj,dj->td", d_projected, full_qkv, preferred_element_type=jnp.float32
    )
    unused_one, pull_one = jax.vjp(rms_scale, resid_in, attn_gain)
    d_resid_norm, d_attn_gain = pull_one(d_normed_one)
    d_tokens = (d_hidden + d_resid_norm).astype(jnp.bfloat16)[None]
    rows_dev = model_width // experts
    kv_count = 2 * KEY_VALUE_HEADS * HEAD_DIMENSION
    kv_grads = d_projected[:, QUERY_HEADS * HEAD_DIMENSION :]
    first_rows = normed_one
    summed = lax.psum_scatter(
        jnp.concatenate(
            [
                jnp.einsum("tc,tj->cj", first_rows, kv_grads, preferred_element_type=jnp.float32),
                jnp.einsum("tc,te->ce", normed_two, d_logits, preferred_element_type=jnp.float32),
            ],
            axis=1,
        ),
        ("seq", "fsdp"),
        scatter_dimension=0,
        tiled=True,
    )
    d_query_low = send_d_query.reshape(seq_rows, local_cols).astype(jnp.bfloat16)
    attended_heads = mixed_heads.reshape(seq_rows, local_cols)
    normed_order = (
        normed_all.reshape(seq_rows, sequence_count, shard_count, rows_dev)
        .transpose(0, 2, 1, 3)
        .reshape(seq_rows, model_width)
    )
    d_attn_order = (
        d_attn_all.reshape(seq_rows, sequence_count, shard_count, rows_dev)
        .transpose(0, 2, 1, 3)
        .reshape(seq_rows, model_width)
    )
    first_rows = normed_order
    head_sums = lax.psum_scatter(
        jnp.concatenate(
            [
                jnp.einsum(
                    "tc,tj->cj", first_rows, d_query_low, preferred_element_type=jnp.float32
                ),
                jnp.einsum(
                    "tc,tj->cj", d_attn_order, attended_heads, preferred_element_type=jnp.float32
                ),
            ],
            axis=1,
        ).astype(jnp.bfloat16),
        "fsdp",
        scatter_dimension=0,
        tiled=True,
    ).astype(jnp.float32)
    row_sums = (
        lax.all_to_all(
            head_sums.astype(jnp.bfloat16), "seq", split_axis=0, concat_axis=1, tiled=True
        )
        .astype(head_sums.dtype)
        .reshape(rows_dev, sequence_count, 2, local_cols)
    )
    d_w_query = row_sums[:, :, 0].reshape(rows_dev, QUERY_HEADS * HEAD_DIMENSION)
    d_w_out_t = row_sums[:, :, 1].reshape(rows_dev, QUERY_HEADS * HEAD_DIMENSION)
    d_w_qkv = jnp.concatenate([d_w_query, summed[:, :kv_count]], axis=1)
    d_w_router = summed[:, kv_count:]
    d_attn_gain, d_ffn_gain, d_q_gain, d_k_gain = lax.psum(
        (d_attn_gain, d_ffn_gain, d_q_gain, d_k_gain), ("seq", "fsdp")
    )
    return (
        output[None],
        d_tokens,
        d_w_qkv,
        d_w_out_t,
        d_w_router,
        d_w_in,
        d_w_down,
        d_attn_gain,
        d_ffn_gain,
        d_q_gain,
        d_k_gain,
    )


def solution(mesh):
    return jax.shard_map(
        body,
        mesh=mesh,
        in_specs=(
            P("fsdp", "seq", None),
            P(("seq", "fsdp"), None),
            P(("seq", "fsdp"), None),
            P(("seq", "fsdp"), None),
            P(("seq", "fsdp"), None, None),
            P(("seq", "fsdp"), None, None),
            P(),
            P(),
            P(),
            P(),
            P("fsdp", "seq", None),
            P("fsdp", "seq", None),
        ),
        out_specs=(
            P("fsdp", "seq", None),
            P("fsdp", "seq", None),
            P(("seq", "fsdp"), None),
            P(("seq", "fsdp"), None),
            P(("seq", "fsdp"), None),
            P(("seq", "fsdp"), None, None),
            P(("seq", "fsdp"), None, None),
            P(),
            P(),
            P(),
            P(),
        ),
        check_vma=False,
    )
```

profile of v0, /device:TPU:16, one launch (start us, length us, event | category | flops | bytes accessed | tf_op | source)
XLA Modules:
  0.0 2068.9 jit_solution(9176338315348297054)
XLA Ops:
  13.9 132.5 %all-gather.6.cloned.1.call-done = bf16[2048,5120]{1,0:T(8,128)(2,1)} async-done(((bf16[64,5120]{1,0:T(8,128)(2,1)}), bf16[2048,5120]{1,0:T(8,128)(2,1)}) %all-gather.6.cloned.1.call-update) | async-done | bytes 20971536 | tf_op jit(solution)/shard_map/all_gather | solution.py:162
  146.4 8.7 fusion.103
  180.1 31.6 %all-to-all-done.1 = bf16[128,32,128]{2,0,1:T(8,128)(2,1)} async-done(((bf16[128,32,128]{2,0,1:T(8,128)(2,1)}), bf16[128,32,128]{2,0,1:T(8,128)(2,1)}, u32[]{:S(2)}, u32[]{:S(2)}) %all-to-all-start.1) | async-done | bytes 1048608 | tf_op jit(solution)/shard_map/all_to_all | solution.py:187
  211.7 10.7 all-to-all-start
  223.3 46.8 %all-to-all-done = bf16[128,32,128]{2,0,1:T(8,128)(2,1)} async-done(((bf16[128,32,128]{2,0,1:T(8,128)(2,1)}), bf16[128,32,128]{2,0,1:T(8,128)(2,1)}, u32[]{:S(2)}, u32[]{:S(2)}) %all-to-all-start) | async-done | bytes 1048608 | tf_op jit(solution)/shard_map/all_to_all | solution.py:186
  271.3 10.1 all-to-all-start.2
  286.1 26.1 %all-to-all-done.2 = bf16[128,32,128]{2,0,1:T(8,128)(2,1)} async-done(((bf16[128,32,128]{2,0,1:T(8,128)(2,1)}), bf16[128,32,128]{2,0,1:T(8,128)(2,1)}, u32[]{:S(2)}, u32[]{:S(2)}) %all-to-all-start.2) | async-done | bytes 1048608 | tf_op jit(solution)/shard_map/all_to_all | solution.py:188
  314.5 21.8 %while.27 = (s32[]{:T(128)}, bf16[2,512,4,128]{3,1,2,0:T(8,128)(2,1)}, f32[2,4,512]{2,1,0:T(4,128)S(1)}, s32[2]{0:T(128)S(1)}, bf16[1024,4,128]{2,0,1:T(8,128)(2...) while((s32[]{:T(128)}, ...), condition=%wide.region_6.7_spmd, body=%wide.region_3.6_spmd.sunk | while | flops 1099692544 | bytes 34673356 | solution.py:91
  347.9 9.0 reduce-window.6
  358.3 12.0 all-to-all-done.3
  374.8 12.7 multiply_reduce_fusion.7
  389.8 12.0 scatter_custom_fusion
  410.1 207.4 %all-gather = bf16[32,64,32]{1,2,0:T(8,128)(2,1)S(1)} all-gather(bf16[1,64,32]{1,2,0:T(8,128)(2,1)S(1)} %bitcast.506), channel_id=1, replica_groups=mesh['seq'=8,'fsdp'=4] {'seq','fsdp'}, dimensions={0}, use_global_device_ids=true | all-gather | bytes 135168 | tf_op jit(solution)/shard_map/all_gather | solution.py:164
  622.7 12.2 scatter_custom_fusion.1
  640.1 8.4 copy.585
  648.5 172.6 %all-to-all-done.8 = bf16[8,4,64,2048]{3,2,1,0:T(8,128)(2,1)} async-done(((bf16[8,4,64,2048]{3,2,1,0:T(8,128)(2,1)}), bf16[8,4,64,2048]{3,2,1,0:T(8,128)(2,1)}, u32[]{:S(2)}, u32[]{:S(2)}) %all-to-all-start.8) | async-done | bytes 8388640 | tf_op jit(solution)/shard_map/all_to_all | solution.py:254
  826.8 8.3 copy.590
  835.1 84.9 %all-to-all-done.5 = bf16[8,4,64,2048]{3,2,0,1:T(8,128)(2,1)} async-done(((bf16[8,4,64,2048]{3,2,0,1:T(8,128)(2,1)}), bf16[8,4,64,2048]{3,2,0,1:T(8,128)(2,1)}, u32[]{:S(2)}, u32[]{:S(2)}) %all-to-all-start.5) | async-done | bytes 8388640 | tf_op jit(solution)/shard_map/all_to_all | solution.py:207
  925.6 8.3 copy.586
  933.9 19.0 fusion.38
  952.9 65.9 %all-to-all-done.9 = bf16[8,4,64,2048]{3,2,0,1:T(8,128)(2,1)} async-done(((bf16[8,4,64,2048]{3,2,0,1:T(8,128)(2,1)}), bf16[8,4,64,2048]{3,2,0,1:T(8,128)(2,1)}, u32[]{:S(2)}, u32[]{:S(2)}) %all-to-all-start.9) | async-done | bytes 8388640 | tf_op jit(solution)/shard_map/all_to_all | solution.py:253
  1018.8 8.4 copy.591
  1027.1 15.8 multiply_convert_fusion.2
  1043.0 9.7 convolution_convert_fusion.1
  1052.7 8.5 all-to-all-start.6
  1061.1 18.5 convolution_convert_fusion
  1079.7 161.4 %all-to-all-done.6 = bf16[8,4,64,2048]{3,2,1,0:T(8,128)(2,1)} async-done(((bf16[8,4,64,2048]{3,2,1,0:T(8,128)(2,1)}), bf16[8,4,64,2048]{3,2,1,0:T(8,128)(2,1)}, u32[]{:S(2)}, u32[]{:S(2)}) %all-to-all-start.6) | async-done | bytes 8388640 | tf_op jit(solution)/shard_map/all_to_all | solution.py:227
  1241.0 8.2 all-to-all-start.10
  1249.3 8.3 copy.587
  1257.6 170.7 %all-to-all-done.10 = bf16[8,4,64,2048]{3,2,1,0:T(8,128)(2,1)} async-done(((bf16[8,4,64,2048]{3,2,1,0:T(8,128)(2,1)}), bf16[8,4,64,2048]{3,2,1,0:T(8,128)(2,1)}, u32[]{:S(2)}, u32[]{:S(2)}) %all-to-all-start.10) | async-done | bytes 8388640 | tf_op jit(solution)/shard_map/all_to_all | solution.py:272
  1434.1 8.4 copy.592
  1442.6 84.7 %all-to-all-done.7 = bf16[8,4,64,2048]{3,2,0,1:T(8,128)(2,1)} async-done(((bf16[8,4,64,2048]{3,2,0,1:T(8,128)(2,1)}), bf16[8,4,64,2048]{3,2,0,1:T(8,128)(2,1)}, u32[]{:S(2)}, u32[]{:S(2)}) %all-to-all-start.7) | async-done | bytes 8388640 | tf_op jit(solution)/shard_map/all_to_all | solution.py:226
  1533.5 8.4 copy.588
  1541.9 26.4 %gather_fusion = bf16[1024,2048]{1,0:T(8,128)(2,1)} fusion(bf16[8,4,64,2048]{3,2,1,0:T(8,128)(2,1)} %copy.588, s32[1024]{0:T(1024)S(1)} %bitcast.458), kind=kCustom, calls=%fused_computation | custom fusion | bytes 8400896 | tf_op jit(solution)/shard_map/gather | solution.py:58
  1574.6 51.5 %all-to-all-done.11 = bf16[8,4,64,2048]{3,2,0,1:T(8,128)(2,1)} async-done(((bf16[8,4,64,2048]{3,2,0,1:T(8,128)(2,1)}), bf16[8,4,64,2048]{3,2,0,1:T(8,128)(2,1)}, u32[]{:S(2)}, u32[]{:S(2)}) %all-to-all-start.11) | async-done | bytes 8388640 | tf_op jit(solution)/shard_map/all_to_all | solution.py:271
  1626.1 8.4 copy.593
  1634.5 26.6 %gather_fusion.1 = bf16[1024,2048]{1,0:T(8,128)(2,1)} fusion(bf16[8,4,64,2048]{3,2,1,0:T(8,128)(2,1)} %copy.593, s32[1024]{0:T(1024)S(1)} %bitcast.459), kind=kCustom, calls=%fused_computation.1 | custom fusion | bytes 8400896 | tf_op jit(solution)/shard_map/gather | solution.py:58
  1668.4 8.3 fusion.57
  1713.9 63.6 %while.28 = (s32[]{:T(128)}, f32[1024,4,128]{0,2,1:T(8,128)S(1)}, f32[1024,4,128]{0,2,1:T(8,128)}, f32[2,512,4,128]{3,1,0,2:T(8,128)}, s32[2]{0:T(128)S(1)}, /*i...) while((s32[]{:T(128)}, f32[1024,4,128]{0,2,1:T(8,128)S(1)}, ...), condition=%wide.region_23.24_spmd.clone, body=%wide.region_21.23_spmd.clone.sunk | while | flops 2719218176 | bytes 163640304 | solution.py:128
  1817.7 19.0 all-to-all-done.14
  1853.7 13.2 all-to-all-done.15
  1882.5 9.5 copy.632
  1892.0 20.2 convolution_bitcast_fusion
  1920.9 12.0 convolution_bitcast_fusion.1
  1932.9 10.7 all-to-all-done.13
  1955.1 12.5 fusion.67
  1967.6 46.9 %all-reduce.4 = (f32[2048]{0:T(1024)}, f32[2048]{0:T(1024)}, f32[128]{0:T(128)}, f32[128]{0:T(128)}) all-reduce(f32[2048]{0:T(1024)S(1)} %get-tuple-element.147, f32[2048]{0:T(1024)S(1)} %copy-done.54, f32[128]{0:T(128)S(1)} %get-tuple-element.141, f32[128]{0:T(128)S(1)} %get-tuple-element.149), channel_id=1, replica_groups=mesh['seq'=8,'fsdp'=4] {'seq','fsdp'}, use_global_device_ids=true, to_apply=%region_35.36 | all-reduce | flops 4352 | bytes 34816 | tf_op jit(solution)/shard_map/psum | solution.py:412
  2017.6 29.8 %reduce-scatter.7.cloned.1.call-done = f32[64,1056]{1,0:T(8,128)} async-done(((f32[2048,1056]{1,0:T(8,128)}), f32[64,1056]{1,0:T(8,128)}) %reduce-scatter.7.cloned.1.call-update) | async-done | bytes 270352
  (390 shorter events, 339.4 us)
Async XLA Ops:
  8.0 1019.1 %copy-start = (bf16[1,768,2048]{2,1,0:T(8,128)(2,1)S(1)}, bf16[1,768,2048]{2,1,0:T(8,128)(2,1)}, u32[]{:S(2)}) copy-start(bf16[1,768,2048]{2,1,0:T(8,128)(2,1)} %param.21) | copy-start | bytes 9437188
  8.0 138.4 %all-gather.6.cloned.1.call-start = ((), (), s32[]{:S(2)}) async-start(), calls=%async_computation.19 | async-start | bytes 21626880 | tf_op jit(solution)/shard_map/all_gather | solution.py:162
  8.8 366.1 %all-gather.8.cloned.1.call-start = ((), (), s32[]{:S(2)}) async-start(), calls=%async_computation.20 | async-start | bytes 17301504 | tf_op jit(solution)/shard_map/all_gather | solution.py:163
  11.9 158.8 %copy-start.35 = (f32[128,64]{0,1:T(8,128)}, f32[128,64]{0,1:T(8,128)S(1)}, u32[]{:S(2)}) copy-start(f32[128,64]{0,1:T(8,128)S(1)} %get-tuple-element.216) | copy-start | bytes 98308
  11.9 158.9 %copy-start.37 = (f32[128,64]{0,1:T(8,128)}, f32[128,64]{0,1:T(8,128)S(1)}, u32[]{:S(2)}) copy-start(f32[128,64]{0,1:T(8,128)S(1)} %get-tuple-element.217) | copy-start | bytes 98308
  13.9 146.0 %copy-start.65 = (f32[128]{0:T(128)S(1)}, f32[128]{0:T(128)}, u32[]{:S(2)}) copy-start(f32[128]{0:T(128)} %param.25) | copy-start | bytes 1540
  165.1 46.6 %all-to-all-start.1 = ((bf16[128,32,128]{2,0,1:T(8,128)(2,1)}), bf16[128,32,128]{2,0,1:T(8,128)(2,1)}, u32[]{:S(2)}, u32[]{:S(2)}) async-start(bf16[128,32,128]{2,0,1:T(8,128)(2,1)} %bitcast.480), calls=%async_computation.1 | async-start | bytes 2097152 | tf_op jit(solution)/shard_map/all_to_all | solution.py:187
  211.7 58.4 %all-to-all-start = ((bf16[128,32,128]{2,0,1:T(8,128)(2,1)}), bf16[128,32,128]{2,0,1:T(8,128)(2,1)}, u32[]{:S(2)}, u32[]{:S(2)}) async-start(bf16[128,32,128]{2,0,1:T(8,128)(2,1)} %pad_maximum_fusion.6), calls=%async_computation | async-start | bytes 2097152 | tf_op jit(solution)/shard_map/all_to_all | solution.py:186
  271.3 40.9 %all-to-all-start.2 = ((bf16[128,32,128]{2,0,1:T(8,128)(2,1)}), bf16[128,32,128]{2,0,1:T(8,128)(2,1)}, u32[]{:S(2)}, u32[]{:S(2)}) async-start(bf16[128,32,128]{2,0,1:T(8,128)(2,1)} %bitcast.481), calls=%async_computation.2 | async-start | bytes 2097152 | tf_op jit(solution)/shard_map/all_to_all | solution.py:188
  339.4 30.9 %all-to-all-start.3 = ((bf16[1024,4,128]{2,1,0:T(4,128)(2,1)}), bf16[1024,4,128]{2,1,0:T(4,128)(2,1)}, u32[]{:S(2)}, u32[]{:S(2)}) async-start(bf16[1024,4,128]{2,1,0:T(4,128)(2,1)} %copy.575), calls=%async_computation.3 | async-start | bytes 2097152 | tf_op jit(solution)/shard_map/all_to_all | solution.py:191
  401.8 233.1 %all-to-all-start.4 = ((bf16[8,4,64,2048]{3,2,1,0:T(8,128)(2,1)}), bf16[8,4,64,2048]{3,2,1,0:T(8,128)(2,1)}, u32[]{:S(2)}, u32[]{:S(2)}) async-start(bf16[8,4,64,2048]{3,2,1,0:T(8,128)(2,1)} %bitcast.463), calls=%async_computation.4 | async-start | bytes 16777216 | tf_op jit(solution)/shard_map/all_to_all | solution.py:208
  634.9 186.2 %all-to-all-start.8 = ((bf16[8,4,64,2048]{3,2,1,0:T(8,128)(2,1)}), bf16[8,4,64,2048]{3,2,1,0:T(8,128)(2,1)}, u32[]{:S(2)}, u32[]{:S(2)}) async-start(bf16[8,4,64,2048]{3,2,1,0:T(8,128)(2,1)} %bitcast.464), calls=%async_computation.8 | async-start | bytes 16777216 | tf_op jit(solution)/shard_map/all_to_all | solution.py:254
  821.1 98.8 %all-to-all-start.5 = ((bf16[8,4,64,2048]{3,2,0,1:T(8,128)(2,1)}), bf16[8,4,64,2048]{3,2,0,1:T(8,128)(2,1)}, u32[]{:S(2)}, u32[]{:S(2)}) async-start(bf16[8,4,64,2048]{3,2,0,1:T(8,128)(2,1)} %copy.585), calls=%async_computation.5 | async-start | bytes 16777216 | tf_op jit(solution)/shard_map/all_to_all | solution.py:207
  920.0 98.8 %all-to-all-start.9 = ((bf16[8,4,64,2048]{3,2,0,1:T(8,128)(2,1)}), bf16[8,4,64,2048]{3,2,0,1:T(8,128)(2,1)}, u32[]{:S(2)}, u32[]{:S(2)}) async-start(bf16[8,4,64,2048]{3,2,0,1:T(8,128)(2,1)} %copy.590), calls=%async_computation.9 | async-start | bytes 16777216 | tf_op jit(solution)/shard_map/all_to_all | solution.py:253
  1052.7 188.4 %all-to-all-start.6 = ((bf16[8,4,64,2048]{3,2,1,0:T(8,128)(2,1)}), bf16[8,4,64,2048]{3,2,1,0:T(8,128)(2,1)}, u32[]{:S(2)}, u32[]{:S(2)}) async-start(bf16[8,4,64,2048]{3,2,1,0:T(8,128)(2,1)} %bitcast.473), calls=%async_computation.6 | async-start | bytes 16777216 | tf_op jit(solution)/shard_map/all_to_all | solution.py:227
  1241.0 187.3 %all-to-all-start.10 = ((bf16[8,4,64,2048]{3,2,1,0:T(8,128)(2,1)}), bf16[8,4,64,2048]{3,2,1,0:T(8,128)(2,1)}, u32[]{:S(2)}, u32[]{:S(2)}) async-start(bf16[8,4,64,2048]{3,2,1,0:T(8,128)(2,1)} %bitcast.472), calls=%async_computation.10 | async-start | bytes 16777216 | tf_op jit(solution)/shard_map/all_to_all | solution.py:272
  1428.3 99.0 %all-to-all-start.7 = ((bf16[8,4,64,2048]{3,2,0,1:T(8,128)(2,1)}), bf16[8,4,64,2048]{3,2,0,1:T(8,128)(2,1)}, u32[]{:S(2)}, u32[]{:S(2)}) async-start(bf16[8,4,64,2048]{3,2,0,1:T(8,128)(2,1)} %copy.587), calls=%async_computation.7 | async-start | bytes 16777216 | tf_op jit(solution)/shard_map/all_to_all | solution.py:226
  1527.3 98.8 %all-to-all-start.11 = ((bf16[8,4,64,2048]{3,2,0,1:T(8,128)(2,1)}), bf16[8,4,64,2048]{3,2,0,1:T(8,128)(2,1)}, u32[]{:S(2)}, u32[]{:S(2)}) async-start(bf16[8,4,64,2048]{3,2,0,1:T(8,128)(2,1)} %copy.592), calls=%async_computation.11 | async-start | bytes 16777216 | tf_op jit(solution)/shard_map/all_to_all | solution.py:271
  1532.9 155.8 %all-gather.10.cloned.1.call-start = ((), (), s32[]{:S(2)}) async-start(), calls=%async_computation.21 | async-start | bytes 4718592 | tf_op jit(solution)/shard_map/all_gather | solution.py:309
  1541.9 26.4 %copy-start.14 = (f32[128,2048]{1,0:T(8,128)S(1)}, f32[128,2048]{1,0:T(8,128)}, u32[]{:S(2)}) copy-start(f32[128,2048]{1,0:T(8,128)} %bitcast_convert_fusion) | copy-start | bytes 3145732
  1541.9 26.4 %copy-start.32 = (f32[128,8]{1,0:T(8,128)S(1)}, f32[128,8]{1,0:T(8,128)}, u32[]{:S(2)}) copy-start(f32[128,8]{1,0:T(8,128)} %copy-done.31) | copy-start | bytes 12292
  1574.6 91.8 %copy-start.39 = (bf16[128,32]{1,0:T(8,128)(2,1)}, bf16[128,32]{1,0:T(8,128)(2,1)S(1)}, u32[]{:S(2)}) copy-start(bf16[128,32]{1,0:T(8,128)(2,1)S(1)} %copy.631) | copy-start | bytes 24580
  1678.0 33.5 %all-to-all-start.12 = ((bf16[128,32,128]{2,0,1:T(8,128)(2,1)}), bf16[128,32,128]{2,0,1:T(8,128)(2,1)}, u32[]{:S(2)}, u32[]{:S(2)}) async-start(bf16[128,32,128]{2,0,1:T(8,128)(2,1)} %bitcast.479), calls=%async_computation.12 | async-start | bytes 2097152 | tf_op jit(solution)/shard_map/all_to_all | solution.py:296
  1685.5 106.6 %all-gather.12.cloned.1.call-start = ((), (), s32[]{:S(2)}) async-start(), calls=%async_computation.22 | async-start | bytes 4718592 | tf_op jit(solution)/shard_map/all_gather | solution.py:310
  1711.5 233.5 %reduce-scatter.5.cloned.1.call-start = ((), (), s32[]{:S(2)}) async-start(), calls=%async_computation.23 | async-start | bytes 5242880 | tf_op jit(solution)/shard_map/reduce_scatter | solution.py:385
  1808.1 36.3 %copy-start.19 = (bf16[128,2048]{1,0:T(8,128)(2,1)S(1)}, bf16[128,2048]{1,0:T(8,128)(2,1)}, u32[]{:S(2)}) copy-start(bf16[128,2048]{1,0:T(8,128)(2,1)} %multiply_convert_fusion.4) | copy-start | bytes 1572868
  1808.1 36.3 %copy-start.40 = (bf16[128,32]{1,0:T(8,128)(2,1)S(1)}, bf16[128,32]{1,0:T(8,128)(2,1)}, u32[]{:S(2)}) copy-start(bf16[128,32]{1,0:T(8,128)(2,1)} %copy-done.39) | copy-start | bytes 24580
  1808.1 28.5 %all-to-all-start.14 = ((bf16[1024,4,128]{2,1,0:T(4,128)(2,1)}), bf16[1024,4,128]{2,1,0:T(4,128)(2,1)S(1)}, u32[]{:S(2)}, u32[]{:S(2)}) async-start(bf16[1024,4,128]{2,1,0:T(4,128)(2,1)} %copy.604), calls=%async_computation.14 | async-start | bytes 2097152 | tf_op jit(solution)/shard_map/all_to_all | solution.py:327
  1814.3 37.0 %copy-start.36 = (f32[128,64]{0,1:T(8,128)S(1)}, f32[128,64]{0,1:T(8,128)}, u32[]{:S(2)}) copy-start(f32[128,64]{0,1:T(8,128)} %copy-done.35) | copy-start | bytes 98308
  1814.3 37.0 %copy-start.38 = (f32[128,64]{0,1:T(8,128)S(1)}, f32[128,64]{0,1:T(8,128)}, u32[]{:S(2)}) copy-start(f32[128,64]{0,1:T(8,128)} %copy-done.37) | copy-start | bytes 98308
  1817.6 34.8 %copy-start.24 = (f32[128,4,128]{0,1,2:T(4,128)S(1)}, f32[128,4,128]{0,1,2:T(4,128)}, u32[]{:S(2)}) copy-start(f32[128,4,128]{0,1,2:T(4,128)} %copy-done.23) | copy-start | bytes 786436
  1817.6 34.8 %copy-start.53 = (f32[128,4]{0,1:T(4,128)S(1)}, f32[128,4]{0,1:T(4,128)}, u32[]{:S(2)}) copy-start(f32[128,4]{0,1:T(4,128)} %copy-done.52) | copy-start | bytes 6148
  1817.6 34.8 %copy-start.66 = (f32[128]{0:T(128)S(1)}, f32[128]{0:T(128)}, u32[]{:S(2)}) copy-start(f32[128]{0:T(128)} %param.25) | copy-start | bytes 1540
  1817.7 35.8 %copy-start.56 = (f32[128,4]{0,1:T(4,128)S(1)}, f32[128,4]{0,1:T(4,128)}, u32[]{:S(2)}) copy-start(f32[128,4]{0,1:T(4,128)} %copy-done.55) | copy-start | bytes 6148
  1837.6 29.3 %all-to-all-start.15 = ((bf16[1024,4,128]{2,1,0:T(4,128)(2,1)}), bf16[1024,4,128]{2,1,0:T(4,128)(2,1)S(1)}, u32[]{:S(2)}, u32[]{:S(2)}) async-start(bf16[1024,4,128]{2,1,0:T(4,128)(2,1)} %copy.610), calls=%async_computation.15 | async-start | bytes 2097152 | tf_op jit(solution)/shard_map/all_to_all | solution.py:330
  1844.4 203.0 %reduce-scatter.7.cloned.1.call-start = ((), (), s32[]{:S(2)}) async-start(), calls=%async_computation.24 | async-start | bytes 9732096
  1844.6 25.2 %copy-start.17 = (bf16[128,2048]{1,0:T(8,128)(2,1)S(1)}, bf16[128,2048]{1,0:T(8,128)(2,1)}, u32[]{:S(2)}) copy-start(bf16[128,2048]{1,0:T(8,128)(2,1)} %fusion.66) | copy-start | bytes 1572868
  1914.0 29.6 %all-to-all-start.13 = ((bf16[1024,4,128]{2,1,0:T(4,128)(2,1)}), bf16[1024,4,128]{2,1,0:T(4,128)(2,1)S(1)}, u32[]{:S(2)}, u32[]{:S(2)}) async-start(bf16[1024,4,128]{2,1,0:T(4,128)(2,1)} %copy.601), calls=%async_computation.13 | async-start | bytes 2097152 | tf_op jit(solution)/shard_map/all_to_all | solution.py:324
  1932.9 22.2 %copy-start.51 = (f32[2048]{0:T(1024)S(1)}, f32[2048]{0:T(1024)}, u32[]{:S(2)}) copy-start(f32[2048]{0:T(1024)} %param.22) | copy-start | bytes 24580
  1932.9 22.2 %copy-start.70 = (f32[128]{0:T(128)S(1)}, f32[128]{0:T(128)}, u32[]{:S(2)}) copy-start(f32[128]{0:T(128)} %copy-done.69) | copy-start | bytes 1540
  1947.5 101.3 %all-to-all-start.16 = ((bf16[8,64,1024]{2,1,0:T(8,128)(2,1)}), bf16[8,64,1024]{2,1,0:T(8,128)(2,1)}, u32[]{:S(2)}, u32[]{:S(2)}) async-start(bf16[8,64,1024]{2,1,0:T(8,128)(2,1)} %bitcast.65), calls=%async_computation.17 | async-start | bytes 2097152 | tf_op jit(solution)/shard_map/all_to_all | solution.py:402
  1955.1 59.4 %copy-start.76 = (f32[128]{0:T(128)S(1)}, f32[128]{0:T(128)}, u32[]{:S(2)}) copy-start(f32[128]{0:T(128)} %copy-done.75) | copy-start | bytes 1540
  1955.1 59.4 %copy-start.10 = (f32[128,2048]{1,0:T(8,128)S(1)}, f32[128,2048]{1,0:T(8,128)}, u32[]{:S(2)}) copy-start(f32[128,2048]{1,0:T(8,128)} %get-tuple-element.219) | copy-start | bytes 3145732
  1955.1 59.4 %copy-start.16 = (f32[128,2048]{1,0:T(8,128)S(1)}, f32[128,2048]{1,0:T(8,128)}, u32[]{:S(2)}) copy-start(f32[128,2048]{1,0:T(8,128)} %copy-done.15) | copy-start | bytes 3145732
  1955.1 59.4 %copy-start.22 = (bf16[1,128,2048]{2,1,0:T(8,128)(2,1)S(1)}, bf16[1,128,2048]{2,1,0:T(8,128)(2,1)}, u32[]{:S(2)}) copy-start(bf16[1,128,2048]{2,1,0:T(8,128)(2,1)} %param.27) | copy-start | bytes 1572868
  1955.1 59.4 %copy-start.46 = (f32[2048]{0:T(1024)S(1)}, f32[2048]{0:T(1024)}, u32[]{:S(2)}) copy-start(f32[2048]{0:T(1024)} %param.23) | copy-start | bytes 24580
  1955.1 59.4 %copy-start.61 = (f32[128]{0:T(128)S(1)}, f32[128]{0:T(128)}, u32[]{:S(2)}) copy-start(f32[128]{0:T(128)} %copy-done.59) | copy-start | bytes 1540
  1955.1 59.4 %copy-start.74 = (f32[128]{0:T(128)S(1)}, f32[128]{0:T(128)}, u32[]{:S(2)}) copy-start(f32[128]{0:T(128)} %copy-done.73) | copy-start | bytes 1540
  (69 other events, 473.3 us)
Sparse Core Ops, SparseCore 0:
  11.7 134.6 all-gather.5
  149.3 158.3 all-gather.7
Sparse Core Ops, SparseCore 1:
  1536.1 74.6 all-gather.9
  1711.6 72.3 all-gather.11
  1806.5 44.5 reduce-scatter.4
  1892.1 155.3 reduce-scatter.6
where the time goes:
time: 2080 us; the launch traced here: 2070 us
  waiting for transfers between devices  1120 us (54%)
  blocking collectives  254 us (12%)
  local copies, waits for them, and re-layouts  235 us (11%)
  matrix products  218 us (10%)
  starting transfers between devices  122 us (6%)
  other arithmetic  98.8 us (5%)
    all_gather x1, blocking collectives, body(): lax.all_gather(w_router, ('seq', 'fsdp'), axis=0, tiled=True)  207 us
    all_to_all x1, waiting for transfers between devices, body(): lax.all_to_all(d_send, 'seq', split_axis=0, concat_axis=0, tiled=True)  173 us
    all_to_all x1, waiting for transfers between devices, body(): lax.all_to_all(d_rows.reshape(slot_shape), 'seq', split_axis=0, concat_ax...  171 us
    all_to_all x1, waiting for transfers between devices, body(): lax.all_to_all(expert_out.reshape(slot_shape), 'seq', split_axis=0, conca...  161 us
    all_gather x1, waiting for transfers between devices, body(): lax.all_gather(query_key_value_weight, ('seq', 'fsdp'), axis=0, tiled=True)  133 us
    all_to_all x1, waiting for transfers between devices, body(): lax.all_to_all(lax.all_to_all(send_rows, 'seq', split_axis=0, concat_axis...  84.9 us
    all_to_all x1, waiting for transfers between devices, body(): lax.all_to_all(lax.all_to_all(expert_out.reshape(slot_shape), 'seq', spli...  84.7 us
    all_to_all x1, waiting for transfers between devices, body(): lax.all_to_all(lax.all_to_all(d_send, 'seq', split_axis=0, concat_axis=0,...  65.9 us
  transfers between devices with their start and end apart: 23, of which 16 were waited for; matrix products, arithmetic and copies ran while one was open for 22% of the time, Pallas kernels for 0%

commit v1 on v0

--- a/solution.py
+++ b/solution.py
@@ -133,7 +133,7 @@
     return (d_query.reshape(query_rows_all.shape), d_key_sum, d_value_sum)
 
 
-def body(
+def routed_body(
     tokens,
     query_key_value_weight,
     w_out_t,
@@ -427,9 +427,261 @@
     )
 
 
+def all_gather_rows(rows, axes):
+    return lax.all_gather(rows, axes, axis=0, tiled=True)
+
+
+def sum_scatter_rows(partial_rows, axes):
+    return lax.psum_scatter(partial_rows, axes, scatter_dimension=0, tiled=True)
+
+
+def head_columns(weight, group_index):
+    rows = weight.shape[0]
+    query_width = QUERY_HEADS * HEAD_DIMENSION
+    key_width = KEY_VALUE_HEADS * HEAD_DIMENSION
+    query = weight[:, :query_width].reshape(rows, len(group_index), -1).transpose(1, 0, 2)
+    keys = weight[:, query_width : query_width + key_width].reshape(rows, KEY_VALUE_HEADS, -1)
+    values = weight[:, query_width + key_width :].reshape(rows, KEY_VALUE_HEADS, -1)
+    keys = jnp.stack([keys[:, group] for group in group_index])
+    values = jnp.stack([values[:, group] for group in group_index])
+    return jnp.concatenate([query, keys, values], axis=2)
+
+
+def gathered_body(
+    tokens,
+    query_key_value_weight,
+    w_out_t,
+    w_router,
+    w_in,
+    w_down,
+    attn_gain,
+    ffn_gain,
+    q_gain,
+    k_gain,
+    routes,
+    cotangent,
+):
+    bf16, f32 = jnp.bfloat16, jnp.float32
+    both = ("seq", "fsdp")
+    seq_size = lax.axis_size("seq")
+    shard_size = lax.axis_size("fsdp")
+    experts = seq_size * shard_size
+    rows = tokens.shape[1]
+    width = tokens.shape[2]
+    length = rows * seq_size
+    weight_rows = query_key_value_weight.shape[0]
+    heads = QUERY_HEADS // seq_size
+    head_cols = heads * HEAD_DIMENSION
+    kv_cols = HEAD_DIMENSION
+    proj_cols = head_cols + 2 * kv_cols
+    all_cols = proj_cols + head_cols
+    group_index = [s * heads * KEY_VALUE_HEADS // QUERY_HEADS for s in range(seq_size)]
+    capacity = 2 * rows * TOPK // experts
+
+    pieces = jnp.concatenate(
+        [
+            head_columns(query_key_value_weight, group_index),
+            w_out_t.reshape(weight_rows, seq_size, head_cols).transpose(1, 0, 2),
+        ],
+        axis=2,
+    )
+    pieces = lax.all_to_all(pieces, "seq", split_axis=0, concat_axis=0, tiled=True)
+    columns = lax.all_gather(pieces, "fsdp", axis=1).reshape(width, all_cols)
+    proj_weight = columns[:, :proj_cols]
+    out_weight = columns[:, proj_cols:]
+    full_router = all_gather_rows(w_router, both)
+    cot_all = all_gather_rows(cotangent[0], both)
+
+    resid_in = tokens[0].astype(f32)
+    normed_one = rms_scale(resid_in, attn_gain).astype(bf16)
+    normed_all = all_gather_rows(normed_one, "seq")
+    projected = jnp.dot(normed_all, proj_weight, preferred_element_type=f32)
+    seq_positions = jnp.arange(length, dtype=jnp.int32)
+    prepare = partial(head_prepare, positions=seq_positions)
+    q_raw = projected[:, :head_cols].reshape(length, heads, HEAD_DIMENSION)
+    k_raw = projected[:, head_cols : head_cols + kv_cols].reshape(length, 1, HEAD_DIMENSION)
+    values = projected[:, head_cols + kv_cols :].astype(bf16).reshape(length, 1, HEAD_DIMENSION)
+    queries = prepare(q_raw, q_gain).astype(bf16)
+    keys = prepare(k_raw, k_gain).astype(bf16)
+    repeat_keys = jnp.repeat(keys, heads, axis=1)
+    repeat_values = jnp.repeat(values, heads, axis=1)
+    mixed_heads, log_total = attend_forward(queries, repeat_keys, repeat_values)
+    attended = mixed_heads.reshape(length, head_cols)
+    attn_part = jnp.einsum("tj,dj->td", attended, out_weight, preferred_element_type=f32)
+    attn_out = sum_scatter_rows(attn_part.astype(bf16), "seq")
+    hidden = resid_in + attn_out.astype(f32)
+    normed_two = rms_scale(hidden, ffn_gain).astype(bf16)
+
+    logits = jnp.dot(normed_two, full_router, preferred_element_type=f32)
+    onehot = routes[0][:, :, None] == jnp.arange(experts, dtype=jnp.int32)
+    onehot_float = onehot.astype(f32)
+    named = jnp.sum(onehot_float, axis=1)
+    chosen = jnp.sum(onehot_float * logits[:, None, :], axis=-1)
+    row_max = jnp.max(chosen, axis=-1, keepdims=True)
+    exp_part = jnp.exp(chosen - row_max)
+    gate_probs = exp_part / jnp.sum(exp_part, axis=-1, keepdims=True)
+    gate_dense = jnp.sum(onehot_float * gate_probs[..., None], axis=1)
+
+    gate_high = gate_dense.astype(bf16)
+    gate_low = (gate_dense - gate_high.astype(f32)).astype(bf16)
+    route_info = jnp.concatenate([gate_high, gate_low, named.astype(bf16)], axis=1)
+    route_info = jnp.pad(route_info, ((0, 0), (0, 128 - route_info.shape[1] % 128)))
+    gathered = all_gather_rows(jnp.concatenate([normed_two, route_info], axis=1), both)
+    blocks = experts
+    rows_all = gathered[:, :width].reshape(blocks, rows, width)
+    info = gathered[:, width : width + 3 * experts].reshape(blocks, rows, 3, experts)
+    me = lax.axis_index("seq") * shard_size + lax.axis_index("fsdp")
+    own = lax.dynamic_index_in_dim(info, me, 3, keepdims=False).astype(f32)
+    gate_own = own[:, :, 0] + own[:, :, 1]
+    named_own = own[:, :, 2]
+    slot = jnp.cumsum(named_own, axis=1) - named_own
+    pick = (
+        (slot[:, None, :] == jnp.arange(capacity, dtype=f32)[None, :, None])
+        & (named_own[:, None, :] > 0)
+    ).astype(bf16)
+    gate_slots = jnp.einsum(
+        "bct,bt->bc", pick.astype(f32), gate_own, precision=lax.Precision.HIGHEST
+    ).reshape(-1, 1)
+    rows_in = jnp.einsum("bct,btd->bcd", pick, rows_all, preferred_element_type=f32)
+    rows_in = rows_in.astype(bf16).reshape(-1, width)
+    cot_rows = jnp.einsum(
+        "bct,btd->bcd",
+        pick,
+        cot_all.reshape(blocks, rows, width),
+        preferred_element_type=f32,
+    ).reshape(-1, width)
+
+    gate_weight = w_in[0]
+    down_weight = w_down[0]
+    gate_up = jnp.dot(rows_in, gate_weight, preferred_element_type=f32)
+    gate_half = gate_up[:, :FF]
+    up_half = gate_up[:, FF:]
+    gate_sig = jax.nn.sigmoid(gate_half)
+    silu_gate = gate_half * gate_sig
+    inner_act = (silu_gate * up_half).astype(bf16)
+    expert_out = (
+        jnp.dot(inner_act, down_weight, preferred_element_type=f32).astype(bf16).astype(f32)
+    )
+    d_gate_slots = jnp.sum(expert_out * cot_rows, axis=1)
+    weighted = (gate_slots * expert_out).astype(bf16).reshape(blocks, capacity, width)
+    out_part = jnp.einsum("bct,bcd->btd", pick, weighted, preferred_element_type=f32)
+    mixture = sum_scatter_rows(out_part.astype(bf16).reshape(-1, width), both)
+    output = (hidden + mixture.astype(f32)).astype(bf16)
+
+    d_expert = (gate_slots * cot_rows).astype(bf16)
+    d_inner = jnp.einsum("rd,fd->rf", d_expert, down_weight, preferred_element_type=f32)
+    d_gate_half = d_inner * up_half * gate_sig * (1.0 + gate_half * (1.0 - gate_sig))
+    d_up_half = d_inner * silu_gate
+    d_gate_up = jnp.concatenate([d_gate_half, d_up_half], axis=1).astype(bf16)
+    d_w_down = jnp.einsum("rf,rd->fd", inner_act, d_expert, preferred_element_type=f32)[None]
+    d_w_in = jnp.einsum("rd,rf->df", rows_in, d_gate_up, preferred_element_type=f32)[None]
+    d_rows = jnp.einsum("rf,df->rd", d_gate_up, gate_weight, preferred_element_type=f32)
+    d_rows = d_rows.astype(bf16).reshape(blocks, capacity, width)
+    d_gate_own = jnp.einsum(
+        "bct,bc->bt",
+        pick.astype(f32),
+        d_gate_slots.reshape(blocks, capacity),
+        precision=lax.Precision.HIGHEST,
+    )
+    d_gate_high = d_gate_own.astype(bf16)
+    d_gate_low = (d_gate_own - d_gate_high.astype(f32)).astype(bf16)
+    mine = (jnp.arange(experts, dtype=jnp.int32) == me).astype(bf16)
+    d_info = jnp.concatenate([d_gate_high[..., None] * mine, d_gate_low[..., None] * mine], axis=2)
+    d_info = jnp.pad(d_info, ((0, 0), (0, 0), (0, 128 - d_info.shape[2] % 128)))
+    d_part = jnp.einsum("bct,bcd->btd", pick, d_rows, preferred_element_type=f32)
+    d_part = jnp.concatenate([d_part.astype(bf16), d_info], axis=2)
+    d_back = sum_scatter_rows(d_part.reshape(-1, d_part.shape[2]), both).astype(f32)
+
+    d_gate_dense = d_back[:, width : width + experts] + d_back[:, width + experts : width + 2 * experts]
+    d_gates = jnp.sum(onehot_float * d_gate_dense[:, None, :], axis=-1)
+    d_chosen = gate_probs * (d_gates - jnp.sum(gate_probs * d_gates, axis=-1, keepdims=True))
+    d_logits = jnp.sum(d_chosen[..., None] * onehot_float, axis=1).astype(bf16)
+    d_normed_two = d_back[:, :width] + jnp.einsum(
+        "te,de->td", d_logits, full_router, preferred_element_type=f32
+    )
+    out_grad = cotangent[0].astype(f32)
+    unused_two, pull_two = jax.vjp(rms_scale, hidden, ffn_gain)
+    d_hidden_norm, d_ffn_gain = pull_two(d_normed_two)
+    d_hidden = out_grad + d_hidden_norm
+    d_attn = d_hidden.astype(bf16)
+
+    d_attn_all = all_gather_rows(d_attn, "seq")
+    d_attended = jnp.dot(d_attn_all, out_weight, preferred_element_type=f32).astype(bf16)
+    d_query, d_key_sum, d_value_sum = attend_backward(
+        queries,
+        repeat_keys,
+        repeat_values,
+        log_total,
+        d_attended.reshape(length, heads, HEAD_DIMENSION),
+    )
+    unused_q, pull_q = jax.vjp(prepare, q_raw, q_gain)
+    d_q_raw, d_q_gain = pull_q(d_query)
+    unused_k, pull_k = jax.vjp(prepare, k_raw, k_gain)
+    d_k_raw, d_k_gain = pull_k(jnp.sum(d_key_sum, axis=1, keepdims=True))
+    d_projected = jnp.concatenate(
+        [
+            d_q_raw.reshape(length, head_cols),
+            d_k_raw.reshape(length, kv_cols),
+            jnp.sum(d_value_sum, axis=1),
+        ],
+        axis=1,
+    ).astype(bf16)
+    d_normed_part = jnp.einsum("tj,dj->td", d_projected, proj_weight, preferred_element_type=f32)
+    d_normed_one = sum_scatter_rows(d_normed_part.astype(bf16), "seq").astype(f32)
+    unused_one, pull_one = jax.vjp(rms_scale, resid_in, attn_gain)
+    d_resid_norm, d_attn_gain = pull_one(d_normed_one)
+    d_tokens = (d_hidden + d_resid_norm).astype(bf16)[None]
+
+    d_columns = jnp.concatenate(
+        [
+            jnp.einsum("tc,tj->cj", normed_all, d_projected, preferred_element_type=f32),
+            jnp.einsum("tc,tj->cj", d_attn_all, attended, preferred_element_type=f32),
+        ],
+        axis=1,
+    ).astype(bf16)
+    d_columns = (
+        d_columns.reshape(seq_size, shard_size, weight_rows, all_cols)
+        .transpose(1, 0, 2, 3)
+        .reshape(width, all_cols)
+    )
+    d_columns = sum_scatter_rows(d_columns, "fsdp").reshape(seq_size, weight_rows, all_cols)
+    d_pieces = lax.all_to_all(d_columns, "seq", split_axis=0, concat_axis=0, tiled=True).astype(f32)
+    d_pieces = d_pieces.transpose(1, 0, 2)
+    per_group = seq_size // KEY_VALUE_HEADS
+    d_kv = d_pieces[:, :, head_cols:proj_cols].reshape(
+        weight_rows, KEY_VALUE_HEADS, per_group, 2, kv_cols
+    )
+    d_kv = jnp.sum(d_kv, axis=2).transpose(0, 2, 1, 3).reshape(weight_rows, -1)
+    d_w_qkv = jnp.concatenate([d_pieces[:, :, :head_cols].reshape(weight_rows, -1), d_kv], axis=1)
+    d_w_out_t = d_pieces[:, :, proj_cols:].reshape(weight_rows, -1)
+    d_w_router = sum_scatter_rows(
+        jnp.einsum("tc,te->ce", normed_two, d_logits, preferred_element_type=f32), both
+    )
+    d_attn_gain, d_ffn_gain, d_q_gain, d_k_gain = lax.psum(
+        (d_attn_gain, d_ffn_gain, d_q_gain, d_k_gain), both
+    )
+    return (
+        output[None],
+        d_tokens,
+        d_w_qkv,
+        d_w_out_t,
+        d_w_router,
+        d_w_in,
+        d_w_down,
+        d_attn_gain,
+        d_ffn_gain,
+        d_q_gain,
+        d_k_gain,
+    )
+
+
+def gathered_fits(mesh):
+    return mesh.shape["seq"] * mesh.shape["fsdp"] <= 4 * TOPK
+
+
 def solution(mesh):
     return jax.shard_map(
-        body,
+        gathered_body if gathered_fits(mesh) else routed_body,
         mesh=mesh,
         in_specs=(
             P("fsdp", "seq", None),

time: 2080 us -> 1520 us (0.73)
  local copies, waits for them, and re-layouts: 235 us -> 84.4 us
  waiting for transfers between devices: 1120 us -> 972 us
  blocking collectives: 254 us -> 117 us
  starting transfers between devices: 122 us -> 6.64 us
  other arithmetic: 98.8 us -> 73.1 us
    all_to_all x17 -> x1, waiting for transfers between devices: 951 us -> 0.01 us  [gathered_body(): lax.all_to_all(d_columns, 'seq', split_axis=0, concat_axis=0, tiled=True)]
    reduce_scatter x1 -> x5, waiting for transfers between devices: 0.01 us -> 494 us  [sum_scatter_rows(): return lax.psum_scatter(partial_rows, axes, scatter_dimension=0, tiled=True)]
    all_gather x4 -> x5, waiting for transfers between devices: 133 us -> 378 us  [the longest x4 344 us: all_gather_rows(): return lax.all_gather(rows, axes, axis=0, tiled=True)]
    all_gather x1, blocking collectives: 207 us -> 35.2 us  [all_gather_rows(): return lax.all_gather(rows, axes, axis=0, tiled=True)]
    all_to_all x17 -> x1, starting transfers between devices: 122 us -> 6.01 us  [gathered_body(): lax.all_to_all(d_columns, 'seq', split_axis=0, concat_axis=0, tiled=True)]
    all_to_all x15 -> x1, local copies, waits for them, and re-layouts: 81 us -> 1.78 us  [gathered_body(): lax.all_to_all(pieces, 'seq', split_axis=0, concat_axis=0, tiled=True)]
    unnamed x7 -> x12, waiting for transfers between devices: 31.7 us -> 100 us
    gather x2 -> x0, local copies, waits for them, and re-layouts: 53 us -> none  [unpack_slots(): buffer[expert_ids // buffer.shape[1], expert_ids % buffer.shape[1], slot_...]
  transfers between devices with their start and end apart: 23 -> 12, of which waited for: 16 -> 11; matrix products, arithmetic and copies ran while one was open for 22% -> 7% of each run, Pallas kernels for 0% -> 0%
where the time goes in v1:
time: 1520 us; the launch traced here: 1500 us
  waiting for transfers between devices  972 us (64%)
  matrix products  226 us (15%)
  blocking collectives  117 us (8%)
  local copies, waits for them, and re-layouts  84.4 us (6%)
  other arithmetic  73.1 us (5%)
    reduce_scatter x5, waiting for transfers between devices, sum_scatter_rows(): return lax.psum_scatter(partial_rows, axes, scatter_dimension=0, tiled=True)  494 us
    all_gather x4, waiting for transfers between devices, all_gather_rows(): return lax.all_gather(rows, axes, axis=0, tiled=True)  344 us
    unnamed x12, waiting for transfers between devices  100 us
    psum x1, blocking collectives, gathered_body(): lax.psum((d_attn_gain, d_ffn_gain, d_q_gain, d_k_gain), both)  45.9 us
    all_to_all x1, blocking collectives, gathered_body(): lax.all_to_all(pieces, 'seq', split_axis=0, concat_axis=0, tiled=True)  35.5 us
    all_gather x1, blocking collectives, all_gather_rows(): return lax.all_gather(rows, axes, axis=0, tiled=True)  35.2 us
    all_gather x1, waiting for transfers between devices, gathered_body(): columns = lax.all_gather(pieces, 'fsdp', axis=1).reshape(width, all_cols)  33.4 us
  transfers between devices with their start and end apart: 12, of which 11 were waited for; matrix products, arithmetic and copies ran while one was open for 7% of the time, Pallas kernels for 0%

profile of v1, /device:TPU:16, one launch (start us, length us, event | category | flops | bytes accessed | tf_op | source)
XLA Modules:
  0.0 1502.0 jit_solution(16058212498634635540)
XLA Ops:
  16.8 35.5 %all_to_all.10 = bf16[8,64,1280]{2,1,0:T(8,128)(2,1)S(1)} all-to-all(bf16[8,64,1280]{2,1,0:T(8,128)(2,1)S(1)} %copy.255), channel_id=1, replica_groups=mesh['seq'=8,'fsdp'=4] {'seq'}, dimensions={0} | all-to-all | bytes 2621440 | tf_op jit(solution)/shard_map/all_to_all | solution.py:488
  58.5 3.1 multiply_cosine_fusion
  61.6 33.4 %all-gather.15.cloned.1.call-done = bf16[8,256,1280]{2,0,1:T(8,128)(2,1)} async-done(((bf16[8,64,1280]{2,0,1:T(8,128)(2,1)}), bf16[8,256,1280]{2,0,1:T(8,128)(2,1)}) %all-gather.15.cloned.1.call-update) | async-done | bytes 5242896 | tf_op jit(solution)/shard_map/all_gather | solution.py:489
  95.0 5.9 copy.257
  100.9 69.4 %all-gather.9.cloned.1.call-done = bf16[1024,2048]{1,0:T(8,128)(2,1)} async-done(((bf16[128,2048]{1,0:T(8,128)(2,1)}), bf16[1024,2048]{1,0:T(8,128)(2,1)}) %all-gather.9.cloned.1.call-update) | async-done | bytes 4194320 | tf_op jit(solution)/shard_map/all_gather | solution.py:431
  170.3 6.2 fusion.57
  184.7 2.9 copy.258
  192.1 23.0 %while.28 = (s32[]{:T(128)}, bf16[2,512,4,128]{3,2,1,0:T(4,128)(2,1)}, f32[2,4,512]{2,1,0:T(4,128)S(1)}, s32[2]{0:T(128)S(1)}, bf16[1024,4,128]{2,0,1:T(8,128)(2...) while((s32[]{:T(128)}, ...), condition=%wide.region_6.7_spmd.clone, body=%wide.region_3.6_spmd.clone.sunk | while | flops 1099692544 | bytes 39391508 | solution.py:91
  194.2 2.8 fusion.184
  199.5 2.9 fusion.186
  205.5 2.8 fusion.184
  210.7 2.9 fusion.186
  215.1 6.4 convolution_convert_fusion.5
  222.2 35.2 %all-gather.2 = bf16[32,64,32]{1,2,0:T(8,128)(2,1)S(1)} all-gather(bf16[1,64,32]{1,2,0:T(8,128)(2,1)S(1)} %bitcast.281), channel_id=1, replica_groups=mesh['seq'=8,'fsdp'=4] {'seq','fsdp'}, dimensions={0}, use_global_device_ids=true | all-gather | bytes 135168 | tf_op jit(solution)/shard_map/all_gather | solution.py:431
  257.8 51.8 %reduce-scatter.9.cloned.1.call-done = bf16[128,2048]{1,0:T(8,128)(2,1)} async-done(((bf16[1024,2048]{1,0:T(8,128)(2,1)}), bf16[128,2048]{1,0:T(8,128)(2,1)}) %reduce-scatter.9.cloned.1.call-update) | async-done | bytes 524304 | tf_op jit(solution)/shard_map/reduce_scatter | solution.py:435
  318.0 118.4 %all-gather.11.cloned.1.call-done = bf16[4096,2176]{1,0:T(8,128)(2,1)} async-done(((bf16[128,2176]{1,0:T(8,128)(2,1)}), bf16[4096,2176]{1,0:T(8,128)(2,1)}) %all-gather.11.cloned.1.call-update) | async-done | bytes 17825808 | tf_op jit(solution)/shard_map/all_gather | solution.py:431
  443.7 14.2 slice.162
  457.9 11.4 convolution_convert_fusion.4
  469.3 83.3 %all-gather.17.cloned.1.call-done = bf16[1,4096,2048]{2,1,0:T(8,128)(2,1)} async-done(((bf16[1,128,2048]{2,1,0:T(8,128)(2,1)}), bf16[1,4096,2048]{2,1,0:T(8,128)(2,1)}) %all-gather.17.cloned.1.call-update) | async-done | bytes 16777232 | tf_op jit(solution)/shard_map/all_gather | solution.py:431
  552.6 13.0 multiply_convert_fusion.1
  565.6 19.1 %fusion.50 = f32[2048,1536]{0,1:T(8,128)} fusion(bf16[2048,2048]{1,0:T(8,128)(2,1)} %bitcast.244, bf16[1,2048,1536]{2,1,0:T(8,128)(2,1)} %param.20), kind=kOutput, calls=%fused_computation.70 | convolution fusion | flops 12884901888 | bytes 27262976 | tf_op jit(solution)/shard_map/dot_general | solution.py:556
  584.8 14.1 multiply_convert_fusion.3
  598.8 16.6 %fusion.48 = (bf16[2048,2048]{1,0:T(8,128)(2,1)}, f32[2048]{0:T(1024)S(1)}, bf16[2048,2048]{1,0:T(8,128)(2,1)}) fusion(f32[32,64,2048]{2,1,0:T(8,128)} %get-tuple-element.376, f32[2048]{0:T(1024)S(1)} %mul.673, bf16[2048,768]{0,1:T(8,128)(2,1)S(1)} %get-tuple-element.345, bf16[1,768,2048]{2,1,0:T(8,128)(2,1)S(1)} %copy-done), kind=kOutput, calls=%fused_computation.61 | convolution fusion | flops 6476003328 | bytes 39862272 | tf_op jit(solution)/shard_map/dot_general | solution.py:563
  616.1 19.6 %convolution_convert_fusion.2 = bf16[2048,2048]{1,0:T(8,128)(2,1)} fusion(bf16[1,2048,1536]{2,1,0:T(8,128)(2,1)} %param.20, bf16[2048,768]{0,1:T(8,128)(2,1)} %get-tuple-element.342, bf16[2048,768]{0,1:T(8,128)(2,1)} %get-tuple-element.341), kind=kOutput, calls=%fused_computation.66 | convolution fusion | flops 12901679104 | bytes 20971520 | tf_op jit(solution)/shard_map/rf,df->rd/dot_general | solution.py:578
  635.7 13.7 convolution_convert_fusion
  651.4 14.4 pad_maximum_fusion
  665.9 192.0 %reduce-scatter.13.cloned.1.call-done = bf16[128,2176]{1,0:T(8,128)(2,1)} async-done(((bf16[4096,2176]{1,0:T(8,128)(2,1)}), bf16[128,2176]{1,0:T(8,128)(2,1)}) %reduce-scatter.13.cloned.1.call-update) | async-done | bytes 557072 | tf_op jit(solution)/shard_map/reduce_scatter | solution.py:435
  866.2 73.2 %all-gather.13.cloned.1.call-done = bf16[1024,2048]{1,0:T(8,128)(2,1)} async-done(((bf16[128,2048]{1,0:T(8,128)(2,1)}), bf16[1024,2048]{1,0:T(8,128)(2,1)}) %all-gather.13.cloned.1.call-update) | async-done | bytes 4194320 | tf_op jit(solution)/shard_map/all_gather | solution.py:431
  939.4 6.2 fusion.65
  945.7 38.1 %while.29 = (s32[]{:T(128)}, f32[1024,4,128]{0,2,1:T(8,128)S(1)}, f32[1024,4,128]{0,2,1:T(8,128)}, f32[2,512,4,128]{3,1,0,2:T(8,128)}, s32[2]{0:T(128)S(1)}, /*i...) while((s32[]{:T(128)}, f32[1024,4,128]{0,2,1:T(8,128)S(1)}, ...), condition=%wide.region_24.25_spmd.clone, body=%wide.region_22.24_spmd.clone.sunk | while | flops 2719218176 | bytes 119337416 | solution.py:128
  951.8 2.9 bitcast_add_fusion.5
  954.7 3.5 multiply_reduce_fusion.10
  970.8 2.9 bitcast_add_fusion.5
  973.7 3.5 multiply_reduce_fusion.10
  999.2 6.5 copy.274
  1005.8 4.7 convolution_convert_fusion.8
  1010.5 3.8 convolution_convert_fusion.7
  1019.9 7.0 convolution_convert_fusion.6
  1027.6 14.6 convolution_convert_fusion.1
  1044.1 18.1 %convolution_bitcast_fusion = f32[1,2048,1536]{2,1,0:T(8,128)} fusion(bf16[2048,2048]{1,0:T(8,128)(2,1)} %bitcast.245, bf16[2048,768]{0,1:T(8,128)(2,1)} %get-tuple-element.342, bf16[2048,768]{0,1:T(8,128)(2,1)S(1)} %copy-done.92), kind=kOutput, calls=%fused_computation.65 | convolution fusion | flops 12897484800 | bytes 27262976 | tf_op jit(solution)/shard_map/rd,rf->df/dot_general | solution.py:577
  1062.3 5.9 reduce-scatter.17.cloned.1.call-done
  1068.1 6.0 all-to-all-start.1
  1074.3 11.8 convolution_bitcast_fusion.1
  1086.1 99.4 %reduce-scatter.19.cloned.1.call-done = f32[64,32]{1,0:T(8,128)} async-done(((f32[2048,32]{1,0:T(8,128)}), f32[64,32]{1,0:T(8,128)}) %reduce-scatter.19.cloned.1.call-update) | async-done | bytes 8208
  1187.0 107.2 %reduce-scatter.15.cloned.1.call-done = bf16[128,2048]{1,0:T(8,128)(2,1)} async-done(((bf16[1024,2048]{1,0:T(8,128)(2,1)}), bf16[128,2048]{1,0:T(8,128)(2,1)}) %reduce-scatter.15.cloned.1.call-update) | async-done | bytes 524304 | tf_op jit(solution)/shard_map/reduce_scatter | solution.py:435
  1295.8 45.9 %all-reduce.6 = (f32[2048]{0:T(1024)}, f32[2048]{0:T(1024)}, f32[128]{0:T(128)}, f32[128]{0:T(128)}) all-reduce(f32[2048]{0:T(1024)S(1)} %get-tuple-element.291, f32[2048]{0:T(1024)S(1)} %copy-done.67, f32[128]{0:T(128)S(1)} %get-tuple-element.285, f32[128]{0:T(128)S(1)} %get-tuple-element.287), channel_id=1, replica_groups=mesh['seq'=8,'fsdp'=4] {'seq','fsdp'}, use_global_device_ids=true, to_apply=%region_35.36 | all-reduce | flops 4352 | bytes 34816 | tf_op jit(solution)/shard_map/psum | solution.py:660
  1341.7 137.6 %reduce-scatter.11.cloned.1.call-done = bf16[128,2048]{1,0:T(8,128)(2,1)} async-done(((bf16[4096,2048]{1,0:T(8,128)(2,1)}), bf16[128,2048]{1,0:T(8,128)(2,1)}) %reduce-scatter.11.cloned.1.call-update) | async-done | bytes 524304 | tf_op jit(solution)/shard_map/reduce_scatter | solution.py:435
  1479.4 3.0 fusion.95
  (363 shorter events, 124.6 us)
Async XLA Ops:
  7.2 577.6 %copy-start = (bf16[1,768,2048]{2,1,0:T(8,128)(2,1)S(1)}, bf16[1,768,2048]{2,1,0:T(8,128)(2,1)}, u32[]{:S(2)}) copy-start(bf16[1,768,2048]{2,1,0:T(8,128)(2,1)} %param.21) | copy-start | bytes 9437188
  7.2 87.8 %all-gather.15.cloned.1.call-start = ((), (), s32[]{:S(2)}) async-start(), calls=%async_computation.16 | async-start | bytes 6553600 | tf_op jit(solution)/shard_map/all_gather | solution.py:489
  16.8 39.6 %copy-start.55 = (f32[2048]{0:T(1024)S(1)}, f32[2048]{0:T(1024)}, u32[]{:S(2)}) copy-start(f32[2048]{0:T(1024)} %param.22) | copy-start | bytes 24580
  54.0 116.3 %all-gather.9.cloned.1.call-start = ((), (), s32[]{:S(2)}) async-start(), calls=%async_computation.8 | async-start | bytes 4718592 | tf_op jit(solution)/shard_map/all_gather | solution.py:431
  58.4 251.1 %reduce-scatter.9.cloned.1.call-start = ((), (), s32[]{:S(2)}) async-start(), calls=%async_computation.9 | async-start | bytes 4718592 | tf_op jit(solution)/shard_map/reduce_scatter | solution.py:435
  58.5 123.2 %copy-start.80 = (f32[64]{0:T(128)}, f32[64]{0:T(128)S(1)}, u32[]{:S(2)}) copy-start(f32[64]{0:T(128)S(1)} %multiply_power_fusion) | copy-start | bytes 772
  58.5 123.2 %copy-start.59 = (f32[1024]{0:T(1024)}, f32[1024]{0:T(1024)S(1)}, u32[]{:S(2)}) copy-start(f32[1024]{0:T(1024)S(1)} %iota_convert_fusion) | copy-start | bytes 12292
  221.5 90.1 %copy-start.50 = (f32[2048]{0:T(1024)S(1)}, f32[2048]{0:T(1024)}, u32[]{:S(2)}) copy-start(f32[2048]{0:T(1024)} %param.23) | copy-start | bytes 24580
  221.5 92.6 %copy-start.63 = (s32[1,128,8]{1,2,0:T(8,128)S(1)}, s32[1,128,8]{1,2,0:T(8,128)}, u32[]{:S(2)}) copy-start(s32[1,128,8]{1,2,0:T(8,128)} %param.26) | copy-start | bytes 12292
  221.5 214.9 %all-gather.11.cloned.1.call-start = ((), (), s32[]{:S(2)}) async-start(), calls=%async_computation.10 | async-start | bytes 18382848 | tf_op jit(solution)/shard_map/all_gather | solution.py:431
  257.7 183.3 %copy-start.33 = (bf16[2048,32]{0,1:T(8,128)(2,1)}, bf16[2048,32]{0,1:T(8,128)(2,1)S(1)}, u32[]{:S(2)}) copy-start(bf16[2048,32]{0,1:T(8,128)(2,1)S(1)} %reshape.568) | copy-start | bytes 393220
  314.2 129.4 %copy-start.48 = (f32[128,8]{0,1:T(8,128)}, f32[128,8]{0,1:T(8,128)S(1)}, u32[]{:S(2)}) copy-start(f32[128,8]{0,1:T(8,128)S(1)} %select_reduce_fusion.3) | copy-start | bytes 12292
  317.3 235.3 %all-gather.17.cloned.1.call-start = ((), (), s32[]{:S(2)}) async-start(), calls=%async_computation.17 | async-start | bytes 17301504 | tf_op jit(solution)/shard_map/all_gather | solution.py:431
  317.9 539.9 %reduce-scatter.13.cloned.1.call-start = ((), (), s32[]{:S(2)}) async-start(), calls=%async_computation.12 | async-start | bytes 18382848 | tf_op jit(solution)/shard_map/reduce_scatter | solution.py:435
  442.6 193.1 %copy-start.40 = (pred[32,128]{1,0:T(8,128)(4,1)}, pred[32,128]{1,0:T(8,128)(4,1)S(1)}, u32[]{:S(2)}) copy-start(pred[32,128]{1,0:T(8,128)(4,1)S(1)} %broadcast_compare_fusion) | copy-start | bytes 12292
  442.7 193.1 %copy-start.31 = (f32[32,128]{1,0:T(8,128)}, f32[32,128]{1,0:T(8,128)S(1)}, u32[]{:S(2)}) copy-start(f32[32,128]{1,0:T(8,128)S(1)} %fusion.140) | copy-start | bytes 49156
  565.6 19.1 %copy-start.8 = (bf16[32,64,2048]{2,1,0:T(8,128)(2,1)S(1)}, bf16[32,64,2048]{2,1,0:T(8,128)(2,1)}, u32[]{:S(2)}) copy-start(bf16[32,64,2048]{2,1,0:T(8,128)(2,1)} %get-tuple-element.375) | copy-start | bytes 25165828
  665.7 193.4 %copy-start.64 = (s32[1,128,8]{1,2,0:T(8,128)S(1)}, s32[1,128,8]{1,2,0:T(8,128)}, u32[]{:S(2)}) copy-start(s32[1,128,8]{1,2,0:T(8,128)} %param.26) | copy-start | bytes 12292
  665.7 193.5 %copy-start.49 = (f32[128,8]{0,1:T(8,128)S(1)}, f32[128,8]{0,1:T(8,128)}, u32[]{:S(2)}) copy-start(f32[128,8]{0,1:T(8,128)} %copy-done.48) | copy-start | bytes 12292
  665.7 193.5 %copy-start.69 = (f32[128]{0:T(128)S(1)}, f32[128]{0:T(128)}, u32[]{:S(2)}) copy-start(f32[128]{0:T(128)} %copy-done.68) | copy-start | bytes 1540
  665.7 193.5 %copy-start.74 = (f32[128]{0:T(128)S(1)}, f32[128]{0:T(128)}, u32[]{:S(2)}) copy-start(f32[128]{0:T(128)} %copy-done.73) | copy-start | bytes 1540
  665.7 194.3 %copy-start.4 = (bf16[1,128,2048]{2,1,0:T(8,128)(2,1)S(1)}, bf16[1,128,2048]{2,1,0:T(8,128)(2,1)}, u32[]{:S(2)}) copy-start(bf16[1,128,2048]{2,1,0:T(8,128)(2,1)} %param.16) | copy-start | bytes 1572868
  665.7 194.3 %copy-start.10 = (bf16[128,2048]{1,0:T(8,128)(2,1)S(1)}, bf16[128,2048]{1,0:T(8,128)(2,1)}, u32[]{:S(2)}) copy-start(bf16[128,2048]{1,0:T(8,128)(2,1)} %reduce-scatter.9.cloned.1.call-done) | copy-start | bytes 1572868
  665.8 194.3 %copy-start.34 = (bf16[2048,32]{0,1:T(8,128)(2,1)S(1)}, bf16[2048,32]{0,1:T(8,128)(2,1)}, u32[]{:S(2)}) copy-start(bf16[2048,32]{0,1:T(8,128)(2,1)} %copy-done.33) | copy-start | bytes 393220
  665.8 194.3 %copy-start.51 = (f32[2048]{0:T(1024)S(1)}, f32[2048]{0:T(1024)}, u32[]{:S(2)}) copy-start(f32[2048]{0:T(1024)} %param.23) | copy-start | bytes 24580
  665.8 194.3 %copy-start.71 = (f32[128]{0:T(128)S(1)}, f32[128]{0:T(128)}, u32[]{:S(2)}) copy-start(f32[128]{0:T(128)} %copy-done.70) | copy-start | bytes 1540
  665.8 196.6 %copy-start.89 = (f32[128]{0:T(128)S(1)}, f32[128]{0:T(128)}, u32[]{:S(2)}) copy-start(f32[128]{0:T(128)} %copy-done.88) | copy-start | bytes 1540
  665.8 196.7 %copy-start.27 = (bf16[1,128,2048]{2,1,0:T(8,128)(2,1)S(1)}, bf16[1,128,2048]{2,1,0:T(8,128)(2,1)}, u32[]{:S(2)}) copy-start(bf16[1,128,2048]{2,1,0:T(8,128)(2,1)} %param.27) | copy-start | bytes 1572868
  665.8 273.6 %all-gather.13.cloned.1.call-start = ((), (), s32[]{:S(2)}) async-start(), calls=%async_computation.13 | async-start | bytes 4718592 | tf_op jit(solution)/shard_map/all_gather | solution.py:431
  863.8 204.3 %reduce-scatter.17.cloned.1.call-start = ((), (), s32[]{:S(2)}) async-start(), calls=%async_computation.15 | async-start | bytes 6553600 | tf_op jit(solution)/shard_map/reduce_scatter | solution.py:435
  866.2 79.5 %copy-start.7 = (bf16[1024,128]{1,0:T(8,128)(2,1)S(1)}, bf16[1024,128]{1,0:T(8,128)(2,1)}, u32[]{:S(2)}) copy-start(bf16[1024,128]{1,0:T(8,128)(2,1)} %copy-done.6) | copy-start | bytes 786436
  866.2 79.5 %copy-start.13 = (bf16[1024,128]{1,0:T(8,128)(2,1)S(1)}, bf16[1024,128]{1,0:T(8,128)(2,1)}, u32[]{:S(2)}) copy-start(bf16[1024,128]{1,0:T(8,128)(2,1)} %get-tuple-element.590) | copy-start | bytes 786436
  866.2 79.5 %copy-start.54 = (f32[2,4,512]{2,1,0:T(4,128)S(1)}, f32[2,4,512]{2,1,0:T(4,128)}, u32[]{:S(2)}) copy-start(f32[2,4,512]{2,1,0:T(4,128)} %copy-done.53) | copy-start | bytes 49156
  1017.5 168.0 %reduce-scatter.19.cloned.1.call-start = ((), (), s32[]{:S(2)}) async-start(), calls=%async_computation.18 | async-start | bytes 1081344
  1019.9 274.3 %reduce-scatter.15.cloned.1.call-start = ((), (), s32[]{:S(2)}) async-start(), calls=%async_computation.14 | async-start | bytes 4718592 | tf_op jit(solution)/shard_map/reduce_scatter | solution.py:435
  1026.9 452.4 %reduce-scatter.11.cloned.1.call-start = ((), (), s32[]{:S(2)}) async-start(), calls=%async_computation.11 | async-start | bytes 17301504 | tf_op jit(solution)/shard_map/reduce_scatter | solution.py:435
  1068.1 414.3 %all-to-all-start.1 = ((bf16[8,64,1280]{2,1,0:T(8,128)(2,1)}), bf16[8,64,1280]{2,1,0:T(8,128)(2,1)}, u32[]{:S(2)}, u32[]{:S(2)}) async-start(bf16[8,64,1280]{2,1,0:T(8,128)(2,1)} %bitcast.264), calls=%async_computation.6 | async-start | bytes 2621440 | tf_op jit(solution)/shard_map/all_to_all | solution.py:648
  1074.2 220.0 %copy-start.5 = (bf16[1,128,2048]{2,1,0:T(8,128)(2,1)S(1)}, bf16[1,128,2048]{2,1,0:T(8,128)(2,1)}, u32[]{:S(2)}) copy-start(bf16[1,128,2048]{2,1,0:T(8,128)(2,1)} %param.16) | copy-start | bytes 1572868
  1074.2 220.0 %copy-start.56 = (f32[2048]{0:T(1024)S(1)}, f32[2048]{0:T(1024)}, u32[]{:S(2)}) copy-start(f32[2048]{0:T(1024)} %param.22) | copy-start | bytes 24580
  1074.2 220.0 %copy-start.79 = (f32[128]{0:T(128)S(1)}, f32[128]{0:T(128)}, u32[]{:S(2)}) copy-start(f32[128]{0:T(128)} %copy-done.78) | copy-start | bytes 1540
  1074.2 221.6 %copy-start.67 = (f32[2048]{0:T(1024)S(1)}, f32[2048]{0:T(1024)}, u32[]{:S(2)}) copy-start(f32[2048]{0:T(1024)} %get-tuple-element.289) | copy-start | bytes 24580
  1074.2 267.6 %copy-start.87 = (f32[128]{0:T(128)S(1)}, f32[128]{0:T(128)}, u32[]{:S(2)}) copy-start(f32[128]{0:T(128)} %copy-done.86) | copy-start | bytes 1540
  1074.2 405.2 %copy-start.11 = (bf16[128,2048]{1,0:T(8,128)(2,1)S(1)}, bf16[128,2048]{1,0:T(8,128)(2,1)}, u32[]{:S(2)}) copy-start(bf16[128,2048]{1,0:T(8,128)(2,1)} %reduce-scatter.9.cloned.1.call-done) | copy-start | bytes 1572868
  1074.2 405.2 %copy-start.15 = (f32[128,2048]{1,0:T(8,128)S(1)}, f32[128,2048]{1,0:T(8,128)}, u32[]{:S(2)}) copy-start(f32[128,2048]{1,0:T(8,128)} %copy-done.14) | copy-start | bytes 3145732
  1074.2 405.2 %copy-start.28 = (bf16[1,128,2048]{2,1,0:T(8,128)(2,1)S(1)}, bf16[1,128,2048]{2,1,0:T(8,128)(2,1)}, u32[]{:S(2)}) copy-start(bf16[1,128,2048]{2,1,0:T(8,128)(2,1)} %param.27) | copy-start | bytes 1572868
  1074.2 405.2 %copy-start.52 = (f32[2048]{0:T(1024)S(1)}, f32[2048]{0:T(1024)}, u32[]{:S(2)}) copy-start(f32[2048]{0:T(1024)} %param.23) | copy-start | bytes 24580
  1074.2 405.2 %copy-start.72 = (f32[128]{0:T(128)S(1)}, f32[128]{0:T(128)}, u32[]{:S(2)}) copy-start(f32[128]{0:T(128)} %copy-done.70) | copy-start | bytes 1540
  1074.2 405.2 %copy-start.85 = (f32[128]{0:T(128)S(1)}, f32[128]{0:T(128)}, u32[]{:S(2)}) copy-start(f32[128]{0:T(128)} %copy-done.84) | copy-start | bytes 1540
  (66 other events, 222.4 us)
Sparse Core Ops, SparseCore 0:
  54.1 40.8 all-gather.14
  97.7 72.5 all-gather.8
  221.7 87.8 reduce-scatter.8
  317.4 118.9 all-gather.10
  439.5 113.0 all-gather.16
  665.9 191.8 reduce-scatter.12
  863.9 75.4 all-gather.12
  1017.6 50.4 reduce-scatter.16
  1070.4 115.1 reduce-scatter.18
  1189.5 104.6 reduce-scatter.14
  1296.5 182.8 reduce-scatter.10

commit v2 on v1

--- a/solution.py
+++ b/solution.py
@@ -4,6 +4,8 @@
 import jax
 import jax.numpy as jnp
 from jax import lax
+from jax.experimental import pallas as pl
+from jax.experimental.pallas import tpu as pltpu
 from jax.sharding import PartitionSpec as P
 
 QUERY_HEADS = 32
@@ -427,12 +429,505 @@
     )
 
 
-def all_gather_rows(rows, axes):
-    return lax.all_gather(rows, axes, axis=0, tiled=True)
-
-
-def sum_scatter_rows(partial_rows, axes):
-    return lax.psum_scatter(partial_rows, axes, scatter_dimension=0, tiled=True)
+MESH = pl.DeviceIdType.MESH
+VMEM_LIMIT = 60 * 2**20
+
+
+class Place:
+    def __init__(self):
+        seq, shard = lax.axis_index("seq"), lax.axis_index("fsdp")
+        self.z, self.x = seq // 2, seq % 2
+        self.y, self.c = shard // 2, shard % 2
+        self.z0, self.z1 = self.z % 2, self.z // 2
+        self.low, self.high = self.z == 0, self.z == 3
+        self.inner = (self.z0 + self.z1) == 1
+        self.me = self.block(self.z, self.x, self.y, self.c)
+
+    def device(self, z, x, y, c):
+        return (z * 2 + x, y * 2 + c)
+
+    def block(self, z, x, y, c):
+        return (z * 2 + x) * 4 + y * 2 + c
+
+    @property
+    def by_x(self):
+        return self.device(self.z, 1 - self.x, self.y, self.c)
+
+    @property
+    def by_y(self):
+        return self.device(self.z, self.x, 1 - self.y, self.c)
+
+    @property
+    def by_core(self):
+        return self.device(self.z, self.x, self.y, 1 - self.c)
+
+    def by_z(self, step):
+        return self.device(self.z + step, self.x, self.y, self.c)
+
+    def near(self, k):
+        return [self.z, 1 + self.z0, 2 - 2 * self.z0 + self.z1, 3 - 3 * self.z1][k]
+
+    def onward(self, k):
+        return [None, 2 * self.z1 - 1, 1 - 2 * self.z1, 2 * self.z1 - 1][k]
+
+    def far(self, k):
+        return self.near(3 - k)
+
+    def toward(self, k):
+        return [1 - 2 * self.z1, 1 - 2 * self.z0, 1 - 2 * self.z1][k]
+
+    def greet(self, sides):
+        barrier = pltpu.get_barrier_semaphore()
+        for side in sides:
+            if side != "z":
+                target = {"x": self.by_x, "y": self.by_y, "core": self.by_core}[side]
+                pl.semaphore_signal(barrier, inc=1, device_id=target, device_id_type=MESH)
+        count = len([side for side in sides if side != "z"])
+        if "z" in sides:
+
+            @pl.when(jnp.logical_not(self.low))
+            def _():
+                pl.semaphore_signal(barrier, inc=1, device_id=self.by_z(-1), device_id_type=MESH)
+
+            @pl.when(jnp.logical_not(self.high))
+            def _():
+                pl.semaphore_signal(barrier, inc=1, device_id=self.by_z(1), device_id_type=MESH)
+
+            count = count + 1 + (self.z0 + self.z1) % 2
+        pl.semaphore_wait(barrier, count)
+
+
+def send(source, target, send_sem, recv_sem, device):
+    pltpu.make_async_remote_copy(
+        src_ref=source,
+        dst_ref=target,
+        send_sem=send_sem,
+        recv_sem=recv_sem,
+        device_id=device,
+        device_id_type=MESH,
+    ).start()
+
+
+def await_bytes(ref, sem):
+    pltpu.make_async_copy(ref, ref, sem).wait()
+
+
+G_Z, G_X, G_Y, G_DX, G_DY, G_C0 = 0, 1, 2, 3, 4, 5
+G_KINDS = 9
+
+
+def gather_steps(place, own, out, ss, rs, zs, local_sem):
+    p = place
+    rows = out.shape[1]
+    half = rows // 2
+    x, y, c = p.x, p.y, p.c
+
+    def cols(q):
+        return [
+            p.block(q, x, y, c),
+            p.block(q, 1 - x, y, c),
+            p.block(q, x, 1 - y, c),
+            p.block(q, 1 - x, 1 - y, c),
+        ]
+
+    def to_core(q, j, src=None):
+        b = cols(q)[j]
+        send(out.at[b] if src is None else src, out.at[b], ss.at[q, G_C0 + j], rs.at[q, G_C0 + j], p.by_core)
+
+    def plane_out(k):
+        q = p.near(k)
+        b = cols(q)[0]
+        if k == 0:
+            src = own
+            for step, there in ((1, p.high), (-1, p.low)):
+
+                @pl.when(jnp.logical_not(there))
+                def _():
+                    send(src, out.at[b], zs.at[q, 0 if step > 0 else 1], rs.at[q, G_Z], p.by_z(step))
+
+            pltpu.make_async_copy(own, out.at[b], local_sem).start()
+        else:
+            src = out.at[b]
+            await_bytes(src, rs.at[q, G_Z])
+
+            @pl.when(p.inner)
+            def _():
+                send(src, src, zs.at[q, 0], rs.at[q, G_Z], p.by_z(p.onward(k)))
+
+        send(src, out.at[b], ss.at[q, G_X], rs.at[q, G_X], p.by_x)
+        send(src, out.at[b], ss.at[q, G_Y], rs.at[q, G_Y], p.by_y)
+        to_core(q, 0, src)
+
+    def plane_turn(k):
+        q = p.near(k)
+        bx, by = out.at[cols(q)[1]], out.at[cols(q)[2]]
+        await_bytes(bx, rs.at[q, G_X])
+        first = bx.at[pl.ds(0, half)]
+        send(first, first, ss.at[q, G_DY], rs.at[q, G_DY], p.by_y)
+        to_core(q, 1)
+        await_bytes(by, rs.at[q, G_Y])
+        second = by.at[pl.ds(half, half)]
+        send(second, second, ss.at[q, G_DX], rs.at[q, G_DX], p.by_x)
+        to_core(q, 2)
+
+    def plane_end(k):
+        q = p.near(k)
+        bd = out.at[cols(q)[3]]
+        await_bytes(bd.at[pl.ds(0, half)], rs.at[q, G_DY])
+        await_bytes(bd.at[pl.ds(half, half)], rs.at[q, G_DX])
+        to_core(q, 3)
+
+    def plane_core(k):
+        q = p.near(k)
+        for j in range(4):
+            await_bytes(own, rs.at[q, G_C0 + j])
+
+    def finish():
+        pltpu.make_async_copy(own, out.at[cols(p.z)[0]], local_sem).wait()
+        piece = own.at[pl.ds(0, half)]
+        for q in range(4):
+            for kind in (G_X, G_Y, G_C0, G_C0 + 1, G_C0 + 2, G_C0 + 3):
+                await_bytes(own, ss.at[q, kind])
+            for kind in (G_DX, G_DY):
+                await_bytes(piece, ss.at[q, kind])
+        for there, slot in ((p.high, 0), (p.low, 1)):
+
+            @pl.when(jnp.logical_not(there))
+            def _():
+                await_bytes(own, zs.at[p.z, slot])
+
+        for k in range(1, 4):
+
+            @pl.when(p.inner)
+            def _():
+                await_bytes(own, zs.at[p.near(k), 0])
+
+    return plane_out, plane_turn, plane_end, plane_core, finish
+
+
+def gather_all_kernel(own, out, ss, rs, zs, local_sem):
+    p = Place()
+    p.greet(("x", "y", "core", "z"))
+    plane_out, plane_turn, plane_end, plane_core, finish = gather_steps(p, own, out, ss, rs, zs, local_sem)
+    plane_out(0)
+    plane_out(1)
+    plane_turn(0)
+    plane_out(2)
+    plane_end(0)
+    plane_turn(1)
+    plane_out(3)
+    plane_end(1)
+    plane_turn(2)
+    plane_end(2)
+    plane_turn(3)
+    plane_end(3)
+    for k in range(4):
+        plane_core(k)
+    finish()
+
+
+def gather_all(own, blocks, collective_id):
+    dma = pltpu.SemaphoreType.DMA
+    return pl.pallas_call(
+        gather_all_kernel,
+        out_shape=jax.ShapeDtypeStruct((blocks, *own.shape), own.dtype),
+        in_specs=[pl.BlockSpec(memory_space=pl.ANY)],
+        out_specs=pl.BlockSpec(memory_space=pl.ANY),
+        scratch_shapes=[dma((4, G_KINDS)), dma((4, G_KINDS)), dma((4, 2)), dma],
+        compiler_params=pltpu.CompilerParams(
+            collective_id=collective_id, has_side_effects=True, vmem_limit_bytes=VMEM_LIMIT
+        ),
+        name="gather_all",
+    )(own)
+
+
+def sum_all_parts(p, part, held, core_in, x_half, y_half, x_in, y_in, z_in, out, ls, cs, cr, ss, rs, zs, zr):
+    rows, width = part.shape[1], part.shape[2]
+    half = rows // 2
+    x, y, c = p.x, p.y, p.c
+
+    def columns(q):
+        return [(q, x, y), (q, 1 - x, y), (q, x, 1 - y), (q, 1 - x, 1 - y)]
+
+    def start():
+        for k in range(4):
+            q = p.far(k)
+            for j, (zz, xx, yy) in reversed(list(enumerate(columns(q)))):
+                send(
+                    part.at[p.block(zz, xx, yy, 1 - c)],
+                    core_in.at[q * 4 + j],
+                    cs.at[q, j],
+                    cr.at[q, j],
+                    p.by_core,
+                )
+                pltpu.make_async_copy(
+                    part.at[p.block(zz, xx, yy, c)], held.at[q * 4 + j], ls.at[q, j]
+                ).start()
+
+    chunk = 16
+
+    def add(target, source, count):
+        @pl.loop(0, count // chunk)
+        def _(i):
+            at = pl.ds(pl.multiple_of(i * chunk, chunk), chunk)
+            target[at, :] = (
+                target[at, :].astype(jnp.float32) + source[at, :].astype(jnp.float32)
+            ).astype(target.dtype)
+
+    def plane_core(k, js=(3, 1, 2, 0)):
+        q = p.far(k)
+        for j in js:
+            slot = q * 4 + j
+            await_bytes(held.at[slot], ls.at[q, j])
+            await_bytes(core_in.at[slot], cr.at[q, j])
+            add(held.at[slot], core_in.at[slot], rows)
+            if j == 3:
+                send(held.at[slot, pl.ds(0, half)], y_half.at[q], ss.at[q, 0], rs.at[q, 0], p.by_y)
+                send(held.at[slot, pl.ds(half, half)], x_half.at[q], ss.at[q, 1], rs.at[q, 1], p.by_x)
+
+    def plane_turn(k):
+        q = p.far(k)
+        await_bytes(y_half.at[q], rs.at[q, 0])
+        add(held.at[q * 4 + 1, pl.ds(0, half)], y_half.at[q], half)
+        send(held.at[q * 4 + 1], x_in.at[q], ss.at[q, 2], rs.at[q, 2], p.by_x)
+        await_bytes(x_half.at[q], rs.at[q, 1])
+        add(held.at[q * 4 + 2, pl.ds(half, half)], x_half.at[q], half)
+        send(held.at[q * 4 + 2], y_in.at[q], ss.at[q, 3], rs.at[q, 3], p.by_y)
+
+    def plane_end(k):
+        q = p.far(k)
+        mine = held.at[q * 4]
+        await_bytes(x_in.at[q], rs.at[q, 2])
+        add(mine, x_in.at[q], rows)
+        await_bytes(y_in.at[q], rs.at[q, 3])
+        add(mine, y_in.at[q], rows)
+        if k < 3:
+            step = p.toward(k)
+            slot = (1 - step) // 2
+
+            @pl.when(p.inner)
+            def _():
+                await_bytes(z_in.at[slot, q], zr.at[slot, q])
+                add(mine, z_in.at[slot, q], rows)
+
+            send(mine, z_in.at[slot, q], zs.at[k], zr.at[slot, q], p.by_z(step))
+        else:
+            for slot, there in ((0, p.low), (1, p.high)):
+
+                @pl.when(jnp.logical_not(there))
+                def _():
+                    await_bytes(z_in.at[slot, q], zr.at[slot, q])
+                    add(mine, z_in.at[slot, q], rows)
+
+            out[...] = mine[...]
+
+    def finish():
+        whole, piece = x_in.at[0], x_half.at[0]
+        for q in range(4):
+            for j in range(4):
+                await_bytes(whole, cs.at[q, j])
+            for kind in (0, 1):
+                await_bytes(piece, ss.at[q, kind])
+            for kind in (2, 3):
+                await_bytes(whole, ss.at[q, kind])
+        for k in range(3):
+            await_bytes(whole, zs.at[k])
+
+    return start, plane_core, plane_turn, plane_end, finish
+
+
+def sum_all_kernel(part, out, *scratch):
+    p = Place()
+    p.greet(("x", "y", "core", "z"))
+    start, plane_core, plane_turn, plane_end, finish = sum_all_parts(p, part, *scratch[:7], out, *scratch[7:])
+    start()
+    plane_core(0)
+    plane_core(1)
+    plane_turn(0)
+    plane_core(2)
+    plane_turn(1)
+    plane_end(0)
+    plane_core(3)
+    plane_turn(2)
+    plane_end(1)
+    plane_turn(3)
+    plane_end(2)
+    plane_end(3)
+    finish()
+
+
+def sum_all_scratch(rows, width):
+    dma = pltpu.SemaphoreType.DMA
+    bf16 = jnp.bfloat16
+    return [
+        pltpu.VMEM((16, rows, width), bf16),
+        pltpu.VMEM((16, rows, width), bf16),
+        pltpu.VMEM((4, rows // 2, width), bf16),
+        pltpu.VMEM((4, rows // 2, width), bf16),
+        pltpu.VMEM((4, rows, width), bf16),
+        pltpu.VMEM((4, rows, width), bf16),
+        pltpu.VMEM((2, 4, rows, width), bf16),
+        dma((4, 4)),
+        dma((4, 4)),
+        dma((4, 4)),
+        dma((4, 4)),
+        dma((4, 4)),
+        dma((3,)),
+        dma((2, 4)),
+    ]
+
+
+def sum_all(part, collective_id):
+    blocks, rows, width = part.shape
+    return pl.pallas_call(
+        sum_all_kernel,
+        out_shape=jax.ShapeDtypeStruct((rows, width), part.dtype),
+        in_specs=[pl.BlockSpec(memory_space=pl.ANY)],
+        out_specs=pl.BlockSpec(memory_space=pltpu.VMEM),
+        scratch_shapes=sum_all_scratch(rows, width),
+        compiler_params=pltpu.CompilerParams(
+            collective_id=collective_id, has_side_effects=True, vmem_limit_bytes=VMEM_LIMIT
+        ),
+        name="sum_all",
+    )(part)
+
+
+def gather_seq_kernel(own, out, ss, rs, zs, local_sem):
+    p = Place()
+    p.greet(("x", "z"))
+
+    def at(q, x):
+        return out.at[q * 2 + x]
+
+    def plane_out(k):
+        q = p.near(k)
+        there = at(q, p.x)
+        if k == 0:
+            src = own
+            for step, end in ((1, p.high), (-1, p.low)):
+
+                @pl.when(jnp.logical_not(end))
+                def _():
+                    send(src, there, zs.at[q, 0 if step > 0 else 1], rs.at[q, 0], p.by_z(step))
+
+            pltpu.make_async_copy(own, there, local_sem).start()
+        else:
+            src = there
+            await_bytes(src, rs.at[q, 0])
+
+            @pl.when(p.inner)
+            def _():
+                send(src, src, zs.at[q, 0], rs.at[q, 0], p.by_z(p.onward(k)))
+
+        send(src, there, ss.at[q], rs.at[q, 1], p.by_x)
+
+    for k in range(4):
+        plane_out(k)
+    for k in range(4):
+        await_bytes(own, rs.at[p.near(k), 1])
+    pltpu.make_async_copy(own, at(p.z, p.x), local_sem).wait()
+    for q in range(4):
+        await_bytes(own, ss.at[q])
+    for there, slot in ((p.high, 0), (p.low, 1)):
+
+        @pl.when(jnp.logical_not(there))
+        def _():
+            await_bytes(own, zs.at[p.z, slot])
+
+    for k in range(1, 4):
+
+        @pl.when(p.inner)
+        def _():
+            await_bytes(own, zs.at[p.near(k), 0])
+
+
+def gather_seq(own, collective_id):
+    dma = pltpu.SemaphoreType.DMA
+    return pl.pallas_call(
+        gather_seq_kernel,
+        out_shape=jax.ShapeDtypeStruct((8, *own.shape), own.dtype),
+        in_specs=[pl.BlockSpec(memory_space=pl.ANY)],
+        out_specs=pl.BlockSpec(memory_space=pl.ANY),
+        scratch_shapes=[dma((4,)), dma((4, 2)), dma((4, 2)), dma],
+        compiler_params=pltpu.CompilerParams(
+            collective_id=collective_id, has_side_effects=True, vmem_limit_bytes=VMEM_LIMIT
+        ),
+        name="gather_seq",
+    )(own)
+
+
+def add_rows(target, source, count, chunk=16):
+    @pl.loop(0, count // chunk)
+    def _(i):
+        at = pl.ds(pl.multiple_of(i * chunk, chunk), chunk)
+        target[at, :] = (
+            target[at, :].astype(jnp.float32) + source[at, :].astype(jnp.float32)
+        ).astype(target.dtype)
+
+
+def sum_seq_kernel(part, out, held, x_in, z_in, ls, ss, rs, zs, zr):
+    p = Place()
+    p.greet(("x", "z"))
+    rows = part.shape[1]
+    for k in range(4):
+        q = p.far(k)
+        send(part.at[q * 2 + 1 - p.x], x_in.at[q], ss.at[q], rs.at[q], p.by_x)
+        pltpu.make_async_copy(part.at[q * 2 + p.x], held.at[q], ls.at[q]).start()
+    for k in range(4):
+        q = p.far(k)
+        mine = held.at[q]
+        await_bytes(mine, ls.at[q])
+        await_bytes(x_in.at[q], rs.at[q])
+        add_rows(mine, x_in.at[q], rows)
+        if k < 3:
+            step = p.toward(k)
+            slot = (1 - step) // 2
+
+            @pl.when(p.inner)
+            def _():
+                await_bytes(z_in.at[slot, q], zr.at[slot, q])
+                add_rows(mine, z_in.at[slot, q], rows)
+
+            send(mine, z_in.at[slot, q], zs.at[k], zr.at[slot, q], p.by_z(step))
+        else:
+            for slot, there in ((0, p.low), (1, p.high)):
+
+                @pl.when(jnp.logical_not(there))
+                def _():
+                    await_bytes(z_in.at[slot, q], zr.at[slot, q])
+                    add_rows(mine, z_in.at[slot, q], rows)
+
+            out[...] = mine[...]
+    for q in range(4):
+        await_bytes(x_in.at[0], ss.at[q])
+    for k in range(3):
+        await_bytes(x_in.at[0], zs.at[k])
+
+
+def sum_seq(part, collective_id):
+    _, rows, width = part.shape
+    dma = pltpu.SemaphoreType.DMA
+    bf16 = jnp.bfloat16
+    return pl.pallas_call(
+        sum_seq_kernel,
+        out_shape=jax.ShapeDtypeStruct((rows, width), part.dtype),
+        in_specs=[pl.BlockSpec(memory_space=pl.ANY)],
+        out_specs=pl.BlockSpec(memory_space=pltpu.VMEM),
+        scratch_shapes=[
+            pltpu.VMEM((4, rows, width), bf16),
+            pltpu.VMEM((4, rows, width), bf16),
+            pltpu.VMEM((2, 4, rows, width), bf16),
+            dma((4,)),
+            dma((4,)),
+            dma((4,)),
+            dma((3,)),
+            dma((2, 4)),
+        ],
+        compiler_params=pltpu.CompilerParams(
+            collective_id=collective_id, has_side_effects=True, vmem_limit_bytes=VMEM_LIMIT
+        ),
+        name="sum_seq",
+    )(part)
 
 
 def head_columns(weight, group_index):
@@ -489,12 +984,12 @@
     columns = lax.all_gather(pieces, "fsdp", axis=1).reshape(width, all_cols)
     proj_weight = columns[:, :proj_cols]
     out_weight = columns[:, proj_cols:]
-    full_router = all_gather_rows(w_router, both)
-    cot_all = all_gather_rows(cotangent[0], both)
+    full_router = lax.all_gather(w_router, both, axis=0, tiled=True)
+    cot_all = lax.all_gather(cotangent[0], both)
 
     resid_in = tokens[0].astype(f32)
     normed_one = rms_scale(resid_in, attn_gain).astype(bf16)
-    normed_all = all_gather_rows(normed_one, "seq")
+    normed_all = gather_seq(normed_one, 1).reshape(length, width)
     projected = jnp.dot(normed_all, proj_weight, preferred_element_type=f32)
     seq_positions = jnp.arange(length, dtype=jnp.int32)
     prepare = partial(head_prepare, positions=seq_positions)
@@ -508,7 +1003,7 @@
     mixed_heads, log_total = attend_forward(queries, repeat_keys, repeat_values)
     attended = mixed_heads.reshape(length, head_cols)
     attn_part = jnp.einsum("tj,dj->td", attended, out_weight, preferred_element_type=f32)
-    attn_out = sum_scatter_rows(attn_part.astype(bf16), "seq")
+    attn_out = sum_seq(attn_part.astype(bf16).reshape(seq_size, rows, width), 2)
     hidden = resid_in + attn_out.astype(f32)
     normed_two = rms_scale(hidden, ffn_gain).astype(bf16)
 
@@ -526,10 +1021,10 @@
     gate_low = (gate_dense - gate_high.astype(f32)).astype(bf16)
     route_info = jnp.concatenate([gate_high, gate_low, named.astype(bf16)], axis=1)
     route_info = jnp.pad(route_info, ((0, 0), (0, 128 - route_info.shape[1] % 128)))
-    gathered = all_gather_rows(jnp.concatenate([normed_two, route_info], axis=1), both)
+    gathered = gather_all(jnp.concatenate([normed_two, route_info], axis=1), experts, 3)
     blocks = experts
-    rows_all = gathered[:, :width].reshape(blocks, rows, width)
-    info = gathered[:, width : width + 3 * experts].reshape(blocks, rows, 3, experts)
+    rows_all = gathered[:, :, :width]
+    info = gathered[:, :, width : width + 3 * experts].reshape(blocks, rows, 3, experts)
     me = lax.axis_index("seq") * shard_size + lax.axis_index("fsdp")
     own = lax.dynamic_index_in_dim(info, me, 3, keepdims=False).astype(f32)
     gate_own = own[:, :, 0] + own[:, :, 1]
@@ -565,7 +1060,7 @@
     d_gate_slots = jnp.sum(expert_out * cot_rows, axis=1)
     weighted = (gate_slots * expert_out).astype(bf16).reshape(blocks, capacity, width)
     out_part = jnp.einsum("bct,bcd->btd", pick, weighted, preferred_element_type=f32)
-    mixture = sum_scatter_rows(out_part.astype(bf16).reshape(-1, width), both)
+    mixture = sum_all(out_part.astype(bf16), 4)
     output = (hidden + mixture.astype(f32)).astype(bf16)
 
     d_expert = (gate_slots * cot_rows).astype(bf16)
@@ -590,7 +1085,7 @@
     d_info = jnp.pad(d_info, ((0, 0), (0, 0), (0, 128 - d_info.shape[2] % 128)))
     d_part = jnp.einsum("bct,bcd->btd", pick, d_rows, preferred_element_type=f32)
     d_part = jnp.concatenate([d_part.astype(bf16), d_info], axis=2)
-    d_back = sum_scatter_rows(d_part.reshape(-1, d_part.shape[2]), both).astype(f32)
+    d_back = sum_all(d_part, 5).astype(f32)
 
     d_gate_dense = d_back[:, width : width + experts] + d_back[:, width + experts : width + 2 * experts]
     d_gates = jnp.sum(onehot_float * d_gate_dense[:, None, :], axis=-1)
@@ -605,7 +1100,7 @@
     d_hidden = out_grad + d_hidden_norm
     d_attn = d_hidden.astype(bf16)
 
-    d_attn_all = all_gather_rows(d_attn, "seq")
+    d_attn_all = gather_seq(d_attn, 6).reshape(length, width)
     d_attended = jnp.dot(d_attn_all, out_weight, preferred_element_type=f32).astype(bf16)
     d_query, d_key_sum, d_value_sum = attend_backward(
         queries,
@@ -627,7 +1122,7 @@
         axis=1,
     ).astype(bf16)
     d_normed_part = jnp.einsum("tj,dj->td", d_projected, proj_weight, preferred_element_type=f32)
-    d_normed_one = sum_scatter_rows(d_normed_part.astype(bf16), "seq").astype(f32)
+    d_normed_one = sum_seq(d_normed_part.astype(bf16).reshape(seq_size, rows, width), 7).astype(f32)
     unused_one, pull_one = jax.vjp(rms_scale, resid_in, attn_gain)
     d_resid_norm, d_attn_gain = pull_one(d_normed_one)
     d_tokens = (d_hidden + d_resid_norm).astype(bf16)[None]
@@ -644,7 +1139,7 @@
         .transpose(1, 0, 2, 3)
         .reshape(width, all_cols)
     )
-    d_columns = sum_scatter_rows(d_columns, "fsdp").reshape(seq_size, weight_rows, all_cols)
+    d_columns = lax.psum_scatter(d_columns, "fsdp", scatter_dimension=0, tiled=True).reshape(seq_size, weight_rows, all_cols)
     d_pieces = lax.all_to_all(d_columns, "seq", split_axis=0, concat_axis=0, tiled=True).astype(f32)
     d_pieces = d_pieces.transpose(1, 0, 2)
     per_group = seq_size // KEY_VALUE_HEADS
@@ -654,12 +1149,19 @@
     d_kv = jnp.sum(d_kv, axis=2).transpose(0, 2, 1, 3).reshape(weight_rows, -1)
     d_w_qkv = jnp.concatenate([d_pieces[:, :, :head_cols].reshape(weight_rows, -1), d_kv], axis=1)
     d_w_out_t = d_pieces[:, :, proj_cols:].reshape(weight_rows, -1)
-    d_w_router = sum_scatter_rows(
-        jnp.einsum("tc,te->ce", normed_two, d_logits, preferred_element_type=f32), both
-    )
-    d_attn_gain, d_ffn_gain, d_q_gain, d_k_gain = lax.psum(
-        (d_attn_gain, d_ffn_gain, d_q_gain, d_k_gain), both
-    )
+    d_w_router = lax.psum_scatter(
+        jnp.einsum("tc,te->ce", normed_two, d_logits, preferred_element_type=f32),
+        both,
+        scatter_dimension=0,
+        tiled=True,
+    )
+    gains = jnp.concatenate([d_attn_gain, d_ffn_gain, d_q_gain, d_k_gain])
+    gains = jnp.pad(gains, (0, -gains.shape[0] % 2048)).reshape(16, -1)
+    gains = jnp.sum(gather_all(gains, experts, 8), axis=0).reshape(-1)
+    d_attn_gain = gains[:width]
+    d_ffn_gain = gains[width : 2 * width]
+    d_q_gain = gains[2 * width : 2 * width + HEAD_DIMENSION]
+    d_k_gain = gains[2 * width + HEAD_DIMENSION : 2 * width + 2 * HEAD_DIMENSION]
     return (
         output[None],
         d_tokens,
@@ -676,7 +1178,7 @@
 
 
 def gathered_fits(mesh):
-    return mesh.shape["seq"] * mesh.shape["fsdp"] <= 4 * TOPK
+    return mesh.shape["seq"] == 8 and mesh.shape["fsdp"] == 4
 
 
 def solution(mesh):

time: 1520 us -> 1090 us (0.72)
  the two profiles are of different devices: /device:TPU:16 before, /device:TPU:0 now
where the time goes in v2:
time: 1090 us; the launch traced here: 1080 us
  Pallas kernels  474 us (43%)
  matrix products  220 us (20%)
  waiting for transfers between devices  118 us (11%)
  local copies, waits for them, and re-layouts  82 us (8%)
  blocking collectives  79.3 us (7%)
  other arithmetic  79.1 us (7%)
  between operations  15.4 us (1%)
    pallas_call x2, Pallas kernels, sum_all(): pl.pallas_call(sum_all_kernel, out_shape=jax.ShapeDtypeStruct((rows, widt...  154 us
    pallas_call x2, Pallas kernels, gather_seq(): pl.pallas_call(gather_seq_kernel, out_shape=jax.ShapeDtypeStruct((8, *own...  124 us
    unnamed x5, waiting for transfers between devices  118 us
    pallas_call x2, Pallas kernels, gather_all(): pl.pallas_call(gather_all_kernel, out_shape=jax.ShapeDtypeStruct((blocks,...  101 us
    pallas_call x2, Pallas kernels, sum_seq(): pl.pallas_call(sum_seq_kernel, out_shape=jax.ShapeDtypeStruct((rows, widt...  95.4 us
    all_gather x1, blocking collectives, gathered_body(): full_router = lax.all_gather(w_router, both, axis=0, tiled=True)  40.9 us
    all_to_all x1, blocking collectives, gathered_body(): lax.all_to_all(pieces, 'seq', split_axis=0, concat_axis=0, tiled=True)  38.4 us
    unnamed x183, local copies, waits for them, and re-layouts  22.5 us
  transfers between devices with their start and end apart: 5, of which 1 were waited for; matrix products, arithmetic and copies ran while one was open for 15% of the time, Pallas kernels for 32%

profile of v2, /device:TPU:0, one launch (start us, length us, event | category | flops | bytes accessed | tf_op | source)
XLA Modules:
  0.0 1081.2 jit_solution(6885045843105106382)
XLA Ops:
  16.8 38.4 %all_to_all.10 = bf16[8,64,1280]{2,1,0:T(8,128)(2,1)S(1)} all-to-all(bf16[8,64,1280]{2,1,0:T(8,128)(2,1)S(1)} %copy.265), channel_id=1, replica_groups=mesh['seq'=8,'fsdp'=4] {'seq'}, dimensions={0} | all-to-all | bytes 2621440 | tf_op jit(solution)/shard_map/all_to_all | solution.py:983
  57.9 40.9 %all-gather.1 = bf16[32,64,32]{1,2,0:T(8,128)(2,1)S(1)} all-gather(bf16[1,64,32]{1,2,0:T(8,128)(2,1)S(1)} %bitcast.286), channel_id=1, replica_groups=mesh['seq'=8,'fsdp'=4] {'seq','fsdp'}, dimensions={0}, use_global_device_ids=true | all-gather | bytes 135168 | tf_op jit(solution)/shard_map/all_gather | solution.py:987
  103.6 74.9 %gather_seq.2 = bf16[8,128,2048]{2,1,0:T(8,128)(2,1)} custom-call(bf16[128,2048]{1,0:T(8,128)(2,1)} %fusion.76.own), custom_call_target="tpu_custom_call" | custom-call | tf_op jit(solution)/shard_map/gather_seq/pallas_call | solution.py:846
  178.4 6.5 copy.289
  186.6 3.0 multiply_cosine_fusion
  189.7 3.7 copy.267
  193.5 3.6 fusion.62
  208.2 2.9 copy.268
  218.0 24.0 %while.28 = (s32[]{:T(128)}, bf16[2,512,4,128]{3,2,1,0:T(4,128)(2,1)}, f32[2,4,512]{2,1,0:T(4,128)S(1)}, s32[2]{0:T(128)}, bf16[1024,4,128]{2,0,1:T(8,128)(2,1)}...) while((s32[]{:T(128)}, ...), condition=%wide.region_6.7_spmd.clone, body=%wide.region_3.6_spmd.clone.sunk | while | flops 1099692544 | bytes 39391508 | solution.py:93
  220.4 2.8 fusion.197
  225.7 2.9 fusion.199
  232.3 2.8 fusion.197
  237.5 2.9 fusion.199
  244.3 6.3 convolution_convert_fusion.4
  250.6 48.9 %sum_seq.2 = bf16[128,2048]{1,0:T(8,128)(2,1)} custom-call(bf16[8,128,2048]{2,1,0:T(8,128)(2,1)} %bitcast.263), custom_call_target="tpu_custom_call" | custom-call | tf_op jit(solution)/shard_map/sum_seq/pallas_call | solution.py:911
  308.0 81.0 %gather_all.2 = bf16[32,128,2176]{2,1,0:T(8,128)(2,1)} custom-call(bf16[128,2176]{1,0:T(8,128)(2,1)} %pad_maximum_fusion.10.own), custom_call_target="tpu_custom_call" | custom-call | tf_op jit(solution)/shard_map/gather_all/pallas_call | solution.py:631
  396.1 7.0 fusion.55
  403.2 3.3 copy-done.10
  406.4 17.4 %fusion.52 = f32[2048,1536]{0,1:T(8,128)} fusion(bf16[2048,2048]{1,0:T(8,128)(2,1)S(1)} %bitcast.249, bf16[1,2048,1536]{2,1,0:T(8,128)(2,1)} %param.20), kind=kOutput, calls=%fused_computation.72 | convolution fusion | flops 12884901888 | bytes 27262976 | tf_op jit(solution)/shard_map/dot_general | solution.py:1051
  423.8 13.0 %multiply_convert_fusion.1 = (bf16[32,64,2048]{2,1,0:T(8,128)(2,1)}, f32[32,64,2048]{2,1,0:T(8,128)}) fusion(f32[32,64]{1,0:T(8,128)S(1)} %bitcast.278, bf16[32,128,2048]{2,1,0:T(8,128)(2,1)} %all-gather.5.cloned.1.call-done, f32[32,128]{1,0:T(8,128)S(1)} %fusion.151, pred[32,128]{1,0:T(8,128)(4,1)S(1)} %broadcast_compare_fusion), kind=kOutput, calls=%fused_computation.62 | convolution fusion | flops 1082654720 | bytes 41971712 | tf_op jit(solution)/shard_map/bct,btd->bcd/dot_general | solution.py:1042
  436.8 16.3 %multiply_convert_fusion.3 = (bf16[2048,768]{0,1:T(8,128)(2,1)}, bf16[2048,768]{0,1:T(8,128)(2,1)}, bf16[2048,768]{0,1:T(8,128)(2,1)S(1)}) fusion(f32[2048,1536]{0,1:T(8,128)} %fusion.52, bf16[2048,2048]{1,0:T(8,128)(2,1)} %bitcast.248, bf16[1,768,2048]{2,1,0:T(8,128)(2,1)S(1)} %copy-done), kind=kOutput, calls=%fused_computation.75 | convolution fusion | flops 6466043904 | bytes 33554432 | tf_op jit(solution)/shard_map/rd,fd->rf/dot_general | solution.py:1067
  453.1 16.6 %fusion.48 = (bf16[2048,2048]{1,0:T(8,128)(2,1)}, f32[2048]{0:T(1024)S(1)}, bf16[2048,2048]{1,0:T(8,128)(2,1)}) fusion(f32[32,64,2048]{2,1,0:T(8,128)} %get-tuple-element.374, f32[2048]{0:T(1024)S(1)} %mul.673, bf16[2048,768]{0,1:T(8,128)(2,1)S(1)} %get-tuple-element.339, bf16[1,768,2048]{2,1,0:T(8,128)(2,1)S(1)} %copy-done), kind=kOutput, calls=%fused_computation.61 | convolution fusion | flops 6476003328 | bytes 39862272 | tf_op jit(solution)/shard_map/dot_general | solution.py:1058
  470.4 19.4 %convolution_convert_fusion.2 = bf16[2048,2048]{1,0:T(8,128)(2,1)} fusion(bf16[1,2048,1536]{2,1,0:T(8,128)(2,1)} %param.20, bf16[2048,768]{0,1:T(8,128)(2,1)} %get-tuple-element.336, bf16[2048,768]{0,1:T(8,128)(2,1)} %get-tuple-element.335), kind=kOutput, calls=%fused_computation.68 | convolution fusion | flops 12901679104 | bytes 20971520 | tf_op jit(solution)/shard_map/rf,df->rd/dot_general | solution.py:1073
  489.9 13.7 %convolution_convert_fusion = bf16[32,128,2048]{2,1,0:T(8,128)(2,1)} fusion(bf16[32,64,2048]{2,1,0:T(8,128)(2,1)} %bitcast.246, f32[32,128]{1,0:T(8,128)S(1)} %fusion.151, pred[32,128]{1,0:T(8,128)(4,1)S(1)} %broadcast_compare_fusion), kind=kOutput, calls=%fused_computation.65 | convolution fusion | flops 1082654720 | bytes 25186304 | tf_op jit(solution)/shard_map/bct,bcd->btd/dot_general | solution.py:1086
  505.5 14.6 %pad_maximum_fusion.part = bf16[32,128,2176]{2,1,0:T(8,128)(2,1)} fusion(bf16[32,128,128]{2,1,0:T(8,128)(2,1)S(1)} %fusion.83, bf16[32,128,2048]{2,1,0:T(8,128)(2,1)} %convolution_convert_fusion), kind=kLoop, calls=%fused_computation.57 | loop fusion | flops 35651584 | bytes 35651584 | tf_op jit(solution)/shard_map/concatenate | solution.py:1087
  520.1 79.2 %sum_all.3 = bf16[128,2176]{1,0:T(8,128)(2,1)} custom-call(bf16[32,128,2176]{2,1,0:T(8,128)(2,1)} %pad_maximum_fusion.part), custom_call_target="tpu_custom_call" | custom-call | tf_op jit(solution)/shard_map/sum_all/pallas_call | solution.py:782
  605.3 49.0 %gather_seq.3 = bf16[8,128,2048]{2,1,0:T(8,128)(2,1)} custom-call(bf16[128,2048]{1,0:T(8,128)(2,1)} %fusion.152.own), custom_call_target="tpu_custom_call" | custom-call | tf_op jit(solution)/shard_map/gather_seq/pallas_call | solution.py:846
  654.4 6.4 fusion.71
  660.8 38.2 %while.29 = (s32[]{:T(128)}, f32[1024,4,128]{0,2,1:T(8,128)S(1)}, f32[1024,4,128]{0,2,1:T(8,128)}, f32[2,512,4,128]{3,1,0,2:T(8,128)}, s32[2]{0:T(128)S(1)}, /*i...) while((s32[]{:T(128)}, f32[1024,4,128]{0,2,1:T(8,128)S(1)}, ...), condition=%wide.region_21.22_spmd.clone, body=%wide.region_19.21_spmd.clone.sunk | while | flops 2719218176 | bytes 119337416 | solution.py:130
  666.9 2.9 bitcast_add_fusion.5
  669.8 3.5 multiply_reduce_fusion.10
  686.0 2.9 bitcast_add_fusion.5
  688.9 3.5 multiply_reduce_fusion.10
  708.4 3.0 multiply_add_fusion.1
  713.3 2.8 copy_bitcast_fusion
  716.1 6.5 copy.290
  722.7 4.7 convolution_convert_fusion.7
  727.4 3.6 convolution_convert_fusion.6
  731.5 2.7 copy.291
  735.4 6.9 convolution_convert_fusion.5
  742.4 46.5 %sum_seq.3 = bf16[128,2048]{1,0:T(8,128)(2,1)} custom-call(bf16[8,128,2048]{2,1,0:T(8,128)(2,1)} %bitcast.262), custom_call_target="tpu_custom_call" | custom-call | tf_op jit(solution)/shard_map/sum_seq/pallas_call | solution.py:911
  791.1 19.9 %gather_all.3 = f32[32,16,384]{2,1,0:T(8,128)} custom-call(f32[16,384]{1,0:T(8,128)} %reshape.568.own), custom_call_target="tpu_custom_call" | custom-call | tf_op jit(solution)/shard_map/gather_all/pallas_call | solution.py:631
  812.3 13.7 %convolution_convert_fusion.1.part = bf16[32,128,2048]{2,1,0:T(8,128)(2,1)} fusion(bf16[32,64,2048]{2,1,0:T(8,128)(2,1)} %bitcast.245, f32[32,128]{1,0:T(8,128)S(1)} %copy-done.38, pred[32,128]{1,0:T(8,128)(4,1)S(1)} %copy-done.47), kind=kOutput, calls=%fused_computation.66 | convolution fusion | flops 1082654720 | bytes 25186304 | tf_op jit(solution)/shard_map/bct,bcd->btd/dot_general | solution.py:1062
  826.0 74.8 %sum_all.2 = bf16[128,2048]{1,0:T(8,128)(2,1)} custom-call(bf16[32,128,2048]{2,1,0:T(8,128)(2,1)} %convolution_convert_fusion.1.part), custom_call_target="tpu_custom_call" | custom-call | tf_op jit(solution)/shard_map/sum_all/pallas_call | solution.py:782
  903.3 20.2 %convolution_bitcast_fusion = f32[1,2048,1536]{2,1,0:T(8,128)} fusion(bf16[2048,2048]{1,0:T(8,128)(2,1)} %bitcast.250, bf16[2048,768]{0,1:T(8,128)(2,1)} %get-tuple-element.336, bf16[2048,768]{0,1:T(8,128)(2,1)} %get-tuple-element.335), kind=kOutput, calls=%fused_computation.67 | convolution fusion | flops 12897484800 | bytes 27262976 | tf_op jit(solution)/shard_map/rd,rf->df/dot_general | solution.py:1072
  923.6 5.6 all-to-all-start.1
  929.2 11.8 %convolution_bitcast_fusion.1 = f32[1,768,2048]{2,1,0:T(8,128)} fusion(bf16[2048,768]{0,1:T(8,128)(2,1)} %copy-done.96, bf16[2048,2048]{1,0:T(8,128)(2,1)} %get-tuple-element.337), kind=kOutput, calls=%fused_computation.81 | convolution fusion | flops 6442450944 | bytes 17825792 | tf_op jit(solution)/shard_map/rf,rd->fd/dot_general | solution.py:1071
  943.0 117.1 %reduce-scatter.7.cloned.1.call-done = f32[64,32]{1,0:T(8,128)} async-done(((f32[2048,32]{1,0:T(8,128)}), f32[64,32]{1,0:T(8,128)}) %reduce-scatter.7.cloned.1.call-update) | async-done | bytes 8208
  (367 shorter events, 128.6 us)
Async XLA Ops:
  7.2 429.6 %copy-start = (bf16[1,768,2048]{2,1,0:T(8,128)(2,1)S(1)}, bf16[1,768,2048]{2,1,0:T(8,128)(2,1)}, u32[]{:S(2)}) copy-start(bf16[1,768,2048]{2,1,0:T(8,128)(2,1)} %param.21) | copy-start | bytes 9437188
  7.2 182.5 %all-gather.7.cloned.1.call-start = ((), (), s32[]{:S(2)}) async-start(), calls=%async_computation.6 | async-start | bytes 6553600 | tf_op jit(solution)/shard_map/all_gather | solution.py:984
  16.8 41.1 %copy-start.82 = (bf16[64,32]{0,1:T(8,128)(2,1)S(1)}, bf16[64,32]{0,1:T(8,128)(2,1)}, u32[]{:S(2)}) copy-start(bf16[64,32]{0,1:T(8,128)(2,1)} %param.19) | copy-start | bytes 12292
  57.0 366.8 %all-gather.5.cloned.1.call-start = ((), (), s32[]{:S(2)}) async-start(), calls=%async_computation.4 | async-start | bytes 17301504 | tf_op jit(solution)/shard_map/all_gather | solution.py:988
  57.8 865.8 %reduce-scatter.5.cloned.1.call-start = ((), (), s32[]{:S(2)}) async-start(), calls=%async_computation.5 | async-start | bytes 6553600 | tf_op jit(solution)/shard_map/reduce_scatter | solution.py:1142
  99.1 204.2 %copy-start.39 = (bf16[2048,32]{0,1:T(8,128)(2,1)}, bf16[2048,32]{0,1:T(8,128)(2,1)S(1)}, u32[]{:S(2)}) copy-start(bf16[2048,32]{0,1:T(8,128)(2,1)S(1)} %reshape.576) | copy-start | bytes 393220
  250.6 49.0 %copy-start.5 = (bf16[1,128,2048]{2,1,0:T(8,128)(2,1)S(1)}, bf16[1,128,2048]{2,1,0:T(8,128)(2,1)}, u32[]{:S(2)}) copy-start(bf16[1,128,2048]{2,1,0:T(8,128)(2,1)} %param.16) | copy-start | bytes 1572868
  250.6 51.4 %copy-start.57 = (f32[2048]{0:T(1024)S(1)}, f32[2048]{0:T(1024)}, u32[]{:S(2)}) copy-start(f32[2048]{0:T(1024)} %param.23) | copy-start | bytes 24580
  250.6 53.8 %copy-start.69 = (s32[1,128,8]{1,2,0:T(8,128)S(1)}, s32[1,128,8]{1,2,0:T(8,128)}, u32[]{:S(2)}) copy-start(s32[1,128,8]{1,2,0:T(8,128)} %param.26) | copy-start | bytes 12292
  250.6 55.0 %copy-start.70 = (s32[1,128,8]{1,2,0:T(8,128)S(1)}, s32[1,128,8]{1,2,0:T(8,128)}, u32[]{:S(2)}) copy-start(s32[1,128,8]{1,2,0:T(8,128)} %param.26) | copy-start | bytes 12292
  395.1 94.8 %copy-start.46 = (pred[32,128]{1,0:T(8,128)(4,1)}, pred[32,128]{1,0:T(8,128)(4,1)S(1)}, u32[]{:S(2)}) copy-start(pred[32,128]{1,0:T(8,128)(4,1)S(1)} %broadcast_compare_fusion) | copy-start | bytes 12292
  395.1 94.8 %copy-start.37 = (f32[32,128]{1,0:T(8,128)}, f32[32,128]{1,0:T(8,128)S(1)}, u32[]{:S(2)}) copy-start(f32[32,128]{1,0:T(8,128)S(1)} %fusion.151) | copy-start | bytes 49156
  453.1 16.6 %copy-start.96 = (bf16[2048,768]{0,1:T(8,128)(2,1)}, bf16[2048,768]{0,1:T(8,128)(2,1)S(1)}, u32[]{:S(2)}) copy-start(bf16[2048,768]{0,1:T(8,128)(2,1)S(1)} %get-tuple-element.339) | copy-start | bytes 9437188
  489.8 13.7 %copy-start.93 = (bf16[32]{0:T(256)(128)(2,1)S(1)}, bf16[32]{0:T(256)(128)(2,1)}, u32[]{:S(2)}) copy-start(bf16[32]{0:T(256)(128)(2,1)} %compare_convert_fusion) | copy-start | bytes 196
  520.1 80.6 %copy-start.71 = (s32[1,128,8]{1,2,0:T(8,128)S(1)}, s32[1,128,8]{1,2,0:T(8,128)}, u32[]{:S(2)}) copy-start(s32[1,128,8]{1,2,0:T(8,128)} %param.26) | copy-start | bytes 12292
  520.1 80.7 %copy-start.56 = (f32[128,8]{0,1:T(8,128)S(1)}, f32[128,8]{0,1:T(8,128)}, u32[]{:S(2)}) copy-start(f32[128,8]{0,1:T(8,128)} %copy-done.55) | copy-start | bytes 12292
  520.1 80.7 %copy-start.76 = (f32[128]{0:T(128)S(1)}, f32[128]{0:T(128)}, u32[]{:S(2)}) copy-start(f32[128]{0:T(128)} %copy-done.75) | copy-start | bytes 1540
  520.1 80.7 %copy-start.81 = (f32[128]{0:T(128)S(1)}, f32[128]{0:T(128)}, u32[]{:S(2)}) copy-start(f32[128]{0:T(128)} %copy-done.80) | copy-start | bytes 1540
  520.1 81.5 %copy-start.6 = (bf16[1,128,2048]{2,1,0:T(8,128)(2,1)S(1)}, bf16[1,128,2048]{2,1,0:T(8,128)(2,1)}, u32[]{:S(2)}) copy-start(bf16[1,128,2048]{2,1,0:T(8,128)(2,1)} %param.16) | copy-start | bytes 1572868
  520.1 81.5 %copy-start.11 = (bf16[128,2048]{1,0:T(8,128)(2,1)S(1)}, bf16[128,2048]{1,0:T(8,128)(2,1)}, u32[]{:S(2)}) copy-start(bf16[128,2048]{1,0:T(8,128)(2,1)} %sum_seq.2) | copy-start | bytes 1572868
  520.1 81.5 %copy-start.40 = (bf16[2048,32]{0,1:T(8,128)(2,1)S(1)}, bf16[2048,32]{0,1:T(8,128)(2,1)}, u32[]{:S(2)}) copy-start(bf16[2048,32]{0,1:T(8,128)(2,1)} %copy-done.39) | copy-start | bytes 393220
  520.1 81.5 %copy-start.58 = (f32[2048]{0:T(1024)S(1)}, f32[2048]{0:T(1024)}, u32[]{:S(2)}) copy-start(f32[2048]{0:T(1024)} %param.23) | copy-start | bytes 24580
  520.1 81.5 %copy-start.78 = (f32[128]{0:T(128)S(1)}, f32[128]{0:T(128)}, u32[]{:S(2)}) copy-start(f32[128]{0:T(128)} %copy-done.77) | copy-start | bytes 1540
  601.6 52.8 %copy-start.63 = (bf16[128,32]{0,1:T(8,128)(2,1)}, bf16[128,32]{0,1:T(8,128)(2,1)S(1)}, u32[]{:S(2)}) copy-start(bf16[128,32]{0,1:T(8,128)(2,1)S(1)} %select_reduce_fusion) | copy-start | bytes 24580
  604.0 50.4 %copy-start.17 = (f32[128,2048]{1,0:T(8,128)}, f32[128,2048]{1,0:T(8,128)S(1)}, u32[]{:S(2)}) copy-start(f32[128,2048]{1,0:T(8,128)S(1)} %get-tuple-element.375) | copy-start | bytes 3145732
  604.0 50.4 %copy-start.89 = (f32[128]{0:T(128)}, f32[128]{0:T(128)S(1)}, u32[]{:S(2)}) copy-start(f32[128]{0:T(128)S(1)} %multiply_multiply_fusion.4) | copy-start | bytes 1540
  699.0 9.3 copy-start.27
  699.0 9.3 copy-start.29
  734.2 325.9 %reduce-scatter.7.cloned.1.call-start = ((), (), s32[]{:S(2)}) async-start(), calls=%async_computation.7 | async-start | bytes 1081344
  742.4 46.5 %copy-start.7 = (bf16[1,128,2048]{2,1,0:T(8,128)(2,1)S(1)}, bf16[1,128,2048]{2,1,0:T(8,128)(2,1)}, u32[]{:S(2)}) copy-start(bf16[1,128,2048]{2,1,0:T(8,128)(2,1)} %param.16) | copy-start | bytes 1572868
  742.4 46.5 %copy-start.62 = (f32[2048]{0:T(1024)S(1)}, f32[2048]{0:T(1024)}, u32[]{:S(2)}) copy-start(f32[2048]{0:T(1024)} %param.22) | copy-start | bytes 24580
  742.4 46.5 %copy-start.85 = (f32[128]{0:T(128)S(1)}, f32[128]{0:T(128)}, u32[]{:S(2)}) copy-start(f32[128]{0:T(128)} %copy-done.84) | copy-start | bytes 1540
  742.4 48.1 %copy-start.74 = (f32[2048]{0:T(1024)S(1)}, f32[2048]{0:T(1024)}, u32[]{:S(2)}) copy-start(f32[2048]{0:T(1024)} %get-tuple-element.289) | copy-start | bytes 24580
  742.4 69.9 %copy-start.38 = (f32[32,128]{1,0:T(8,128)S(1)}, f32[32,128]{1,0:T(8,128)}, u32[]{:S(2)}) copy-start(f32[32,128]{1,0:T(8,128)} %copy-done.37) | copy-start | bytes 49156
  742.4 69.9 %copy-start.47 = (pred[32,128]{1,0:T(8,128)(4,1)S(1)}, pred[32,128]{1,0:T(8,128)(4,1)}, u32[]{:S(2)}) copy-start(pred[32,128]{1,0:T(8,128)(4,1)} %copy-done.46) | copy-start | bytes 12292
  826.0 74.9 %copy-start.92 = (f32[128]{0:T(128)S(1)}, f32[128]{0:T(128)}, u32[]{:S(2)}) copy-start(f32[128]{0:T(128)} %copy-done.91) | copy-start | bytes 1540
  826.0 76.0 %copy-start.20 = (bf16[128,2048]{1,0:T(8,128)(2,1)S(1)}, bf16[128,2048]{1,0:T(8,128)(2,1)}, u32[]{:S(2)}) copy-start(bf16[128,2048]{1,0:T(8,128)(2,1)} %copy-done.19) | copy-start | bytes 1572868
  826.0 76.0 %copy-start.64 = (bf16[128,32]{0,1:T(8,128)(2,1)S(1)}, bf16[128,32]{0,1:T(8,128)(2,1)}, u32[]{:S(2)}) copy-start(bf16[128,32]{0,1:T(8,128)(2,1)} %copy-done.63) | copy-start | bytes 24580
  923.6 137.9 %all-to-all-start.1 = ((bf16[8,64,1280]{2,1,0:T(8,128)(2,1)}), bf16[8,64,1280]{2,1,0:T(8,128)(2,1)}, u32[]{:S(2)}, u32[]{:S(2)}) async-start(bf16[8,64,1280]{2,1,0:T(8,128)(2,1)} %bitcast.271), calls=%async_computation.2 | async-start | bytes 2621440 | tf_op jit(solution)/shard_map/all_to_all | solution.py:1143
  929.1 11.9 %copy-start.12 = (bf16[128,2048]{1,0:T(8,128)(2,1)S(1)}, bf16[128,2048]{1,0:T(8,128)(2,1)}, u32[]{:S(2)}) copy-start(bf16[128,2048]{1,0:T(8,128)(2,1)} %sum_seq.2) | copy-start | bytes 1572868
  929.2 11.9 %copy-start.18 = (f32[128,2048]{1,0:T(8,128)S(1)}, f32[128,2048]{1,0:T(8,128)}, u32[]{:S(2)}) copy-start(f32[128,2048]{1,0:T(8,128)} %copy-done.17) | copy-start | bytes 3145732
  929.2 11.9 %copy-start.30 = (bf16[128,2048]{1,0:T(8,128)(2,1)S(1)}, bf16[128,2048]{1,0:T(8,128)(2,1)}, u32[]{:S(2)}) copy-start(bf16[128,2048]{1,0:T(8,128)(2,1)} %sum_seq.3) | copy-start | bytes 1572868
  929.2 11.9 %copy-start.32 = (bf16[1,128,2048]{2,1,0:T(8,128)(2,1)S(1)}, bf16[1,128,2048]{2,1,0:T(8,128)(2,1)}, u32[]{:S(2)}) copy-start(bf16[1,128,2048]{2,1,0:T(8,128)(2,1)} %param.27) | copy-start | bytes 1572868
  929.2 11.9 %copy-start.34 = (bf16[128,2048]{1,0:T(8,128)(2,1)S(1)}, bf16[128,2048]{1,0:T(8,128)(2,1)}, u32[]{:S(2)}) copy-start(bf16[128,2048]{1,0:T(8,128)(2,1)} %sum_all.2) | copy-start | bytes 1572868
  929.2 11.9 %copy-start.59 = (f32[2048]{0:T(1024)S(1)}, f32[2048]{0:T(1024)}, u32[]{:S(2)}) copy-start(f32[2048]{0:T(1024)} %param.23) | copy-start | bytes 24580
  929.2 11.9 %copy-start.79 = (f32[128]{0:T(128)S(1)}, f32[128]{0:T(128)}, u32[]{:S(2)}) copy-start(f32[128]{0:T(128)} %copy-done.77) | copy-start | bytes 1540
  929.2 11.9 %copy-start.90 = (f32[128]{0:T(128)S(1)}, f32[128]{0:T(128)}, u32[]{:S(2)}) copy-start(f32[128]{0:T(128)} %copy-done.89) | copy-start | bytes 1540
  1065.1 9.3 copy-start.1
  (63 other events, 191.0 us)
Sparse Core Ops, SparseCore 0:
  57.1 41.5 all-gather.6
  101.6 133.6 all-gather.4
  734.3 49.8 reduce-scatter.4
  923.7 136.3 reduce-scatter.6

commit v3 on v2

--- a/solution.py
+++ b/solution.py
@@ -583,7 +583,6 @@
             await_bytes(own, rs.at[q, G_C0 + j])
 
     def finish():
-        pltpu.make_async_copy(own, out.at[cols(p.z)[0]], local_sem).wait()
         piece = own.at[pl.ds(0, half)]
         for q in range(4):
             for kind in (G_X, G_Y, G_C0, G_C0 + 1, G_C0 + 2, G_C0 + 3):
@@ -623,6 +622,7 @@
     plane_end(3)
     for k in range(4):
         plane_core(k)
+    pltpu.make_async_copy(own, out.at[p.me], local_sem).wait()
     finish()
 
 
@@ -928,6 +928,589 @@
         ),
         name="sum_seq",
     )(part)
+
+
+def seq_peer(p, d):
+    return ((p.z * 2 + p.x + d) % 8, p.y * 2 + p.c)
+
+
+def greet_seq(p, sides=("y", "core")):
+    barrier = pltpu.get_barrier_semaphore()
+    for d in range(1, 8):
+        pl.semaphore_signal(barrier, inc=1, device_id=seq_peer(p, d), device_id_type=MESH)
+    for side in sides:
+        target = {"y": p.by_y, "core": p.by_core}[side]
+        pl.semaphore_signal(barrier, inc=1, device_id=target, device_id_type=MESH)
+    pl.semaphore_wait(barrier, 7 + len(sides))
+
+
+def enter_kernel(own, pieces, rows_out, columns, ss, rs, zs, cs, cr, ys, yr, ks, kr, local_sems):
+    p = Place()
+    greet_seq(p)
+    place, shard = p.z * 2 + p.x, p.y * 2 + p.c
+    mine = place * 4 + shard
+
+    def rows_at(q, x):
+        return rows_out.at[q * 2 + x]
+
+    def plane_out(k):
+        q = p.near(k)
+        there = rows_at(q, p.x)
+        if k == 0:
+            src = own
+            for step, end in ((1, p.high), (-1, p.low)):
+
+                @pl.when(jnp.logical_not(end))
+                def _():
+                    send(src, there, zs.at[q, 0 if step > 0 else 1], rs.at[q, 0], p.by_z(step))
+
+            pltpu.make_async_copy(own, there, local_sems.at[0]).start()
+        else:
+            src = there
+            await_bytes(src, rs.at[q, 0])
+
+            @pl.when(p.inner)
+            def _():
+                send(src, src, zs.at[q, 0], rs.at[q, 0], p.by_z(p.onward(k)))
+
+        send(src, there, ss.at[q], rs.at[q, 1], p.by_x)
+
+    def pass_on(d):
+        block = ((place + 8 - d) % 8) * 4 + shard
+        src = pieces.at[place] if d == 0 else columns.at[block]
+        if d > 0:
+            await_bytes(src, cr.at[d])
+        send(src, columns.at[block], ys.at[d], yr.at[d], p.by_y)
+        send(src, columns.at[block], ks.at[0, d], kr.at[0, d], p.by_core)
+
+    plane_out(0)
+    for d in range(1, 8):
+        send(pieces.at[(place + d) % 8], columns.at[mine], cs.at[d], cr.at[d], seq_peer(p, d))
+    pltpu.make_async_copy(pieces.at[place], columns.at[mine], local_sems.at[1]).start()
+    pass_on(0)
+    plane_out(1)
+    for d in (1, 2, 7):
+        pass_on(d)
+    plane_out(2)
+    for d in (6, 3, 5):
+        pass_on(d)
+    plane_out(3)
+    pass_on(4)
+    other = p.y * 2 + 1 - p.c
+    across = (1 - p.y) * 2 + p.c
+    piece = pieces.at[0]
+    for d in (0, 1, 2, 7, 6, 3, 5, 4):
+        block = columns.at[((place + 8 - d) % 8) * 4 + across]
+        await_bytes(block, yr.at[d])
+        send(block, block, ks.at[1, d], kr.at[1, d], p.by_core)
+    for k in range(4):
+        await_bytes(own, rs.at[p.near(k), 1])
+    for d in range(8):
+        await_bytes(piece, kr.at[0, d])
+        await_bytes(piece, kr.at[1, d])
+    pltpu.make_async_copy(own, rows_at(p.z, p.x), local_sems.at[0]).wait()
+    pltpu.make_async_copy(pieces.at[place], columns.at[mine], local_sems.at[1]).wait()
+    for q in range(4):
+        await_bytes(own, ss.at[q])
+    for there, slot in ((p.high, 0), (p.low, 1)):
+
+        @pl.when(jnp.logical_not(there))
+        def _():
+            await_bytes(own, zs.at[p.z, slot])
+
+    for k in range(1, 4):
+
+        @pl.when(p.inner)
+        def _():
+            await_bytes(own, zs.at[p.near(k), 0])
+
+    for d in range(8):
+        if d > 0:
+            await_bytes(piece, cs.at[d])
+        await_bytes(piece, ys.at[d])
+        await_bytes(piece, ks.at[0, d])
+        await_bytes(piece, ks.at[1, d])
+
+
+def enter(own, pieces, collective_id):
+    dma = pltpu.SemaphoreType.DMA
+    count, piece_rows, piece_width = pieces.shape
+    return pl.pallas_call(
+        enter_kernel,
+        out_shape=[
+            jax.ShapeDtypeStruct((count, *own.shape), own.dtype),
+            jax.ShapeDtypeStruct((count * 4, piece_rows, piece_width), pieces.dtype),
+        ],
+        in_specs=[pl.BlockSpec(memory_space=pl.ANY)] * 2,
+        out_specs=[pl.BlockSpec(memory_space=pl.ANY)] * 2,
+        scratch_shapes=[
+            dma((4,)),
+            dma((4, 2)),
+            dma((4, 2)),
+            dma((8,)),
+            dma((8,)),
+            dma((8,)),
+            dma((8,)),
+            dma((2, 8)),
+            dma((2, 8)),
+            dma((2,)),
+        ],
+        compiler_params=pltpu.CompilerParams(
+            collective_id=collective_id, has_side_effects=True, vmem_limit_bytes=VMEM_LIMIT
+        ),
+        name="enter",
+    )(own, pieces)
+
+
+def leave_kernel(
+    part, cols, tokens, d_hidden, gain, gains,
+    d_tokens, cols_out, gains_out,
+    held, x_in, z_in, c_held, c_core, c_y, g_send, g_in,
+    ls, ss, rs, zs, zr, cl, cs, cr, ys, yr, ts, tr, gs, gr,
+):
+    p = Place()
+    greet_seq(p)
+    rows = part.shape[1]
+    place = p.z * 2 + p.x
+    for turn, side in ((0, 1 - p.y), (1, p.y)):
+        send(cols.at[:, side, 1 - p.c], c_core.at[turn], cs.at[turn], cr.at[turn], p.by_core)
+        pltpu.make_async_copy(cols.at[:, side, p.c], c_held.at[turn], cl.at[turn]).start()
+    for k in range(4):
+        q = p.far(k)
+        send(part.at[q * 2 + 1 - p.x], x_in.at[q], ss.at[q], rs.at[q], p.by_x)
+        pltpu.make_async_copy(part.at[q * 2 + p.x], held.at[q], ls.at[q]).start()
+    piece_rows = c_held.shape[2]
+    order = [(place + d) % 8 for d in range(1, 9)]
+    for turn in range(2):
+        await_bytes(c_held.at[turn], cl.at[turn])
+        await_bytes(c_core.at[turn], cr.at[turn])
+        for i, s in enumerate(order):
+            add_rows(c_held.at[turn, s], c_core.at[turn, s], piece_rows)
+            if turn == 0:
+                send(c_held.at[0, s], c_y.at[s], ys.at[s], yr.at[s], p.by_y)
+
+    def turn_in(i):
+        s = order[i]
+        await_bytes(c_y.at[s], yr.at[s])
+        add_rows(c_held.at[1, s], c_y.at[s], piece_rows)
+        if i < 7:
+            send(c_held.at[1, s], cols_out.at[place], ts.at[i], tr.at[i], seq_peer(p, i + 1))
+        else:
+            pltpu.make_async_copy(c_held.at[1, s], cols_out.at[place], ts.at[7]).start()
+
+    for k in range(4):
+        q = p.far(k)
+        mine = held.at[q]
+        await_bytes(mine, ls.at[q])
+        await_bytes(x_in.at[q], rs.at[q])
+        add_rows(mine, x_in.at[q], rows)
+        if k < 3:
+            step = p.toward(k)
+            slot = (1 - step) // 2
+
+            @pl.when(p.inner)
+            def _():
+                await_bytes(z_in.at[slot, q], zr.at[slot, q])
+                add_rows(mine, z_in.at[slot, q], rows)
+
+            send(mine, z_in.at[slot, q], zs.at[k], zr.at[slot, q], p.by_z(step))
+            for i in ((0, 1), (2, 3), (4, 5, 6, 7))[k]:
+                turn_in(i)
+        else:
+            for slot, there in ((0, p.low), (1, p.high)):
+
+                @pl.when(jnp.logical_not(there))
+                def _():
+                    await_bytes(z_in.at[slot, q], zr.at[slot, q])
+                    add_rows(mine, z_in.at[slot, q], rows)
+
+    mine = held.at[p.z]
+    g_send[0] = jnp.zeros_like(g_send[0])
+    chunk = 16
+
+    @pl.loop(0, rows // chunk)
+    def _(i):
+        at = pl.ds(pl.multiple_of(i * chunk, chunk), chunk)
+        d_out = mine[at, :].astype(jnp.float32)
+        x = tokens[at, :].astype(jnp.float32)
+        scale = lax.rsqrt(jnp.mean(x * x, axis=-1, keepdims=True) + EPS)
+        u = d_out * gain[...]
+        dot = jnp.mean(u * x, axis=-1, keepdims=True)
+        d_x = scale * u - x * (scale * scale * scale * dot)
+        d_tokens[at, :] = (d_hidden[at, :] + d_x).astype(d_tokens.dtype)
+        terms = d_out * x * scale
+        g_send[0] += terms[:8] + terms[8:]
+
+    first = jnp.sum(g_send[0], axis=0, keepdims=True)
+    row = lax.broadcasted_iota(jnp.int32, g_send[0].shape, 0)
+    g_send[0] = jnp.where(row == 0, first, gains[...])
+    for t, target in enumerate((p.by_core, p.by_y, p.by_x)):
+        send(g_send.at[t], g_in.at[t], gs.at[t], gr.at[t], target)
+        await_bytes(g_in.at[t], gr.at[t])
+        g_send[t + 1] = g_send[t] + g_in[t]
+    for d in (1, 2, 3):
+        target = p.device((p.z + d) % 4, p.x, p.y, p.c)
+        send(g_send.at[3], g_in.at[3 + p.z], gs.at[2 + d], gr.at[2 + d], target)
+    g_in[3 + p.z] = g_send[3]
+    for d in (1, 2, 3):
+        await_bytes(g_in.at[0], gr.at[2 + d])
+    gains_out[...] = g_in[3] + g_in[4] + g_in[5] + g_in[6]
+
+    piece = c_y.at[0]
+    for i in range(8):
+        if i < 7:
+            await_bytes(piece, tr.at[i])
+        await_bytes(piece, ts.at[i])
+        await_bytes(piece, ys.at[i])
+    for turn in range(2):
+        await_bytes(c_core.at[turn], cs.at[turn])
+    for q in range(4):
+        await_bytes(x_in.at[0], ss.at[q])
+    for k in range(3):
+        await_bytes(x_in.at[0], zs.at[k])
+    for t in range(6):
+        await_bytes(g_in.at[0], gs.at[t])
+
+
+def leave(part, cols, tokens, d_hidden, gain, gains, collective_id):
+    _, rows, width = part.shape
+    piece_rows, piece_width = cols.shape[3:]
+    dma = pltpu.SemaphoreType.DMA
+    bf16, f32 = jnp.bfloat16, jnp.float32
+    anywhere, vmem = pl.BlockSpec(memory_space=pl.ANY), pl.BlockSpec(memory_space=pltpu.VMEM)
+    return pl.pallas_call(
+        leave_kernel,
+        out_shape=[
+            jax.ShapeDtypeStruct((rows, width), bf16),
+            jax.ShapeDtypeStruct((8, piece_rows, piece_width), bf16),
+            jax.ShapeDtypeStruct(gains.shape, f32),
+        ],
+        in_specs=[anywhere] * 2 + [vmem] * 4,
+        out_specs=[vmem, anywhere, vmem],
+        scratch_shapes=[
+            pltpu.VMEM((4, rows, width), bf16),
+            pltpu.VMEM((4, rows, width), bf16),
+            pltpu.VMEM((2, 4, rows, width), bf16),
+            pltpu.VMEM((2, 8, piece_rows, piece_width), bf16),
+            pltpu.VMEM((2, 8, piece_rows, piece_width), bf16),
+            pltpu.VMEM((8, piece_rows, piece_width), bf16),
+            pltpu.VMEM((4, *gains.shape), f32),
+            pltpu.VMEM((7, *gains.shape), f32),
+            dma((4,)),
+            dma((4,)),
+            dma((4,)),
+            dma((3,)),
+            dma((2, 4)),
+            dma((2,)),
+            dma((2,)),
+            dma((2,)),
+            dma((8,)),
+            dma((8,)),
+            dma((8,)),
+            dma((7,)),
+            dma((6,)),
+            dma((6,)),
+        ],
+        compiler_params=pltpu.CompilerParams(
+            collective_id=collective_id, has_side_effects=True, vmem_limit_bytes=VMEM_LIMIT
+        ),
+        name="leave",
+    )(part, cols, tokens, d_hidden, gain, gains)
+
+
+NT = (((1,), (1,)), ((), ()))
+TILE = 256
+
+
+def mxu(a, b, dims=(((1,), (0,)), ((), ()))):
+    return lax.dot_general(a, b, dims, preferred_element_type=jnp.float32)
+
+
+def experts_kernel(
+    own, cot_all, w_in_hbm, w_down_hbm,
+    rows_all, out_part, d_part, x_all, d_expert_all, inner_all, d_gate_up_all,
+    w_in, w_down, row_buf, cot_buf, pick, pick_t, gates, d_gates, x, cot, d_expert,
+    by_d_gate, by_d_up, inner, d_gate_up, out_stage, d_stage,
+    ss, rs, zs, local_sem, load_sems, store_sems,
+):
+    p = Place()
+    bf16, f32 = jnp.bfloat16, jnp.float32
+    width = cot_all.shape[2]
+    blocks = 8
+    slots = gates.shape[0]
+    capacity = slots // blocks
+    tokens = row_buf.shape[2]
+    group = 4
+    experts = rows_all.shape[0]
+    p.greet(("x", "y", "core", "z"))
+    plane_out, plane_turn, plane_end, plane_core, finish = gather_steps(
+        p, own, rows_all, ss, rs, zs, local_sem
+    )
+
+    def weights(start):
+        for i, (src, dst) in enumerate(((w_in_hbm, w_in), (w_down_hbm, w_down))):
+            copy = pltpu.make_async_copy(src, dst, load_sems.at[i])
+            copy.start() if start else copy.wait()
+
+    def cot_load(k):
+        return pltpu.make_async_copy(
+            cot_all.at[pl.ds(p.near(k) * blocks, blocks)], cot_buf.at[k % 2], load_sems.at[2 + k]
+        )
+
+    def row_load(k):
+        return pltpu.make_async_copy(
+            rows_all.at[pl.ds(p.near(k) * blocks, blocks)], row_buf.at[k % 2], load_sems.at[6 + k]
+        )
+
+    def arrived(k):
+        plane_core(k)
+        if k == 0:
+            pltpu.make_async_copy(own, rows_all.at[p.me], local_sem).wait()
+        row_load(k).start()
+
+    at_slot = {}
+
+    def store(k, i, src, dst):
+        if (k, i) not in at_slot:
+            at_slot[k, i] = pltpu.make_async_copy(src, dst, store_sems.at[i, k % 2])
+        return at_slot[k, i]
+
+    def stores(k):
+        q = p.near(k)
+        at = pl.ds(q * slots, slots)
+        plane = pl.ds(q * blocks, blocks)
+        return [
+            (x, x_all.at[at]),
+            (d_expert, d_expert_all.at[at]),
+            (inner, inner_all.at[at]),
+            (d_gate_up, d_gate_up_all.at[at]),
+            (out_stage, out_part.at[plane]),
+            (d_stage, d_part.at[plane]),
+        ]
+
+    def put(k, i):
+        store(k, i, *stores(k)[i]).start()
+
+    def free(k, i):
+        if k > 0:
+            store(k - 1, i, *stores(k - 1)[i]).wait()
+
+    def pick_rows(k):
+        lane = lax.broadcasted_iota(jnp.int32, (8, 128), 1)
+        line = lax.broadcasted_iota(jnp.int32, (8, 128), 0)
+        select = jnp.where((lane == line * experts + p.me) & (line < 3), 1.0, 0.0).astype(bf16)
+        before = jnp.where(
+            lax.broadcasted_iota(jnp.int32, (tokens, tokens), 0)
+            < lax.broadcasted_iota(jnp.int32, (tokens, tokens), 1),
+            1.0,
+            0.0,
+        ).astype(bf16)
+        slot_id = lax.broadcasted_iota(jnp.int32, (capacity, tokens), 0).astype(f32)
+        rows, cots = row_buf.at[k % 2], cot_buf.at[k % 2]
+
+        @pl.loop(0, blocks // group)
+        def _(g):
+            for i in range(group):
+                info = rows[g * group + i, :, width:]
+                lines = mxu(select, info, NT)
+                named = lines[2:3]
+                slot = mxu(lines.astype(bf16), before)[2:3]
+                chosen = jnp.where((slot == slot_id) & (named > 0.5), 1.0, 0.0)
+                gate = jnp.sum(chosen * (lines[0:1] + lines[1:2]), axis=1, keepdims=True)
+                at = pl.ds(pl.multiple_of(g * group * capacity + i * capacity, capacity), capacity)
+                gates[at, :] = jnp.broadcast_to(gate, (capacity, 128))
+                lead = [jnp.zeros((capacity, tokens), bf16)] * i
+                tail = [jnp.zeros((capacity, tokens), bf16)] * (group - 1 - i)
+                pick[g, i * capacity : (i + 1) * capacity, :] = jnp.concatenate(
+                    lead + [chosen.astype(bf16)] + tail, axis=1
+                )
+                turned = chosen.T
+                lead = [jnp.zeros((tokens, capacity), f32)] * i
+                tail = [jnp.zeros((tokens, capacity), f32)] * (group - 1 - i)
+                pick_t[g, i * tokens : (i + 1) * tokens, :] = jnp.concatenate(
+                    lead + [turned] + tail, axis=1
+                ).astype(bf16)
+            at = pl.ds(pl.multiple_of(g * group * capacity, group * capacity), group * capacity)
+            scale = gates[at, :]
+            scale = jnp.concatenate([scale] * (TILE // 128), axis=1)
+            which = pl.ds(g * group, group)
+
+            @pl.loop(0, width // TILE)
+            def _(n):
+                cols = pl.ds(pl.multiple_of(n * TILE, TILE), TILE)
+                row_tile = rows[which, :, cols].reshape(group * tokens, TILE)
+                x[at, cols] = mxu(pick[g], row_tile).astype(bf16)
+                cot_tile = cots[which, :, cols].reshape(group * tokens, TILE)
+                picked = mxu(pick[g], cot_tile)
+                cot[at, cols] = picked.astype(bf16)
+                d_expert[at, cols] = (scale * picked).astype(bf16)
+
+    def up(k):
+        ff = inner.shape[1]
+
+        @pl.loop(0, ff // TILE)
+        def _(n):
+            cols = pl.ds(pl.multiple_of(n * TILE, TILE), TILE)
+            gate = mxu(x[...], w_in[:, cols])
+            raised = mxu(x[...], w_in[:, pl.ds(pl.multiple_of(ff + n * TILE, TILE), TILE)])
+            sig = jax.nn.sigmoid(gate)
+            silu = gate * sig
+            inner[:, cols] = (silu * raised).astype(bf16)
+            by_d_up[:, cols] = silu
+            by_d_gate[:, cols] = raised * sig * (1.0 + gate * (1.0 - sig))
+
+    def d_up(k):
+        ff = inner.shape[1]
+
+        @pl.loop(0, ff // TILE)
+        def _(n):
+            cols = pl.ds(pl.multiple_of(n * TILE, TILE), TILE)
+            d_inner = mxu(d_expert[...], w_down[cols, :], NT)
+            d_gate_up[:, cols] = (d_inner * by_d_gate[:, cols]).astype(bf16)
+            d_gate_up[:, pl.ds(pl.multiple_of(ff + n * TILE, TILE), TILE)] = (
+                d_inner * by_d_up[:, cols]
+            ).astype(bf16)
+
+    def scatter(value, stage, cols, wide):
+        for g in range(blocks // group):
+            part = value[g * group * capacity : (g + 1) * group * capacity]
+            spread = mxu(pick_t[g], part).astype(bf16)
+            stage[g * group : (g + 1) * group, :, cols] = spread.reshape(group, tokens, wide)
+
+    def down(k):
+        d_gates[...] = jnp.zeros_like(d_gates)
+        scale = jnp.concatenate([gates[...]] * (TILE // 128), axis=1)
+
+        @pl.loop(0, width // TILE)
+        def _(n):
+            cols = pl.ds(pl.multiple_of(n * TILE, TILE), TILE)
+            result = mxu(inner[...], w_down[:, cols]).astype(bf16).astype(f32)
+            product = result * cot[:, cols].astype(f32)
+            total = product[:, :128]
+            for j in range(1, TILE // 128):
+                total = total + product[:, j * 128 : (j + 1) * 128]
+            d_gates[...] += total
+            scatter((scale * result).astype(bf16), out_stage, cols, TILE)
+
+    def d_down(k):
+        total = jnp.sum(d_gates[...], axis=1, keepdims=True)
+        high = total.astype(bf16).astype(f32)
+        lane = lax.broadcasted_iota(jnp.int32, (slots, 128), 1)
+        info = jnp.where(lane == p.me, high, jnp.where(lane == experts + p.me, total - high, 0.0))
+        scatter(info.astype(bf16), d_stage, pl.ds(width, 128), 128)
+
+        @pl.loop(0, width // TILE)
+        def _(n):
+            cols = pl.ds(pl.multiple_of(n * TILE, TILE), TILE)
+            d_rows = mxu(d_gate_up[...], w_in[cols, :], NT)
+            scatter(d_rows.astype(bf16), d_stage, cols, TILE)
+
+    plane_out(0)
+    weights(True)
+    cot_load(0).start()
+    plane_out(1)
+    plane_turn(0)
+    plane_end(0)
+    arrived(0)
+    weights(False)
+    after = {
+        0: ([lambda: plane_out(2)], [lambda: plane_turn(1)], [lambda: plane_out(3)], [lambda: plane_end(1)], [lambda: arrived(1)]),
+        1: ([], [lambda: plane_turn(2)], [], [lambda: plane_end(2)], [lambda: arrived(2)]),
+        2: ([], [lambda: plane_turn(3)], [], [lambda: plane_end(3)], [lambda: arrived(3)]),
+        3: ([], [], [], [], []),
+    }
+    for k in range(4):
+
+        def service(i):
+            for step in after[k][i]:
+                step()
+
+        row_load(k).wait()
+        cot_load(k).wait()
+        if k < 3:
+            cot_load(k + 1).start()
+        free(k, 0)
+        free(k, 1)
+        pick_rows(k)
+        put(k, 0)
+        put(k, 1)
+        service(0)
+        free(k, 2)
+        up(k)
+        put(k, 2)
+        service(1)
+        free(k, 3)
+        d_up(k)
+        put(k, 3)
+        service(2)
+        free(k, 4)
+        down(k)
+        put(k, 4)
+        service(3)
+        free(k, 5)
+        d_down(k)
+        put(k, 5)
+        service(4)
+    for i in range(6):
+        free(4, i)
+    finish()
+
+
+def experts_gathered(own, cot_all, w_in, w_down, capacity, collective_id):
+    tokens, wide = own.shape
+    experts, _, width = cot_all.shape
+    ff = w_down.shape[0]
+    slots = 8 * capacity
+    dma = pltpu.SemaphoreType.DMA
+    bf16, f32 = jnp.bfloat16, jnp.float32
+    anywhere = pl.BlockSpec(memory_space=pl.ANY)
+
+    def array(*shape):
+        return jax.ShapeDtypeStruct(shape, bf16)
+
+    return pl.pallas_call(
+        experts_kernel,
+        out_shape=[
+            array(experts, tokens, wide),
+            array(experts, tokens, width),
+            array(experts, tokens, wide),
+            array(experts * capacity, width),
+            array(experts * capacity, width),
+            array(experts * capacity, ff),
+            array(experts * capacity, 2 * ff),
+        ],
+        in_specs=[anywhere] * 4,
+        out_specs=[anywhere] * 7,
+        scratch_shapes=[
+            pltpu.VMEM(w_in.shape, bf16),
+            pltpu.VMEM(w_down.shape, bf16),
+            pltpu.VMEM((2, 8, tokens, wide), bf16),
+            pltpu.VMEM((2, 8, tokens, width), bf16),
+            pltpu.VMEM((2, 4 * capacity, 4 * tokens), bf16),
+            pltpu.VMEM((2, 4 * tokens, 4 * capacity), bf16),
+            pltpu.VMEM((slots, 128), f32),
+            pltpu.VMEM((slots, 128), f32),
+            pltpu.VMEM((slots, width), bf16),
+            pltpu.VMEM((slots, width), bf16),
+            pltpu.VMEM((slots, width), bf16),
+            pltpu.VMEM((slots, ff), f32),
+            pltpu.VMEM((slots, ff), f32),
+            pltpu.VMEM((slots, ff), bf16),
+            pltpu.VMEM((slots, 2 * ff), bf16),
+            pltpu.VMEM((8, tokens, width), bf16),
+            pltpu.VMEM((8, tokens, wide), bf16),
+            dma((4, G_KINDS)),
+            dma((4, G_KINDS)),
+            dma((4, 2)),
+            dma,
+            dma((10,)),
+            dma((6, 2)),
+        ],
+        compiler_params=pltpu.CompilerParams(
+            collective_id=collective_id, has_side_effects=True, vmem_limit_bytes=VMEM_LIMIT
+        ),
+        name="experts",
+    )(own, cot_all, w_in, w_down)
 
 
 def head_columns(weight, group_index):
@@ -970,6 +1553,7 @@
     kv_cols = HEAD_DIMENSION
     proj_cols = head_cols + 2 * kv_cols
     all_cols = proj_cols + head_cols
+    spare_cols = 128
     group_index = [s * heads * KEY_VALUE_HEADS // QUERY_HEADS for s in range(seq_size)]
     capacity = 2 * rows * TOPK // experts
 
@@ -977,19 +1561,24 @@
         [
             head_columns(query_key_value_weight, group_index),
             w_out_t.reshape(weight_rows, seq_size, head_cols).transpose(1, 0, 2),
+            jnp.broadcast_to(
+                jnp.pad(w_router, ((0, 0), (0, spare_cols - experts))),
+                (seq_size, weight_rows, spare_cols),
+            ),
         ],
         axis=2,
     )
-    pieces = lax.all_to_all(pieces, "seq", split_axis=0, concat_axis=0, tiled=True)
-    columns = lax.all_gather(pieces, "fsdp", axis=1).reshape(width, all_cols)
-    proj_weight = columns[:, :proj_cols]
-    out_weight = columns[:, proj_cols:]
-    full_router = lax.all_gather(w_router, both, axis=0, tiled=True)
-    cot_all = lax.all_gather(cotangent[0], both)
-
     resid_in = tokens[0].astype(f32)
     normed_one = rms_scale(resid_in, attn_gain).astype(bf16)
-    normed_all = gather_seq(normed_one, 1).reshape(length, width)
+    normed_all, columns = enter(normed_one, pieces, 1)
+    normed_all = normed_all.reshape(length, width)
+    columns = columns.reshape(width, -1)
+    proj_weight = columns[:, :proj_cols]
+    out_weight = columns[:, proj_cols:all_cols]
+    full_router = columns[:, all_cols : all_cols + experts]
+    columns, cot_own = lax.optimization_barrier((columns, cotangent[0]))
+    cot_all = lax.all_gather(cot_own, both)
+
     projected = jnp.dot(normed_all, proj_weight, preferred_element_type=f32)
     seq_positions = jnp.arange(length, dtype=jnp.int32)
     prepare = partial(head_prepare, positions=seq_positions)
@@ -1021,71 +1610,21 @@
     gate_low = (gate_dense - gate_high.astype(f32)).astype(bf16)
     route_info = jnp.concatenate([gate_high, gate_low, named.astype(bf16)], axis=1)
     route_info = jnp.pad(route_info, ((0, 0), (0, 128 - route_info.shape[1] % 128)))
-    gathered = gather_all(jnp.concatenate([normed_two, route_info], axis=1), experts, 3)
-    blocks = experts
-    rows_all = gathered[:, :, :width]
-    info = gathered[:, :, width : width + 3 * experts].reshape(blocks, rows, 3, experts)
-    me = lax.axis_index("seq") * shard_size + lax.axis_index("fsdp")
-    own = lax.dynamic_index_in_dim(info, me, 3, keepdims=False).astype(f32)
-    gate_own = own[:, :, 0] + own[:, :, 1]
-    named_own = own[:, :, 2]
-    slot = jnp.cumsum(named_own, axis=1) - named_own
-    pick = (
-        (slot[:, None, :] == jnp.arange(capacity, dtype=f32)[None, :, None])
-        & (named_own[:, None, :] > 0)
-    ).astype(bf16)
-    gate_slots = jnp.einsum(
-        "bct,bt->bc", pick.astype(f32), gate_own, precision=lax.Precision.HIGHEST
-    ).reshape(-1, 1)
-    rows_in = jnp.einsum("bct,btd->bcd", pick, rows_all, preferred_element_type=f32)
-    rows_in = rows_in.astype(bf16).reshape(-1, width)
-    cot_rows = jnp.einsum(
-        "bct,btd->bcd",
-        pick,
-        cot_all.reshape(blocks, rows, width),
-        preferred_element_type=f32,
-    ).reshape(-1, width)
-
     gate_weight = w_in[0]
     down_weight = w_down[0]
-    gate_up = jnp.dot(rows_in, gate_weight, preferred_element_type=f32)
-    gate_half = gate_up[:, :FF]
-    up_half = gate_up[:, FF:]
-    gate_sig = jax.nn.sigmoid(gate_half)
-    silu_gate = gate_half * gate_sig
-    inner_act = (silu_gate * up_half).astype(bf16)
-    expert_out = (
-        jnp.dot(inner_act, down_weight, preferred_element_type=f32).astype(bf16).astype(f32)
-    )
-    d_gate_slots = jnp.sum(expert_out * cot_rows, axis=1)
-    weighted = (gate_slots * expert_out).astype(bf16).reshape(blocks, capacity, width)
-    out_part = jnp.einsum("bct,bcd->btd", pick, weighted, preferred_element_type=f32)
-    mixture = sum_all(out_part.astype(bf16), 4)
+    rows_all, out_part, d_part, rows_in, d_expert, inner_act, d_gate_up = experts_gathered(
+        jnp.concatenate([normed_two, route_info], axis=1),
+        cot_all,
+        gate_weight,
+        down_weight,
+        capacity,
+        3,
+    )
+    d_back = sum_all(d_part, 5).astype(f32)
+    mixture = sum_all(out_part, 4)
     output = (hidden + mixture.astype(f32)).astype(bf16)
-
-    d_expert = (gate_slots * cot_rows).astype(bf16)
-    d_inner = jnp.einsum("rd,fd->rf", d_expert, down_weight, preferred_element_type=f32)
-    d_gate_half = d_inner * up_half * gate_sig * (1.0 + gate_half * (1.0 - gate_sig))
-    d_up_half = d_inner * silu_gate
-    d_gate_up = jnp.concatenate([d_gate_half, d_up_half], axis=1).astype(bf16)
     d_w_down = jnp.einsum("rf,rd->fd", inner_act, d_expert, preferred_element_type=f32)[None]
     d_w_in = jnp.einsum("rd,rf->df", rows_in, d_gate_up, preferred_element_type=f32)[None]
-    d_rows = jnp.einsum("rf,df->rd", d_gate_up, gate_weight, preferred_element_type=f32)
-    d_rows = d_rows.astype(bf16).reshape(blocks, capacity, width)
-    d_gate_own = jnp.einsum(
-        "bct,bc->bt",
-        pick.astype(f32),
-        d_gate_slots.reshape(blocks, capacity),
-        precision=lax.Precision.HIGHEST,
-    )
-    d_gate_high = d_gate_own.astype(bf16)
-    d_gate_low = (d_gate_own - d_gate_high.astype(f32)).astype(bf16)
-    mine = (jnp.arange(experts, dtype=jnp.int32) == me).astype(bf16)
-    d_info = jnp.concatenate([d_gate_high[..., None] * mine, d_gate_low[..., None] * mine], axis=2)
-    d_info = jnp.pad(d_info, ((0, 0), (0, 0), (0, 128 - d_info.shape[2] % 128)))
-    d_part = jnp.einsum("bct,bcd->btd", pick, d_rows, preferred_element_type=f32)
-    d_part = jnp.concatenate([d_part.astype(bf16), d_info], axis=2)
-    d_back = sum_all(d_part, 5).astype(f32)
 
     d_gate_dense = d_back[:, width : width + experts] + d_back[:, width + experts : width + 2 * experts]
     d_gates = jnp.sum(onehot_float * d_gate_dense[:, None, :], axis=-1)
@@ -1100,7 +1639,10 @@
     d_hidden = out_grad + d_hidden_norm
     d_attn = d_hidden.astype(bf16)
 
-    d_attn_all = gather_seq(d_attn, 6).reshape(length, width)
+    d_send = jnp.concatenate([d_attn, jnp.pad(d_logits, ((0, 0), (0, 128 - experts)))], axis=1)
+    d_attn_all = gather_seq(d_send, 6).reshape(length, -1)
+    d_logits_all = d_attn_all[:, width:]
+    d_attn_all = d_attn_all[:, :width]
     d_attended = jnp.dot(d_attn_all, out_weight, preferred_element_type=f32).astype(bf16)
     d_query, d_key_sum, d_value_sum = attend_backward(
         queries,
@@ -1122,46 +1664,49 @@
         axis=1,
     ).astype(bf16)
     d_normed_part = jnp.einsum("tj,dj->td", d_projected, proj_weight, preferred_element_type=f32)
-    d_normed_one = sum_seq(d_normed_part.astype(bf16).reshape(seq_size, rows, width), 7).astype(f32)
-    unused_one, pull_one = jax.vjp(rms_scale, resid_in, attn_gain)
-    d_resid_norm, d_attn_gain = pull_one(d_normed_one)
-    d_tokens = (d_hidden + d_resid_norm).astype(bf16)[None]
-
+    router_cols = experts // seq_size
+    shard = lax.axis_index("fsdp")
+    two_all = lax.dynamic_index_in_dim(
+        rows_all.reshape(seq_size, shard_size, rows, -1), shard, 1, keepdims=False
+    )[:, :, :width].reshape(length, width)
+    own_logits = lax.dynamic_slice_in_dim(
+        d_logits_all, lax.axis_index("seq") * router_cols, router_cols, 1
+    )
+    own_logits = jnp.pad(own_logits, ((0, 0), (0, spare_cols - router_cols)))
     d_columns = jnp.concatenate(
         [
             jnp.einsum("tc,tj->cj", normed_all, d_projected, preferred_element_type=f32),
             jnp.einsum("tc,tj->cj", d_attn_all, attended, preferred_element_type=f32),
+            jnp.einsum("tc,tj->cj", two_all, own_logits, preferred_element_type=f32),
         ],
         axis=1,
     ).astype(bf16)
-    d_columns = (
-        d_columns.reshape(seq_size, shard_size, weight_rows, all_cols)
-        .transpose(1, 0, 2, 3)
-        .reshape(width, all_cols)
-    )
-    d_columns = lax.psum_scatter(d_columns, "fsdp", scatter_dimension=0, tiled=True).reshape(seq_size, weight_rows, all_cols)
-    d_pieces = lax.all_to_all(d_columns, "seq", split_axis=0, concat_axis=0, tiled=True).astype(f32)
-    d_pieces = d_pieces.transpose(1, 0, 2)
+    gains = jnp.pad(
+        jnp.stack([d_ffn_gain, jnp.pad(jnp.concatenate([d_q_gain, d_k_gain]), (0, width - 2 * HEAD_DIMENSION))]),
+        ((1, 5), (0, 0)),
+    )
+    d_tokens, d_pieces, gains = leave(
+        d_normed_part.astype(bf16).reshape(seq_size, rows, width),
+        d_columns.reshape(seq_size, 2, shard_size // 2, weight_rows, all_cols + spare_cols),
+        tokens[0],
+        d_hidden,
+        attn_gain[None],
+        gains,
+        7,
+    )
+    d_tokens = d_tokens[None]
+    d_pieces = d_pieces.astype(f32).transpose(1, 0, 2)
     per_group = seq_size // KEY_VALUE_HEADS
     d_kv = d_pieces[:, :, head_cols:proj_cols].reshape(
         weight_rows, KEY_VALUE_HEADS, per_group, 2, kv_cols
     )
     d_kv = jnp.sum(d_kv, axis=2).transpose(0, 2, 1, 3).reshape(weight_rows, -1)
     d_w_qkv = jnp.concatenate([d_pieces[:, :, :head_cols].reshape(weight_rows, -1), d_kv], axis=1)
-    d_w_out_t = d_pieces[:, :, proj_cols:].reshape(weight_rows, -1)
-    d_w_router = lax.psum_scatter(
-        jnp.einsum("tc,te->ce", normed_two, d_logits, preferred_element_type=f32),
-        both,
-        scatter_dimension=0,
-        tiled=True,
-    )
-    gains = jnp.concatenate([d_attn_gain, d_ffn_gain, d_q_gain, d_k_gain])
-    gains = jnp.pad(gains, (0, -gains.shape[0] % 2048)).reshape(16, -1)
-    gains = jnp.sum(gather_all(gains, experts, 8), axis=0).reshape(-1)
-    d_attn_gain = gains[:width]
-    d_ffn_gain = gains[width : 2 * width]
-    d_q_gain = gains[2 * width : 2 * width + HEAD_DIMENSION]
-    d_k_gain = gains[2 * width + HEAD_DIMENSION : 2 * width + 2 * HEAD_DIMENSION]
+    d_w_out_t = d_pieces[:, :, proj_cols:all_cols].reshape(weight_rows, -1)
+    d_w_router = d_pieces[:, :, all_cols : all_cols + router_cols].reshape(weight_rows, experts)
+    d_attn_gain, d_ffn_gain = gains[0], gains[1]
+    d_q_gain = gains[2, :HEAD_DIMENSION]
+    d_k_gain = gains[2, HEAD_DIMENSION : 2 * HEAD_DIMENSION]
     return (
         output[None],
         d_tokens,

time: 1090 us -> 939 us (0.86)
  the two profiles are of different devices: /device:TPU:0 before, /device:TPU:16 now
where the time goes in v3:
time: 939 us; the launch traced here: 927 us
  Pallas kernels  658 us (70%)
  matrix products  128 us (14%)
  other arithmetic  58.8 us (6%)
  local copies, waits for them, and re-layouts  58.1 us (6%)
  between operations  15.4 us (2%)
    pallas_call x1, Pallas kernels, experts_gathered(): pl.pallas_call(experts_kernel, out_shape=[array(experts, tokens, wide), a...  177 us
    pallas_call x2, Pallas kernels, sum_all(): pl.pallas_call(sum_all_kernel, out_shape=jax.ShapeDtypeStruct((rows, widt...  173 us
    pallas_call x1, Pallas kernels, leave(): pl.pallas_call(leave_kernel, out_shape=[jax.ShapeDtypeStruct((rows, width...  94.3 us
    pallas_call x1, Pallas kernels, sum_seq(): pl.pallas_call(sum_seq_kernel, out_shape=jax.ShapeDtypeStruct((rows, widt...  89.5 us
    pallas_call x1, Pallas kernels, enter(): pl.pallas_call(enter_kernel, out_shape=[jax.ShapeDtypeStruct((count, *own...  70.8 us
    pallas_call x1, Pallas kernels, gather_seq(): pl.pallas_call(gather_seq_kernel, out_shape=jax.ShapeDtypeStruct((8, *own...  53.6 us
    dot_general x1, matrix products, gathered_body(): jnp.einsum('rd,rf->df', rows_in, d_gate_up, preferred_element_type=f32)  19 us
  transfers between devices with their start and end apart: 1, of which 0 were waited for; matrix products, arithmetic and copies ran while one was open for 7% of the time, Pallas kernels for 10%

profile of v3, /device:TPU:16, one launch (start us, length us, event | category | flops | bytes accessed | tf_op | source)
XLA Modules:
  0.0 926.7 jit_solution(6468017160016304698)
XLA Ops:
  11.6 70.8 %enter.1 = (bf16[8,128,2048]{2,1,0:T(8,128)(2,1)}, bf16[32,64,1408]{2,1,0:T(8,128)(2,1)}) custom-call(bf16[128,2048]{1,0:T(8,128)(2,1)} %fusion.63.own, bf16[8,64,1408]{2,1,0:T(8,128)(2,1)} %copy-done.21), custom_call_target="tpu_custom_call" | custom-call | tf_op jit(solution)/shard_map/enter/pallas_call | solution.py:1038
  82.5 6.2 fusion.49
  97.5 2.4 multiply_reduce_fusion.3
  105.1 22.9 %while.28 = (s32[]{:T(128)}, bf16[2,512,4,128]{3,2,1,0:T(4,128)(2,1)}, f32[2,4,512]{2,1,0:T(4,128)S(1)}, s32[2]{0:T(128)S(1)}, bf16[1024,4,128]{2,0,1:T(8,128)(2...) while((s32[]{:T(128)}, ...), condition=%wide.region_6.7_spmd.clone, body=%wide.region_3.6_spmd.clone.sunk | while | flops 1099692544 | bytes 38342896 | solution.py:93
  107.3 2.8 fusion.146
  110.1 2.4 fusion.147
  112.5 2.9 fusion.148
  118.5 2.8 fusion.146
  121.3 2.4 fusion.147
  123.7 2.9 fusion.148
  128.1 6.4 convolution_convert_fusion
  134.5 89.5 %sum_seq.1 = bf16[128,2048]{1,0:T(8,128)(2,1)} custom-call(bf16[8,128,2048]{2,1,0:T(8,128)(2,1)} %bitcast.246), custom_call_target="tpu_custom_call" | custom-call | tf_op jit(solution)/shard_map/sum_seq/pallas_call | solution.py:911
  228.9 2.2 reshape.513
  232.1 6.4 copy.216
  239.4 177.5 %experts.1 = (bf16[32,128,2176]{2,1,0:T(8,128)(2,1)}, bf16[32,128,2048]{2,1,0:T(8,128)(2,1)}, bf16[32,128,2176]{2,1,0:T(8,128)(2,1)}, bf16[2048,2048]{1,0:T(8,12...) custom-call(bf16[128,2176]{1,0:T(8,128)(2,1)} %pad_maximum_fusion.6.own, ...), custom_call_target="tpu_custom_call" | custom-call | tf_op jit(solution)/shard_map/experts/pallas_call | solution.py:1471
  417.0 96.7 %sum_all.3 = bf16[128,2176]{1,0:T(8,128)(2,1)} custom-call(bf16[32,128,2176]{2,1,0:T(8,128)(2,1)} %get-tuple-element.122.part), custom_call_target="tpu_custom_call" | custom-call | tf_op jit(solution)/shard_map/sum_all/pallas_call | solution.py:782
  516.3 3.5 multiply_reduce_fusion.4
  519.8 75.8 %sum_all.2 = bf16[128,2048]{1,0:T(8,128)(2,1)} custom-call(bf16[32,128,2048]{2,1,0:T(8,128)(2,1)} %get-tuple-element.120.part), custom_call_target="tpu_custom_call" | custom-call | tf_op jit(solution)/shard_map/sum_all/pallas_call | solution.py:782
  595.6 3.0 fusion.112
  599.5 53.6 %gather_seq.1 = bf16[8,128,2176]{2,1,0:T(8,128)(2,1)} custom-call(bf16[128,2176]{1,0:T(8,128)(2,1)} %fusion.69.own), custom_call_target="tpu_custom_call" | custom-call | tf_op jit(solution)/shard_map/gather_seq/pallas_call | solution.py:846
  653.2 6.3 fusion.55
  659.5 2.6 slice_bitcast_fusion
  662.8 61.5 %while.29 = (s32[]{:T(128)}, f32[1024,4,128]{0,2,1:T(8,128)S(1)}, f32[1024,4,128]{0,2,1:T(8,128)}, f32[2,512,4,128]{3,1,0,2:T(8,128)}, s32[2]{0:T(128)S(1)}, /*i...) while((s32[]{:T(128)}, f32[1024,4,128]{0,2,1:T(8,128)S(1)}, ...), condition=%wide.region_19.20_spmd.clone, body=%wide.region_17.19_spmd.clone.sunk | while | flops 2719218176 | bytes 157086640 | solution.py:130
  664.5 5.7 fusion.157
  672.5 6.0 multiply_reduce_fusion.10
  678.6 3.7 multiply_convert_fusion.3
  682.3 3.8 bitcast_add_fusion.4
  686.1 2.2 fusion.158
  689.2 3.9 bitcast_add_fusion.5
  694.4 5.7 fusion.157
  702.4 6.0 multiply_reduce_fusion.10
  708.5 3.7 multiply_convert_fusion.3
  712.2 3.8 bitcast_add_fusion.4
  716.0 2.2 fusion.158
  719.1 5.1 bitcast_add_fusion.5
  724.3 5.1 multiply_add_fusion.1
  731.3 3.9 multiply_reduce_fusion.1
  742.6 7.2 convolution_convert_fusion.1
  749.8 4.8 convolution_convert_fusion.2
  754.6 6.4 copy.217
  761.0 2.7 dynamic-slice_bitcast_fusion.1
  763.7 2.6 slice.171
  766.3 6.5 copy.219
  773.4 4.7 convolution_convert_fusion.3
  780.2 3.1 pad_maximum_fusion.cols
  783.3 94.3 %leave.1 = (bf16[128,2048]{1,0:T(8,128)(2,1)}, bf16[8,64,1408]{2,1,0:T(8,128)(2,1)}, f32[8,2048]{1,0:T(8,128)}) custom-call(bf16[8,128,2048]{2,1,0:T(8,128)(2,1)} %bitcast.250, bf16[8,2,2,64,1408]{4,3,2,1,0:T(8,128)(2,1)} %pad_maximum_fusion.cols, bf16[128,2048]{1,0:T(8,128)(2,1)} %bitcast.235, f32[128,2048]{1,0:T(8,128)} %get-tuple-element.337.d_hidden, ...), custom_call_target="tpu_custom_call" | custom-call | tf_op jit(solution)/shard_map/leave/pallas_call | solution.py:1181
  886.9 11.8 %convolution_bitcast_fusion.1 = f32[1,768,2048]{2,1,0:T(8,128)} fusion(bf16[2048,768]{1,0:T(8,128)(2,1)} %get-tuple-element.131, bf16[2048,2048]{1,0:T(8,128)(2,1)} %get-tuple-element.132), kind=kOutput, calls=%fused_computation.58 | convolution fusion | flops 6442450944 | bytes 17825792 | tf_op jit(solution)/shard_map/rf,rd->fd/dot_general | solution.py:1626
  898.7 19.0 %convolution_bitcast_fusion = f32[1,2048,1536]{2,1,0:T(8,128)} fusion(bf16[2048,2048]{1,0:T(8,128)(2,1)} %get-tuple-element.129, bf16[2048,1536]{1,0:T(8,128)(2,1)} %get-tuple-element.130), kind=kOutput, calls=%fused_computation.55 | convolution fusion | flops 12884901888 | bytes 27262976 | tf_op jit(solution)/shard_map/rd,rf->df/dot_general | solution.py:1627
  (273 shorter events, 60.3 us)
Async XLA Ops:
  7.2 2.7 copy-start.49
  7.2 2.8 copy-start.4
  7.2 232.2 %all-gather.3.cloned.1.call-start = ((), (), s32[]{:S(2)}) async-start(), calls=%async_computation | async-start | bytes 17301504 | tf_op jit(solution)/shard_map/all_gather | solution.py:1580
  88.7 4.1 copy-start.50
  91.1 8.8 copy-start.54
  91.1 8.8 copy-start.38
  97.3 5.3 copy-start.2
  97.3 4.5 copy-start.56
  99.9 2.7 copy-start.31
  99.9 2.7 copy-start.29
  112.5 2.9 copy-start.25
  123.7 3.0 copy-start.25
  128.1 6.4 copy-start.12
  128.1 6.4 copy-start.33
  134.5 90.9 %copy-start.35 = (f32[2048]{0:T(1024)S(1)}, f32[2048]{0:T(1024)}, u32[]{:S(2)}) copy-start(f32[2048]{0:T(1024)} %param.23) | copy-start | bytes 24580
  224.0 4.0 copy-start.40
  225.3 2.8 copy-start.58
  225.3 2.7 copy-start.52
  228.1 3.1 copy-start.47
  416.9 99.2 %copy-start.46 = (f32[128]{0:T(128)S(1)}, f32[128]{0:T(128)}, u32[]{:S(2)}) copy-start(f32[128]{0:T(128)} %copy-done.45) | copy-start | bytes 1540
  416.9 99.2 %copy-start.48 = (f32[128]{0:T(128)S(1)}, f32[128]{0:T(128)}, u32[]{:S(2)}) copy-start(f32[128]{0:T(128)} %copy-done.47) | copy-start | bytes 1540
  416.9 99.4 %copy-start.53 = (f32[128]{0:T(128)S(1)}, f32[128]{0:T(128)}, u32[]{:S(2)}) copy-start(f32[128]{0:T(128)} %copy-done.52) | copy-start | bytes 1540
  515.9 3.9 copy-start.59
  519.8 75.8 %copy-start.22 = (bf16[1,128,2048]{2,1,0:T(8,128)(2,1)S(1)}, bf16[1,128,2048]{2,1,0:T(8,128)(2,1)}, u32[]{:S(2)}) copy-start(bf16[1,128,2048]{2,1,0:T(8,128)(2,1)} %param.27) | copy-start | bytes 1572868
  653.1 6.4 copy-start.7
  659.5 3.3 copy-start.13
  659.5 3.3 copy-start.34
  672.5 6.1 slice-start
  672.5 6.1 slice-start.1
  682.3 3.8 copy-start.1
  682.3 6.1 copy-start
  686.1 3.1 copy-start.14
  702.4 6.1 slice-start
  702.4 6.1 slice-start.1
  712.2 3.8 copy-start.1
  712.2 6.1 copy-start
  716.0 3.1 copy-start.14
  731.3 3.9 copy-start.32
  731.3 4.0 copy-start.3
  731.3 4.1 copy-start.5
  731.3 4.7 copy-start.6
  736.0 3.2 copy-start.42
  742.6 7.2 copy-start.18
  766.3 6.5 copy-start.44
  766.3 7.2 copy-start.24
  773.4 4.7 copy-start.23
  773.4 4.8 copy-start.8
  881.1 2.8 slice-start.2
  (24 other events, 34.6 us)
Sparse Core Ops, SparseCore 0:
  82.6 156.5 all-gather.2

commit v4 on v3

--- a/solution.py
+++ b/solution.py
@@ -736,24 +736,42 @@
     return start, plane_core, plane_turn, plane_end, finish
 
 
-def sum_all_kernel(part, out, *scratch):
+def sum_all_kernel(part, both, out, pair, both_held, both_in, pair_sems, *scratch):
     p = Place()
     p.greet(("x", "y", "core", "z"))
     start, plane_core, plane_turn, plane_end, finish = sum_all_parts(p, part, *scratch[:7], out, *scratch[7:])
+    rows = both.shape[3]
+
+    def pair_sum(first):
+        for s in (first, first + 1):
+            for y in range(2):
+                add_rows(both_held.at[s, y], both_in.at[s, y], rows)
+
     start()
+    send(both.at[:, :, 1 - p.c], both_in, pair_sems.at[0], pair_sems.at[1], p.by_core)
+    pltpu.make_async_copy(both.at[:, :, p.c], both_held, pair_sems.at[2]).start()
     plane_core(0)
     plane_core(1)
     plane_turn(0)
+    await_bytes(both_held, pair_sems.at[2])
+    await_bytes(both_in, pair_sems.at[1])
+    pair_sum(0)
     plane_core(2)
     plane_turn(1)
     plane_end(0)
+    pair_sum(2)
     plane_core(3)
     plane_turn(2)
     plane_end(1)
+    pair_sum(4)
+    pair_sum(6)
+    pltpu.make_async_copy(both_held, pair, pair_sems.at[2]).start()
     plane_turn(3)
     plane_end(2)
     plane_end(3)
     finish()
+    await_bytes(both_in, pair_sems.at[0])
+    pltpu.make_async_copy(both_held, pair, pair_sems.at[2]).wait()
 
 
 def sum_all_scratch(rows, width):
@@ -777,19 +795,30 @@
     ]
 
 
-def sum_all(part, collective_id):
+def sum_all(part, both, collective_id):
     blocks, rows, width = part.shape
+    both = both.reshape(blocks // 4, 2, 2, rows, -1)
+    pair = (blocks // 4, 2, rows, both.shape[4])
+    anywhere = pl.BlockSpec(memory_space=pl.ANY)
     return pl.pallas_call(
         sum_all_kernel,
-        out_shape=jax.ShapeDtypeStruct((rows, width), part.dtype),
-        in_specs=[pl.BlockSpec(memory_space=pl.ANY)],
-        out_specs=pl.BlockSpec(memory_space=pltpu.VMEM),
-        scratch_shapes=sum_all_scratch(rows, width),
+        out_shape=[
+            jax.ShapeDtypeStruct((rows, width), part.dtype),
+            jax.ShapeDtypeStruct(pair, both.dtype),
+        ],
+        in_specs=[anywhere] * 2,
+        out_specs=[pl.BlockSpec(memory_space=pltpu.VMEM), anywhere],
+        scratch_shapes=[
+            pltpu.VMEM(pair, both.dtype),
+            pltpu.VMEM(pair, both.dtype),
+            pltpu.SemaphoreType.DMA((3,)),
+            *sum_all_scratch(rows, width),
+        ],
         compiler_params=pltpu.CompilerParams(
             collective_id=collective_id, has_side_effects=True, vmem_limit_bytes=VMEM_LIMIT
         ),
         name="sum_all",
-    )(part)
+    )(part, both)
 
 
 def gather_seq_kernel(own, out, ss, rs, zs, local_sem):
@@ -1220,6 +1249,7 @@
 
 NT = (((1,), (1,)), ((), ()))
 TILE = 256
+WIDE = 512
 
 
 def mxu(a, b, dims=(((1,), (0,)), ((), ()))):
@@ -1230,7 +1260,7 @@
     own, cot_all, w_in_hbm, w_down_hbm,
     rows_all, out_part, d_part, x_all, d_expert_all, inner_all, d_gate_up_all,
     w_in, w_down, row_buf, cot_buf, pick, pick_t, gates, d_gates, x, cot, d_expert,
-    by_d_gate, by_d_up, inner, d_gate_up, out_stage, d_stage,
+    by_d_gate, by_d_up, inner, d_gate_up, held, out_stage, d_stage,
     ss, rs, zs, local_sem, load_sems, store_sems,
 ):
     p = Place()
@@ -1299,50 +1329,38 @@
         lane = lax.broadcasted_iota(jnp.int32, (8, 128), 1)
         line = lax.broadcasted_iota(jnp.int32, (8, 128), 0)
         select = jnp.where((lane == line * experts + p.me) & (line < 3), 1.0, 0.0).astype(bf16)
-        before = jnp.where(
-            lax.broadcasted_iota(jnp.int32, (tokens, tokens), 0)
-            < lax.broadcasted_iota(jnp.int32, (tokens, tokens), 1),
-            1.0,
-            0.0,
-        ).astype(bf16)
-        slot_id = lax.broadcasted_iota(jnp.int32, (capacity, tokens), 0).astype(f32)
+        slot_id = lax.broadcasted_iota(jnp.int32, (capacity, tokens), 0).astype(f32) + 1.0
         rows, cots = row_buf.at[k % 2], cot_buf.at[k % 2]
-
-        @pl.loop(0, blocks // group)
-        def _(g):
-            for i in range(group):
-                info = rows[g * group + i, :, width:]
-                lines = mxu(select, info, NT)
-                named = lines[2:3]
-                slot = mxu(lines.astype(bf16), before)[2:3]
-                chosen = jnp.where((slot == slot_id) & (named > 0.5), 1.0, 0.0)
-                gate = jnp.sum(chosen * (lines[0:1] + lines[1:2]), axis=1, keepdims=True)
-                at = pl.ds(pl.multiple_of(g * group * capacity + i * capacity, capacity), capacity)
-                gates[at, :] = jnp.broadcast_to(gate, (capacity, 128))
-                lead = [jnp.zeros((capacity, tokens), bf16)] * i
-                tail = [jnp.zeros((capacity, tokens), bf16)] * (group - 1 - i)
-                pick[g, i * capacity : (i + 1) * capacity, :] = jnp.concatenate(
-                    lead + [chosen.astype(bf16)] + tail, axis=1
-                )
-                turned = chosen.T
-                lead = [jnp.zeros((tokens, capacity), f32)] * i
-                tail = [jnp.zeros((tokens, capacity), f32)] * (group - 1 - i)
-                pick_t[g, i * tokens : (i + 1) * tokens, :] = jnp.concatenate(
-                    lead + [turned] + tail, axis=1
-                ).astype(bf16)
-            at = pl.ds(pl.multiple_of(g * group * capacity, group * capacity), group * capacity)
-            scale = gates[at, :]
-            scale = jnp.concatenate([scale] * (TILE // 128), axis=1)
+        lines = mxu(select, rows[:, :, width:].reshape(blocks * tokens, 128), NT)
+        for j in range(blocks):
+            g, i = j // group, j % group
+            mine = lines[:, j * tokens : (j + 1) * tokens]
+            chosen = jnp.where(mine[2:3] == slot_id, 1.0, 0.0)
+            gate = jnp.sum(chosen * (mine[0:1] + mine[1:2]), axis=1, keepdims=True)
+            gates[j * capacity : (j + 1) * capacity, :] = jnp.broadcast_to(gate, (capacity, 128))
+            lead = [jnp.zeros((capacity, tokens), bf16)] * i
+            tail = [jnp.zeros((capacity, tokens), bf16)] * (group - 1 - i)
+            pick[g, i * capacity : (i + 1) * capacity, :] = jnp.concatenate(
+                lead + [chosen.astype(bf16)] + tail, axis=1
+            )
+            lead = [jnp.zeros((tokens, capacity), f32)] * i
+            tail = [jnp.zeros((tokens, capacity), f32)] * (group - 1 - i)
+            pick_t[g, i * tokens : (i + 1) * tokens, :] = jnp.concatenate(
+                lead + [chosen.T] + tail, axis=1
+            ).astype(bf16)
+        for g in range(blocks // group):
+            at = pl.ds(g * group * capacity, group * capacity)
             which = pl.ds(g * group, group)
 
-            @pl.loop(0, width // TILE)
+            @pl.loop(0, width // WIDE)
             def _(n):
-                cols = pl.ds(pl.multiple_of(n * TILE, TILE), TILE)
-                row_tile = rows[which, :, cols].reshape(group * tokens, TILE)
+                cols = pl.ds(pl.multiple_of(n * WIDE, WIDE), WIDE)
+                row_tile = rows[which, :, cols].reshape(group * tokens, WIDE)
                 x[at, cols] = mxu(pick[g], row_tile).astype(bf16)
-                cot_tile = cots[which, :, cols].reshape(group * tokens, TILE)
+                cot_tile = cots[which, :, cols].reshape(group * tokens, WIDE)
                 picked = mxu(pick[g], cot_tile)
                 cot[at, cols] = picked.astype(bf16)
+                scale = jnp.concatenate([gates[at, :]] * (WIDE // 128), axis=1)
                 d_expert[at, cols] = (scale * picked).astype(bf16)
 
     def up(k):
@@ -1371,15 +1389,17 @@
                 d_inner * by_d_up[:, cols]
             ).astype(bf16)
 
-    def scatter(value, stage, cols, wide):
-        for g in range(blocks // group):
-            part = value[g * group * capacity : (g + 1) * group * capacity]
-            spread = mxu(pick_t[g], part).astype(bf16)
-            stage[g * group : (g + 1) * group, :, cols] = spread.reshape(group, tokens, wide)
+    def spread(stage):
+        @pl.loop(0, width // WIDE)
+        def _(n):
+            cols = pl.ds(pl.multiple_of(n * WIDE, WIDE), WIDE)
+            for g in range(blocks // group):
+                part = held[g * group * capacity : (g + 1) * group * capacity, cols]
+                result = mxu(pick_t[g], part).astype(bf16)
+                stage[g * group : (g + 1) * group, :, cols] = result.reshape(group, tokens, WIDE)
 
     def down(k):
         d_gates[...] = jnp.zeros_like(d_gates)
-        scale = jnp.concatenate([gates[...]] * (TILE // 128), axis=1)
 
         @pl.loop(0, width // TILE)
         def _(n):
@@ -1390,40 +1410,50 @@
             for j in range(1, TILE // 128):
                 total = total + product[:, j * 128 : (j + 1) * 128]
             d_gates[...] += total
-            scatter((scale * result).astype(bf16), out_stage, cols, TILE)
+            scale = jnp.concatenate([gates[...]] * (TILE // 128), axis=1)
+            held[:, cols] = (scale * result).astype(bf16)
 
     def d_down(k):
         total = jnp.sum(d_gates[...], axis=1, keepdims=True)
         high = total.astype(bf16).astype(f32)
         lane = lax.broadcasted_iota(jnp.int32, (slots, 128), 1)
         info = jnp.where(lane == p.me, high, jnp.where(lane == experts + p.me, total - high, 0.0))
-        scatter(info.astype(bf16), d_stage, pl.ds(width, 128), 128)
+        info = info.astype(bf16)
+        for g in range(blocks // group):
+            result = mxu(pick_t[g], info[g * group * capacity : (g + 1) * group * capacity])
+            d_stage[g * group : (g + 1) * group, :, width:] = result.astype(bf16).reshape(
+                group, tokens, 128
+            )
 
         @pl.loop(0, width // TILE)
         def _(n):
             cols = pl.ds(pl.multiple_of(n * TILE, TILE), TILE)
-            d_rows = mxu(d_gate_up[...], w_in[cols, :], NT)
-            scatter(d_rows.astype(bf16), d_stage, cols, TILE)
+            held[:, cols] = mxu(d_gate_up[...], w_in[cols, :], NT).astype(bf16)
 
     plane_out(0)
     weights(True)
     cot_load(0).start()
+    plane_turn(0)
     plane_out(1)
-    plane_turn(0)
     plane_end(0)
     arrived(0)
     weights(False)
     after = {
-        0: ([lambda: plane_out(2)], [lambda: plane_turn(1)], [lambda: plane_out(3)], [lambda: plane_end(1)], [lambda: arrived(1)]),
-        1: ([], [lambda: plane_turn(2)], [], [lambda: plane_end(2)], [lambda: arrived(2)]),
-        2: ([], [lambda: plane_turn(3)], [], [lambda: plane_end(3)], [lambda: arrived(3)]),
-        3: ([], [], [], [], []),
+        (0, 1): ((plane_turn, 1), (plane_out, 2)),
+        (0, 3): ((plane_end, 1),),
+        (0, 5): ((arrived, 1),),
+        (1, 0): ((plane_turn, 2), (plane_out, 3)),
+        (1, 3): ((plane_end, 2),),
+        (1, 5): ((arrived, 2),),
+        (2, 0): ((plane_turn, 3),),
+        (2, 3): ((plane_end, 3),),
+        (2, 5): ((arrived, 3),),
     }
     for k in range(4):
 
         def service(i):
-            for step in after[k][i]:
-                step()
+            for step, plane in after.get((k, i), ()):
+                step(plane)
 
         row_load(k).wait()
         cot_load(k).wait()
@@ -1445,12 +1475,15 @@
         service(2)
         free(k, 4)
         down(k)
+        service(3)
+        spread(out_stage)
         put(k, 4)
-        service(3)
+        service(4)
         free(k, 5)
         d_down(k)
+        service(5)
+        spread(d_stage)
         put(k, 5)
-        service(4)
     for i in range(6):
         free(4, i)
     finish()
@@ -1497,6 +1530,7 @@
             pltpu.VMEM((slots, ff), f32),
             pltpu.VMEM((slots, ff), bf16),
             pltpu.VMEM((slots, 2 * ff), bf16),
+            pltpu.VMEM((slots, width), bf16),
             pltpu.VMEM((8, tokens, width), bf16),
             pltpu.VMEM((8, tokens, wide), bf16),
             dma((4, G_KINDS)),
@@ -1511,6 +1545,324 @@
         ),
         name="experts",
     )(own, cot_all, w_in, w_down)
+
+
+TN = (((0,), (0,)), ((), ()))
+
+
+def back_kernel(
+    own, pair, rows_all, columns_hbm, normed_hbm, queries, keys, values, attended,
+    q_raw, k_raw, cosine, sine, q_gain, k_gain,
+    d_normed, d_columns, head_gains, mixture,
+    d_attn, columns, normed, d_heads, d_query, d_key, d_value, d_proj, logits, q_sum, k_sum,
+    held, x_in, y_in, z_in,
+    gs, gr, gz, load_sems, local_sem, hs, ys, yr, xs, xr, zs, zr,
+):
+    p = Place()
+    bf16, f32 = jnp.bfloat16, jnp.float32
+    p.greet(("x", "y", "z"))
+    rows, wide = own.shape
+    length, head_cols = queries.shape
+    heads = head_cols // HEAD_DIMENSION
+    width = normed.shape[1]
+    proj_cols = d_proj.shape[1]
+    plane_rows = 2 * rows
+    score_scale = 1.0 / math.sqrt(HEAD_DIMENSION)
+    place, shard = p.z * 2 + p.x, p.y * 2 + p.c
+
+    def rows_at(q, x):
+        return d_attn.at[q * 2 + x]
+
+    def gather_out(k):
+        q = p.near(k)
+        there = rows_at(q, p.x)
+        if k == 0:
+            src = own
+            for step, end in ((1, p.high), (-1, p.low)):
+
+                @pl.when(jnp.logical_not(end))
+                def _():
+                    send(src, there, gz.at[q, 0 if step > 0 else 1], gr.at[q, 0], p.by_z(step))
+
+            pltpu.make_async_copy(own, there, local_sem).start()
+        else:
+            src = there
+            await_bytes(src, gr.at[q, 0])
+
+            @pl.when(p.inner)
+            def _():
+                send(src, src, gz.at[q, 0], gr.at[q, 0], p.by_z(p.onward(k)))
+
+        send(src, there, gs.at[q], gr.at[q, 1], p.by_x)
+
+    def gather_in(k):
+        if k == 0:
+            pltpu.make_async_copy(own, rows_at(p.z, p.x), local_sem).wait()
+        await_bytes(own, gr.at[p.near(k), 1])
+
+    def at_pair(q, x, y):
+        return pair.at[q * 4 + x * 2 + y]
+
+    def sum_start():
+        for k in range(4):
+            q = p.far(k)
+            for j, x in ((1, 1 - p.x), (0, p.x)):
+                send(at_pair(q, x, 1 - p.y), y_in.at[q * 2 + j], ys.at[q * 2 + j], yr.at[q * 2 + j], p.by_y)
+                pltpu.make_async_copy(at_pair(q, x, p.y), held.at[q * 2 + j], hs.at[q * 2 + j]).start()
+
+    def sum_turn(k):
+        q = p.far(k)
+        for j in (1, 0):
+            slot = q * 2 + j
+            await_bytes(held.at[slot], hs.at[slot])
+            await_bytes(y_in.at[slot], yr.at[slot])
+            add_rows(held.at[slot], y_in.at[slot], rows)
+            if j == 1:
+                send(held.at[slot], x_in.at[q], xs.at[q], xr.at[q], p.by_x)
+
+    def sum_end(k):
+        q = p.far(k)
+        mine = held.at[q * 2]
+        await_bytes(x_in.at[q], xr.at[q])
+        add_rows(mine, x_in.at[q], rows)
+        if k < 3:
+            step = p.toward(k)
+            slot = (1 - step) // 2
+
+            @pl.when(p.inner)
+            def _():
+                await_bytes(z_in.at[slot, q], zr.at[slot, q])
+                add_rows(mine, z_in.at[slot, q], rows)
+
+            send(mine, z_in.at[slot, q], zs.at[k], zr.at[slot, q], p.by_z(step))
+        else:
+            for slot, there in ((0, p.low), (1, p.high)):
+
+                @pl.when(jnp.logical_not(there))
+                def _():
+                    await_bytes(z_in.at[slot, q], zr.at[slot, q])
+                    add_rows(mine, z_in.at[slot, q], rows)
+
+            mixture[...] = mine[...]
+
+    def attention(q):
+        row_start = pl.multiple_of(q * plane_rows, plane_rows)
+        at = pl.ds(row_start, plane_rows)
+
+        @pl.loop(0, head_cols // TILE)
+        def _(n):
+            cols = pl.ds(pl.multiple_of(n * TILE, TILE), TILE)
+            grad = d_attn[pl.ds(q * 2, 2), :, :width].reshape(plane_rows, width)
+            weight_cols = pl.ds(pl.multiple_of(proj_cols + n * TILE, TILE), TILE)
+            d_heads[at, cols] = mxu(grad, columns[:, weight_cols]).astype(bf16)
+
+        def block(count):
+            key, value = keys[:count], values[:count]
+            row_pos = row_start + lax.broadcasted_iota(jnp.int32, (plane_rows, count), 0)
+            allowed = lax.broadcasted_iota(jnp.int32, (plane_rows, count), 1) <= row_pos
+
+            @pl.loop(0, heads)
+            def _(h):
+                cols = pl.ds(pl.multiple_of(h * HEAD_DIMENSION, HEAD_DIMENSION), HEAD_DIMENSION)
+                query, d_out = queries[at, cols], d_heads[at, cols]
+                scores = jnp.where(allowed, mxu(query, key, NT) * score_scale, -1e30)
+                raised = jnp.exp(scores - jnp.max(scores, axis=-1, keepdims=True))
+                prob = raised / jnp.sum(raised, axis=-1, keepdims=True)
+                d_prob = mxu(d_out, value, NT)
+                delta = jnp.sum(prob * d_prob, axis=-1, keepdims=True)
+                d_scores = (prob * (d_prob - delta)).astype(bf16)
+                d_query[at, cols] = mxu(d_scores, key) * score_scale
+                d_key[:count] += mxu(d_scores, query, TN) * score_scale
+                d_value[:count] += mxu(prob.astype(bf16), d_out, TN)
+
+        half = length // 2
+
+        @pl.when(q < 2)
+        def _():
+            block(half)
+
+        @pl.when(q >= 2)
+        def _():
+            block(length)
+
+    def unrotate(grad, at):
+        swapped = jnp.concatenate(
+            [grad[:, HEAD_DIMENSION // 2 :], grad[:, : HEAD_DIMENSION // 2]], axis=1
+        )
+        return grad * cosine[at, :] + swapped * sine[at, :]
+
+    def raw_grads():
+        q_sum[...] = jnp.zeros_like(q_sum)
+        k_sum[...] = jnp.zeros_like(k_sum)
+
+        def one(grad, raw, gain, total, at):
+            turned = unrotate(grad, at)
+            scale = lax.rsqrt(jnp.mean(raw * raw, axis=-1, keepdims=True) + EPS)
+            total[...] += jnp.sum((turned * raw * scale).reshape(-1, 8, HEAD_DIMENSION), axis=0)
+            u = turned * gain[...]
+            dot = jnp.mean(u * raw, axis=-1, keepdims=True)
+            return (scale * u - raw * (scale * scale * scale * dot)).astype(bf16)
+
+        chunk = 128
+
+        @pl.loop(0, length // chunk)
+        def _(i):
+            at = pl.ds(pl.multiple_of(i * chunk, chunk), chunk)
+            for h in range(heads):
+                cols = slice(h * HEAD_DIMENSION, (h + 1) * HEAD_DIMENSION)
+                d_proj[at, cols] = one(d_query[at, cols], q_raw[at, cols], q_gain, q_sum, at)
+            d_proj[at, head_cols : head_cols + HEAD_DIMENSION] = one(
+                d_key[at, :], k_raw[at, :], k_gain, k_sum, at
+            )
+            d_proj[at, head_cols + HEAD_DIMENSION :] = d_value[at, :].astype(bf16)
+
+        line = lax.broadcasted_iota(jnp.int32, (8, HEAD_DIMENSION), 0)
+        head_gains[...] = jnp.where(
+            line == 0,
+            jnp.sum(q_sum[...], axis=0, keepdims=True),
+            jnp.where(line == 1, jnp.sum(k_sum[...], axis=0, keepdims=True), 0.0),
+        )
+
+    def normed_grads():
+        @pl.loop(0, width // TILE)
+        def _(n):
+            cols = pl.ds(pl.multiple_of(n * TILE, TILE), TILE)
+            part = mxu(d_proj[...], columns[cols, :proj_cols], NT).astype(bf16)
+            d_normed[:, :, cols] = part.reshape(length // rows, rows, TILE)
+
+    def column_grads(source, value, first, count):
+        @pl.loop(0, width // TILE)
+        def _(n):
+            cols = pl.ds(pl.multiple_of(n * TILE, TILE), TILE)
+            part = source[..., cols].reshape(length, TILE)
+            d_columns[cols, first : first + count] = mxu(part, value[...], TN).astype(bf16)
+
+    loads = [
+        pltpu.make_async_copy(columns_hbm, columns, load_sems.at[0]),
+        pltpu.make_async_copy(normed_hbm, normed, load_sems.at[1]),
+        pltpu.make_async_copy(rows_all.at[:, shard], d_attn, load_sems.at[2]),
+    ]
+    gather_out(0)
+    loads[0].start()
+    loads[1].start()
+    sum_start()
+    d_key[...] = jnp.zeros_like(d_key)
+    d_value[...] = jnp.zeros_like(d_value)
+    loads[0].wait()
+    gather_in(0)
+    gather_out(1)
+    attention(p.near(0))
+    gather_out(2)
+    gather_in(1)
+    attention(p.near(1))
+    sum_turn(0)
+    gather_out(3)
+    gather_in(2)
+    attention(p.near(2))
+    sum_end(0)
+    sum_turn(1)
+    gather_in(3)
+    attention(p.near(3))
+    raw_grads()
+    sum_end(1)
+    normed_grads()
+    loads[1].wait()
+    column_grads(normed, d_proj, 0, proj_cols)
+    sum_turn(2)
+    column_grads(d_attn.at[:, :, pl.ds(0, width)], attended, proj_cols, head_cols)
+    line = lax.broadcasted_iota(jnp.int32, (128, 128), 0)
+    lane = lax.broadcasted_iota(jnp.int32, (128, 128), 1)
+    router_cols = rows_all.shape[0] * rows_all.shape[1] // 8
+    mine = (line == lane + place * router_cols) & (lane < router_cols)
+    select = jnp.where(mine, 1.0, 0.0).astype(bf16)
+    logits[...] = mxu(d_attn[:, :, width:].reshape(length, 128), select).astype(bf16)
+    sum_end(2)
+    for q in range(4):
+        await_bytes(own, gs.at[q])
+    for there, slot in ((p.high, 0), (p.low, 1)):
+
+        @pl.when(jnp.logical_not(there))
+        def _():
+            await_bytes(own, gz.at[p.z, slot])
+
+    for k in range(1, 4):
+
+        @pl.when(p.inner)
+        def _():
+            await_bytes(own, gz.at[p.near(k), 0])
+
+    loads[2].start()
+    loads[2].wait()
+    column_grads(d_attn.at[:, :, pl.ds(0, width)], logits, proj_cols + head_cols, 128)
+    sum_turn(3)
+    sum_end(3)
+    piece = x_in.at[0]
+    for i in range(8):
+        await_bytes(piece, ys.at[i])
+    for q in range(4):
+        await_bytes(piece, xs.at[q])
+    for k in range(3):
+        await_bytes(piece, zs.at[k])
+
+
+def back(
+    own, pair, rows_all, columns, normed, queries, keys, values, attended,
+    q_raw, k_raw, cosine, sine, q_gain, k_gain, collective_id,
+):
+    rows, wide = own.shape
+    length, head_cols = queries.shape
+    width = normed.shape[1]
+    proj_cols = head_cols + 2 * HEAD_DIMENSION
+    dma = pltpu.SemaphoreType.DMA
+    bf16, f32 = jnp.bfloat16, jnp.float32
+    anywhere, vmem = pl.BlockSpec(memory_space=pl.ANY), pl.BlockSpec(memory_space=pltpu.VMEM)
+    return pl.pallas_call(
+        back_kernel,
+        out_shape=[
+            jax.ShapeDtypeStruct((length // rows, rows, width), bf16),
+            jax.ShapeDtypeStruct(columns.shape, bf16),
+            jax.ShapeDtypeStruct((8, HEAD_DIMENSION), f32),
+            jax.ShapeDtypeStruct((rows, width), bf16),
+        ],
+        in_specs=[anywhere] * 5 + [vmem] * 10,
+        out_specs=[vmem] * 4,
+        scratch_shapes=[
+            pltpu.VMEM((8, rows, wide), bf16),
+            pltpu.VMEM(columns.shape, bf16),
+            pltpu.VMEM((length, width), bf16),
+            pltpu.VMEM((length, head_cols), bf16),
+            pltpu.VMEM((length, head_cols), f32),
+            pltpu.VMEM((length, HEAD_DIMENSION), f32),
+            pltpu.VMEM((length, HEAD_DIMENSION), f32),
+            pltpu.VMEM((length, proj_cols), bf16),
+            pltpu.VMEM((length, 128), bf16),
+            pltpu.VMEM((8, HEAD_DIMENSION), f32),
+            pltpu.VMEM((8, HEAD_DIMENSION), f32),
+            pltpu.VMEM((8, rows, width), bf16),
+            pltpu.VMEM((4, rows, width), bf16),
+            pltpu.VMEM((8, rows, width), bf16),
+            pltpu.VMEM((2, 4, rows, width), bf16),
+            dma((4,)),
+            dma((4, 2)),
+            dma((4, 2)),
+            dma((3,)),
+            dma,
+            dma((8,)),
+            dma((8,)),
+            dma((8,)),
+            dma((4,)),
+            dma((4,)),
+            dma((3,)),
+            dma((2, 4)),
+        ],
+        compiler_params=pltpu.CompilerParams(
+            collective_id=collective_id, has_side_effects=True, vmem_limit_bytes=VMEM_LIMIT
+        ),
+        name="back",
+    )(
+        own, pair, rows_all, columns, normed, queries, keys, values, attended,
+        q_raw, k_raw, cosine, sine, q_gain, k_gain,
+    )
 
 
 def head_columns(weight, group_index):
@@ -1589,7 +1941,7 @@
     keys = prepare(k_raw, k_gain).astype(bf16)
     repeat_keys = jnp.repeat(keys, heads, axis=1)
     repeat_values = jnp.repeat(values, heads, axis=1)
-    mixed_heads, log_total = attend_forward(queries, repeat_keys, repeat_values)
+    mixed_heads, unused_total = attend_forward(queries, repeat_keys, repeat_values)
     attended = mixed_heads.reshape(length, head_cols)
     attn_part = jnp.einsum("tj,dj->td", attended, out_weight, preferred_element_type=f32)
     attn_out = sum_seq(attn_part.astype(bf16).reshape(seq_size, rows, width), 2)
@@ -1600,6 +1952,9 @@
     onehot = routes[0][:, :, None] == jnp.arange(experts, dtype=jnp.int32)
     onehot_float = onehot.astype(f32)
     named = jnp.sum(onehot_float, axis=1)
+    order = jnp.arange(rows, dtype=jnp.int32)
+    upto = (order[None, :] <= order[:, None]).astype(bf16)
+    slot_info = named * jnp.dot(upto, named.astype(bf16), preferred_element_type=f32)
     chosen = jnp.sum(onehot_float * logits[:, None, :], axis=-1)
     row_max = jnp.max(chosen, axis=-1, keepdims=True)
     exp_part = jnp.exp(chosen - row_max)
@@ -1608,7 +1963,7 @@
 
     gate_high = gate_dense.astype(bf16)
     gate_low = (gate_dense - gate_high.astype(f32)).astype(bf16)
-    route_info = jnp.concatenate([gate_high, gate_low, named.astype(bf16)], axis=1)
+    route_info = jnp.concatenate([gate_high, gate_low, slot_info.astype(bf16)], axis=1)
     route_info = jnp.pad(route_info, ((0, 0), (0, 128 - route_info.shape[1] % 128)))
     gate_weight = w_in[0]
     down_weight = w_down[0]
@@ -1620,9 +1975,8 @@
         capacity,
         3,
     )
-    d_back = sum_all(d_part, 5).astype(f32)
-    mixture = sum_all(out_part, 4)
-    output = (hidden + mixture.astype(f32)).astype(bf16)
+    d_back, out_pair = sum_all(d_part, out_part, 5)
+    d_back = d_back.astype(f32)
     d_w_down = jnp.einsum("rf,rd->fd", inner_act, d_expert, preferred_element_type=f32)[None]
     d_w_in = jnp.einsum("rd,rf->df", rows_in, d_gate_up, preferred_element_type=f32)[None]
 
@@ -1640,53 +1994,38 @@
     d_attn = d_hidden.astype(bf16)
 
     d_send = jnp.concatenate([d_attn, jnp.pad(d_logits, ((0, 0), (0, 128 - experts)))], axis=1)
-    d_attn_all = gather_seq(d_send, 6).reshape(length, -1)
-    d_logits_all = d_attn_all[:, width:]
-    d_attn_all = d_attn_all[:, :width]
-    d_attended = jnp.dot(d_attn_all, out_weight, preferred_element_type=f32).astype(bf16)
-    d_query, d_key_sum, d_value_sum = attend_backward(
-        queries,
-        repeat_keys,
-        repeat_values,
-        log_total,
-        d_attended.reshape(length, heads, HEAD_DIMENSION),
-    )
-    unused_q, pull_q = jax.vjp(prepare, q_raw, q_gain)
-    d_q_raw, d_q_gain = pull_q(d_query)
-    unused_k, pull_k = jax.vjp(prepare, k_raw, k_gain)
-    d_k_raw, d_k_gain = pull_k(jnp.sum(d_key_sum, axis=1, keepdims=True))
-    d_projected = jnp.concatenate(
-        [
-            d_q_raw.reshape(length, head_cols),
-            d_k_raw.reshape(length, kv_cols),
-            jnp.sum(d_value_sum, axis=1),
-        ],
-        axis=1,
-    ).astype(bf16)
-    d_normed_part = jnp.einsum("tj,dj->td", d_projected, proj_weight, preferred_element_type=f32)
+    half_dim = HEAD_DIMENSION // 2
+    frequency = ROPE_BASE ** (-2.0 * jnp.arange(half_dim, dtype=f32) / HEAD_DIMENSION)
+    angles = seq_positions.astype(f32)[:, None] * frequency[None, :]
+    cosine, sine = jnp.cos(angles), jnp.sin(angles)
+    d_normed_part, d_columns, head_gains, mixture = back(
+        d_send,
+        out_pair.reshape(2 * seq_size, rows, width),
+        rows_all.reshape(seq_size, shard_size, rows, -1),
+        columns,
+        normed_all,
+        queries.reshape(length, head_cols),
+        keys.reshape(length, kv_cols),
+        values.reshape(length, kv_cols),
+        attended,
+        q_raw.reshape(length, head_cols),
+        k_raw.reshape(length, kv_cols),
+        jnp.concatenate([cosine, cosine], axis=1),
+        jnp.concatenate([sine, -sine], axis=1),
+        q_gain[None],
+        k_gain[None],
+        6,
+    )
+    output = (hidden + mixture.astype(f32)).astype(bf16)
     router_cols = experts // seq_size
-    shard = lax.axis_index("fsdp")
-    two_all = lax.dynamic_index_in_dim(
-        rows_all.reshape(seq_size, shard_size, rows, -1), shard, 1, keepdims=False
-    )[:, :, :width].reshape(length, width)
-    own_logits = lax.dynamic_slice_in_dim(
-        d_logits_all, lax.axis_index("seq") * router_cols, router_cols, 1
-    )
-    own_logits = jnp.pad(own_logits, ((0, 0), (0, spare_cols - router_cols)))
-    d_columns = jnp.concatenate(
-        [
-            jnp.einsum("tc,tj->cj", normed_all, d_projected, preferred_element_type=f32),
-            jnp.einsum("tc,tj->cj", d_attn_all, attended, preferred_element_type=f32),
-            jnp.einsum("tc,tj->cj", two_all, own_logits, preferred_element_type=f32),
-        ],
-        axis=1,
-    ).astype(bf16)
     gains = jnp.pad(
-        jnp.stack([d_ffn_gain, jnp.pad(jnp.concatenate([d_q_gain, d_k_gain]), (0, width - 2 * HEAD_DIMENSION))]),
+        jnp.stack(
+            [d_ffn_gain, jnp.pad(head_gains[:2].reshape(-1), (0, width - 2 * HEAD_DIMENSION))]
+        ),
         ((1, 5), (0, 0)),
     )
     d_tokens, d_pieces, gains = leave(
-        d_normed_part.astype(bf16).reshape(seq_size, rows, width),
+        d_normed_part,
         d_columns.reshape(seq_size, 2, shard_size // 2, weight_rows, all_cols + spare_cols),
         tokens[0],
         d_hidden,

time: 939 us -> 755 us (0.80)
  Pallas kernels: 658 us -> 597 us
  matrix products: 128 us -> 68.7 us
  local copies, waits for them, and re-layouts: 58.1 us -> 28.5 us
  other arithmetic: 58.8 us -> 32.4 us
    dot_general x17 -> x1, matrix products: 74.4 us -> 0.76 us  [gathered_body(): jnp.dot(upto, named.astype(bf16), preferred_element_type=f32)]
    pallas_call x1, Pallas kernels: 177 us -> 123 us  [experts_gathered(): pl.pallas_call(experts_kernel, out_shape=[array(experts, tokens, wide), a...]
    dot_general x3 -> x0, local copies, waits for them, and re-layouts: 15.4 us -> none  [the longest x2 9 us: gathered_body(): jnp.einsum('tc,tj->cj', d_attn_all, attended, preferred_element_type=f32)]
    sub x0 -> x2, matrix products: none -> 15 us  [one_block(): weights = jnp.exp(scores - row_max)]
    pallas_call x3 -> x2, Pallas kernels: 226 us -> 211 us  [the longest x1 118 us: back(): pl.pallas_call(back_kernel, out_shape=[jax.ShapeDtypeStruct((length // ro...]
    reduce_sum x6 -> x0, other arithmetic: 11.9 us -> none  [the longest x2 5.07 us: rms_scale(): values * lax.rsqrt(jnp.mean(values * values, axis=-1, keepdims=True) + EPS)]
    pallas_call x1, Pallas kernels: 89.5 us -> 99.2 us  [sum_seq(): pl.pallas_call(sum_seq_kernel, out_shape=jax.ShapeDtypeStruct((rows, widt...]
  transfers between devices with their start and end apart: 1 -> 1, of which waited for: 0 -> 0; matrix products, arithmetic and copies ran while one was open for 7% -> 10% of each run, Pallas kernels for 10% -> 13%
where the time goes in v4:
time: 755 us; the launch traced here: 744 us
  Pallas kernels  597 us (79%)
  matrix products  68.7 us (9%)
  other arithmetic  32.4 us (4%)
  local copies, waits for them, and re-layouts  28.5 us (4%)
  between operations  15.3 us (2%)
    pallas_call x1, Pallas kernels, experts_gathered(): pl.pallas_call(experts_kernel, out_shape=[array(experts, tokens, wide), a...  123 us
    pallas_call x1, Pallas kernels, back(): pl.pallas_call(back_kernel, out_shape=[jax.ShapeDtypeStruct((length // ro...  118 us
    pallas_call x1, Pallas kernels, sum_seq(): pl.pallas_call(sum_seq_kernel, out_shape=jax.ShapeDtypeStruct((rows, widt...  99.2 us
    pallas_call x1, Pallas kernels, sum_all(): pl.pallas_call(sum_all_kernel, out_shape=[jax.ShapeDtypeStruct((rows, wid...  93.6 us
    pallas_call x1, Pallas kernels, leave(): pl.pallas_call(leave_kernel, out_shape=[jax.ShapeDtypeStruct((rows, width...  92.4 us
    pallas_call x1, Pallas kernels, enter(): pl.pallas_call(enter_kernel, out_shape=[jax.ShapeDtypeStruct((count, *own...  70.8 us
    dot_general x1, matrix products, gathered_body(): jnp.einsum('rd,rf->df', rows_in, d_gate_up, preferred_element_type=f32)  16.5 us
  transfers between devices with their start and end apart: 1, of which 0 were waited for; matrix products, arithmetic and copies ran while one was open for 10% of the time, Pallas kernels for 13%

profile of v4, /device:TPU:16, one launch (start us, length us, event | category | flops | bytes accessed | tf_op | source)
XLA Modules:
  0.0 743.6 jit_solution(9910996767101666459)
XLA Ops:
  7.2 0.9 fusion.82
  8.2 1.3 fusion.37
  10.9 1.0 fusion.39.own
  12.0 1.1 copy-done.13
  13.1 70.8 %enter.1 = (bf16[8,128,2048]{2,1,0:T(8,128)(2,1)}, bf16[32,64,1408]{2,1,0:T(8,128)(2,1)}) custom-call(bf16[128,2048]{1,0:T(8,128)(2,1)} %fusion.39.own, bf16[8,64,1408]{2,1,0:T(8,128)(2,1)} %copy-done.13), custom_call_target="tpu_custom_call" | custom-call | tf_op jit(solution)/shard_map/enter/pallas_call | solution.py:1067
  84.0 6.1 fusion.32
  90.9 1.9 fusion.81
  92.8 1.9 reshape.383
  94.7 2.8 multiply_reduce_fusion
  97.7 1.9 fusion.80
  99.6 1.2 multiply_bitcast_fusion
  100.9 2.4 fusion.57
  103.5 3.0 fusion.58
  108.2 1.5 maximum_convert_fusion
  109.8 30.9 %while.11 = (s32[]{:T(128)}, bf16[2,512,4,128]{3,2,1,0:T(4,128)(2,1)}, s32[2]{0:T(128)S(1)}, bf16[1024,4,128]{2,0,1:T(8,128)(2,1)}, bf16[1024,128]{1,0:T(8,128)(...) while((s32[]{:T(128)}, ...), condition=%wide.region_6.7_spmd.clone, body=%wide.region_3.6_spmd.clone.sunk | while | flops 1087112704 | bytes 28856556 | solution.py:93
  111.6 7.5 %fusion.103 = (f32[4,512]{1,0:T(4,128)S(1)}, f32[4,512,1024]{2,1,0:T(8,128)}) fusion(pred[512,1024]{1,0:T(8,128)(4,1)S(1)} %iota_compare_fusion.9, bf16[1024,128]{1,0:T(8,128)(2,1)S(1)} %get-tuple-element.216, bf16[1024,4,128]{2,0,1:T(8,128)(2,1)} %get-tuple-element.215, s32[]{:T(128)S(6)} %select_n.22), kind=kOutput, calls=%fused_computation.156.clone.1 | convolution fusion | flops 545260544 | bytes 9707524 | tf_op jit(solution)/shard_map/while/body/eval_jaxpr/sub | solution.py:85
  119.1 4.8 fusion.104
  124.4 1.0 copy-done.18
  127.0 7.5 %fusion.103 = (f32[4,512]{1,0:T(4,128)S(1)}, f32[4,512,1024]{2,1,0:T(8,128)}) fusion(pred[512,1024]{1,0:T(8,128)(4,1)S(1)} %iota_compare_fusion.9, bf16[1024,128]{1,0:T(8,128)(2,1)S(1)} %get-tuple-element.216, bf16[1024,4,128]{2,0,1:T(8,128)(2,1)} %get-tuple-element.215, s32[]{:T(128)S(6)} %select_n.22), kind=kOutput, calls=%fused_computation.156.clone.1 | convolution fusion | flops 545260544 | bytes 9707524 | tf_op jit(solution)/shard_map/while/body/eval_jaxpr/sub | solution.py:85
  134.5 4.8 fusion.104
  139.8 1.0 copy-done.18
  140.7 2.5 copy.230
  143.2 6.1 convolution_convert_fusion
  149.3 99.2 %sum_seq.1 = bf16[128,2048]{1,0:T(8,128)(2,1)} custom-call(bf16[8,128,2048]{2,1,0:T(8,128)(2,1)} %bitcast.174), custom_call_target="tpu_custom_call" | custom-call | tf_op jit(solution)/shard_map/sum_seq/pallas_call | solution.py:940
  248.5 1.3 multiply_reduce_fusion.3
  249.8 1.3 multiply_convert_fusion
  251.9 1.4 fusion.54
  255.8 1.5 copy_bitcast_fusion.1.queries
  257.3 1.3 pad_maximum_fusion.2
  258.6 0.8 pad_maximum_fusion.1.own
  259.5 123.3 %experts.1 = (bf16[32,128,2176]{2,1,0:T(8,128)(2,1)}, bf16[32,128,2048]{2,1,0:T(8,128)(2,1)}, bf16[32,128,2176]{2,1,0:T(8,128)(2,1)}, bf16[2048,2048]{1,0:T(8,12...) custom-call(bf16[128,2176]{1,0:T(8,128)(2,1)} %pad_maximum_fusion.1.own, ...), custom_call_target="tpu_custom_call" | custom-call | tf_op jit(solution)/shard_map/experts/pallas_call | solution.py:1504
  382.8 93.6 %sum_all.1 = (bf16[128,2176]{1,0:T(8,128)(2,1)}, bf16[8,2,128,2048]{3,2,1,0:T(8,128)(2,1)}) custom-call(bf16[32,128,2176]{2,1,0:T(8,128)(2,1)} %get-tuple-element.67.part, bf16[8,2,2,128,2048]{4,3,2,1,0:T(8,128)(2,1)} %bitcast.164), custom_call_target="tpu_custom_call" | custom-call | tf_op jit(solution)/shard_map/sum_all/pallas_call | solution.py:803
  476.4 1.2 convert_element_type.130
  478.0 1.6 multiply_reduce_fusion.1
  479.7 1.4 fusion.69
  481.2 0.8 fusion.45.own
  482.0 117.8 %back.1 = (bf16[8,128,2048]{2,1,0:T(8,128)(2,1)}, bf16[2048,1408]{1,0:T(8,128)(2,1)}, f32[8,128]{1,0:T(8,128)}, bf16[128,2048]{1,0:T(8,128)(2,1)}) custom-call(bf16[128,2176]{1,0:T(8,128)(2,1)} %fusion.45.own, bf16[16,128,2048]{2,1,0:T(8,128)(2,1)} %bitcast.165, bf16[8,4,128,2176]{3,2,1,0:T(8,128)(2,1)} %bitcast.162, bf16[2048,1408]{1,0:T(8,128)(2,1)} %bitcast.170, ...), custom_call_target="tpu_custom_call" | custom-call | tf_op jit(solution)/shard_map/back/pallas_call | solution.py:1819
  601.2 92.4 %leave.1 = (bf16[128,2048]{1,0:T(8,128)(2,1)}, bf16[8,64,1408]{2,1,0:T(8,128)(2,1)}, f32[8,2048]{1,0:T(8,128)}) custom-call(bf16[8,128,2048]{2,1,0:T(8,128)(2,1)} %get-tuple-element.74.part, bf16[8,2,2,64,1408]{4,3,2,1,0:T(8,128)(2,1)} %bitcast.172, bf16[128,2048]{1,0:T(8,128)(2,1)} %bitcast.161, f32[128,2048]{1,0:T(8,128)} %get-tuple-element.118.d_hidden, ...), custom_call_target="tpu_custom_call" | custom-call | tf_op jit(solution)/shard_map/leave/pallas_call | solution.py:1210
  693.6 1.2 slice_bitcast_fusion.3
  694.8 1.5 fusion.83
  696.3 1.6 convert_bitcast_fusion
  697.9 1.3 slice_bitcast_fusion
  699.9 1.0 fusion.50
  701.6 2.3 copy.181
  705.0 1.2 pad_maximum_fusion
  706.2 1.1 copy-done.36
  707.3 11.7 %convolution_bitcast_fusion.1 = f32[1,768,2048]{2,1,0:T(8,128)} fusion(bf16[2048,768]{1,0:T(8,128)(2,1)S(1)} %copy-done.36, bf16[2048,2048]{1,0:T(8,128)(2,1)} %get-tuple-element.82), kind=kOutput, calls=%fused_computation.28 | convolution fusion | flops 6442450944 | bytes 17825792 | tf_op jit(solution)/shard_map/rf,rd->fd/dot_general | solution.py:1980
  719.0 16.5 %convolution_bitcast_fusion = f32[1,2048,1536]{2,1,0:T(8,128)} fusion(bf16[2048,2048]{1,0:T(8,128)(2,1)S(1)} %bitcast.200, bf16[2048,1536]{1,0:T(8,128)(2,1)S(1)} %bitcast.202), kind=kOutput, calls=%fused_computation.27 | convolution fusion | flops 12884901888 | bytes 27262976 | tf_op jit(solution)/shard_map/rd,rf->df/dot_general | solution.py:1981
  (169 shorter events, 15.5 us)
Async XLA Ops:
  7.2 3.4 slice-start.2
  7.2 252.3 %all-gather.3.cloned.1.call-start = ((), (), s32[]{:S(2)}) async-start(), calls=%async_computation | async-start | bytes 17301504 | tf_op jit(solution)/shard_map/all_gather | solution.py:1932
  8.2 2.8 copy-start
  8.2 2.8 copy-start.25
  8.2 3.7 copy-start.20
  12.0 1.1 copy-start.13
  90.1 2.7 copy-start.12
  92.8 1.9 copy-start.3
  94.7 4.9 copy-start.33
  100.9 5.6 copy-start.5
  100.9 5.6 copy-start.32
  106.5 0.8 copy-start.6
  106.5 1.0 copy-start.8
  119.1 4.8 copy-start.17
  124.4 1.0 copy-start.18
  134.5 4.8 copy-start.17
  139.8 1.0 copy-start.18
  140.7 2.5 copy-start.19
  149.3 100.5 %copy-start.23 = (f32[2048]{0:T(1024)S(1)}, f32[2048]{0:T(1024)}, u32[]{:S(2)}) copy-start(f32[2048]{0:T(1024)} %param.21) | copy-start | bytes 24580
  248.5 4.8 copy-start.24
  249.8 3.6 copy-start.34
  249.8 3.5 copy-start.30
  251.1 0.8 copy-start.10
  253.2 4.0 copy-start.7
  253.3 0.5 copy-start.26
  253.4 0.7 copy-start.28
  255.6 1.7 copy-start.9
  255.6 1.7 copy-start.15
  257.3 1.3 copy-start.11
  382.8 95.0 %copy-start.27 = (f32[128]{0:T(128)S(1)}, f32[128]{0:T(128)}, u32[]{:S(2)}) copy-start(f32[128]{0:T(128)} %copy-done.26) | copy-start | bytes 1540
  382.8 95.0 %copy-start.29 = (f32[128]{0:T(128)S(1)}, f32[128]{0:T(128)}, u32[]{:S(2)}) copy-start(f32[128]{0:T(128)} %copy-done.28) | copy-start | bytes 1540
  382.8 95.2 %copy-start.31 = (f32[128]{0:T(128)S(1)}, f32[128]{0:T(128)}, u32[]{:S(2)}) copy-start(f32[128]{0:T(128)} %copy-done.30) | copy-start | bytes 1540
  476.4 1.6 copy-start.2
  477.6 2.1 copy-start.35
  477.6 2.1 copy-start.14
  479.7 2.3 copy-start.16
  697.9 1.9 copy-start.4
  697.9 1.9 copy-start.1
  697.9 2.0 copy-start.22
  699.9 1.0 slice-start
  699.9 4.1 slice-start.1
  704.9 2.4 copy-start.36
  705.0 14.0 %slice-start.3 = ((s8[8388608]{0:T(1024)(128)(4,1)}), s8[4194304]{0:T(1024)(128)(4,1)S(1)}, s32[]{:S(2)}) async-start(s8[8388608]{0:T(1024)(128)(4,1)} %bitcast.199), calls=%async_computation.4 | async-start | bytes 8388608
  705.0 13.9 %slice-start.5 = ((s8[6291456]{0:T(1024)(128)(4,1)}), s8[4194304]{0:T(1024)(128)(4,1)S(1)}, s32[]{:S(2)}) async-start(s8[6291456]{0:T(1024)(128)(4,1)} %bitcast.201), calls=%async_computation.6 | async-start | bytes 8388608
  707.3 11.7 %slice-start.4 = ((s8[8388608]{0:T(1024)(128)(4,1)}), s8[4194304]{0:T(1024)(128)(4,1)S(1)}, s32[]{:S(2)}) async-start(s8[8388608]{0:T(1024)(128)(4,1)} %bitcast.199), calls=%async_computation.5 | async-start | bytes 8388608
  707.3 11.7 %slice-start.6 = ((s8[6291456]{0:T(1024)(128)(4,1)}), s8[2097152]{0:T(1024)(128)(4,1)S(1)}, s32[]{:S(2)}) async-start(s8[6291456]{0:T(1024)(128)(4,1)} %bitcast.201), calls=%async_computation.7 | async-start | bytes 4194304
  719.0 16.5 %copy-start.21 = (bf16[128,2048]{1,0:T(8,128)(2,1)S(1)}, bf16[128,2048]{1,0:T(8,128)(2,1)}, u32[]{:S(2)}) copy-start(bf16[128,2048]{1,0:T(8,128)(2,1)} %get-tuple-element.77) | copy-start | bytes 1572868
Sparse Core Ops, SparseCore 0:
  84.1 164.9 all-gather.2

commit v5 on v4

--- a/solution.py
+++ b/solution.py
@@ -604,43 +604,6 @@
     return plane_out, plane_turn, plane_end, plane_core, finish
 
 
-def gather_all_kernel(own, out, ss, rs, zs, local_sem):
-    p = Place()
-    p.greet(("x", "y", "core", "z"))
-    plane_out, plane_turn, plane_end, plane_core, finish = gather_steps(p, own, out, ss, rs, zs, local_sem)
-    plane_out(0)
-    plane_out(1)
-    plane_turn(0)
-    plane_out(2)
-    plane_end(0)
-    plane_turn(1)
-    plane_out(3)
-    plane_end(1)
-    plane_turn(2)
-    plane_end(2)
-    plane_turn(3)
-    plane_end(3)
-    for k in range(4):
-        plane_core(k)
-    pltpu.make_async_copy(own, out.at[p.me], local_sem).wait()
-    finish()
-
-
-def gather_all(own, blocks, collective_id):
-    dma = pltpu.SemaphoreType.DMA
-    return pl.pallas_call(
-        gather_all_kernel,
-        out_shape=jax.ShapeDtypeStruct((blocks, *own.shape), own.dtype),
-        in_specs=[pl.BlockSpec(memory_space=pl.ANY)],
-        out_specs=pl.BlockSpec(memory_space=pl.ANY),
-        scratch_shapes=[dma((4, G_KINDS)), dma((4, G_KINDS)), dma((4, 2)), dma],
-        compiler_params=pltpu.CompilerParams(
-            collective_id=collective_id, has_side_effects=True, vmem_limit_bytes=VMEM_LIMIT
-        ),
-        name="gather_all",
-    )(own)
-
-
 def sum_all_parts(p, part, held, core_in, x_half, y_half, x_in, y_in, z_in, out, ls, cs, cr, ss, rs, zs, zr):
     rows, width = part.shape[1], part.shape[2]
     half = rows // 2
@@ -821,70 +784,6 @@
     )(part, both)
 
 
-def gather_seq_kernel(own, out, ss, rs, zs, local_sem):
-    p = Place()
-    p.greet(("x", "z"))
-
-    def at(q, x):
-        return out.at[q * 2 + x]
-
-    def plane_out(k):
-        q = p.near(k)
-        there = at(q, p.x)
-        if k == 0:
-            src = own
-            for step, end in ((1, p.high), (-1, p.low)):
-
-                @pl.when(jnp.logical_not(end))
-                def _():
-                    send(src, there, zs.at[q, 0 if step > 0 else 1], rs.at[q, 0], p.by_z(step))
-
-            pltpu.make_async_copy(own, there, local_sem).start()
-        else:
-            src = there
-            await_bytes(src, rs.at[q, 0])
-
-            @pl.when(p.inner)
-            def _():
-                send(src, src, zs.at[q, 0], rs.at[q, 0], p.by_z(p.onward(k)))
-
-        send(src, there, ss.at[q], rs.at[q, 1], p.by_x)
-
-    for k in range(4):
-        plane_out(k)
-    for k in range(4):
-        await_bytes(own, rs.at[p.near(k), 1])
-    pltpu.make_async_copy(own, at(p.z, p.x), local_sem).wait()
-    for q in range(4):
-        await_bytes(own, ss.at[q])
-    for there, slot in ((p.high, 0), (p.low, 1)):
-
-        @pl.when(jnp.logical_not(there))
-        def _():
-            await_bytes(own, zs.at[p.z, slot])
-
-    for k in range(1, 4):
-
-        @pl.when(p.inner)
-        def _():
-            await_bytes(own, zs.at[p.near(k), 0])
-
-
-def gather_seq(own, collective_id):
-    dma = pltpu.SemaphoreType.DMA
-    return pl.pallas_call(
-        gather_seq_kernel,
-        out_shape=jax.ShapeDtypeStruct((8, *own.shape), own.dtype),
-        in_specs=[pl.BlockSpec(memory_space=pl.ANY)],
-        out_specs=pl.BlockSpec(memory_space=pl.ANY),
-        scratch_shapes=[dma((4,)), dma((4, 2)), dma((4, 2)), dma],
-        compiler_params=pltpu.CompilerParams(
-            collective_id=collective_id, has_side_effects=True, vmem_limit_bytes=VMEM_LIMIT
-        ),
-        name="gather_seq",
-    )(own)
-
-
 def add_rows(target, source, count, chunk=16):
     @pl.loop(0, count // chunk)
     def _(i):
@@ -892,71 +791,6 @@
         target[at, :] = (
             target[at, :].astype(jnp.float32) + source[at, :].astype(jnp.float32)
         ).astype(target.dtype)
-
-
-def sum_seq_kernel(part, out, held, x_in, z_in, ls, ss, rs, zs, zr):
-    p = Place()
-    p.greet(("x", "z"))
-    rows = part.shape[1]
-    for k in range(4):
-        q = p.far(k)
-        send(part.at[q * 2 + 1 - p.x], x_in.at[q], ss.at[q], rs.at[q], p.by_x)
-        pltpu.make_async_copy(part.at[q * 2 + p.x], held.at[q], ls.at[q]).start()
-    for k in range(4):
-        q = p.far(k)
-        mine = held.at[q]
-        await_bytes(mine, ls.at[q])
-        await_bytes(x_in.at[q], rs.at[q])
-        add_rows(mine, x_in.at[q], rows)
-        if k < 3:
-            step = p.toward(k)
-            slot = (1 - step) // 2
-
-            @pl.when(p.inner)
-            def _():
-                await_bytes(z_in.at[slot, q], zr.at[slot, q])
-                add_rows(mine, z_in.at[slot, q], rows)
-
-            send(mine, z_in.at[slot, q], zs.at[k], zr.at[slot, q], p.by_z(step))
-        else:
-            for slot, there in ((0, p.low), (1, p.high)):
-
-                @pl.when(jnp.logical_not(there))
-                def _():
-                    await_bytes(z_in.at[slot, q], zr.at[slot, q])
-                    add_rows(mine, z_in.at[slot, q], rows)
-
-            out[...] = mine[...]
-    for q in range(4):
-        await_bytes(x_in.at[0], ss.at[q])
-    for k in range(3):
-        await_bytes(x_in.at[0], zs.at[k])
-
-
-def sum_seq(part, collective_id):
-    _, rows, width = part.shape
-    dma = pltpu.SemaphoreType.DMA
-    bf16 = jnp.bfloat16
-    return pl.pallas_call(
-        sum_seq_kernel,
-        out_shape=jax.ShapeDtypeStruct((rows, width), part.dtype),
-        in_specs=[pl.BlockSpec(memory_space=pl.ANY)],
-        out_specs=pl.BlockSpec(memory_space=pltpu.VMEM),
-        scratch_shapes=[
-            pltpu.VMEM((4, rows, width), bf16),
-            pltpu.VMEM((4, rows, width), bf16),
-            pltpu.VMEM((2, 4, rows, width), bf16),
-            dma((4,)),
-            dma((4,)),
-            dma((4,)),
-            dma((3,)),
-            dma((2, 4)),
-        ],
-        compiler_params=pltpu.CompilerParams(
-            collective_id=collective_id, has_side_effects=True, vmem_limit_bytes=VMEM_LIMIT
-        ),
-        name="sum_seq",
-    )(part)
 
 
 def seq_peer(p, d):
@@ -973,133 +807,54 @@
     pl.semaphore_wait(barrier, 7 + len(sides))
 
 
-def enter_kernel(own, pieces, rows_out, columns, ss, rs, zs, cs, cr, ys, yr, ks, kr, local_sems):
-    p = Place()
-    greet_seq(p)
-    place, shard = p.z * 2 + p.x, p.y * 2 + p.c
-    mine = place * 4 + shard
-
-    def rows_at(q, x):
-        return rows_out.at[q * 2 + x]
-
-    def plane_out(k):
-        q = p.near(k)
-        there = rows_at(q, p.x)
-        if k == 0:
-            src = own
-            for step, end in ((1, p.high), (-1, p.low)):
-
-                @pl.when(jnp.logical_not(end))
-                def _():
-                    send(src, there, zs.at[q, 0 if step > 0 else 1], rs.at[q, 0], p.by_z(step))
-
-            pltpu.make_async_copy(own, there, local_sems.at[0]).start()
-        else:
-            src = there
-            await_bytes(src, rs.at[q, 0])
-
-            @pl.when(p.inner)
-            def _():
-                send(src, src, zs.at[q, 0], rs.at[q, 0], p.by_z(p.onward(k)))
-
-        send(src, there, ss.at[q], rs.at[q, 1], p.by_x)
-
-    def pass_on(d):
-        block = ((place + 8 - d) % 8) * 4 + shard
-        src = pieces.at[place] if d == 0 else columns.at[block]
-        if d > 0:
-            await_bytes(src, cr.at[d])
-        send(src, columns.at[block], ys.at[d], yr.at[d], p.by_y)
-        send(src, columns.at[block], ks.at[0, d], kr.at[0, d], p.by_core)
-
-    plane_out(0)
-    for d in range(1, 8):
-        send(pieces.at[(place + d) % 8], columns.at[mine], cs.at[d], cr.at[d], seq_peer(p, d))
-    pltpu.make_async_copy(pieces.at[place], columns.at[mine], local_sems.at[1]).start()
-    pass_on(0)
-    plane_out(1)
-    for d in (1, 2, 7):
-        pass_on(d)
-    plane_out(2)
-    for d in (6, 3, 5):
-        pass_on(d)
-    plane_out(3)
-    pass_on(4)
-    other = p.y * 2 + 1 - p.c
-    across = (1 - p.y) * 2 + p.c
-    piece = pieces.at[0]
-    for d in (0, 1, 2, 7, 6, 3, 5, 4):
-        block = columns.at[((place + 8 - d) % 8) * 4 + across]
-        await_bytes(block, yr.at[d])
-        send(block, block, ks.at[1, d], kr.at[1, d], p.by_core)
-    for k in range(4):
-        await_bytes(own, rs.at[p.near(k), 1])
-    for d in range(8):
-        await_bytes(piece, kr.at[0, d])
-        await_bytes(piece, kr.at[1, d])
-    pltpu.make_async_copy(own, rows_at(p.z, p.x), local_sems.at[0]).wait()
-    pltpu.make_async_copy(pieces.at[place], columns.at[mine], local_sems.at[1]).wait()
-    for q in range(4):
-        await_bytes(own, ss.at[q])
-    for there, slot in ((p.high, 0), (p.low, 1)):
-
-        @pl.when(jnp.logical_not(there))
-        def _():
-            await_bytes(own, zs.at[p.z, slot])
-
-    for k in range(1, 4):
-
-        @pl.when(p.inner)
-        def _():
-            await_bytes(own, zs.at[p.near(k), 0])
-
-    for d in range(8):
-        if d > 0:
-            await_bytes(piece, cs.at[d])
-        await_bytes(piece, ys.at[d])
-        await_bytes(piece, ks.at[0, d])
-        await_bytes(piece, ks.at[1, d])
-
-
-def enter(own, pieces, collective_id):
-    dma = pltpu.SemaphoreType.DMA
-    count, piece_rows, piece_width = pieces.shape
-    return pl.pallas_call(
-        enter_kernel,
-        out_shape=[
-            jax.ShapeDtypeStruct((count, *own.shape), own.dtype),
-            jax.ShapeDtypeStruct((count * 4, piece_rows, piece_width), pieces.dtype),
-        ],
-        in_specs=[pl.BlockSpec(memory_space=pl.ANY)] * 2,
-        out_specs=[pl.BlockSpec(memory_space=pl.ANY)] * 2,
-        scratch_shapes=[
-            dma((4,)),
-            dma((4, 2)),
-            dma((4, 2)),
-            dma((8,)),
-            dma((8,)),
-            dma((8,)),
-            dma((8,)),
-            dma((2, 8)),
-            dma((2, 8)),
-            dma((2,)),
-        ],
-        compiler_params=pltpu.CompilerParams(
-            collective_id=collective_id, has_side_effects=True, vmem_limit_bytes=VMEM_LIMIT
-        ),
-        name="enter",
-    )(own, pieces)
-
-
 def leave_kernel(
-    part, cols, tokens, d_hidden, gain, gains,
-    d_tokens, cols_out, gains_out,
-    held, x_in, z_in, c_held, c_core, c_y, g_send, g_in,
-    ls, ss, rs, zs, zr, cl, cs, cr, ys, yr, ts, tr, gs, gr,
+    part, cols, rows_in, d_gate_up_hbm, inner, d_expert_hbm, tokens, d_hidden, gain,
+    d_tokens, cols_out, d_w_in, d_w_down,
+    held, x_in, z_in, c_held, c_core, c_y, d_gate_up, d_expert, left, product,
+    ls, ss, rs, zs, zr, cl, cs, cr, ys, yr, ts, tr, load_sems, left_sems, product_sems,
 ):
     p = Place()
     greet_seq(p)
-    rows = part.shape[1]
+    wide_loads = [
+        pltpu.make_async_copy(d_gate_up_hbm, d_gate_up, load_sems.at[0]),
+        pltpu.make_async_copy(d_expert_hbm, d_expert, load_sems.at[1]),
+    ]
+
+    def left_load(source, i, slot):
+        cols = pl.ds(pl.multiple_of(i * TILE, TILE), TILE)
+        return pltpu.make_async_copy(source.at[:, cols], left.at[slot], left_sems.at[slot])
+
+    def product_store(target, i, slot):
+        at = pl.ds(pl.multiple_of(i * TILE, TILE), TILE)
+        piece = product.at[slot, :, pl.ds(0, target.shape[1])]
+        return pltpu.make_async_copy(piece, target.at[at], product_sems.at[slot])
+
+    def tiles(source, right, target, first, last):
+        count = source.shape[1] // TILE
+
+        @pl.loop(first, last)
+        def _(i):
+            slot = i % 2
+            left_load(source, i, slot).wait()
+
+            @pl.when(i + 1 < count)
+            def _():
+                left_load(source, i + 1, 1 - slot).start()
+
+            @pl.when(i >= 2)
+            def _():
+                product_store(target, i - 2, slot).wait()
+
+            result = mxu(left[slot], right[...], TN)
+            product[slot, :, : target.shape[1]] = result.astype(product.dtype)
+            product_store(target, i, slot).start()
+
+    def tiles_end(source, target):
+        count = source.shape[1] // TILE
+        for i in (count - 2, count - 1):
+            product_store(target, i, i % 2).wait()
+
+    rows, width = part.shape[1:]
     place = p.z * 2 + p.x
     for turn, side in ((0, 1 - p.y), (1, p.y)):
         send(cols.at[:, side, 1 - p.c], c_core.at[turn], cs.at[turn], cr.at[turn], p.by_core)
@@ -1109,6 +864,9 @@
         send(part.at[q * 2 + 1 - p.x], x_in.at[q], ss.at[q], rs.at[q], p.by_x)
         pltpu.make_async_copy(part.at[q * 2 + p.x], held.at[q], ls.at[q]).start()
     piece_rows = c_held.shape[2]
+    for load in wide_loads:
+        load.start()
+    left_load(rows_in, 0, 0).start()
     order = [(place + d) % 8 for d in range(1, 9)]
     for turn in range(2):
         await_bytes(c_held.at[turn], cl.at[turn])
@@ -1127,9 +885,12 @@
         else:
             pltpu.make_async_copy(c_held.at[1, s], cols_out.at[place], ts.at[7]).start()
 
+    wide_loads[0].wait()
+    per_plane = width // TILE // 4
     for k in range(4):
         q = p.far(k)
         mine = held.at[q]
+        tiles(rows_in, d_gate_up, d_w_in, k * per_plane, (k + 1) * per_plane)
         await_bytes(mine, ls.at[q])
         await_bytes(x_in.at[q], rs.at[q])
         add_rows(mine, x_in.at[q], rows)
@@ -1154,7 +915,6 @@
                     add_rows(mine, z_in.at[slot, q], rows)
 
     mine = held.at[p.z]
-    g_send[0] = jnp.zeros_like(g_send[0])
     chunk = 16
 
     @pl.loop(0, rows // chunk)
@@ -1167,24 +927,12 @@
         dot = jnp.mean(u * x, axis=-1, keepdims=True)
         d_x = scale * u - x * (scale * scale * scale * dot)
         d_tokens[at, :] = (d_hidden[at, :] + d_x).astype(d_tokens.dtype)
-        terms = d_out * x * scale
-        g_send[0] += terms[:8] + terms[8:]
-
-    first = jnp.sum(g_send[0], axis=0, keepdims=True)
-    row = lax.broadcasted_iota(jnp.int32, g_send[0].shape, 0)
-    g_send[0] = jnp.where(row == 0, first, gains[...])
-    for t, target in enumerate((p.by_core, p.by_y, p.by_x)):
-        send(g_send.at[t], g_in.at[t], gs.at[t], gr.at[t], target)
-        await_bytes(g_in.at[t], gr.at[t])
-        g_send[t + 1] = g_send[t] + g_in[t]
-    for d in (1, 2, 3):
-        target = p.device((p.z + d) % 4, p.x, p.y, p.c)
-        send(g_send.at[3], g_in.at[3 + p.z], gs.at[2 + d], gr.at[2 + d], target)
-    g_in[3 + p.z] = g_send[3]
-    for d in (1, 2, 3):
-        await_bytes(g_in.at[0], gr.at[2 + d])
-    gains_out[...] = g_in[3] + g_in[4] + g_in[5] + g_in[6]
-
+
+    tiles_end(rows_in, d_w_in)
+    left_load(inner, 0, 0).start()
+    wide_loads[1].wait()
+    tiles(inner, d_expert, d_w_down, 0, inner.shape[1] // TILE)
+    tiles_end(inner, d_w_down)
     piece = c_y.at[0]
     for i in range(8):
         if i < 7:
@@ -1197,25 +945,24 @@
         await_bytes(x_in.at[0], ss.at[q])
     for k in range(3):
         await_bytes(x_in.at[0], zs.at[k])
-    for t in range(6):
-        await_bytes(g_in.at[0], gs.at[t])
-
-
-def leave(part, cols, tokens, d_hidden, gain, gains, collective_id):
+
+
+def leave(part, cols, rows_in, d_gate_up, inner, d_expert, tokens, d_hidden, gain, collective_id):
     _, rows, width = part.shape
     piece_rows, piece_width = cols.shape[3:]
     dma = pltpu.SemaphoreType.DMA
-    bf16, f32 = jnp.bfloat16, jnp.float32
+    bf16 = jnp.bfloat16
     anywhere, vmem = pl.BlockSpec(memory_space=pl.ANY), pl.BlockSpec(memory_space=pltpu.VMEM)
     return pl.pallas_call(
         leave_kernel,
         out_shape=[
             jax.ShapeDtypeStruct((rows, width), bf16),
             jax.ShapeDtypeStruct((8, piece_rows, piece_width), bf16),
-            jax.ShapeDtypeStruct(gains.shape, f32),
+            jax.ShapeDtypeStruct((rows_in.shape[1], d_gate_up.shape[1]), bf16),
+            jax.ShapeDtypeStruct((inner.shape[1], d_expert.shape[1]), bf16),
         ],
-        in_specs=[anywhere] * 2 + [vmem] * 4,
-        out_specs=[vmem, anywhere, vmem],
+        in_specs=[anywhere] * 6 + [vmem] * 3,
+        out_specs=[vmem] + [anywhere] * 3,
         scratch_shapes=[
             pltpu.VMEM((4, rows, width), bf16),
             pltpu.VMEM((4, rows, width), bf16),
@@ -1223,8 +970,10 @@
             pltpu.VMEM((2, 8, piece_rows, piece_width), bf16),
             pltpu.VMEM((2, 8, piece_rows, piece_width), bf16),
             pltpu.VMEM((8, piece_rows, piece_width), bf16),
-            pltpu.VMEM((4, *gains.shape), f32),
-            pltpu.VMEM((7, *gains.shape), f32),
+            pltpu.VMEM(d_gate_up.shape, bf16),
+            pltpu.VMEM(d_expert.shape, bf16),
+            pltpu.VMEM((2, rows_in.shape[0], TILE), bf16),
+            pltpu.VMEM((2, TILE, d_expert.shape[1]), bf16),
             dma((4,)),
             dma((4,)),
             dma((4,)),
@@ -1237,14 +986,15 @@
             dma((8,)),
             dma((8,)),
             dma((7,)),
-            dma((6,)),
-            dma((6,)),
+            dma((2,)),
+            dma((2,)),
+            dma((2,)),
         ],
         compiler_params=pltpu.CompilerParams(
             collective_id=collective_id, has_side_effects=True, vmem_limit_bytes=VMEM_LIMIT
         ),
         name="leave",
-    )(part, cols, tokens, d_hidden, gain, gains)
+    )(part, cols, rows_in, d_gate_up, inner, d_expert, tokens, d_hidden, gain)
 
 
 NT = (((1,), (1,)), ((), ()))
@@ -1552,15 +1302,19 @@
 
 def back_kernel(
     own, pair, rows_all, columns_hbm, normed_hbm, queries, keys, values, attended,
-    q_raw, k_raw, cosine, sine, q_gain, k_gain,
-    d_normed, d_columns, head_gains, mixture,
+    q_raw, k_raw, cosine, sine, q_gain, k_gain, attn_gain, gains,
+    d_normed, d_columns, gains_out, mixture,
     d_attn, columns, normed, d_heads, d_query, d_key, d_value, d_proj, logits, q_sum, k_sum,
-    held, x_in, y_in, z_in,
-    gs, gr, gz, load_sems, local_sem, hs, ys, yr, xs, xr, zs, zr,
+    held, x_in, y_in, z_in, g_send, g_in,
+    gs, gr, gz, load_sems, local_sem, hs, ys, yr, xs, xr, zs, zr, ts, tr,
 ):
     p = Place()
     bf16, f32 = jnp.bfloat16, jnp.float32
-    p.greet(("x", "y", "z"))
+    columns_z = [p.device((p.z + d) % 4, p.x, p.y, p.c) for d in (1, 2, 3)]
+    barrier = pltpu.get_barrier_semaphore()
+    for target in (p.by_core, p.by_x, p.by_y, *columns_z):
+        pl.semaphore_signal(barrier, inc=1, device_id=target, device_id_type=MESH)
+    pl.semaphore_wait(barrier, 6)
     rows, wide = own.shape
     length, head_cols = queries.shape
     heads = head_cols // HEAD_DIMENSION
@@ -1716,19 +1470,37 @@
             )
             d_proj[at, head_cols + HEAD_DIMENSION :] = d_value[at, :].astype(bf16)
 
-        line = lax.broadcasted_iota(jnp.int32, (8, HEAD_DIMENSION), 0)
-        head_gains[...] = jnp.where(
-            line == 0,
-            jnp.sum(q_sum[...], axis=0, keepdims=True),
-            jnp.where(line == 1, jnp.sum(k_sum[...], axis=0, keepdims=True), 0.0),
+        g_send[0] = gains[...]
+        g_send[0, 2:3, :HEAD_DIMENSION] = jnp.sum(q_sum[...], axis=0, keepdims=True)
+        g_send[0, 2:3, HEAD_DIMENSION : 2 * HEAD_DIMENSION] = jnp.sum(
+            k_sum[...], axis=0, keepdims=True
         )
 
     def normed_grads():
         @pl.loop(0, width // TILE)
         def _(n):
             cols = pl.ds(pl.multiple_of(n * TILE, TILE), TILE)
-            part = mxu(d_proj[...], columns[cols, :proj_cols], NT).astype(bf16)
-            d_normed[:, :, cols] = part.reshape(length // rows, rows, TILE)
+            part = mxu(d_proj[...], columns[cols, :proj_cols], NT)
+            d_normed[:, :, cols] = part.astype(bf16).reshape(length // rows, rows, TILE)
+            total = jnp.sum(part * normed[:, cols].astype(f32), axis=0, keepdims=True)
+            g_send[0, 0:1, cols] = total / attn_gain[:, cols]
+
+    def gains_pass(t, target):
+        send(g_send.at[t], g_in.at[t], ts.at[t], tr.at[t], target)
+
+    def gains_take(t):
+        await_bytes(g_in.at[t], tr.at[t])
+        g_send[t + 1] = g_send[t] + g_in[t]
+
+    def gains_z_pass():
+        g_in[2 + p.z] = g_send[2]
+        for d, target in enumerate(columns_z):
+            send(g_send.at[2], g_in.at[2 + p.z], ts.at[2 + d], tr.at[2 + d], target)
+
+    def gains_z_take():
+        for d in range(3):
+            await_bytes(g_in.at[0], tr.at[2 + d])
+        g_send[3] = g_in[2] + g_in[3] + g_in[4] + g_in[5]
 
     def column_grads(source, value, first, count):
         @pl.loop(0, width // TILE)
@@ -1765,10 +1537,15 @@
     attention(p.near(3))
     raw_grads()
     sum_end(1)
+    loads[1].wait()
     normed_grads()
-    loads[1].wait()
+    gains_pass(0, p.by_core)
     column_grads(normed, d_proj, 0, proj_cols)
+    gains_take(0)
+    gains_pass(1, p.by_x)
     sum_turn(2)
+    gains_take(1)
+    gains_z_pass()
     column_grads(d_attn.at[:, :, pl.ds(0, width)], attended, proj_cols, head_cols)
     line = lax.broadcasted_iota(jnp.int32, (128, 128), 0)
     lane = lax.broadcasted_iota(jnp.int32, (128, 128), 1)
@@ -1777,6 +1554,8 @@
     select = jnp.where(mine, 1.0, 0.0).astype(bf16)
     logits[...] = mxu(d_attn[:, :, width:].reshape(length, 128), select).astype(bf16)
     sum_end(2)
+    gains_z_take()
+    send(g_send.at[3], g_in.at[6], ts.at[5], tr.at[5], p.by_y)
     for q in range(4):
         await_bytes(own, gs.at[q])
     for there, slot in ((p.high, 0), (p.low, 1)):
@@ -1796,6 +1575,10 @@
     column_grads(d_attn.at[:, :, pl.ds(0, width)], logits, proj_cols + head_cols, 128)
     sum_turn(3)
     sum_end(3)
+    await_bytes(g_in.at[6], tr.at[5])
+    gains_out[...] = g_send[3] + g_in[6]
+    for t in range(6):
+        await_bytes(g_in.at[0], ts.at[t])
     piece = x_in.at[0]
     for i in range(8):
         await_bytes(piece, ys.at[i])
@@ -1807,7 +1590,7 @@
 
 def back(
     own, pair, rows_all, columns, normed, queries, keys, values, attended,
-    q_raw, k_raw, cosine, sine, q_gain, k_gain, collective_id,
+    q_raw, k_raw, cosine, sine, q_gain, k_gain, attn_gain, gains, collective_id,
 ):
     rows, wide = own.shape
     length, head_cols = queries.shape
@@ -1821,10 +1604,10 @@
         out_shape=[
             jax.ShapeDtypeStruct((length // rows, rows, width), bf16),
             jax.ShapeDtypeStruct(columns.shape, bf16),
-            jax.ShapeDtypeStruct((8, HEAD_DIMENSION), f32),
+            jax.ShapeDtypeStruct(gains.shape, f32),
             jax.ShapeDtypeStruct((rows, width), bf16),
         ],
-        in_specs=[anywhere] * 5 + [vmem] * 10,
+        in_specs=[anywhere] * 5 + [vmem] * 12,
         out_specs=[vmem] * 4,
         scratch_shapes=[
             pltpu.VMEM((8, rows, wide), bf16),
@@ -1842,6 +1625,8 @@
             pltpu.VMEM((4, rows, width), bf16),
             pltpu.VMEM((8, rows, width), bf16),
             pltpu.VMEM((2, 4, rows, width), bf16),
+            pltpu.VMEM((4, *gains.shape), f32),
+            pltpu.VMEM((7, *gains.shape), f32),
             dma((4,)),
             dma((4, 2)),
             dma((4, 2)),
@@ -1854,6 +1639,8 @@
             dma((4,)),
             dma((3,)),
             dma((2, 4)),
+            dma((6,)),
+            dma((6,)),
         ],
         compiler_params=pltpu.CompilerParams(
             collective_id=collective_id, has_side_effects=True, vmem_limit_bytes=VMEM_LIMIT
@@ -1861,8 +1648,339 @@
         name="back",
     )(
         own, pair, rows_all, columns, normed, queries, keys, values, attended,
-        q_raw, k_raw, cosine, sine, q_gain, k_gain,
-    )
+        q_raw, k_raw, cosine, sine, q_gain, k_gain, attn_gain, gains,
+    )
+
+
+C_Z, C_X, C_Y, C_C, C_KINDS = 0, 1, 2, 4, 8
+
+
+def front_kernel(
+    own, pieces, cot, cosine, sine, q_gain, k_gain,
+    normed_out, columns_out, cot_all, queries, keys, values, attended, q_raw, k_raw, attn_out,
+    normed, columns, part, x_in, z_in,
+    ss, rs, zs, cs, cr, ys, yr, ks, kr, local_sems, gs, gr, gz, xs, xr, us, ur,
+):
+    p = Place()
+    bf16 = jnp.bfloat16
+    greet_seq(p)
+    place, shard = p.z * 2 + p.x, p.y * 2 + p.c
+    mine = place * 4 + shard
+    rows, width = own.shape
+    length, head_cols = queries.shape
+    heads = head_cols // HEAD_DIMENSION
+    proj_cols = head_cols + 2 * HEAD_DIMENSION
+    plane_rows = 2 * rows
+    score_scale = 1.0 / math.sqrt(HEAD_DIMENSION)
+
+    def rows_at(q, x):
+        return normed.at[q * 2 + x]
+
+    def rows_move(k):
+        q = p.near(k)
+        there = rows_at(q, p.x)
+        if k == 0:
+            src = own
+            for step, end in ((1, p.high), (-1, p.low)):
+
+                @pl.when(jnp.logical_not(end))
+                def _():
+                    send(src, there, zs.at[q, 0 if step > 0 else 1], rs.at[q, 0], p.by_z(step))
+
+            pltpu.make_async_copy(own, there, local_sems.at[0]).start()
+        else:
+            src = there
+            await_bytes(src, rs.at[q, 0])
+
+            @pl.when(p.inner)
+            def _():
+                send(src, src, zs.at[q, 0], rs.at[q, 0], p.by_z(p.onward(k)))
+
+        send(src, there, ss.at[q], rs.at[q, 1], p.by_x)
+
+    def pass_on(d):
+        block = ((place + 8 - d) % 8) * 4 + shard
+        src = pieces.at[place] if d == 0 else columns.at[block]
+        if d > 0:
+            await_bytes(src, cr.at[d])
+        send(src, columns.at[block], ys.at[d], yr.at[d], p.by_y)
+        send(src, columns.at[block], ks.at[0, d], kr.at[0, d], p.by_core)
+
+    def pass_across(d):
+        block = columns.at[((place + 8 - d) % 8) * 4 + (1 - p.y) * 2 + p.c]
+        await_bytes(block, yr.at[d])
+        send(block, block, ks.at[1, d], kr.at[1, d], p.by_core)
+
+    def cot_at(q, x, y):
+        return cot_all.at[p.block(q, x, y, p.c)]
+
+    def cot_core(q, j, src):
+        x, y = (p.x, 1 - p.x)[j % 2], (p.y, 1 - p.y)[j // 2]
+        send(src, cot_at(q, x, y), gs.at[q, C_C + j], gr.at[q, C_C + j], p.by_core)
+
+    def cot_move(k):
+        q = p.near(k)
+        there = cot_at(q, p.x, p.y)
+        if k == 0:
+            src = cot
+            for step, end in ((1, p.high), (-1, p.low)):
+
+                @pl.when(jnp.logical_not(end))
+                def _():
+                    send(src, there, gz.at[q, 0 if step > 0 else 1], gr.at[q, C_Z], p.by_z(step))
+
+            pltpu.make_async_copy(cot, there, local_sems.at[2]).start()
+        else:
+            src = there
+            await_bytes(src, gr.at[q, C_Z])
+
+            @pl.when(p.inner)
+            def _():
+                send(src, src, gz.at[q, 0], gr.at[q, C_Z], p.by_z(p.onward(k)))
+
+        send(src, there, gs.at[q, C_Y], gr.at[q, C_Y], p.by_y)
+        send(src, there, gs.at[q, C_X], gr.at[q, C_X], p.by_x)
+        cot_core(q, 0, src)
+
+    def cot_turn(k):
+        q = p.near(k)
+        there = cot_at(q, 1 - p.x, p.y)
+        await_bytes(there, gr.at[q, C_X])
+        send(there, there, gs.at[q, C_Y + 1], gr.at[q, C_Y + 1], p.by_y)
+        cot_core(q, 1, there)
+
+    def cot_end(k):
+        q = p.near(k)
+        for j, x in ((0, p.x), (1, 1 - p.x)):
+            there = cot_at(q, x, 1 - p.y)
+            await_bytes(there, gr.at[q, C_Y + j])
+            cot_core(q, 2 + j, there)
+
+    def sum_end(k):
+        q = p.far(k)
+        held = part.at[q * 2 + p.x]
+        await_bytes(x_in.at[q], xr.at[q])
+        add_rows(held, x_in.at[q], rows)
+        if k < 3:
+            step = p.toward(k)
+            slot = (1 - step) // 2
+
+            @pl.when(p.inner)
+            def _():
+                await_bytes(z_in.at[slot, q], ur.at[slot, q])
+                add_rows(held, z_in.at[slot, q], rows)
+
+            send(held, z_in.at[slot, q], us.at[k], ur.at[slot, q], p.by_z(step))
+        else:
+            for slot, there in ((0, p.low), (1, p.high)):
+
+                @pl.when(jnp.logical_not(there))
+                def _():
+                    await_bytes(z_in.at[slot, q], ur.at[slot, q])
+                    add_rows(held, z_in.at[slot, q], rows)
+
+            attn_out[...] = held[...]
+
+    def project(n):
+        cols = slice(n * TILE, (n + 1) * TILE)
+        weight = columns[:, :, cols].reshape(width, TILE)
+        result = mxu(normed[...].reshape(length, width), weight)
+        if n * TILE < head_cols:
+            q_raw[:, cols] = result
+        else:
+            k_raw[...] = result[:, :HEAD_DIMENSION]
+            values[...] = result[:, HEAD_DIMENSION:].astype(bf16)
+
+    def prepare():
+        def one(raw, gain, at):
+            scaled = raw * lax.rsqrt(jnp.mean(raw * raw, axis=-1, keepdims=True) + EPS) * gain[...]
+            swapped = jnp.concatenate(
+                [scaled[:, HEAD_DIMENSION // 2 :], scaled[:, : HEAD_DIMENSION // 2]], axis=1
+            )
+            return (scaled * cosine[at, :] - swapped * sine[at, :]).astype(bf16)
+
+        chunk = 128
+
+        @pl.loop(0, length // chunk)
+        def _(i):
+            at = pl.ds(pl.multiple_of(i * chunk, chunk), chunk)
+            for h in range(heads):
+                cols = slice(h * HEAD_DIMENSION, (h + 1) * HEAD_DIMENSION)
+                queries[at, cols] = one(q_raw[at, cols], q_gain, at)
+            keys[at, :] = one(k_raw[at, :], k_gain, at)
+
+    def attention(k):
+        q = p.far(k)
+        row_start = pl.multiple_of(q * plane_rows, plane_rows)
+        at = pl.ds(row_start, plane_rows)
+
+        def block(count):
+            row_pos = row_start + lax.broadcasted_iota(jnp.int32, (plane_rows, count), 0)
+            allowed = lax.broadcasted_iota(jnp.int32, (plane_rows, count), 1) <= row_pos
+
+            @pl.loop(0, heads)
+            def _(h):
+                cols = pl.ds(pl.multiple_of(h * HEAD_DIMENSION, HEAD_DIMENSION), HEAD_DIMENSION)
+                scores = mxu(queries[at, cols], keys[:count], NT) * score_scale
+                scores = jnp.where(allowed, scores, -1e30)
+                raised = jnp.exp(scores - jnp.max(scores, axis=-1, keepdims=True))
+                prob = raised / jnp.sum(raised, axis=-1, keepdims=True)
+                attended[at, cols] = mxu(prob.astype(bf16), values[:count]).astype(bf16)
+
+        @pl.when(q < 2)
+        def _():
+            block(length // 2)
+
+        @pl.when(q >= 2)
+        def _():
+            block(length)
+
+        per_tile = TILE // columns.shape[1]
+
+        @pl.loop(0, width // TILE)
+        def _(n):
+            cols = pl.ds(pl.multiple_of(n * TILE, TILE), TILE)
+            weight = columns[pl.ds(n * per_tile, per_tile), :, proj_cols : proj_cols + head_cols]
+            result = mxu(attended[at, :], weight.reshape(TILE, head_cols), NT).astype(bf16)
+            part[pl.ds(q * 2, 2), :, cols] = result.reshape(2, rows, TILE)
+
+        send(part.at[q * 2 + 1 - p.x], x_in.at[q], xs.at[q], xr.at[q], p.by_x)
+
+    rows_move(0)
+    for d in range(1, 8):
+        send(pieces.at[(place + d) % 8], columns.at[mine], cs.at[d], cr.at[d], seq_peer(p, d))
+    pltpu.make_async_copy(pieces.at[place], columns.at[mine], local_sems.at[1]).start()
+    pass_on(0)
+    rows_move(1)
+    for d in (1, 2, 7):
+        pass_on(d)
+    rows_move(2)
+    cot_move(0)
+    for d in (6, 3, 5):
+        pass_on(d)
+    rows_move(3)
+    pass_on(4)
+    for d in (0, 1, 2, 7, 6, 3, 5, 4):
+        pass_across(d)
+    cot_move(1)
+    for k in range(4):
+        await_bytes(own, rs.at[p.near(k), 1])
+    pltpu.make_async_copy(own, rows_at(p.z, p.x), local_sems.at[0]).wait()
+    pltpu.make_async_copy(pieces.at[place], columns.at[mine], local_sems.at[1]).wait()
+    piece = pieces.at[0]
+    for d in range(8):
+        await_bytes(piece, kr.at[0, d])
+        await_bytes(piece, kr.at[1, d])
+    pltpu.make_async_copy(normed, normed_out, local_sems.at[0]).start()
+    pltpu.make_async_copy(columns, columns_out, local_sems.at[1]).start()
+    cot_turn(0)
+    for n in range(proj_cols // TILE):
+        project(n)
+    cot_move(2)
+    prepare()
+    cot_turn(1)
+    attention(0)
+    cot_end(0)
+    attention(1)
+    cot_move(3)
+    sum_end(0)
+    attention(2)
+    cot_turn(2)
+    cot_end(1)
+    sum_end(1)
+    attention(3)
+    cot_turn(3)
+    sum_end(2)
+    cot_end(2)
+    sum_end(3)
+    cot_end(3)
+    for q in range(4):
+        for j in range(4):
+            await_bytes(cot, gr.at[q, C_C + j])
+            await_bytes(cot, gs.at[q, C_C + j])
+        for kind in (C_X, C_Y, C_Y + 1):
+            await_bytes(cot, gs.at[q, kind])
+        await_bytes(own, ss.at[q])
+        await_bytes(own, xs.at[q])
+    for there, slot in ((p.high, 0), (p.low, 1)):
+
+        @pl.when(jnp.logical_not(there))
+        def _():
+            await_bytes(own, zs.at[p.z, slot])
+            await_bytes(cot, gz.at[p.z, slot])
+
+    for k in range(1, 4):
+
+        @pl.when(p.inner)
+        def _():
+            await_bytes(own, zs.at[p.near(k), 0])
+            await_bytes(cot, gz.at[p.near(k), 0])
+
+    for k in range(3):
+        await_bytes(own, us.at[k])
+    for d in range(8):
+        if d > 0:
+            await_bytes(piece, cs.at[d])
+        await_bytes(piece, ys.at[d])
+        await_bytes(piece, ks.at[0, d])
+        await_bytes(piece, ks.at[1, d])
+    pltpu.make_async_copy(cot, cot_at(p.z, p.x, p.y), local_sems.at[2]).wait()
+    pltpu.make_async_copy(normed, normed_out, local_sems.at[0]).wait()
+    pltpu.make_async_copy(columns, columns_out, local_sems.at[1]).wait()
+
+
+def front(own, pieces, cot, cosine, sine, q_gain, k_gain, head_cols, collective_id):
+    dma = pltpu.SemaphoreType.DMA
+    bf16, f32 = jnp.bfloat16, jnp.float32
+    rows, width = own.shape
+    count, piece_rows, piece_width = pieces.shape
+    length = count * rows
+    anywhere, vmem = pl.BlockSpec(memory_space=pl.ANY), pl.BlockSpec(memory_space=pltpu.VMEM)
+    return pl.pallas_call(
+        front_kernel,
+        out_shape=[
+            jax.ShapeDtypeStruct((count, rows, width), bf16),
+            jax.ShapeDtypeStruct((count * 4, piece_rows, piece_width), bf16),
+            jax.ShapeDtypeStruct((count * 4, rows, width), bf16),
+            jax.ShapeDtypeStruct((length, head_cols), bf16),
+            jax.ShapeDtypeStruct((length, HEAD_DIMENSION), bf16),
+            jax.ShapeDtypeStruct((length, HEAD_DIMENSION), bf16),
+            jax.ShapeDtypeStruct((length, head_cols), bf16),
+            jax.ShapeDtypeStruct((length, head_cols), f32),
+            jax.ShapeDtypeStruct((length, HEAD_DIMENSION), f32),
+            jax.ShapeDtypeStruct((rows, width), bf16),
+        ],
+        in_specs=[anywhere] * 3 + [vmem] * 4,
+        out_specs=[anywhere] * 3 + [vmem] * 7,
+        scratch_shapes=[
+            pltpu.VMEM((count, rows, width), bf16),
+            pltpu.VMEM((count * 4, piece_rows, piece_width), bf16),
+            pltpu.VMEM((count, rows, width), bf16),
+            pltpu.VMEM((4, rows, width), bf16),
+            pltpu.VMEM((2, 4, rows, width), bf16),
+            dma((4,)),
+            dma((4, 2)),
+            dma((4, 2)),
+            dma((8,)),
+            dma((8,)),
+            dma((8,)),
+            dma((8,)),
+            dma((2, 8)),
+            dma((2, 8)),
+            dma((3,)),
+            dma((4, C_KINDS)),
+            dma((4, C_KINDS)),
+            dma((4, 2)),
+            dma((4,)),
+            dma((4,)),
+            dma((3,)),
+            dma((2, 4)),
+        ],
+        compiler_params=pltpu.CompilerParams(
+            collective_id=collective_id, has_side_effects=True, vmem_limit_bytes=VMEM_LIMIT
+        ),
+        name="front",
+    )(own, pieces, cot, cosine, sine, q_gain, k_gain)
 
 
 def head_columns(weight, group_index):
@@ -1922,29 +2040,18 @@
     )
     resid_in = tokens[0].astype(f32)
     normed_one = rms_scale(resid_in, attn_gain).astype(bf16)
-    normed_all, columns = enter(normed_one, pieces, 1)
+    half_dim = HEAD_DIMENSION // 2
+    frequency = ROPE_BASE ** (-2.0 * jnp.arange(half_dim, dtype=f32) / HEAD_DIMENSION)
+    angles = jnp.arange(length, dtype=f32)[:, None] * frequency[None, :]
+    cosine, sine = jnp.cos(angles), jnp.sin(angles)
+    cosine = jnp.concatenate([cosine, cosine], axis=1)
+    sine = jnp.concatenate([sine, -sine], axis=1)
+    normed_all, columns, cot_all, queries, keys, values, attended, q_raw, k_raw, attn_out = front(
+        normed_one, pieces, cotangent[0], cosine, sine, q_gain[None], k_gain[None], head_cols, 1
+    )
     normed_all = normed_all.reshape(length, width)
     columns = columns.reshape(width, -1)
-    proj_weight = columns[:, :proj_cols]
-    out_weight = columns[:, proj_cols:all_cols]
     full_router = columns[:, all_cols : all_cols + experts]
-    columns, cot_own = lax.optimization_barrier((columns, cotangent[0]))
-    cot_all = lax.all_gather(cot_own, both)
-
-    projected = jnp.dot(normed_all, proj_weight, preferred_element_type=f32)
-    seq_positions = jnp.arange(length, dtype=jnp.int32)
-    prepare = partial(head_prepare, positions=seq_positions)
-    q_raw = projected[:, :head_cols].reshape(length, heads, HEAD_DIMENSION)
-    k_raw = projected[:, head_cols : head_cols + kv_cols].reshape(length, 1, HEAD_DIMENSION)
-    values = projected[:, head_cols + kv_cols :].astype(bf16).reshape(length, 1, HEAD_DIMENSION)
-    queries = prepare(q_raw, q_gain).astype(bf16)
-    keys = prepare(k_raw, k_gain).astype(bf16)
-    repeat_keys = jnp.repeat(keys, heads, axis=1)
-    repeat_values = jnp.repeat(values, heads, axis=1)
-    mixed_heads, unused_total = attend_forward(queries, repeat_keys, repeat_values)
-    attended = mixed_heads.reshape(length, head_cols)
-    attn_part = jnp.einsum("tj,dj->td", attended, out_weight, preferred_element_type=f32)
-    attn_out = sum_seq(attn_part.astype(bf16).reshape(seq_size, rows, width), 2)
     hidden = resid_in + attn_out.astype(f32)
     normed_two = rms_scale(hidden, ffn_gain).astype(bf16)
 
@@ -1977,8 +2084,6 @@
     )
     d_back, out_pair = sum_all(d_part, out_part, 5)
     d_back = d_back.astype(f32)
-    d_w_down = jnp.einsum("rf,rd->fd", inner_act, d_expert, preferred_element_type=f32)[None]
-    d_w_in = jnp.einsum("rd,rf->df", rows_in, d_gate_up, preferred_element_type=f32)[None]
 
     d_gate_dense = d_back[:, width : width + experts] + d_back[:, width + experts : width + 2 * experts]
     d_gates = jnp.sum(onehot_float * d_gate_dense[:, None, :], axis=-1)
@@ -1994,45 +2099,42 @@
     d_attn = d_hidden.astype(bf16)
 
     d_send = jnp.concatenate([d_attn, jnp.pad(d_logits, ((0, 0), (0, 128 - experts)))], axis=1)
-    half_dim = HEAD_DIMENSION // 2
-    frequency = ROPE_BASE ** (-2.0 * jnp.arange(half_dim, dtype=f32) / HEAD_DIMENSION)
-    angles = seq_positions.astype(f32)[:, None] * frequency[None, :]
-    cosine, sine = jnp.cos(angles), jnp.sin(angles)
-    d_normed_part, d_columns, head_gains, mixture = back(
+    gains = jnp.pad(d_ffn_gain[None], ((1, 6), (0, 0)))
+    d_normed_part, d_columns, gains, mixture = back(
         d_send,
         out_pair.reshape(2 * seq_size, rows, width),
         rows_all.reshape(seq_size, shard_size, rows, -1),
         columns,
         normed_all,
-        queries.reshape(length, head_cols),
-        keys.reshape(length, kv_cols),
-        values.reshape(length, kv_cols),
+        queries,
+        keys,
+        values,
         attended,
-        q_raw.reshape(length, head_cols),
-        k_raw.reshape(length, kv_cols),
-        jnp.concatenate([cosine, cosine], axis=1),
-        jnp.concatenate([sine, -sine], axis=1),
+        q_raw,
+        k_raw,
+        cosine,
+        sine,
         q_gain[None],
         k_gain[None],
+        attn_gain[None],
+        gains,
         6,
     )
     output = (hidden + mixture.astype(f32)).astype(bf16)
     router_cols = experts // seq_size
-    gains = jnp.pad(
-        jnp.stack(
-            [d_ffn_gain, jnp.pad(head_gains[:2].reshape(-1), (0, width - 2 * HEAD_DIMENSION))]
-        ),
-        ((1, 5), (0, 0)),
-    )
-    d_tokens, d_pieces, gains = leave(
+    d_tokens, d_pieces, d_w_in, d_w_down = leave(
         d_normed_part,
         d_columns.reshape(seq_size, 2, shard_size // 2, weight_rows, all_cols + spare_cols),
+        rows_in,
+        d_gate_up,
+        inner_act,
+        d_expert,
         tokens[0],
         d_hidden,
         attn_gain[None],
-        gains,
         7,
     )
+    d_w_in, d_w_down = d_w_in.astype(f32)[None], d_w_down.astype(f32)[None]
     d_tokens = d_tokens[None]
     d_pieces = d_pieces.astype(f32).transpose(1, 0, 2)
     per_group = seq_size // KEY_VALUE_HEADS

time: 755 us -> 664 us (0.88)
  matrix products: 68.7 us -> 3.17 us
  local copies, waits for them, and re-layouts: 28.5 us -> 13 us
  Pallas kernels: 597 us -> 611 us
  between operations: 15.3 us -> 1.56 us
    dot_general x6 -> x0, matrix products: 50 us -> none  [the longest x1 16.5 us: gathered_body(): jnp.einsum('rd,rf->df', rows_in, d_gate_up, preferred_element_type=f32)]
    sub x2 -> x0, matrix products: 15 us -> none  [one_block(): weights = jnp.exp(scores - row_max)]
    broadcast_in_dim x1 -> x2, other arithmetic: 0.01 us -> 10.1 us  [gathered_body(): d_w_in, d_w_down = (d_w_in.astype(f32)[None], d_w_down.astype(f32)[None])]
    pallas_call x1, Pallas kernels: 123 us -> 133 us  [experts_gathered(): pl.pallas_call(experts_kernel, out_shape=[array(experts, tokens, wide), a...]
    pallas_call x2 -> x1, Pallas kernels: 170 us -> 172 us  [front(): pl.pallas_call(front_kernel, out_shape=[jax.ShapeDtypeStruct((count, rows...]
  transfers between devices with their start and end apart: 1 -> 0, of which waited for: 0 -> 0; matrix products, arithmetic and copies ran while one was open for 10% -> 0% of each run, Pallas kernels for 13% -> 0%
where the time goes in v5:
time: 664 us; the launch traced here: 655 us
  Pallas kernels  611 us (92%)
  other arithmetic  25.8 us (4%)
  local copies, waits for them, and re-layouts  13 us (2%)
    pallas_call x1, Pallas kernels, front(): pl.pallas_call(front_kernel, out_shape=[jax.ShapeDtypeStruct((count, rows...  172 us
    pallas_call x1, Pallas kernels, experts_gathered(): pl.pallas_call(experts_kernel, out_shape=[array(experts, tokens, wide), a...  133 us
    pallas_call x1, Pallas kernels, back(): pl.pallas_call(back_kernel, out_shape=[jax.ShapeDtypeStruct((length // ro...  120 us
    pallas_call x1, Pallas kernels, sum_all(): pl.pallas_call(sum_all_kernel, out_shape=[jax.ShapeDtypeStruct((rows, wid...  94.4 us
    pallas_call x1, Pallas kernels, leave(): pl.pallas_call(leave_kernel, out_shape=[jax.ShapeDtypeStruct((rows, width...  91.8 us

profile of v5, /device:TPU:16, one launch (start us, length us, event | category | flops | bytes accessed | tf_op | source)
XLA Modules:
  0.0 654.6 jit_solution(5768763392994305507)
XLA Ops:
  0.7 1.3 fusion.1
  2.0 0.8 copy.129
  2.8 0.9 fusion.26
  3.7 0.1 fusion.29
  3.8 0.1 fusion.28
  4.0 1.0 fusion.3.own
  5.3 0.7 copy-done.9
  6.1 2.0 fusion.9
  8.1 1.3 pad_maximum_fusion.2
  9.4 172.0 %front.1 = (bf16[8,128,2048]{2,1,0:T(8,128)(2,1)}, bf16[32,64,1408]{2,1,0:T(8,128)(2,1)}, bf16[32,128,2048]{2,1,0:T(8,128)(2,1)}, bf16[1024,512]{1,0:T(8,128)(2,...) custom-call(bf16[128,2048]{1,0:T(8,128)(2,1)} %fusion.3.own, ...), custom_call_target="tpu_custom_call" | custom-call | tf_op jit(solution)/shard_map/front/pallas_call | solution.py:1939
  181.4 1.3 multiply_reduce_fusion.2
  182.7 1.3 multiply_convert_fusion
  184.0 1.4 fusion.12
  185.5 0.1 convolution_multiply_fusion
  185.6 0.1 copy.114
  185.8 0.1 copy.113
  185.9 0.1 copy.112
  186.0 0.1 fusion.19
  186.1 0.9 pad_maximum_fusion.1.own
  187.0 132.8 %experts.1 = (bf16[32,128,2176]{2,1,0:T(8,128)(2,1)}, bf16[32,128,2048]{2,1,0:T(8,128)(2,1)}, bf16[32,128,2176]{2,1,0:T(8,128)(2,1)}, bf16[2048,2048]{1,0:T(8,12...) custom-call(bf16[128,2176]{1,0:T(8,128)(2,1)} %pad_maximum_fusion.1.own, ...), custom_call_target="tpu_custom_call" | custom-call | tf_op jit(solution)/shard_map/experts/pallas_call | solution.py:1254
  319.8 94.4 %sum_all.1 = (bf16[128,2176]{1,0:T(8,128)(2,1)}, bf16[8,2,128,2048]{3,2,1,0:T(8,128)(2,1)}) custom-call(bf16[32,128,2176]{2,1,0:T(8,128)(2,1)} %get-tuple-element.41.part, bf16[8,2,2,128,2048]{4,3,2,1,0:T(8,128)(2,1)} %bitcast.123), custom_call_target="tpu_custom_call" | custom-call | tf_op jit(solution)/shard_map/sum_all/pallas_call | solution.py:766
  414.2 1.2 convert_element_type.71
  415.7 0.1 copy.116
  415.8 1.7 multiply_reduce_fusion
  417.5 0.7 pad.19.gains
  418.2 1.4 fusion.24
  419.6 0.8 fusion.5.own
  420.5 120.1 %back.1 = (bf16[8,128,2048]{2,1,0:T(8,128)(2,1)}, bf16[2048,1408]{1,0:T(8,128)(2,1)}, f32[8,2048]{1,0:T(8,128)}, bf16[128,2048]{1,0:T(8,128)(2,1)}) custom-call(bf16[128,2176]{1,0:T(8,128)(2,1)} %fusion.5.own, bf16[16,128,2048]{2,1,0:T(8,128)(2,1)} %bitcast.124, bf16[8,4,128,2176]{3,2,1,0:T(8,128)(2,1)} %bitcast.122, bf16[2048,1408]{1,0:T(8,128)(2,1)} %bitcast.127, ...), custom_call_target="tpu_custom_call" | custom-call | tf_op jit(solution)/shard_map/back/pallas_call | solution.py:1602
  540.6 91.8 %leave.1 = (bf16[128,2048]{1,0:T(8,128)(2,1)}, bf16[8,64,1408]{2,1,0:T(8,128)(2,1)}, bf16[2048,1536]{1,0:T(8,128)(2,1)}, bf16[768,2048]{1,0:T(8,128)(2,1)}) custom-call(bf16[8,128,2048]{2,1,0:T(8,128)(2,1)} %get-tuple-element.54.part, bf16[8,2,2,64,1408]{4,3,2,1,0:T(8,128)(2,1)} %bitcast.131, bf16[2048,2048]{1,0:T(8,128)(2,1)} %get-tuple-element.56.rows_in, ...), custom_call_target="tpu_custom_call" | custom-call | tf_op jit(solution)/shard_map/leave/pallas_call | solution.py:956
  632.4 1.0 fusion.6
  633.4 1.2 slice_bitcast_fusion.2
  634.6 1.5 fusion.27
  636.1 0.2 convert_bitcast_fusion
  636.4 0.9 copy.120
  637.3 1.1 slice_bitcast_fusion
  638.5 1.1 copy.133
  639.6 0.1 slice-done
  639.7 0.3 reshape.200
  639.9 0.4 reduce_sum.131
  640.3 0.2 copy.118
  640.5 0.1 reshape.201
  640.6 0.2 copy-done.4
  640.9 0.1 copy.132
  641.0 1.2 pad_maximum_fusion
  642.1 1.1 copy-done.5
  643.2 3.5 bitcast_convert_fusion.1
  646.8 6.6 %bitcast_convert_fusion = f32[1,2048,1536]{2,1,0:T(8,128)} fusion(bf16[2048,1536]{1,0:T(8,128)(2,1)S(1)} %bitcast.130), kind=kLoop, calls=%fused_computation | loop fusion | flops 3145728 | bytes 18874368 | tf_op jit(solution)/shard_map/broadcast_in_dim | solution.py:2137
  653.4 0.8 copy.195
  (75 shorter events, 0.9 us)
Async XLA Ops:
  0.6 3.3 copy-start
  0.7 3.3 copy-start.13
  3.7 1.3 slice-start.3
  4.9 1.0 copy-start.9
  6.1 3.3 copy-start.6
  9.4 173.3 %copy-start.12 = (f32[2048]{0:T(1024)S(1)}, f32[2048]{0:T(1024)}, u32[]{:S(2)}) copy-start(f32[2048]{0:T(1024)} %param.19) | copy-start | bytes 24580
  182.7 2.7 copy-start.14
  414.2 1.6 copy-start.2
  415.8 2.4 copy-start.7
  540.5 91.8 %copy-start.1 = (bf16[1,128,2048]{2,1,0:T(8,128)(2,1)S(1)}, bf16[1,128,2048]{2,1,0:T(8,128)(2,1)}, u32[]{:S(2)}) copy-start(bf16[1,128,2048]{2,1,0:T(8,128)(2,1)} %param.12) | copy-start | bytes 1572868
  540.5 91.8 %copy-start.11 = (bf16[128,2048]{1,0:T(8,128)(2,1)S(1)}, bf16[128,2048]{1,0:T(8,128)(2,1)}, u32[]{:S(2)}) copy-start(bf16[128,2048]{1,0:T(8,128)(2,1)} %get-tuple-element.53) | copy-start | bytes 1572868
  632.4 3.8 copy-start.8
  636.4 2.1 copy-start.3
  638.5 1.2 slice-start
  639.6 1.2 copy-start.4
  640.9 2.4 copy-start.5
  641.0 5.8 slice-start.1
  643.2 3.6 slice-start.2
  646.8 6.6 %copy-start.10 = (bf16[128,2048]{1,0:T(8,128)(2,1)S(1)}, bf16[128,2048]{1,0:T(8,128)(2,1)}, u32[]{:S(2)}) copy-start(bf16[128,2048]{1,0:T(8,128)(2,1)} %get-tuple-element.60) | copy-start | bytes 1572868

commit v6 on v5

--- a/solution.py
+++ b/solution.py
@@ -3,6 +3,7 @@
 
 import jax
 import jax.numpy as jnp
+import numpy as np
 from jax import lax
 from jax.experimental import pallas as pl
 from jax.experimental.pallas import tpu as pltpu
@@ -627,15 +628,7 @@
                     part.at[p.block(zz, xx, yy, c)], held.at[q * 4 + j], ls.at[q, j]
                 ).start()
 
-    chunk = 16
-
-    def add(target, source, count):
-        @pl.loop(0, count // chunk)
-        def _(i):
-            at = pl.ds(pl.multiple_of(i * chunk, chunk), chunk)
-            target[at, :] = (
-                target[at, :].astype(jnp.float32) + source[at, :].astype(jnp.float32)
-            ).astype(target.dtype)
+    add = add_rows
 
     def plane_core(k, js=(3, 1, 2, 0)):
         q = p.far(k)
@@ -699,7 +692,11 @@
     return start, plane_core, plane_turn, plane_end, finish
 
 
-def sum_all_kernel(part, both, out, pair, both_held, both_in, pair_sems, *scratch):
+def sum_all_kernel(
+    part, both, rows_in, d_gate_up, inner, d_expert,
+    out, pair, d_w_in, d_w_down,
+    both_held, both_in, left, product, pair_sems, load_sems, left_sems, product_sems, *scratch,
+):
     p = Place()
     p.greet(("x", "y", "core", "z"))
     start, plane_core, plane_turn, plane_end, finish = sum_all_parts(p, part, *scratch[:7], out, *scratch[7:])
@@ -709,6 +706,44 @@
         for s in (first, first + 1):
             for y in range(2):
                 add_rows(both_held.at[s, y], both_in.at[s, y], rows)
+
+    def right_load(source, i):
+        width = source.shape[3]
+        return pltpu.make_async_copy(source, both_in.at[:, :, :, pl.ds(0, width)], load_sems.at[i])
+
+    def left_load(source, i, slot):
+        cols = pl.ds(pl.multiple_of(i * TILE, TILE), TILE)
+        return pltpu.make_async_copy(source.at[:, cols], left.at[slot], left_sems.at[slot])
+
+    def product_store(target, i, slot):
+        at = pl.ds(pl.multiple_of(i * TILE, TILE), TILE)
+        piece = product.at[slot, :, pl.ds(0, target.shape[1])]
+        return pltpu.make_async_copy(piece, target.at[at], product_sems.at[slot])
+
+    def tiles(source, target, first, last):
+        count, wide = source.shape[1] // TILE, target.shape[1]
+
+        @pl.loop(first, last)
+        def _(i):
+            slot = i % 2
+            left_load(source, i, slot).wait()
+
+            @pl.when(i + 1 < count)
+            def _():
+                left_load(source, i + 1, 1 - slot).start()
+
+            @pl.when(i >= 2)
+            def _():
+                product_store(target, i - 2, slot).wait()
+
+            right = both_in[:, :, :, :wide].reshape(source.shape[0], wide)
+            product[slot, :, :wide] = mxu(left[slot], right, TN).astype(product.dtype)
+            product_store(target, i, slot).start()
+
+    def tiles_end(source, target):
+        count = source.shape[1] // TILE
+        for i in (count - 2, count - 1):
+            product_store(target, i, i % 2).wait()
 
     start()
     send(both.at[:, :, 1 - p.c], both_in, pair_sems.at[0], pair_sems.at[1], p.by_core)
@@ -718,22 +753,33 @@
     plane_turn(0)
     await_bytes(both_held, pair_sems.at[2])
     await_bytes(both_in, pair_sems.at[1])
-    pair_sum(0)
+    for first in (0, 2, 4, 6):
+        pair_sum(first)
+    pltpu.make_async_copy(both_held, pair, pair_sems.at[2]).start()
+    right_load(d_gate_up, 0).start()
+    left_load(rows_in, 0, 0).start()
     plane_core(2)
     plane_turn(1)
     plane_end(0)
-    pair_sum(2)
     plane_core(3)
+    right_load(d_gate_up, 0).wait()
+    tiles(rows_in, d_w_in, 0, 2)
     plane_turn(2)
+    tiles(rows_in, d_w_in, 2, 4)
     plane_end(1)
-    pair_sum(4)
-    pair_sum(6)
-    pltpu.make_async_copy(both_held, pair, pair_sems.at[2]).start()
+    tiles(rows_in, d_w_in, 4, 6)
     plane_turn(3)
+    tiles(rows_in, d_w_in, 6, 8)
+    right_load(d_expert, 1).start()
+    tiles_end(rows_in, d_w_in)
+    left_load(inner, 0, 0).start()
     plane_end(2)
+    right_load(d_expert, 1).wait()
+    tiles(inner, d_w_down, 0, 3)
     plane_end(3)
+    tiles_end(inner, d_w_down)
     finish()
-    await_bytes(both_in, pair_sems.at[0])
+    await_bytes(both_held, pair_sems.at[0])
     pltpu.make_async_copy(both_held, pair, pair_sems.at[2]).wait()
 
 
@@ -758,7 +804,7 @@
     ]
 
 
-def sum_all(part, both, collective_id):
+def sum_all(part, both, rows_in, d_gate_up, inner, d_expert, collective_id):
     blocks, rows, width = part.shape
     both = both.reshape(blocks // 4, 2, 2, rows, -1)
     pair = (blocks // 4, 2, rows, both.shape[4])
@@ -768,29 +814,41 @@
         out_shape=[
             jax.ShapeDtypeStruct((rows, width), part.dtype),
             jax.ShapeDtypeStruct(pair, both.dtype),
+            jax.ShapeDtypeStruct((rows_in.shape[1], d_gate_up.shape[1]), both.dtype),
+            jax.ShapeDtypeStruct((inner.shape[1], d_expert.shape[1]), both.dtype),
         ],
-        in_specs=[anywhere] * 2,
-        out_specs=[pl.BlockSpec(memory_space=pltpu.VMEM), anywhere],
+        in_specs=[anywhere] * 6,
+        out_specs=[pl.BlockSpec(memory_space=pltpu.VMEM)] + [anywhere] * 3,
         scratch_shapes=[
             pltpu.VMEM(pair, both.dtype),
             pltpu.VMEM(pair, both.dtype),
+            pltpu.VMEM((2, rows_in.shape[0], TILE), both.dtype),
+            pltpu.VMEM((2, TILE, d_expert.shape[1]), both.dtype),
             pltpu.SemaphoreType.DMA((3,)),
+            pltpu.SemaphoreType.DMA((2,)),
+            pltpu.SemaphoreType.DMA((2,)),
+            pltpu.SemaphoreType.DMA((2,)),
             *sum_all_scratch(rows, width),
         ],
         compiler_params=pltpu.CompilerParams(
             collective_id=collective_id, has_side_effects=True, vmem_limit_bytes=VMEM_LIMIT
         ),
         name="sum_all",
-    )(part, both)
-
-
-def add_rows(target, source, count, chunk=16):
+    )(
+        part,
+        both,
+        rows_in,
+        d_gate_up.reshape(*pair[:3], -1),
+        inner,
+        d_expert.reshape(*pair[:3], -1),
+    )
+
+
+def add_rows(target, source, count, chunk=32):
     @pl.loop(0, count // chunk)
     def _(i):
         at = pl.ds(pl.multiple_of(i * chunk, chunk), chunk)
-        target[at, :] = (
-            target[at, :].astype(jnp.float32) + source[at, :].astype(jnp.float32)
-        ).astype(target.dtype)
+        target[at, :] = target[at, :] + source[at, :]
 
 
 def seq_peer(p, d):
@@ -805,196 +863,6 @@
         target = {"y": p.by_y, "core": p.by_core}[side]
         pl.semaphore_signal(barrier, inc=1, device_id=target, device_id_type=MESH)
     pl.semaphore_wait(barrier, 7 + len(sides))
-
-
-def leave_kernel(
-    part, cols, rows_in, d_gate_up_hbm, inner, d_expert_hbm, tokens, d_hidden, gain,
-    d_tokens, cols_out, d_w_in, d_w_down,
-    held, x_in, z_in, c_held, c_core, c_y, d_gate_up, d_expert, left, product,
-    ls, ss, rs, zs, zr, cl, cs, cr, ys, yr, ts, tr, load_sems, left_sems, product_sems,
-):
-    p = Place()
-    greet_seq(p)
-    wide_loads = [
-        pltpu.make_async_copy(d_gate_up_hbm, d_gate_up, load_sems.at[0]),
-        pltpu.make_async_copy(d_expert_hbm, d_expert, load_sems.at[1]),
-    ]
-
-    def left_load(source, i, slot):
-        cols = pl.ds(pl.multiple_of(i * TILE, TILE), TILE)
-        return pltpu.make_async_copy(source.at[:, cols], left.at[slot], left_sems.at[slot])
-
-    def product_store(target, i, slot):
-        at = pl.ds(pl.multiple_of(i * TILE, TILE), TILE)
-        piece = product.at[slot, :, pl.ds(0, target.shape[1])]
-        return pltpu.make_async_copy(piece, target.at[at], product_sems.at[slot])
-
-    def tiles(source, right, target, first, last):
-        count = source.shape[1] // TILE
-
-        @pl.loop(first, last)
-        def _(i):
-            slot = i % 2
-            left_load(source, i, slot).wait()
-
-            @pl.when(i + 1 < count)
-            def _():
-                left_load(source, i + 1, 1 - slot).start()
-
-            @pl.when(i >= 2)
-            def _():
-                product_store(target, i - 2, slot).wait()
-
-            result = mxu(left[slot], right[...], TN)
-            product[slot, :, : target.shape[1]] = result.astype(product.dtype)
-            product_store(target, i, slot).start()
-
-    def tiles_end(source, target):
-        count = source.shape[1] // TILE
-        for i in (count - 2, count - 1):
-            product_store(target, i, i % 2).wait()
-
-    rows, width = part.shape[1:]
-    place = p.z * 2 + p.x
-    for turn, side in ((0, 1 - p.y), (1, p.y)):
-        send(cols.at[:, side, 1 - p.c], c_core.at[turn], cs.at[turn], cr.at[turn], p.by_core)
-        pltpu.make_async_copy(cols.at[:, side, p.c], c_held.at[turn], cl.at[turn]).start()
-    for k in range(4):
-        q = p.far(k)
-        send(part.at[q * 2 + 1 - p.x], x_in.at[q], ss.at[q], rs.at[q], p.by_x)
-        pltpu.make_async_copy(part.at[q * 2 + p.x], held.at[q], ls.at[q]).start()
-    piece_rows = c_held.shape[2]
-    for load in wide_loads:
-        load.start()
-    left_load(rows_in, 0, 0).start()
-    order = [(place + d) % 8 for d in range(1, 9)]
-    for turn in range(2):
-        await_bytes(c_held.at[turn], cl.at[turn])
-        await_bytes(c_core.at[turn], cr.at[turn])
-        for i, s in enumerate(order):
-            add_rows(c_held.at[turn, s], c_core.at[turn, s], piece_rows)
-            if turn == 0:
-                send(c_held.at[0, s], c_y.at[s], ys.at[s], yr.at[s], p.by_y)
-
-    def turn_in(i):
-        s = order[i]
-        await_bytes(c_y.at[s], yr.at[s])
-        add_rows(c_held.at[1, s], c_y.at[s], piece_rows)
-        if i < 7:
-            send(c_held.at[1, s], cols_out.at[place], ts.at[i], tr.at[i], seq_peer(p, i + 1))
-        else:
-            pltpu.make_async_copy(c_held.at[1, s], cols_out.at[place], ts.at[7]).start()
-
-    wide_loads[0].wait()
-    per_plane = width // TILE // 4
-    for k in range(4):
-        q = p.far(k)
-        mine = held.at[q]
-        tiles(rows_in, d_gate_up, d_w_in, k * per_plane, (k + 1) * per_plane)
-        await_bytes(mine, ls.at[q])
-        await_bytes(x_in.at[q], rs.at[q])
-        add_rows(mine, x_in.at[q], rows)
-        if k < 3:
-            step = p.toward(k)
-            slot = (1 - step) // 2
-
-            @pl.when(p.inner)
-            def _():
-                await_bytes(z_in.at[slot, q], zr.at[slot, q])
-                add_rows(mine, z_in.at[slot, q], rows)
-
-            send(mine, z_in.at[slot, q], zs.at[k], zr.at[slot, q], p.by_z(step))
-            for i in ((0, 1), (2, 3), (4, 5, 6, 7))[k]:
-                turn_in(i)
-        else:
-            for slot, there in ((0, p.low), (1, p.high)):
-
-                @pl.when(jnp.logical_not(there))
-                def _():
-                    await_bytes(z_in.at[slot, q], zr.at[slot, q])
-                    add_rows(mine, z_in.at[slot, q], rows)
-
-    mine = held.at[p.z]
-    chunk = 16
-
-    @pl.loop(0, rows // chunk)
-    def _(i):
-        at = pl.ds(pl.multiple_of(i * chunk, chunk), chunk)
-        d_out = mine[at, :].astype(jnp.float32)
-        x = tokens[at, :].astype(jnp.float32)
-        scale = lax.rsqrt(jnp.mean(x * x, axis=-1, keepdims=True) + EPS)
-        u = d_out * gain[...]
-        dot = jnp.mean(u * x, axis=-1, keepdims=True)
-        d_x = scale * u - x * (scale * scale * scale * dot)
-        d_tokens[at, :] = (d_hidden[at, :] + d_x).astype(d_tokens.dtype)
-
-    tiles_end(rows_in, d_w_in)
-    left_load(inner, 0, 0).start()
-    wide_loads[1].wait()
-    tiles(inner, d_expert, d_w_down, 0, inner.shape[1] // TILE)
-    tiles_end(inner, d_w_down)
-    piece = c_y.at[0]
-    for i in range(8):
-        if i < 7:
-            await_bytes(piece, tr.at[i])
-        await_bytes(piece, ts.at[i])
-        await_bytes(piece, ys.at[i])
-    for turn in range(2):
-        await_bytes(c_core.at[turn], cs.at[turn])
-    for q in range(4):
-        await_bytes(x_in.at[0], ss.at[q])
-    for k in range(3):
-        await_bytes(x_in.at[0], zs.at[k])
-
-
-def leave(part, cols, rows_in, d_gate_up, inner, d_expert, tokens, d_hidden, gain, collective_id):
-    _, rows, width = part.shape
-    piece_rows, piece_width = cols.shape[3:]
-    dma = pltpu.SemaphoreType.DMA
-    bf16 = jnp.bfloat16
-    anywhere, vmem = pl.BlockSpec(memory_space=pl.ANY), pl.BlockSpec(memory_space=pltpu.VMEM)
-    return pl.pallas_call(
-        leave_kernel,
-        out_shape=[
-            jax.ShapeDtypeStruct((rows, width), bf16),
-            jax.ShapeDtypeStruct((8, piece_rows, piece_width), bf16),
-            jax.ShapeDtypeStruct((rows_in.shape[1], d_gate_up.shape[1]), bf16),
-            jax.ShapeDtypeStruct((inner.shape[1], d_expert.shape[1]), bf16),
-        ],
-        in_specs=[anywhere] * 6 + [vmem] * 3,
-        out_specs=[vmem] + [anywhere] * 3,
-        scratch_shapes=[
-            pltpu.VMEM((4, rows, width), bf16),
-            pltpu.VMEM((4, rows, width), bf16),
-            pltpu.VMEM((2, 4, rows, width), bf16),
-            pltpu.VMEM((2, 8, piece_rows, piece_width), bf16),
-            pltpu.VMEM((2, 8, piece_rows, piece_width), bf16),
-            pltpu.VMEM((8, piece_rows, piece_width), bf16),
-            pltpu.VMEM(d_gate_up.shape, bf16),
-            pltpu.VMEM(d_expert.shape, bf16),
-            pltpu.VMEM((2, rows_in.shape[0], TILE), bf16),
-            pltpu.VMEM((2, TILE, d_expert.shape[1]), bf16),
-            dma((4,)),
-            dma((4,)),
-            dma((4,)),
-            dma((3,)),
-            dma((2, 4)),
-            dma((2,)),
-            dma((2,)),
-            dma((2,)),
-            dma((8,)),
-            dma((8,)),
-            dma((8,)),
-            dma((7,)),
-            dma((2,)),
-            dma((2,)),
-            dma((2,)),
-        ],
-        compiler_params=pltpu.CompilerParams(
-            collective_id=collective_id, has_side_effects=True, vmem_limit_bytes=VMEM_LIMIT
-        ),
-        name="leave",
-    )(part, cols, rows_in, d_gate_up, inner, d_expert, tokens, d_hidden, gain)
 
 
 NT = (((1,), (1,)), ((), ()))
@@ -1302,23 +1170,21 @@
 
 def back_kernel(
     own, pair, rows_all, columns_hbm, normed_hbm, queries, keys, values, attended,
-    q_raw, k_raw, cosine, sine, q_gain, k_gain, attn_gain, gains,
-    d_normed, d_columns, gains_out, mixture,
-    d_attn, columns, normed, d_heads, d_query, d_key, d_value, d_proj, logits, q_sum, k_sum,
-    held, x_in, y_in, z_in, g_send, g_in,
+    q_raw, k_raw, cosine, sine, q_gain, k_gain, attn_gain, gains, tokens, d_hidden,
+    d_tokens, cols_out, gains_out, mixture,
+    d_attn, columns, normed, d_normed, d_heads, d_query, d_key, d_value, d_proj, logits, q_sum, k_sum,
+    held, x_in, y_in, z_in, g_send, g_in, x_two, z_two, c_core, c_y,
     gs, gr, gz, load_sems, local_sem, hs, ys, yr, xs, xr, zs, zr, ts, tr,
+    normed_sems, free, xs2, xr2, zs2, zr2, cs, cr, cys, cyr, as_, ar,
 ):
     p = Place()
     bf16, f32 = jnp.bfloat16, jnp.float32
     columns_z = [p.device((p.z + d) % 4, p.x, p.y, p.c) for d in (1, 2, 3)]
-    barrier = pltpu.get_barrier_semaphore()
-    for target in (p.by_core, p.by_x, p.by_y, *columns_z):
-        pl.semaphore_signal(barrier, inc=1, device_id=target, device_id_type=MESH)
-    pl.semaphore_wait(barrier, 6)
+    greet_seq(p)
     rows, wide = own.shape
     length, head_cols = queries.shape
     heads = head_cols // HEAD_DIMENSION
-    width = normed.shape[1]
+    width = d_normed.shape[2]
     proj_cols = d_proj.shape[1]
     plane_rows = 2 * rows
     score_scale = 1.0 / math.sqrt(HEAD_DIMENSION)
@@ -1357,47 +1223,116 @@
     def at_pair(q, x, y):
         return pair.at[q * 4 + x * 2 + y]
 
+    def sum_send(k):
+        q = p.far(k)
+        for j, x in ((1, 1 - p.x), (0, p.x)):
+            i = q * 2 + j
+            send(at_pair(q, x, 1 - p.y), y_in.at[k % 2 * 2 + j], ys.at[i], yr.at[i], p.by_y)
+
     def sum_start():
+        sum_send(0)
+        sum_send(1)
         for k in range(4):
             q = p.far(k)
             for j, x in ((1, 1 - p.x), (0, p.x)):
-                send(at_pair(q, x, 1 - p.y), y_in.at[q * 2 + j], ys.at[q * 2 + j], yr.at[q * 2 + j], p.by_y)
                 pltpu.make_async_copy(at_pair(q, x, p.y), held.at[q * 2 + j], hs.at[q * 2 + j]).start()
 
     def sum_turn(k):
         q = p.far(k)
         for j in (1, 0):
             slot = q * 2 + j
+            landed = y_in.at[k % 2 * 2 + j]
             await_bytes(held.at[slot], hs.at[slot])
-            await_bytes(y_in.at[slot], yr.at[slot])
-            add_rows(held.at[slot], y_in.at[slot], rows)
+            await_bytes(landed, yr.at[slot])
+            add_rows(held.at[slot], landed, rows)
             if j == 1:
                 send(held.at[slot], x_in.at[q], xs.at[q], xr.at[q], p.by_x)
+        if k < 2:
+            pl.semaphore_signal(free, inc=1, device_id=p.by_y, device_id_type=MESH)
+            pl.semaphore_wait(free, 1)
+            sum_send(k + 2)
+
+    def line_sum(k, mine, landed, sends, arrivals):
+        q = p.far(k)
+        if k < 3:
+            step = p.toward(k)
+            slot, hops = (1 - step) // 2, (q - p.z) * step
+
+            @pl.when(p.inner)
+            def _():
+                await_bytes(landed.at[slot, hops], arrivals.at[slot, hops])
+                add_rows(mine, landed.at[slot, hops], rows)
+
+            send(mine, landed.at[slot, hops - 1], sends.at[k], arrivals.at[slot, hops - 1], p.by_z(step))
+        else:
+            for slot, there in ((0, p.low), (1, p.high)):
+
+                @pl.when(jnp.logical_not(there))
+                def _():
+                    await_bytes(landed.at[slot, 0], arrivals.at[slot, 0])
+                    add_rows(mine, landed.at[slot, 0], rows)
 
     def sum_end(k):
         q = p.far(k)
         mine = held.at[q * 2]
         await_bytes(x_in.at[q], xr.at[q])
         add_rows(mine, x_in.at[q], rows)
-        if k < 3:
-            step = p.toward(k)
-            slot = (1 - step) // 2
-
-            @pl.when(p.inner)
-            def _():
-                await_bytes(z_in.at[slot, q], zr.at[slot, q])
-                add_rows(mine, z_in.at[slot, q], rows)
-
-            send(mine, z_in.at[slot, q], zs.at[k], zr.at[slot, q], p.by_z(step))
-        else:
-            for slot, there in ((0, p.low), (1, p.high)):
-
-                @pl.when(jnp.logical_not(there))
-                def _():
-                    await_bytes(z_in.at[slot, q], zr.at[slot, q])
-                    add_rows(mine, z_in.at[slot, q], rows)
-
+        line_sum(k, mine, z_in, zs, zr)
+        if k == 3:
             mixture[...] = mine[...]
+
+    def two_start(*steps):
+        for k in steps:
+            q = p.far(k)
+            send(d_normed.at[q * 2 + 1 - p.x], x_two.at[q], xs2.at[q], xr2.at[q], p.by_x)
+
+    def two_end(k):
+        q = p.far(k)
+        mine = d_normed.at[q * 2 + p.x]
+        await_bytes(x_two.at[q], xr2.at[q])
+        add_rows(mine, x_two.at[q], rows)
+        line_sum(k, mine, z_two, zs2, zr2)
+
+    piece_rows = c_y.shape[1]
+    order = [(place + d) % 8 for d in range(1, 9)]
+
+    def cols_start():
+        for turn, side in ((0, 1 - p.y), (1, p.y)):
+            send(columns.at[:, side, 1 - p.c], c_core.at[turn], cs.at[turn], cr.at[turn], p.by_core)
+
+    def cols_core():
+        for turn, side in ((0, 1 - p.y), (1, p.y)):
+            await_bytes(c_core.at[turn], cr.at[turn])
+            for s in order:
+                add_rows(columns.at[s, side, p.c], c_core.at[turn, s], piece_rows)
+                if turn == 0:
+                    send(columns.at[s, side, p.c], c_y.at[s], cys.at[s], cyr.at[s], p.by_y)
+
+    def cols_turn(*steps):
+        for i in steps:
+            s = order[i]
+            mine = columns.at[s, p.y, p.c]
+            await_bytes(c_y.at[s], cyr.at[s])
+            add_rows(mine, c_y.at[s], piece_rows)
+            if i < 7:
+                send(mine, cols_out.at[place], as_.at[i], ar.at[i], seq_peer(p, i + 1))
+            else:
+                pltpu.make_async_copy(mine, cols_out.at[place], as_.at[7]).start()
+
+    def norm_back():
+        mine = d_normed.at[p.z * 2 + p.x]
+        chunk = 16
+
+        @pl.loop(0, rows // chunk)
+        def _(i):
+            at = pl.ds(pl.multiple_of(i * chunk, chunk), chunk)
+            d_out = mine[at, :].astype(f32)
+            x = tokens[at, :].astype(f32)
+            scale = lax.rsqrt(jnp.mean(x * x, axis=-1, keepdims=True) + EPS)
+            u = d_out * attn_gain[...]
+            dot = jnp.mean(u * x, axis=-1, keepdims=True)
+            d_x = scale * u - x * (scale * scale * scale * dot)
+            d_tokens[at, :] = (d_hidden[at, :] + d_x).astype(d_tokens.dtype)
 
     def attention(q):
         row_start = pl.multiple_of(q * plane_rows, plane_rows)
@@ -1408,7 +1343,8 @@
             cols = pl.ds(pl.multiple_of(n * TILE, TILE), TILE)
             grad = d_attn[pl.ds(q * 2, 2), :, :width].reshape(plane_rows, width)
             weight_cols = pl.ds(pl.multiple_of(proj_cols + n * TILE, TILE), TILE)
-            d_heads[at, cols] = mxu(grad, columns[:, weight_cols]).astype(bf16)
+            weight = columns[..., weight_cols].reshape(width, TILE)
+            d_heads[at, cols] = mxu(grad, weight).astype(bf16)
 
         def block(count):
             key, value = keys[:count], values[:count]
@@ -1476,14 +1412,28 @@
             k_sum[...], axis=0, keepdims=True
         )
 
+    def normed_load(n, slot):
+        cols = pl.ds(pl.multiple_of(n * TILE, TILE), TILE)
+        return pltpu.make_async_copy(normed_hbm.at[:, cols], normed.at[slot], normed_sems.at[slot])
+
     def normed_grads():
         @pl.loop(0, width // TILE)
         def _(n):
             cols = pl.ds(pl.multiple_of(n * TILE, TILE), TILE)
-            part = mxu(d_proj[...], columns[cols, :proj_cols], NT)
+            slot = n % 2
+            normed_load(n, slot).wait()
+
+            @pl.when(n + 1 < width // TILE)
+            def _():
+                normed_load(n + 1, 1 - slot).start()
+
+            weight = columns[n, :, :, :, :proj_cols].reshape(TILE, proj_cols)
+            part = mxu(d_proj[...], weight, NT)
             d_normed[:, :, cols] = part.astype(bf16).reshape(length // rows, rows, TILE)
-            total = jnp.sum(part * normed[:, cols].astype(f32), axis=0, keepdims=True)
+            total = jnp.sum(part * normed[slot].astype(f32), axis=0, keepdims=True)
             g_send[0, 0:1, cols] = total / attn_gain[:, cols]
+            grad = mxu(normed[slot], d_proj[...], TN).astype(bf16)
+            columns[n, :, :, :, :proj_cols] = grad.reshape(2, 2, -1, proj_cols)
 
     def gains_pass(t, target):
         send(g_send.at[t], g_in.at[t], ts.at[t], tr.at[t], target)
@@ -1502,21 +1452,21 @@
             await_bytes(g_in.at[0], tr.at[2 + d])
         g_send[3] = g_in[2] + g_in[3] + g_in[4] + g_in[5]
 
-    def column_grads(source, value, first, count):
+    def column_grads(value, first, count):
         @pl.loop(0, width // TILE)
         def _(n):
             cols = pl.ds(pl.multiple_of(n * TILE, TILE), TILE)
-            part = source[..., cols].reshape(length, TILE)
-            d_columns[cols, first : first + count] = mxu(part, value[...], TN).astype(bf16)
+            part = d_attn[:, :, cols].reshape(length, TILE)
+            grad = mxu(part, value[...], TN).astype(bf16)
+            columns[n, :, :, :, first : first + count] = grad.reshape(2, 2, -1, count)
 
     loads = [
         pltpu.make_async_copy(columns_hbm, columns, load_sems.at[0]),
-        pltpu.make_async_copy(normed_hbm, normed, load_sems.at[1]),
-        pltpu.make_async_copy(rows_all.at[:, shard], d_attn, load_sems.at[2]),
+        pltpu.make_async_copy(rows_all.at[:, shard], d_attn, load_sems.at[1]),
     ]
     gather_out(0)
     loads[0].start()
-    loads[1].start()
+    normed_load(0, 0).start()
     sum_start()
     d_key[...] = jnp.zeros_like(d_key)
     d_value[...] = jnp.zeros_like(d_value)
@@ -1537,25 +1487,18 @@
     attention(p.near(3))
     raw_grads()
     sum_end(1)
-    loads[1].wait()
     normed_grads()
     gains_pass(0, p.by_core)
-    column_grads(normed, d_proj, 0, proj_cols)
+    column_grads(attended, proj_cols, head_cols)
     gains_take(0)
     gains_pass(1, p.by_x)
-    sum_turn(2)
-    gains_take(1)
-    gains_z_pass()
-    column_grads(d_attn.at[:, :, pl.ds(0, width)], attended, proj_cols, head_cols)
+    two_start(0, 1)
     line = lax.broadcasted_iota(jnp.int32, (128, 128), 0)
     lane = lax.broadcasted_iota(jnp.int32, (128, 128), 1)
     router_cols = rows_all.shape[0] * rows_all.shape[1] // 8
     mine = (line == lane + place * router_cols) & (lane < router_cols)
     select = jnp.where(mine, 1.0, 0.0).astype(bf16)
     logits[...] = mxu(d_attn[:, :, width:].reshape(length, 128), select).astype(bf16)
-    sum_end(2)
-    gains_z_take()
-    send(g_send.at[3], g_in.at[6], ts.at[5], tr.at[5], p.by_y)
     for q in range(4):
         await_bytes(own, gs.at[q])
     for there, slot in ((p.high, 0), (p.low, 1)):
@@ -1570,10 +1513,27 @@
         def _():
             await_bytes(own, gz.at[p.near(k), 0])
 
-    loads[2].start()
-    loads[2].wait()
-    column_grads(d_attn.at[:, :, pl.ds(0, width)], logits, proj_cols + head_cols, 128)
+    loads[1].start()
+    loads[1].wait()
+    column_grads(logits, proj_cols + head_cols, 128)
+    cols_start()
+    gains_take(1)
+    gains_z_pass()
+    sum_turn(2)
+    two_start(2, 3)
+    cols_core()
+    two_end(0)
     sum_turn(3)
+    gains_z_take()
+    send(g_send.at[3], g_in.at[6], ts.at[5], tr.at[5], p.by_y)
+    two_end(1)
+    cols_turn(0, 1)
+    sum_end(2)
+    cols_turn(2, 3, 4, 5)
+    two_end(2)
+    cols_turn(6, 7)
+    two_end(3)
+    norm_back()
     sum_end(3)
     await_bytes(g_in.at[6], tr.at[5])
     gains_out[...] = g_send[3] + g_in[6]
@@ -1586,15 +1546,27 @@
         await_bytes(piece, xs.at[q])
     for k in range(3):
         await_bytes(piece, zs.at[k])
+        await_bytes(piece, zs2.at[k])
+    for q in range(4):
+        await_bytes(piece, xs2.at[q])
+    for turn in range(2):
+        await_bytes(c_core.at[turn], cs.at[turn])
+    for i in range(8):
+        if i < 7:
+            await_bytes(c_y.at[0], ar.at[i])
+        await_bytes(c_y.at[0], as_.at[i])
+        await_bytes(c_y.at[0], cys.at[i])
 
 
 def back(
     own, pair, rows_all, columns, normed, queries, keys, values, attended,
-    q_raw, k_raw, cosine, sine, q_gain, k_gain, attn_gain, gains, collective_id,
+    q_raw, k_raw, cosine, sine, q_gain, k_gain, attn_gain, gains, tokens, d_hidden,
+    collective_id,
 ):
     rows, wide = own.shape
     length, head_cols = queries.shape
     width = normed.shape[1]
+    piece_rows, piece_width = columns.shape[3:]
     proj_cols = head_cols + 2 * HEAD_DIMENSION
     dma = pltpu.SemaphoreType.DMA
     bf16, f32 = jnp.bfloat16, jnp.float32
@@ -1602,17 +1574,18 @@
     return pl.pallas_call(
         back_kernel,
         out_shape=[
-            jax.ShapeDtypeStruct((length // rows, rows, width), bf16),
-            jax.ShapeDtypeStruct(columns.shape, bf16),
+            jax.ShapeDtypeStruct((rows, width), bf16),
+            jax.ShapeDtypeStruct((8, piece_rows, piece_width), bf16),
             jax.ShapeDtypeStruct(gains.shape, f32),
             jax.ShapeDtypeStruct((rows, width), bf16),
         ],
-        in_specs=[anywhere] * 5 + [vmem] * 12,
-        out_specs=[vmem] * 4,
+        in_specs=[anywhere] * 5 + [vmem] * 14,
+        out_specs=[vmem, anywhere, vmem, vmem],
         scratch_shapes=[
             pltpu.VMEM((8, rows, wide), bf16),
             pltpu.VMEM(columns.shape, bf16),
-            pltpu.VMEM((length, width), bf16),
+            pltpu.VMEM((2, length, TILE), bf16),
+            pltpu.VMEM((length // rows, rows, width), bf16),
             pltpu.VMEM((length, head_cols), bf16),
             pltpu.VMEM((length, head_cols), f32),
             pltpu.VMEM((length, HEAD_DIMENSION), f32),
@@ -1623,14 +1596,18 @@
             pltpu.VMEM((8, HEAD_DIMENSION), f32),
             pltpu.VMEM((8, rows, width), bf16),
             pltpu.VMEM((4, rows, width), bf16),
-            pltpu.VMEM((8, rows, width), bf16),
-            pltpu.VMEM((2, 4, rows, width), bf16),
+            pltpu.VMEM((4, rows, width), bf16),
+            pltpu.VMEM((2, 3, rows, width), bf16),
             pltpu.VMEM((4, *gains.shape), f32),
             pltpu.VMEM((7, *gains.shape), f32),
+            pltpu.VMEM((4, rows, width), bf16),
+            pltpu.VMEM((2, 3, rows, width), bf16),
+            pltpu.VMEM((2, 8, piece_rows, piece_width), bf16),
+            pltpu.VMEM((8, piece_rows, piece_width), bf16),
             dma((4,)),
             dma((4, 2)),
             dma((4, 2)),
-            dma((3,)),
+            dma((2,)),
             dma,
             dma((8,)),
             dma((8,)),
@@ -1638,9 +1615,21 @@
             dma((4,)),
             dma((4,)),
             dma((3,)),
-            dma((2, 4)),
+            dma((2, 3)),
             dma((6,)),
             dma((6,)),
+            dma((2,)),
+            pltpu.SemaphoreType.REGULAR,
+            dma((4,)),
+            dma((4,)),
+            dma((3,)),
+            dma((2, 3)),
+            dma((2,)),
+            dma((2,)),
+            dma((8,)),
+            dma((8,)),
+            dma((8,)),
+            dma((7,)),
         ],
         compiler_params=pltpu.CompilerParams(
             collective_id=collective_id, has_side_effects=True, vmem_limit_bytes=VMEM_LIMIT
@@ -1648,7 +1637,7 @@
         name="back",
     )(
         own, pair, rows_all, columns, normed, queries, keys, values, attended,
-        q_raw, k_raw, cosine, sine, q_gain, k_gain, attn_gain, gains,
+        q_raw, k_raw, cosine, sine, q_gain, k_gain, attn_gain, gains, tokens, d_hidden,
     )
 
 
@@ -1656,9 +1645,9 @@
 
 
 def front_kernel(
-    own, pieces, cot, cosine, sine, q_gain, k_gain,
+    tokens, pieces, cot, cosine, sine, q_gain, k_gain, attn_gain,
     normed_out, columns_out, cot_all, queries, keys, values, attended, q_raw, k_raw, attn_out,
-    normed, columns, part, x_in, z_in,
+    own, normed, columns, part, x_in, z_in,
     ss, rs, zs, cs, cr, ys, yr, ks, kr, local_sems, gs, gr, gz, xs, xr, us, ur,
 ):
     p = Place()
@@ -1672,6 +1661,10 @@
     proj_cols = head_cols + 2 * HEAD_DIMENSION
     plane_rows = 2 * rows
     score_scale = 1.0 / math.sqrt(HEAD_DIMENSION)
+
+    x = tokens[...].astype(jnp.float32)
+    scale = lax.rsqrt(jnp.mean(x * x, axis=-1, keepdims=True) + EPS)
+    own[...] = (x * scale * attn_gain[...]).astype(bf16)
 
     def rows_at(q, x):
         return normed.at[q * 2 + x]
@@ -1929,10 +1922,10 @@
     pltpu.make_async_copy(columns, columns_out, local_sems.at[1]).wait()
 
 
-def front(own, pieces, cot, cosine, sine, q_gain, k_gain, head_cols, collective_id):
+def front(tokens, pieces, cot, cosine, sine, q_gain, k_gain, attn_gain, head_cols, collective_id):
     dma = pltpu.SemaphoreType.DMA
     bf16, f32 = jnp.bfloat16, jnp.float32
-    rows, width = own.shape
+    rows, width = tokens.shape
     count, piece_rows, piece_width = pieces.shape
     length = count * rows
     anywhere, vmem = pl.BlockSpec(memory_space=pl.ANY), pl.BlockSpec(memory_space=pltpu.VMEM)
@@ -1950,9 +1943,10 @@
             jax.ShapeDtypeStruct((length, HEAD_DIMENSION), f32),
             jax.ShapeDtypeStruct((rows, width), bf16),
         ],
-        in_specs=[anywhere] * 3 + [vmem] * 4,
+        in_specs=[vmem] + [anywhere] * 2 + [vmem] * 5,
         out_specs=[anywhere] * 3 + [vmem] * 7,
         scratch_shapes=[
+            pltpu.VMEM((rows, width), bf16),
             pltpu.VMEM((count, rows, width), bf16),
             pltpu.VMEM((count * 4, piece_rows, piece_width), bf16),
             pltpu.VMEM((count, rows, width), bf16),
@@ -1980,7 +1974,7 @@
             collective_id=collective_id, has_side_effects=True, vmem_limit_bytes=VMEM_LIMIT
         ),
         name="front",
-    )(own, pieces, cot, cosine, sine, q_gain, k_gain)
+    )(tokens, pieces, cot, cosine, sine, q_gain, k_gain, attn_gain)
 
 
 def head_columns(weight, group_index):
@@ -2039,15 +2033,24 @@
         axis=2,
     )
     resid_in = tokens[0].astype(f32)
-    normed_one = rms_scale(resid_in, attn_gain).astype(bf16)
     half_dim = HEAD_DIMENSION // 2
-    frequency = ROPE_BASE ** (-2.0 * jnp.arange(half_dim, dtype=f32) / HEAD_DIMENSION)
-    angles = jnp.arange(length, dtype=f32)[:, None] * frequency[None, :]
-    cosine, sine = jnp.cos(angles), jnp.sin(angles)
-    cosine = jnp.concatenate([cosine, cosine], axis=1)
-    sine = jnp.concatenate([sine, -sine], axis=1)
+    exponents = -2.0 * np.arange(half_dim, dtype=np.float32) / HEAD_DIMENSION
+    frequency = np.float32(ROPE_BASE) ** exponents.astype(np.float32)
+    angles = np.arange(length, dtype=np.float32)[:, None] * frequency[None, :]
+    cosine, sine = np.cos(angles), np.sin(angles)
+    cosine = jnp.asarray(np.concatenate([cosine, cosine], axis=1), f32)
+    sine = jnp.asarray(np.concatenate([sine, -sine], axis=1), f32)
     normed_all, columns, cot_all, queries, keys, values, attended, q_raw, k_raw, attn_out = front(
-        normed_one, pieces, cotangent[0], cosine, sine, q_gain[None], k_gain[None], head_cols, 1
+        tokens[0],
+        pieces,
+        cotangent[0],
+        cosine,
+        sine,
+        q_gain[None],
+        k_gain[None],
+        attn_gain[None],
+        head_cols,
+        1,
     )
     normed_all = normed_all.reshape(length, width)
     columns = columns.reshape(width, -1)
@@ -2082,7 +2085,10 @@
         capacity,
         3,
     )
-    d_back, out_pair = sum_all(d_part, out_part, 5)
+    d_back, out_pair, d_w_in, d_w_down = sum_all(
+        d_part, out_part, rows_in, d_gate_up, inner_act, d_expert, 5
+    )
+    d_w_in, d_w_down = d_w_in.astype(f32)[None], d_w_down.astype(f32)[None]
     d_back = d_back.astype(f32)
 
     d_gate_dense = d_back[:, width : width + experts] + d_back[:, width + experts : width + 2 * experts]
@@ -2100,11 +2106,11 @@
 
     d_send = jnp.concatenate([d_attn, jnp.pad(d_logits, ((0, 0), (0, 128 - experts)))], axis=1)
     gains = jnp.pad(d_ffn_gain[None], ((1, 6), (0, 0)))
-    d_normed_part, d_columns, gains, mixture = back(
+    d_tokens, d_pieces, gains, mixture = back(
         d_send,
         out_pair.reshape(2 * seq_size, rows, width),
         rows_all.reshape(seq_size, shard_size, rows, -1),
-        columns,
+        columns.reshape(seq_size, 2, shard_size // 2, weight_rows, all_cols + spare_cols),
         normed_all,
         queries,
         keys,
@@ -2118,23 +2124,12 @@
         k_gain[None],
         attn_gain[None],
         gains,
+        tokens[0],
+        d_hidden,
         6,
     )
     output = (hidden + mixture.astype(f32)).astype(bf16)
     router_cols = experts // seq_size
-    d_tokens, d_pieces, d_w_in, d_w_down = leave(
-        d_normed_part,
-        d_columns.reshape(seq_size, 2, shard_size // 2, weight_rows, all_cols + spare_cols),
-        rows_in,
-        d_gate_up,
-        inner_act,
-        d_expert,
-        tokens[0],
-        d_hidden,
-        attn_gain[None],
-        7,
-    )
-    d_w_in, d_w_down = d_w_in.astype(f32)[None], d_w_down.astype(f32)[None]
     d_tokens = d_tokens[None]
     d_pieces = d_pieces.astype(f32).transpose(1, 0, 2)
     per_group = seq_size // KEY_VALUE_HEADS

time: 664 us -> 621 us (0.935)
  Pallas kernels: 611 us -> 573 us
    pallas_call x2 -> x1, Pallas kernels: 212 us -> 182 us  [back(): pl.pallas_call(back_kernel, out_shape=[jax.ShapeDtypeStruct((rows, width)...]
    pallas_call x1, Pallas kernels: 133 us -> 124 us  [experts_gathered(): pl.pallas_call(experts_kernel, out_shape=[array(experts, tokens, wide), a...]
where the time goes in v6:
time: 621 us; the launch traced here: 613 us
  Pallas kernels  573 us (92%)
  other arithmetic  21.4 us (3%)
  local copies, waits for them, and re-layouts  14.1 us (2%)
    pallas_call x1, Pallas kernels, back(): pl.pallas_call(back_kernel, out_shape=[jax.ShapeDtypeStruct((rows, width)...  182 us
    pallas_call x1, Pallas kernels, front(): pl.pallas_call(front_kernel, out_shape=[jax.ShapeDtypeStruct((count, rows...  172 us
    pallas_call x1, Pallas kernels, experts_gathered(): pl.pallas_call(experts_kernel, out_shape=[array(experts, tokens, wide), a...  124 us
    pallas_call x1, Pallas kernels, sum_all(): pl.pallas_call(sum_all_kernel, out_shape=[jax.ShapeDtypeStruct((rows, wid...  95.5 us

profile of v6, /device:TPU:16, one launch (start us, length us, event | category | flops | bytes accessed | tf_op | source)
XLA Modules:
  0.0 613.5 jit_solution(16867246737484410767)
XLA Ops:
  0.6 0.0 slice-start.3
  0.7 0.8 copy.131
  1.5 0.9 fusion.20
  2.5 0.1 fusion.23
  2.6 0.1 fusion.22
  3.0 0.7 copy-done.9
  3.8 0.0 copy-start.6
  3.8 1.1 copy-done.6
  4.9 171.7 %front.1 = (bf16[8,128,2048]{2,1,0:T(8,128)(2,1)}, bf16[32,64,1408]{2,1,0:T(8,128)(2,1)}, bf16[32,128,2048]{2,1,0:T(8,128)(2,1)}, bf16[1024,512]{1,0:T(8,128)(2,...) custom-call(bf16[128,2048]{1,0:T(8,128)(2,1)} %bitcast.121, ...), custom_call_target="tpu_custom_call" | custom-call | tf_op jit(solution)/shard_map/front/pallas_call | solution.py:1932
  176.6 1.3 multiply_reduce_fusion.2
  178.0 1.3 multiply_convert_fusion
  179.2 1.4 fusion.7
  180.7 0.1 convolution_multiply_fusion
  180.9 0.1 copy.116
  181.0 0.1 copy.115
  181.1 0.1 copy.114
  181.2 0.1 fusion.13
  181.3 0.9 pad_maximum_fusion.1.own
  182.2 123.7 %experts.1 = (bf16[32,128,2176]{2,1,0:T(8,128)(2,1)}, bf16[32,128,2048]{2,1,0:T(8,128)(2,1)}, bf16[32,128,2176]{2,1,0:T(8,128)(2,1)}, bf16[2048,2048]{1,0:T(8,12...) custom-call(bf16[128,2176]{1,0:T(8,128)(2,1)} %pad_maximum_fusion.1.own, ...), custom_call_target="tpu_custom_call" | custom-call | tf_op jit(solution)/shard_map/experts/pallas_call | solution.py:1122
  305.9 95.5 %sum_all.1 = (bf16[128,2176]{1,0:T(8,128)(2,1)}, bf16[8,2,128,2048]{3,2,1,0:T(8,128)(2,1)}, bf16[2048,1536]{1,0:T(8,128)(2,1)}, bf16[768,2048]{1,0:T(8,128)(2,1)}) custom-call(bf16[32,128,2176]{2,1,0:T(8,128)(2,1)} %get-tuple-element.39.part, bf16[8,2,2,128,2048]{4,3,2,1,0:T(8,128)(2,1)} %bitcast.124, bf16[2048,2048]{1,0:T(8,128)(2,1)} %get-tuple-element.41.rows_in, ...), custom_call_target="tpu_custom_call" | custom-call | tf_op jit(solution)/shard_map/sum_all/pallas_call | solution.py:812
  401.5 1.2 convert_element_type.67
  402.7 0.1 slice_add_fusion
  402.8 0.1 copy.117
  403.0 0.1 copy.118
  403.1 1.7 multiply_reduce_fusion
  404.8 0.7 pad.19.gains
  405.4 1.4 fusion.18
  406.9 0.8 fusion.2.own
  407.7 182.4 %back.1 = (bf16[128,2048]{1,0:T(8,128)(2,1)}, bf16[8,64,1408]{2,1,0:T(8,128)(2,1)}, f32[8,2048]{1,0:T(8,128)}, bf16[128,2048]{1,0:T(8,128)(2,1)}) custom-call(bf16[128,2176]{1,0:T(8,128)(2,1)} %fusion.2.own, bf16[16,128,2048]{2,1,0:T(8,128)(2,1)} %bitcast.125, bf16[8,4,128,2176]{3,2,1,0:T(8,128)(2,1)} %bitcast.123, bf16[8,2,2,64,1408]{4,3,2,1,0:T(8,128)(2,1)} %bitcast.129, ...), custom_call_target="tpu_custom_call" | custom-call | tf_op jit(solution)/shard_map/back/pallas_call | solution.py:1574
  590.1 2.2 fusion.3
  592.3 1.2 slice_bitcast_fusion.2
  593.5 1.5 fusion.21
  595.0 0.2 convert_bitcast_fusion
  595.3 0.9 copy.122
  596.2 1.1 slice_bitcast_fusion
  597.4 1.1 copy.135
  598.4 0.1 slice-done
  598.5 0.3 reshape.190
  598.8 0.4 reduce_sum.121
  599.2 0.2 copy.120
  599.4 0.1 reshape.191
  599.5 0.2 copy-done.4
  599.8 0.1 copy.134
  599.9 1.2 pad_maximum_fusion
  601.0 1.1 copy-done.5
  602.1 3.5 bitcast_convert_fusion.1
  605.7 6.6 %bitcast_convert_fusion = f32[1,2048,1536]{2,1,0:T(8,128)} fusion(bf16[2048,1536]{1,0:T(8,128)(2,1)S(1)} %bitcast.133), kind=kLoop, calls=%fused_computation | loop fusion | flops 3145728 | bytes 18874368 | tf_op jit(solution)/shard_map/broadcast_in_dim | solution.py:2091
  612.3 0.8 copy.197
  (64 shorter events, 0.7 us)
Async XLA Ops:
  0.6 2.0 slice-start.3
  2.7 1.0 copy-start.9
  3.8 1.1 copy-start.6
  4.9 171.7 %copy-start = (bf16[1,128,2048]{2,1,0:T(8,128)(2,1)S(1)}, bf16[1,128,2048]{2,1,0:T(8,128)(2,1)}, u32[]{:S(2)}) copy-start(bf16[1,128,2048]{2,1,0:T(8,128)(2,1)} %param.14) | copy-start | bytes 1572868
  4.9 173.0 %copy-start.11 = (f32[2048]{0:T(1024)S(1)}, f32[2048]{0:T(1024)}, u32[]{:S(2)}) copy-start(f32[2048]{0:T(1024)} %param.21) | copy-start | bytes 24580
  177.9 2.7 copy-start.12
  401.5 1.6 copy-start.2
  403.1 2.4 copy-start.7
  407.7 182.4 %copy-start.1 = (bf16[1,128,2048]{2,1,0:T(8,128)(2,1)S(1)}, bf16[1,128,2048]{2,1,0:T(8,128)(2,1)}, u32[]{:S(2)}) copy-start(bf16[1,128,2048]{2,1,0:T(8,128)(2,1)} %param.14) | copy-start | bytes 1572868
  590.1 4.9 copy-start.8
  595.3 2.1 copy-start.3
  597.4 1.2 slice-start
  598.5 1.2 copy-start.4
  599.8 2.4 copy-start.5
  599.9 5.8 slice-start.1
  602.1 3.6 slice-start.2
  605.7 6.6 %copy-start.10 = (bf16[128,2048]{1,0:T(8,128)(2,1)S(1)}, bf16[128,2048]{1,0:T(8,128)(2,1)}, u32[]{:S(2)}) copy-start(bf16[128,2048]{1,0:T(8,128)(2,1)} %get-tuple-element.56) | copy-start | bytes 1572868

commit v7 on v6

--- a/solution.py
+++ b/solution.py
@@ -549,15 +549,23 @@
             pltpu.make_async_copy(own, out.at[b], local_sem).start()
         else:
             src = out.at[b]
-            await_bytes(src, rs.at[q, G_Z])
-
-            @pl.when(p.inner)
+
+            @pl.when(jnp.logical_not(p.inner))
             def _():
-                send(src, src, zs.at[q, 0], rs.at[q, G_Z], p.by_z(p.onward(k)))
+                await_bytes(src, rs.at[q, G_Z])
 
         send(src, out.at[b], ss.at[q, G_X], rs.at[q, G_X], p.by_x)
         send(src, out.at[b], ss.at[q, G_Y], rs.at[q, G_Y], p.by_y)
         to_core(q, 0, src)
+
+    def plane_hop(k):
+        q = p.near(k)
+        src = out.at[cols(q)[0]]
+
+        @pl.when(p.inner)
+        def _():
+            await_bytes(src, rs.at[q, G_Z])
+            send(src, src, zs.at[q, 0], rs.at[q, G_Z], p.by_z(p.onward(k)))
 
     def plane_turn(k):
         q = p.near(k)
@@ -578,9 +586,9 @@
         await_bytes(bd.at[pl.ds(half, half)], rs.at[q, G_DX])
         to_core(q, 3)
 
-    def plane_core(k):
+    def plane_core(k, js=(0, 1, 2, 3)):
         q = p.near(k)
-        for j in range(4):
+        for j in js:
             await_bytes(own, rs.at[q, G_C0 + j])
 
     def finish():
@@ -602,7 +610,7 @@
             def _():
                 await_bytes(own, zs.at[p.near(k), 0])
 
-    return plane_out, plane_turn, plane_end, plane_core, finish
+    return plane_out, plane_hop, plane_turn, plane_end, plane_core, finish
 
 
 def sum_all_parts(p, part, held, core_in, x_half, y_half, x_in, y_in, z_in, out, ls, cs, cr, ss, rs, zs, zr):
@@ -693,13 +701,13 @@
 
 
 def sum_all_kernel(
-    part, both, rows_in, d_gate_up, inner, d_expert,
-    out, pair, d_w_in, d_w_down,
-    both_held, both_in, left, product, pair_sems, load_sems, left_sems, product_sems, *scratch,
+    part, both, rows_in, d_gate_up, inner, d_expert, columns, hidden, cot, gates, ffn_gain,
+    out, d_hidden, gains, pair, d_w_in, d_w_down,
+    d_rows, router, router_sem, both_held, both_in, left, product, pair_sems, load_sems, left_sems, product_sems, *scratch,
 ):
     p = Place()
     p.greet(("x", "y", "core", "z"))
-    start, plane_core, plane_turn, plane_end, finish = sum_all_parts(p, part, *scratch[:7], out, *scratch[7:])
+    start, plane_core, plane_turn, plane_end, finish = sum_all_parts(p, part, *scratch[:7], d_rows, *scratch[7:])
     rows = both.shape[3]
 
     def pair_sum(first):
@@ -745,6 +753,9 @@
         for i in (count - 2, count - 1):
             product_store(target, i, i % 2).wait()
 
+    first = columns.shape[2] - 128
+    router_load = pltpu.make_async_copy(columns.at[:, :, pl.ds(first, 128)], router, router_sem)
+    router_load.start()
     start()
     send(both.at[:, :, 1 - p.c], both_in, pair_sems.at[0], pair_sems.at[1], p.by_core)
     pltpu.make_async_copy(both.at[:, :, p.c], both_held, pair_sems.at[2]).start()
@@ -753,13 +764,15 @@
     plane_turn(0)
     await_bytes(both_held, pair_sems.at[2])
     await_bytes(both_in, pair_sems.at[1])
-    for first in (0, 2, 4, 6):
-        pair_sum(first)
+    pair_sum(0)
+    plane_core(2)
+    pair_sum(2)
+    plane_turn(1)
+    pair_sum(4)
+    pair_sum(6)
     pltpu.make_async_copy(both_held, pair, pair_sems.at[2]).start()
     right_load(d_gate_up, 0).start()
     left_load(rows_in, 0, 0).start()
-    plane_core(2)
-    plane_turn(1)
     plane_end(0)
     plane_core(3)
     right_load(d_gate_up, 0).wait()
@@ -777,6 +790,32 @@
     right_load(d_expert, 1).wait()
     tiles(inner, d_w_down, 0, 3)
     plane_end(3)
+    router_load.wait()
+    width = hidden.shape[1]
+    experts = part.shape[0]
+    tail = d_rows[:, width:].astype(jnp.float32)
+    lane = lax.broadcasted_iota(jnp.int32, tail.shape, 1)
+    d_gates = jnp.where(lane < experts, tail + pltpu.roll(tail, 128 - experts, 1), 0.0)
+    gate = gates[...]
+    d_chosen = gate * (d_gates - jnp.sum(gate * d_gates, axis=-1, keepdims=True))
+    out[:, width:] = d_chosen.astype(out.dtype)
+    gains[...] = jnp.zeros_like(gains)
+    chunk = 32
+
+    @pl.loop(0, rows // chunk)
+    def _(i):
+        at = pl.ds(pl.multiple_of(i * chunk, chunk), chunk)
+        routed = mxu(out[at, width:], router[...].reshape(width, 128), NT)
+        d_out = d_rows[at, :width].astype(jnp.float32) + routed
+        x = hidden[at, :]
+        scale = lax.rsqrt(jnp.mean(x * x, axis=-1, keepdims=True) + EPS)
+        u = d_out * ffn_gain[...]
+        dot = jnp.mean(u * x, axis=-1, keepdims=True)
+        grad = cot[at, :].astype(jnp.float32) + scale * u - x * (scale * scale * scale * dot)
+        d_hidden[at, :] = grad
+        out[at, :width] = grad.astype(out.dtype)
+        gains[1:2, :] += jnp.sum(d_out * x * scale, axis=0, keepdims=True)
+
     tiles_end(inner, d_w_down)
     finish()
     await_bytes(both_held, pair_sems.at[0])
@@ -804,22 +843,29 @@
     ]
 
 
-def sum_all(part, both, rows_in, d_gate_up, inner, d_expert, collective_id):
+def sum_all(
+    part, both, rows_in, d_gate_up, inner, d_expert, columns, hidden, cot, gates, ffn_gain, collective_id
+):
     blocks, rows, width = part.shape
     both = both.reshape(blocks // 4, 2, 2, rows, -1)
     pair = (blocks // 4, 2, rows, both.shape[4])
-    anywhere = pl.BlockSpec(memory_space=pl.ANY)
+    anywhere, vmem = pl.BlockSpec(memory_space=pl.ANY), pl.BlockSpec(memory_space=pltpu.VMEM)
     return pl.pallas_call(
         sum_all_kernel,
         out_shape=[
             jax.ShapeDtypeStruct((rows, width), part.dtype),
+            jax.ShapeDtypeStruct(hidden.shape, jnp.float32),
+            jax.ShapeDtypeStruct((8, hidden.shape[1]), jnp.float32),
             jax.ShapeDtypeStruct(pair, both.dtype),
             jax.ShapeDtypeStruct((rows_in.shape[1], d_gate_up.shape[1]), both.dtype),
             jax.ShapeDtypeStruct((inner.shape[1], d_expert.shape[1]), both.dtype),
         ],
-        in_specs=[anywhere] * 6,
-        out_specs=[pl.BlockSpec(memory_space=pltpu.VMEM)] + [anywhere] * 3,
+        in_specs=[anywhere] * 7 + [vmem] * 4,
+        out_specs=[vmem] * 3 + [anywhere] * 3,
         scratch_shapes=[
+            pltpu.VMEM((rows, width), part.dtype),
+            pltpu.VMEM((*columns.shape[:2], 128), part.dtype),
+            pltpu.SemaphoreType.DMA,
             pltpu.VMEM(pair, both.dtype),
             pltpu.VMEM(pair, both.dtype),
             pltpu.VMEM((2, rows_in.shape[0], TILE), both.dtype),
@@ -841,6 +887,11 @@
         d_gate_up.reshape(*pair[:3], -1),
         inner,
         d_expert.reshape(*pair[:3], -1),
+        columns,
+        hidden,
+        cot,
+        gates,
+        ffn_gain,
     )
 
 
@@ -891,7 +942,7 @@
     group = 4
     experts = rows_all.shape[0]
     p.greet(("x", "y", "core", "z"))
-    plane_out, plane_turn, plane_end, plane_core, finish = gather_steps(
+    plane_out, plane_hop, plane_turn, plane_end, plane_core, finish = gather_steps(
         p, own, rows_all, ss, rs, zs, local_sem
     )
 
@@ -912,9 +963,20 @@
 
     def arrived(k):
         plane_core(k)
-        if k == 0:
+        row_load(k).start()
+
+    sides = (p.x, 1 - p.x)
+
+    def side_load(i):
+        at = pl.ds(sides[i] * group, group)
+        source = rows_all.at[pl.ds(p.z * blocks + sides[i] * group, group)]
+        return pltpu.make_async_copy(source, row_buf.at[0, at], load_sems.at[(6, 10)[i]])
+
+    def side_arrived(i):
+        plane_core(0, ((0, 2), (1, 3))[i])
+        if i == 0:
             pltpu.make_async_copy(own, rows_all.at[p.me], local_sem).wait()
-        row_load(k).start()
+        side_load(i).start()
 
     at_slot = {}
 
@@ -943,19 +1005,20 @@
         if k > 0:
             store(k - 1, i, *stores(k - 1)[i]).wait()
 
-    def pick_rows(k):
+    def pick_rows(k, g):
         lane = lax.broadcasted_iota(jnp.int32, (8, 128), 1)
         line = lax.broadcasted_iota(jnp.int32, (8, 128), 0)
         select = jnp.where((lane == line * experts + p.me) & (line < 3), 1.0, 0.0).astype(bf16)
         slot_id = lax.broadcasted_iota(jnp.int32, (capacity, tokens), 0).astype(f32) + 1.0
         rows, cots = row_buf.at[k % 2], cot_buf.at[k % 2]
-        lines = mxu(select, rows[:, :, width:].reshape(blocks * tokens, 128), NT)
-        for j in range(blocks):
-            g, i = j // group, j % group
-            mine = lines[:, j * tokens : (j + 1) * tokens]
+        which = pl.ds(g * group, group)
+        lines = mxu(select, rows[which, :, width:].reshape(group * tokens, 128), NT)
+        for i in range(group):
+            mine = lines[:, i * tokens : (i + 1) * tokens]
             chosen = jnp.where(mine[2:3] == slot_id, 1.0, 0.0)
             gate = jnp.sum(chosen * (mine[0:1] + mine[1:2]), axis=1, keepdims=True)
-            gates[j * capacity : (j + 1) * capacity, :] = jnp.broadcast_to(gate, (capacity, 128))
+            at = pl.ds(pl.multiple_of((g * group + i) * capacity, capacity), capacity)
+            gates[at, :] = jnp.broadcast_to(gate, (capacity, 128))
             lead = [jnp.zeros((capacity, tokens), bf16)] * i
             tail = [jnp.zeros((capacity, tokens), bf16)] * (group - 1 - i)
             pick[g, i * capacity : (i + 1) * capacity, :] = jnp.concatenate(
@@ -966,100 +1029,137 @@
             pick_t[g, i * tokens : (i + 1) * tokens, :] = jnp.concatenate(
                 lead + [chosen.T] + tail, axis=1
             ).astype(bf16)
-        for g in range(blocks // group):
-            at = pl.ds(g * group * capacity, group * capacity)
-            which = pl.ds(g * group, group)
-
-            @pl.loop(0, width // WIDE)
-            def _(n):
-                cols = pl.ds(pl.multiple_of(n * WIDE, WIDE), WIDE)
-                row_tile = rows[which, :, cols].reshape(group * tokens, WIDE)
-                x[at, cols] = mxu(pick[g], row_tile).astype(bf16)
-                cot_tile = cots[which, :, cols].reshape(group * tokens, WIDE)
-                picked = mxu(pick[g], cot_tile)
-                cot[at, cols] = picked.astype(bf16)
-                scale = jnp.concatenate([gates[at, :]] * (WIDE // 128), axis=1)
-                d_expert[at, cols] = (scale * picked).astype(bf16)
-
-    def up(k):
+        at = slots_at(g)
+
+        @pl.loop(0, width // WIDE)
+        def _(n):
+            cols = pl.ds(pl.multiple_of(n * WIDE, WIDE), WIDE)
+            row_tile = rows[which, :, cols].reshape(group * tokens, WIDE)
+            x[at, cols] = mxu(pick[g], row_tile).astype(bf16)
+            cot_tile = cots[which, :, cols].reshape(group * tokens, WIDE)
+            picked = mxu(pick[g], cot_tile)
+            cot[at, cols] = picked.astype(bf16)
+            scale = jnp.concatenate([gates[at, :]] * (WIDE // 128), axis=1)
+            d_expert[at, cols] = (scale * picked).astype(bf16)
+
+    def slots_at(g):
+        if g is None:
+            return pl.ds(0, slots)
+        return pl.ds(pl.multiple_of(g * group * capacity, group * capacity), group * capacity)
+
+    def up(g=None):
         ff = inner.shape[1]
+        at = slots_at(g)
 
         @pl.loop(0, ff // TILE)
         def _(n):
             cols = pl.ds(pl.multiple_of(n * TILE, TILE), TILE)
-            gate = mxu(x[...], w_in[:, cols])
-            raised = mxu(x[...], w_in[:, pl.ds(pl.multiple_of(ff + n * TILE, TILE), TILE)])
+            gate = mxu(x[at, :], w_in[:, cols])
+            raised = mxu(x[at, :], w_in[:, pl.ds(pl.multiple_of(ff + n * TILE, TILE), TILE)])
             sig = jax.nn.sigmoid(gate)
             silu = gate * sig
-            inner[:, cols] = (silu * raised).astype(bf16)
-            by_d_up[:, cols] = silu
-            by_d_gate[:, cols] = raised * sig * (1.0 + gate * (1.0 - sig))
-
-    def d_up(k):
+            inner[at, cols] = (silu * raised).astype(bf16)
+            by_d_up[at, cols] = silu
+            by_d_gate[at, cols] = raised * sig * (1.0 + gate * (1.0 - sig))
+
+    def d_up(g=None):
         ff = inner.shape[1]
+        at = slots_at(g)
 
         @pl.loop(0, ff // TILE)
         def _(n):
             cols = pl.ds(pl.multiple_of(n * TILE, TILE), TILE)
-            d_inner = mxu(d_expert[...], w_down[cols, :], NT)
-            d_gate_up[:, cols] = (d_inner * by_d_gate[:, cols]).astype(bf16)
-            d_gate_up[:, pl.ds(pl.multiple_of(ff + n * TILE, TILE), TILE)] = (
-                d_inner * by_d_up[:, cols]
+            d_inner = mxu(d_expert[at, :], w_down[cols, :], NT)
+            d_gate_up[at, cols] = (d_inner * by_d_gate[at, cols]).astype(bf16)
+            d_gate_up[at, pl.ds(pl.multiple_of(ff + n * TILE, TILE), TILE)] = (
+                d_inner * by_d_up[at, cols]
             ).astype(bf16)
 
-    def spread(stage):
+    def spread(stage, sides_done=(0, 1)):
         @pl.loop(0, width // WIDE)
         def _(n):
             cols = pl.ds(pl.multiple_of(n * WIDE, WIDE), WIDE)
-            for g in range(blocks // group):
-                part = held[g * group * capacity : (g + 1) * group * capacity, cols]
-                result = mxu(pick_t[g], part).astype(bf16)
-                stage[g * group : (g + 1) * group, :, cols] = result.reshape(group, tokens, WIDE)
-
-    def down(k):
-        d_gates[...] = jnp.zeros_like(d_gates)
+            for g in sides_done:
+                result = mxu(pick_t[g], held[slots_at(g), cols]).astype(bf16)
+                stage[pl.ds(g * group, group), :, cols] = result.reshape(group, tokens, WIDE)
+
+    def down(g=None):
+        at = slots_at(g)
+        d_gates[at, :] = jnp.zeros_like(d_gates[at, :])
 
         @pl.loop(0, width // TILE)
         def _(n):
             cols = pl.ds(pl.multiple_of(n * TILE, TILE), TILE)
-            result = mxu(inner[...], w_down[:, cols]).astype(bf16).astype(f32)
-            product = result * cot[:, cols].astype(f32)
+            result = mxu(inner[at, :], w_down[:, cols]).astype(bf16).astype(f32)
+            product = result * cot[at, cols].astype(f32)
             total = product[:, :128]
             for j in range(1, TILE // 128):
                 total = total + product[:, j * 128 : (j + 1) * 128]
-            d_gates[...] += total
-            scale = jnp.concatenate([gates[...]] * (TILE // 128), axis=1)
-            held[:, cols] = (scale * result).astype(bf16)
-
-    def d_down(k):
-        total = jnp.sum(d_gates[...], axis=1, keepdims=True)
-        high = total.astype(bf16).astype(f32)
-        lane = lax.broadcasted_iota(jnp.int32, (slots, 128), 1)
-        info = jnp.where(lane == p.me, high, jnp.where(lane == experts + p.me, total - high, 0.0))
-        info = info.astype(bf16)
-        for g in range(blocks // group):
-            result = mxu(pick_t[g], info[g * group * capacity : (g + 1) * group * capacity])
-            d_stage[g * group : (g + 1) * group, :, width:] = result.astype(bf16).reshape(
-                group, tokens, 128
+            d_gates[at, :] += total
+            scale = jnp.concatenate([gates[at, :]] * (TILE // 128), axis=1)
+            held[at, cols] = (scale * result).astype(bf16)
+
+    def d_down(g=None, sides_done=(0, 1)):
+        for side in sides_done:
+            at = slots_at(side)
+            total = jnp.sum(d_gates[at, :], axis=1, keepdims=True)
+            high = total.astype(bf16).astype(f32)
+            lane = lax.broadcasted_iota(jnp.int32, (group * capacity, 128), 1)
+            info = jnp.where(
+                lane == p.me, high, jnp.where(lane == experts + p.me, total - high, 0.0)
             )
+            result = mxu(pick_t[side], info.astype(bf16)).astype(bf16)
+            d_stage[pl.ds(side * group, group), :, width:] = result.reshape(group, tokens, 128)
+        at = slots_at(g)
 
         @pl.loop(0, width // TILE)
         def _(n):
             cols = pl.ds(pl.multiple_of(n * TILE, TILE), TILE)
-            held[:, cols] = mxu(d_gate_up[...], w_in[cols, :], NT).astype(bf16)
+            held[at, cols] = mxu(d_gate_up[at, :], w_in[cols, :], NT).astype(bf16)
 
     plane_out(0)
     weights(True)
     cot_load(0).start()
     plane_turn(0)
+    side_arrived(0)
+    plane_hop(1)
     plane_out(1)
+    plane_hop(2)
+    weights(False)
+    cot_load(0).wait()
+    cot_load(1).start()
+    side_load(0).wait()
+    side = sides[0]
+    pick_rows(0, side)
+    up(side)
     plane_end(0)
-    arrived(0)
-    weights(False)
+    d_up(side)
+    down(side)
+    plane_hop(3)
+    side_arrived(1)
+    spread(out_stage, (side,))
+    d_down(side, (side,))
+    plane_turn(1)
+    plane_out(2)
+    spread(d_stage, (side,))
+    side_load(1).wait()
+    side = sides[1]
+    pick_rows(0, side)
+    put(0, 0)
+    put(0, 1)
+    up(side)
+    put(0, 2)
+    plane_end(1)
+    d_up(side)
+    put(0, 3)
+    down(side)
+    spread(out_stage, (side,))
+    put(0, 4)
+    arrived(1)
+    d_down(side, (side,))
+    spread(d_stage, (side,))
+    put(0, 5)
     after = {
-        (0, 1): ((plane_turn, 1), (plane_out, 2)),
-        (0, 3): ((plane_end, 1),),
-        (0, 5): ((arrived, 1),),
         (1, 0): ((plane_turn, 2), (plane_out, 3)),
         (1, 3): ((plane_end, 2),),
         (1, 5): ((arrived, 2),),
@@ -1067,7 +1167,7 @@
         (2, 3): ((plane_end, 3),),
         (2, 5): ((arrived, 3),),
     }
-    for k in range(4):
+    for k in range(1, 4):
 
         def service(i):
             for step, plane in after.get((k, i), ()):
@@ -1079,26 +1179,27 @@
             cot_load(k + 1).start()
         free(k, 0)
         free(k, 1)
-        pick_rows(k)
+        for g in range(2):
+            pick_rows(k, g)
         put(k, 0)
         put(k, 1)
         service(0)
         free(k, 2)
-        up(k)
+        up()
         put(k, 2)
         service(1)
         free(k, 3)
-        d_up(k)
+        d_up()
         put(k, 3)
         service(2)
         free(k, 4)
-        down(k)
+        down()
         service(3)
         spread(out_stage)
         put(k, 4)
         service(4)
         free(k, 5)
-        d_down(k)
+        d_down()
         service(5)
         spread(d_stage)
         put(k, 5)
@@ -1155,7 +1256,7 @@
             dma((4, G_KINDS)),
             dma((4, 2)),
             dma,
-            dma((10,)),
+            dma((11,)),
             dma((6, 2)),
         ],
         compiler_params=pltpu.CompilerParams(
@@ -1171,8 +1272,8 @@
 def back_kernel(
     own, pair, rows_all, columns_hbm, normed_hbm, queries, keys, values, attended,
     q_raw, k_raw, cosine, sine, q_gain, k_gain, attn_gain, gains, tokens, d_hidden,
-    d_tokens, cols_out, gains_out, mixture,
-    d_attn, columns, normed, d_normed, d_heads, d_query, d_key, d_value, d_proj, logits, q_sum, k_sum,
+    d_tokens, d_qkv, d_out_t, d_router, gains_out, mixture,
+    cols_out, d_attn, columns, normed, d_normed, d_heads, d_query, d_key, d_value, d_proj, logits, q_sum, k_sum,
     held, x_in, y_in, z_in, g_send, g_in, x_two, z_two, c_core, c_y,
     gs, gr, gz, load_sems, local_sem, hs, ys, yr, xs, xr, zs, zr, ts, tr,
     normed_sems, free, xs2, xr2, zs2, zr2, cs, cr, cys, cyr, as_, ar,
@@ -1207,13 +1308,21 @@
             pltpu.make_async_copy(own, there, local_sem).start()
         else:
             src = there
-            await_bytes(src, gr.at[q, 0])
-
-            @pl.when(p.inner)
+
+            @pl.when(jnp.logical_not(p.inner))
             def _():
-                send(src, src, gz.at[q, 0], gr.at[q, 0], p.by_z(p.onward(k)))
+                await_bytes(src, gr.at[q, 0])
 
         send(src, there, gs.at[q], gr.at[q, 1], p.by_x)
+
+    def gather_hop(k):
+        q = p.near(k)
+        there = rows_at(q, p.x)
+
+        @pl.when(p.inner)
+        def _():
+            await_bytes(there, gr.at[q, 0])
+            send(there, there, gz.at[q, 0], gr.at[q, 0], p.by_z(p.onward(k)))
 
     def gather_in(k):
         if k == 0:
@@ -1295,6 +1404,8 @@
 
     piece_rows = c_y.shape[1]
     order = [(place + d) % 8 for d in range(1, 9)]
+    piece_width = c_y.shape[2]
+    cols_at = cols_out.at[place]
 
     def cols_start():
         for turn, side in ((0, 1 - p.y), (1, p.y)):
@@ -1315,9 +1426,9 @@
             await_bytes(c_y.at[s], cyr.at[s])
             add_rows(mine, c_y.at[s], piece_rows)
             if i < 7:
-                send(mine, cols_out.at[place], as_.at[i], ar.at[i], seq_peer(p, i + 1))
+                send(mine, cols_at, as_.at[i], ar.at[i], seq_peer(p, i + 1))
             else:
-                pltpu.make_async_copy(mine, cols_out.at[place], as_.at[7]).start()
+                pltpu.make_async_copy(mine, cols_at, as_.at[7]).start()
 
     def norm_back():
         mine = d_normed.at[p.z * 2 + p.x]
@@ -1472,9 +1583,12 @@
     d_value[...] = jnp.zeros_like(d_value)
     loads[0].wait()
     gather_in(0)
+    gather_hop(1)
     gather_out(1)
+    gather_hop(2)
     attention(p.near(0))
     gather_out(2)
+    gather_hop(3)
     gather_in(1)
     attention(p.near(1))
     sum_turn(0)
@@ -1549,13 +1663,32 @@
         await_bytes(piece, zs2.at[k])
     for q in range(4):
         await_bytes(piece, xs2.at[q])
-    for turn in range(2):
-        await_bytes(c_core.at[turn], cs.at[turn])
     for i in range(8):
         if i < 7:
             await_bytes(c_y.at[0], ar.at[i])
         await_bytes(c_y.at[0], as_.at[i])
         await_bytes(c_y.at[0], cys.at[i])
+    for turn in range(2):
+        await_bytes(c_core.at[turn], cs.at[turn])
+    key_cols = KEY_VALUE_HEADS * HEAD_DIMENSION
+    per_group = 8 // KEY_VALUE_HEADS
+    router_total = jnp.zeros((piece_rows, 128), f32)
+    for s in range(8):
+        d_qkv[:, s * head_cols : (s + 1) * head_cols] = cols_out[s, :, :head_cols].astype(f32)
+        d_out_t[:, s * head_cols : (s + 1) * head_cols] = cols_out[
+            s, :, proj_cols : proj_cols + head_cols
+        ].astype(f32)
+        part = cols_out[s, :, proj_cols + head_cols :].astype(f32)
+        router_total = router_total + (pltpu.roll(part, s * router_cols, 1) if s else part)
+    d_router[...] = router_total
+    for g in range(KEY_VALUE_HEADS):
+        for j in range(2):
+            lanes = slice(head_cols + j * HEAD_DIMENSION, head_cols + (j + 1) * HEAD_DIMENSION)
+            total = cols_out[g * per_group, :, lanes].astype(f32)
+            for s in range(1, per_group):
+                total = total + cols_out[g * per_group + s, :, lanes].astype(f32)
+            first = 8 * head_cols + j * key_cols + g * HEAD_DIMENSION
+            d_qkv[:, first : first + HEAD_DIMENSION] = total
 
 
 def back(
@@ -1575,13 +1708,16 @@
         back_kernel,
         out_shape=[
             jax.ShapeDtypeStruct((rows, width), bf16),
-            jax.ShapeDtypeStruct((8, piece_rows, piece_width), bf16),
+            jax.ShapeDtypeStruct((piece_rows, 8 * head_cols + 2 * KEY_VALUE_HEADS * HEAD_DIMENSION), f32),
+            jax.ShapeDtypeStruct((piece_rows, 8 * head_cols), f32),
+            jax.ShapeDtypeStruct((piece_rows, 128), f32),
             jax.ShapeDtypeStruct(gains.shape, f32),
             jax.ShapeDtypeStruct((rows, width), bf16),
         ],
         in_specs=[anywhere] * 5 + [vmem] * 14,
-        out_specs=[vmem, anywhere, vmem, vmem],
+        out_specs=[vmem] * 6,
         scratch_shapes=[
+            pltpu.VMEM((8, piece_rows, piece_width), bf16),
             pltpu.VMEM((8, rows, wide), bf16),
             pltpu.VMEM(columns.shape, bf16),
             pltpu.VMEM((2, length, TILE), bf16),
@@ -1645,8 +1781,8 @@
 
 
 def front_kernel(
-    tokens, pieces, cot, cosine, sine, q_gain, k_gain, attn_gain,
-    normed_out, columns_out, cot_all, queries, keys, values, attended, q_raw, k_raw, attn_out,
+    tokens, pieces, cot, cosine, sine, q_gain, k_gain, attn_gain, ffn_gain, routes,
+    normed_out, columns_out, cot_all, queries, keys, values, attended, q_raw, k_raw, hidden, gates, routed,
     own, normed, columns, part, x_in, z_in,
     ss, rs, zs, cs, cr, ys, yr, ks, kr, local_sems, gs, gr, gz, xs, xr, us, ur,
 ):
@@ -1683,13 +1819,21 @@
             pltpu.make_async_copy(own, there, local_sems.at[0]).start()
         else:
             src = there
-            await_bytes(src, rs.at[q, 0])
-
-            @pl.when(p.inner)
+
+            @pl.when(jnp.logical_not(p.inner))
             def _():
-                send(src, src, zs.at[q, 0], rs.at[q, 0], p.by_z(p.onward(k)))
+                await_bytes(src, rs.at[q, 0])
 
         send(src, there, ss.at[q], rs.at[q, 1], p.by_x)
+
+    def rows_hop(k):
+        q = p.near(k)
+        there = rows_at(q, p.x)
+
+        @pl.when(p.inner)
+        def _():
+            await_bytes(there, rs.at[q, 0])
+            send(there, there, zs.at[q, 0], rs.at[q, 0], p.by_z(p.onward(k)))
 
     def pass_on(d):
         block = ((place + 8 - d) % 8) * 4 + shard
@@ -1725,15 +1869,23 @@
             pltpu.make_async_copy(cot, there, local_sems.at[2]).start()
         else:
             src = there
-            await_bytes(src, gr.at[q, C_Z])
-
-            @pl.when(p.inner)
+
+            @pl.when(jnp.logical_not(p.inner))
             def _():
-                send(src, src, gz.at[q, 0], gr.at[q, C_Z], p.by_z(p.onward(k)))
+                await_bytes(src, gr.at[q, C_Z])
 
         send(src, there, gs.at[q, C_Y], gr.at[q, C_Y], p.by_y)
         send(src, there, gs.at[q, C_X], gr.at[q, C_X], p.by_x)
         cot_core(q, 0, src)
+
+    def cot_hop(k):
+        q = p.near(k)
+        there = cot_at(q, p.x, p.y)
+
+        @pl.when(p.inner)
+        def _():
+            await_bytes(there, gr.at[q, C_Z])
+            send(there, there, gz.at[q, 0], gr.at[q, C_Z], p.by_z(p.onward(k)))
 
     def cot_turn(k):
         q = p.near(k)
@@ -1772,7 +1924,30 @@
                     await_bytes(z_in.at[slot, q], ur.at[slot, q])
                     add_rows(held, z_in.at[slot, q], rows)
 
-            attn_out[...] = held[...]
+    def route():
+        total = tokens[...].astype(jnp.float32) + part[p.z * 2 + p.x].astype(jnp.float32)
+        hidden[...] = total
+        scale = lax.rsqrt(jnp.mean(total * total, axis=-1, keepdims=True) + EPS)
+        routed[:, :width] = (total * scale * ffn_gain[...]).astype(bf16)
+        router = columns[:, :, proj_cols + head_cols :].reshape(width, 128)
+        logits = mxu(routed[:, :width], router)
+        lane = lax.broadcasted_iota(jnp.int32, (rows, 128), 1)
+        line = lax.broadcasted_iota(jnp.int32, (rows, 128), 0)
+        turned = routes[...].astype(jnp.float32).T
+        lanes = lane.astype(jnp.float32)
+        named = lanes == turned[:, 0:1]
+        for k in range(1, TOPK):
+            named = named | (lanes == turned[:, k : k + 1])
+        chosen = jnp.where(named, logits, -1e30)
+        raised = jnp.where(named, jnp.exp(chosen - jnp.max(chosen, axis=-1, keepdims=True)), 0.0)
+        gate = raised / jnp.sum(raised, axis=-1, keepdims=True)
+        gates[...] = gate
+        counted = jnp.where(named, 1.0, 0.0)
+        slot = counted * mxu(jnp.where(lane <= line, 1.0, 0.0).astype(bf16), counted.astype(bf16))
+        high = gate.astype(bf16).astype(jnp.float32)
+        experts = columns.shape[0]
+        info = high + pltpu.roll(gate - high, experts, 1) + pltpu.roll(slot, 2 * experts, 1)
+        routed[:, width:] = info.astype(bf16)
 
     def project(n):
         cols = slice(n * TILE, (n + 1) * TILE)
@@ -1844,17 +2019,21 @@
         send(pieces.at[(place + d) % 8], columns.at[mine], cs.at[d], cr.at[d], seq_peer(p, d))
     pltpu.make_async_copy(pieces.at[place], columns.at[mine], local_sems.at[1]).start()
     pass_on(0)
+    rows_hop(1)
     rows_move(1)
     for d in (1, 2, 7):
         pass_on(d)
+    rows_hop(2)
     rows_move(2)
     cot_move(0)
     for d in (6, 3, 5):
         pass_on(d)
+    rows_hop(3)
     rows_move(3)
     pass_on(4)
     for d in (0, 1, 2, 7, 6, 3, 5, 4):
         pass_across(d)
+    cot_hop(1)
     cot_move(1)
     for k in range(4):
         await_bytes(own, rs.at[p.near(k), 1])
@@ -1869,12 +2048,14 @@
     cot_turn(0)
     for n in range(proj_cols // TILE):
         project(n)
+    cot_hop(2)
     cot_move(2)
     prepare()
     cot_turn(1)
     attention(0)
     cot_end(0)
     attention(1)
+    cot_hop(3)
     cot_move(3)
     sum_end(0)
     attention(2)
@@ -1887,6 +2068,7 @@
     cot_end(2)
     sum_end(3)
     cot_end(3)
+    route()
     for q in range(4):
         for j in range(4):
             await_bytes(cot, gr.at[q, C_C + j])
@@ -1922,7 +2104,9 @@
     pltpu.make_async_copy(columns, columns_out, local_sems.at[1]).wait()
 
 
-def front(tokens, pieces, cot, cosine, sine, q_gain, k_gain, attn_gain, head_cols, collective_id):
+def front(
+    tokens, pieces, cot, cosine, sine, q_gain, k_gain, attn_gain, ffn_gain, routes, head_cols, collective_id
+):
     dma = pltpu.SemaphoreType.DMA
     bf16, f32 = jnp.bfloat16, jnp.float32
     rows, width = tokens.shape
@@ -1941,10 +2125,12 @@
             jax.ShapeDtypeStruct((length, head_cols), bf16),
             jax.ShapeDtypeStruct((length, head_cols), f32),
             jax.ShapeDtypeStruct((length, HEAD_DIMENSION), f32),
-            jax.ShapeDtypeStruct((rows, width), bf16),
+            jax.ShapeDtypeStruct((rows, width), f32),
+            jax.ShapeDtypeStruct((rows, 128), f32),
+            jax.ShapeDtypeStruct((rows, width + 128), bf16),
         ],
-        in_specs=[vmem] + [anywhere] * 2 + [vmem] * 5,
-        out_specs=[anywhere] * 3 + [vmem] * 7,
+        in_specs=[vmem] + [anywhere] * 2 + [vmem] * 7,
+        out_specs=[anywhere] * 3 + [vmem] * 9,
         scratch_shapes=[
             pltpu.VMEM((rows, width), bf16),
             pltpu.VMEM((count, rows, width), bf16),
@@ -1974,7 +2160,7 @@
             collective_id=collective_id, has_side_effects=True, vmem_limit_bytes=VMEM_LIMIT
         ),
         name="front",
-    )(tokens, pieces, cot, cosine, sine, q_gain, k_gain, attn_gain)
+    )(tokens, pieces, cot, cosine, sine, q_gain, k_gain, attn_gain, ffn_gain, routes)
 
 
 def head_columns(weight, group_index):
@@ -2032,7 +2218,6 @@
         ],
         axis=2,
     )
-    resid_in = tokens[0].astype(f32)
     half_dim = HEAD_DIMENSION // 2
     exponents = -2.0 * np.arange(half_dim, dtype=np.float32) / HEAD_DIMENSION
     frequency = np.float32(ROPE_BASE) ** exponents.astype(np.float32)
@@ -2040,7 +2225,20 @@
     cosine, sine = np.cos(angles), np.sin(angles)
     cosine = jnp.asarray(np.concatenate([cosine, cosine], axis=1), f32)
     sine = jnp.asarray(np.concatenate([sine, -sine], axis=1), f32)
-    normed_all, columns, cot_all, queries, keys, values, attended, q_raw, k_raw, attn_out = front(
+    (
+        normed_all,
+        columns,
+        cot_all,
+        queries,
+        keys,
+        values,
+        attended,
+        q_raw,
+        k_raw,
+        hidden,
+        gates,
+        routed,
+    ) = front(
         tokens[0],
         pieces,
         cotangent[0],
@@ -2049,64 +2247,40 @@
         q_gain[None],
         k_gain[None],
         attn_gain[None],
+        ffn_gain[None],
+        routes[0].T,
         head_cols,
         1,
     )
     normed_all = normed_all.reshape(length, width)
-    columns = columns.reshape(width, -1)
-    full_router = columns[:, all_cols : all_cols + experts]
-    hidden = resid_in + attn_out.astype(f32)
-    normed_two = rms_scale(hidden, ffn_gain).astype(bf16)
-
-    logits = jnp.dot(normed_two, full_router, preferred_element_type=f32)
-    onehot = routes[0][:, :, None] == jnp.arange(experts, dtype=jnp.int32)
-    onehot_float = onehot.astype(f32)
-    named = jnp.sum(onehot_float, axis=1)
-    order = jnp.arange(rows, dtype=jnp.int32)
-    upto = (order[None, :] <= order[:, None]).astype(bf16)
-    slot_info = named * jnp.dot(upto, named.astype(bf16), preferred_element_type=f32)
-    chosen = jnp.sum(onehot_float * logits[:, None, :], axis=-1)
-    row_max = jnp.max(chosen, axis=-1, keepdims=True)
-    exp_part = jnp.exp(chosen - row_max)
-    gate_probs = exp_part / jnp.sum(exp_part, axis=-1, keepdims=True)
-    gate_dense = jnp.sum(onehot_float * gate_probs[..., None], axis=1)
-
-    gate_high = gate_dense.astype(bf16)
-    gate_low = (gate_dense - gate_high.astype(f32)).astype(bf16)
-    route_info = jnp.concatenate([gate_high, gate_low, slot_info.astype(bf16)], axis=1)
-    route_info = jnp.pad(route_info, ((0, 0), (0, 128 - route_info.shape[1] % 128)))
+
     gate_weight = w_in[0]
     down_weight = w_down[0]
     rows_all, out_part, d_part, rows_in, d_expert, inner_act, d_gate_up = experts_gathered(
-        jnp.concatenate([normed_two, route_info], axis=1),
+        routed,
         cot_all,
         gate_weight,
         down_weight,
         capacity,
         3,
     )
-    d_back, out_pair, d_w_in, d_w_down = sum_all(
-        d_part, out_part, rows_in, d_gate_up, inner_act, d_expert, 5
+    d_send, d_hidden, gains, out_pair, d_w_in, d_w_down = sum_all(
+        d_part,
+        out_part,
+        rows_in,
+        d_gate_up,
+        inner_act,
+        d_expert,
+        columns,
+        hidden,
+        cotangent[0],
+        gates,
+        ffn_gain[None],
+        5,
     )
     d_w_in, d_w_down = d_w_in.astype(f32)[None], d_w_down.astype(f32)[None]
-    d_back = d_back.astype(f32)
-
-    d_gate_dense = d_back[:, width : width + experts] + d_back[:, width + experts : width + 2 * experts]
-    d_gates = jnp.sum(onehot_float * d_gate_dense[:, None, :], axis=-1)
-    d_chosen = gate_probs * (d_gates - jnp.sum(gate_probs * d_gates, axis=-1, keepdims=True))
-    d_logits = jnp.sum(d_chosen[..., None] * onehot_float, axis=1).astype(bf16)
-    d_normed_two = d_back[:, :width] + jnp.einsum(
-        "te,de->td", d_logits, full_router, preferred_element_type=f32
-    )
-    out_grad = cotangent[0].astype(f32)
-    unused_two, pull_two = jax.vjp(rms_scale, hidden, ffn_gain)
-    d_hidden_norm, d_ffn_gain = pull_two(d_normed_two)
-    d_hidden = out_grad + d_hidden_norm
-    d_attn = d_hidden.astype(bf16)
-
-    d_send = jnp.concatenate([d_attn, jnp.pad(d_logits, ((0, 0), (0, 128 - experts)))], axis=1)
-    gains = jnp.pad(d_ffn_gain[None], ((1, 6), (0, 0)))
-    d_tokens, d_pieces, gains, mixture = back(
+
+    d_tokens, d_w_qkv, d_w_out_t, d_w_router, gains, mixture = back(
         d_send,
         out_pair.reshape(2 * seq_size, rows, width),
         rows_all.reshape(seq_size, shard_size, rows, -1),
@@ -2129,17 +2303,8 @@
         6,
     )
     output = (hidden + mixture.astype(f32)).astype(bf16)
-    router_cols = experts // seq_size
     d_tokens = d_tokens[None]
-    d_pieces = d_pieces.astype(f32).transpose(1, 0, 2)
-    per_group = seq_size // KEY_VALUE_HEADS
-    d_kv = d_pieces[:, :, head_cols:proj_cols].reshape(
-        weight_rows, KEY_VALUE_HEADS, per_group, 2, kv_cols
-    )
-    d_kv = jnp.sum(d_kv, axis=2).transpose(0, 2, 1, 3).reshape(weight_rows, -1)
-    d_w_qkv = jnp.concatenate([d_pieces[:, :, :head_cols].reshape(weight_rows, -1), d_kv], axis=1)
-    d_w_out_t = d_pieces[:, :, proj_cols:all_cols].reshape(weight_rows, -1)
-    d_w_router = d_pieces[:, :, all_cols : all_cols + router_cols].reshape(weight_rows, experts)
+    d_w_router = d_w_router[:, :experts]
     d_attn_gain, d_ffn_gain = gains[0], gains[1]
     d_q_gain = gains[2, :HEAD_DIMENSION]
     d_k_gain = gains[2, HEAD_DIMENSION : 2 * HEAD_DIMENSION]

time: 621 us -> 603 us (0.971)
  other arithmetic: 21.4 us -> 14.2 us
    pallas_call x1, Pallas kernels: 95.5 us -> 84.8 us  [sum_all(): pl.pallas_call(sum_all_kernel, out_shape=[jax.ShapeDtypeStruct((rows, wid...]
where the time goes in v7:
time: 603 us; the launch traced here: 595 us
  Pallas kernels  568 us (94%)
  other arithmetic  14.2 us (2%)
  local copies, waits for them, and re-layouts  11 us (2%)
    pallas_call x1, Pallas kernels, back(): pl.pallas_call(back_kernel, out_shape=[jax.ShapeDtypeStruct((rows, width)...  182 us
    pallas_call x1, Pallas kernels, front(): pl.pallas_call(front_kernel, out_shape=[jax.ShapeDtypeStruct((count, rows...  172 us
    pallas_call x1, Pallas kernels, experts_gathered(): pl.pallas_call(experts_kernel, out_shape=[array(experts, tokens, wide), a...  130 us
    pallas_call x1, Pallas kernels, sum_all(): pl.pallas_call(sum_all_kernel, out_shape=[jax.ShapeDtypeStruct((rows, wid...  84.8 us
    broadcast_in_dim x2, other arithmetic, gathered_body(): d_w_in, d_w_down = (d_w_in.astype(f32)[None], d_w_down.astype(f32)[None])  12.1 us

profile of v7, /device:TPU:16, one launch (start us, length us, event | category | flops | bytes accessed | tf_op | source)
XLA Modules:
  0.0 594.5 jit_solution(13533140667517595888)
XLA Ops:
  0.6 0.0 slice-start.2
  0.7 0.8 copy.47
  1.5 0.9 fusion.3
  2.5 0.1 fusion.6
  2.6 0.1 fusion.5
  2.7 0.0 copy-start.4
  2.7 0.0 slice-done.2
  3.0 0.7 copy-done.4
  3.8 0.0 copy-start.1
  3.8 1.1 copy-done.1
  4.9 172.1 %front.1 = (bf16[8,128,2048]{2,1,0:T(8,128)(2,1)}, bf16[32,64,1408]{2,1,0:T(8,128)(2,1)}, bf16[32,128,2048]{2,1,0:T(8,128)(2,1)}, bf16[1024,512]{1,0:T(8,128)(2,...) custom-call(bf16[128,2048]{1,0:T(8,128)(2,1)} %bitcast.111, ...), custom_call_target="tpu_custom_call" | custom-call | tf_op jit(solution)/shard_map/front/pallas_call | solution.py:2116
  177.0 129.5 %experts.1 = (bf16[32,128,2176]{2,1,0:T(8,128)(2,1)}, bf16[32,128,2048]{2,1,0:T(8,128)(2,1)}, bf16[32,128,2176]{2,1,0:T(8,128)(2,1)}, bf16[2048,2048]{1,0:T(8,12...) custom-call(bf16[128,2176]{1,0:T(8,128)(2,1)} %get-tuple-element.43.own, ...), custom_call_target="tpu_custom_call" | custom-call | tf_op jit(solution)/shard_map/experts/pallas_call | solution.py:1223
  306.5 84.8 %sum_all.1 = (bf16[128,2176]{1,0:T(8,128)(2,1)}, f32[128,2048]{1,0:T(8,128)}, f32[8,2048]{1,0:T(8,128)}, bf16[8,2,128,2048]{3,2,1,0:T(8,128)(2,1)}, bf16[2048,15...) custom-call(bf16[32,128,2176]{2,1,0:T(8,128)(2,1)} %get-tuple-element.45.part, bf16[8,2,2,128,2048]{4,3,2,1,0:T(8,128)(2,1)} %bitcast.102, ...), custom_call_target="tpu_custom_call" | custom-call | tf_op jit(solution)/shard_map/sum_all/pallas_call | solution.py:853
  391.3 0.0 copy-start
  391.3 181.6 %back.1 = (bf16[128,2048]{1,0:T(8,128)(2,1)}, f32[64,5120]{1,0:T(8,128)}, f32[64,4096]{1,0:T(8,128)}, f32[64,128]{1,0:T(8,128)}, f32[8,2048]{1,0:T(8,128)}, /*index=5*/bf16[128,2048]{1,0:T(8,128)(2,1)}) custom-call(bf16[128,2176]{1,0:T(8,128)(2,1)} %get-tuple-element.53.own, bf16[16,128,2048]{2,1,0:T(8,128)(2,1)} %bitcast.103, ...), custom_call_target="tpu_custom_call" | custom-call | tf_op jit(solution)/shard_map/back/pallas_call | solution.py:1707
  572.9 0.0 copy-start.6
  572.9 0.0 copy-done
  572.9 0.0 slice-start
  572.9 2.1 fusion
  575.0 1.2 slice_bitcast_fusion
  576.2 1.5 fusion.4
  577.8 0.0 copy-done.6
  577.8 0.7 copy.38
  578.5 0.0 slice-start.1
  578.5 5.6 bitcast_convert_fusion.1
  584.0 0.0 slice-done
  584.1 0.0 slice-done.1
  584.1 0.0 copy-start.5
  584.1 0.0 copy-start.2
  584.1 6.6 %bitcast_convert_fusion = f32[1,2048,1536]{2,1,0:T(8,128)} fusion(bf16[2048,1536]{1,0:T(8,128)(2,1)S(1)} %bitcast.107), kind=kLoop, calls=%fused_computation | loop fusion | flops 3145728 | bytes 18874368 | tf_op jit(solution)/shard_map/broadcast_in_dim | solution.py:2281
  590.6 0.0 copy-done.5
  590.6 0.8 copy.113
  591.4 0.0 copy-done.2
  591.4 0.0 copy-start.3
  591.4 1.1 copy.114
  592.5 0.6 copy-done.3
  593.1 1.0 copy.115
  (23 shorter events, 0.4 us)
Async XLA Ops:
  0.6 2.0 slice-start.2
  2.7 1.0 copy-start.4
  3.8 1.1 copy-start.1
  391.3 181.6 %copy-start = (f32[128,2048]{1,0:T(8,128)S(1)}, f32[128,2048]{1,0:T(8,128)}, u32[]{:S(2)}) copy-start(f32[128,2048]{1,0:T(8,128)} %get-tuple-element.42.hidden) | copy-start | bytes 3145732
  572.9 4.9 copy-start.6
  572.9 11.1 %slice-start = ((s8[6291456]{0:T(1024)(128)(4,1)}), s8[2097152]{0:T(1024)(128)(4,1)S(1)}, s32[]{:S(2)}) async-start(s8[6291456]{0:T(1024)(128)(4,1)} %bitcast.106), calls=%async_computation | async-start | bytes 4194304
  578.5 5.6 slice-start.1
  584.1 6.6 %copy-start.5 = (bf16[128,2048]{1,0:T(8,128)(2,1)S(1)}, bf16[128,2048]{1,0:T(8,128)(2,1)}, u32[]{:S(2)}) copy-start(bf16[128,2048]{1,0:T(8,128)(2,1)} %get-tuple-element.66) | copy-start | bytes 1572868
  584.1 7.4 %copy-start.2 = (f32[64,5120]{1,0:T(8,128)S(1)}, f32[64,5120]{1,0:T(8,128)}, u32[]{:S(2)}) copy-start(f32[64,5120]{1,0:T(8,128)} %get-tuple-element.122) | copy-start | bytes 3932164
  591.4 1.7 copy-start.3

commit v8 on v7

--- a/solution.py
+++ b/solution.py
@@ -702,7 +702,7 @@
 
 def sum_all_kernel(
     part, both, rows_in, d_gate_up, inner, d_expert, columns, hidden, cot, gates, ffn_gain,
-    out, d_hidden, gains, pair, d_w_in, d_w_down,
+    out, d_logits, d_hidden, gains, pair, d_w_in, d_w_down,
     d_rows, router, router_sem, both_held, both_in, left, product, pair_sems, load_sems, left_sems, product_sems, *scratch,
 ):
     p = Place()
@@ -798,14 +798,14 @@
     d_gates = jnp.where(lane < experts, tail + pltpu.roll(tail, 128 - experts, 1), 0.0)
     gate = gates[...]
     d_chosen = gate * (d_gates - jnp.sum(gate * d_gates, axis=-1, keepdims=True))
-    out[:, width:] = d_chosen.astype(out.dtype)
+    d_logits[...] = d_chosen.astype(d_logits.dtype)
     gains[...] = jnp.zeros_like(gains)
     chunk = 32
 
     @pl.loop(0, rows // chunk)
     def _(i):
         at = pl.ds(pl.multiple_of(i * chunk, chunk), chunk)
-        routed = mxu(out[at, width:], router[...].reshape(width, 128), NT)
+        routed = mxu(d_logits[at, :], router[...].reshape(width, 128), NT)
         d_out = d_rows[at, :width].astype(jnp.float32) + routed
         x = hidden[at, :]
         scale = lax.rsqrt(jnp.mean(x * x, axis=-1, keepdims=True) + EPS)
@@ -813,7 +813,7 @@
         dot = jnp.mean(u * x, axis=-1, keepdims=True)
         grad = cot[at, :].astype(jnp.float32) + scale * u - x * (scale * scale * scale * dot)
         d_hidden[at, :] = grad
-        out[at, :width] = grad.astype(out.dtype)
+        out[at, :] = grad.astype(out.dtype)
         gains[1:2, :] += jnp.sum(d_out * x * scale, axis=0, keepdims=True)
 
     tiles_end(inner, d_w_down)
@@ -853,7 +853,8 @@
     return pl.pallas_call(
         sum_all_kernel,
         out_shape=[
-            jax.ShapeDtypeStruct((rows, width), part.dtype),
+            jax.ShapeDtypeStruct(hidden.shape, part.dtype),
+            jax.ShapeDtypeStruct((rows, 128), part.dtype),
             jax.ShapeDtypeStruct(hidden.shape, jnp.float32),
             jax.ShapeDtypeStruct((8, hidden.shape[1]), jnp.float32),
             jax.ShapeDtypeStruct(pair, both.dtype),
@@ -861,7 +862,7 @@
             jax.ShapeDtypeStruct((inner.shape[1], d_expert.shape[1]), both.dtype),
         ],
         in_specs=[anywhere] * 7 + [vmem] * 4,
-        out_specs=[vmem] * 3 + [anywhere] * 3,
+        out_specs=[vmem] * 4 + [anywhere] * 3,
         scratch_shapes=[
             pltpu.VMEM((rows, width), part.dtype),
             pltpu.VMEM((*columns.shape[:2], 128), part.dtype),
@@ -1270,10 +1271,12 @@
 
 
 def back_kernel(
-    own, pair, rows_all, columns_hbm, normed_hbm, queries, keys, values, attended,
-    q_raw, k_raw, cosine, sine, q_gain, k_gain, attn_gain, gains, tokens, d_hidden,
+    own, pair, columns_hbm, normed_hbm, queries_hbm, keys_hbm, values_hbm, attended_hbm,
+    q_raw_hbm, k_raw_hbm, cosine_hbm, sine_hbm, tokens_hbm, d_hidden_hbm, routed_hbm, d_logits_hbm,
+    q_gain, k_gain, attn_gain, gains,
     d_tokens, d_qkv, d_out_t, d_router, gains_out, mixture,
-    cols_out, d_attn, columns, normed, d_normed, d_heads, d_query, d_key, d_value, d_proj, logits, q_sum, k_sum,
+    queries, keys, values, attended, q_raw, k_raw, cosine, sine, tokens, d_hidden, routed, d_logits, input_sems,
+    cols_out, d_attn, columns, normed, d_normed, d_heads, d_query, d_key, d_value, d_proj, q_sum, k_sum,
     held, x_in, y_in, z_in, g_send, g_in, x_two, z_two, c_core, c_y,
     gs, gr, gz, load_sems, local_sem, hs, ys, yr, xs, xr, zs, zr, ts, tr,
     normed_sems, free, xs2, xr2, zs2, zr2, cs, cr, cys, cyr, as_, ar,
@@ -1289,7 +1292,7 @@
     proj_cols = d_proj.shape[1]
     plane_rows = 2 * rows
     score_scale = 1.0 / math.sqrt(HEAD_DIMENSION)
-    place, shard = p.z * 2 + p.x, p.y * 2 + p.c
+    place = p.z * 2 + p.x
 
     def rows_at(q, x):
         return d_attn.at[q * 2 + x]
@@ -1452,7 +1455,7 @@
         @pl.loop(0, head_cols // TILE)
         def _(n):
             cols = pl.ds(pl.multiple_of(n * TILE, TILE), TILE)
-            grad = d_attn[pl.ds(q * 2, 2), :, :width].reshape(plane_rows, width)
+            grad = d_attn[pl.ds(q * 2, 2)].reshape(plane_rows, width)
             weight_cols = pl.ds(pl.multiple_of(proj_cols + n * TILE, TILE), TILE)
             weight = columns[..., weight_cols].reshape(width, TILE)
             d_heads[at, cols] = mxu(grad, weight).astype(bf16)
@@ -1563,6 +1566,13 @@
             await_bytes(g_in.at[0], tr.at[2 + d])
         g_send[3] = g_in[2] + g_in[3] + g_in[4] + g_in[5]
 
+    def router_grads():
+        @pl.loop(0, width // TILE)
+        def _(n):
+            cols = pl.ds(pl.multiple_of(n * TILE, TILE), TILE)
+            grad = mxu(routed[:, cols], d_logits[...], TN).astype(bf16)
+            columns[n, :, :, :, proj_cols + head_cols :] = grad.reshape(2, 2, -1, 128)
+
     def column_grads(value, first, count):
         @pl.loop(0, width // TILE)
         def _(n):
@@ -1573,15 +1583,37 @@
 
     loads = [
         pltpu.make_async_copy(columns_hbm, columns, load_sems.at[0]),
-        pltpu.make_async_copy(rows_all.at[:, shard], d_attn, load_sems.at[1]),
     ]
     gather_out(0)
+    inputs = [
+        pltpu.make_async_copy(source, target, input_sems.at[i])
+        for i, (source, target) in enumerate(
+            (
+                (queries_hbm, queries),
+                (keys_hbm, keys),
+                (values_hbm, values),
+                (attended_hbm, attended),
+                (q_raw_hbm, q_raw),
+                (k_raw_hbm, k_raw),
+                (cosine_hbm, cosine),
+                (sine_hbm, sine),
+                (tokens_hbm, tokens),
+                (d_hidden_hbm, d_hidden),
+                (routed_hbm, routed),
+                (d_logits_hbm, d_logits),
+            )
+        )
+    ]
     loads[0].start()
+    for copy in inputs:
+        copy.start()
     normed_load(0, 0).start()
     sum_start()
     d_key[...] = jnp.zeros_like(d_key)
     d_value[...] = jnp.zeros_like(d_value)
     loads[0].wait()
+    for copy in inputs:
+        copy.wait()
     gather_in(0)
     gather_hop(1)
     gather_out(1)
@@ -1607,29 +1639,7 @@
     gains_take(0)
     gains_pass(1, p.by_x)
     two_start(0, 1)
-    line = lax.broadcasted_iota(jnp.int32, (128, 128), 0)
-    lane = lax.broadcasted_iota(jnp.int32, (128, 128), 1)
-    router_cols = rows_all.shape[0] * rows_all.shape[1] // 8
-    mine = (line == lane + place * router_cols) & (lane < router_cols)
-    select = jnp.where(mine, 1.0, 0.0).astype(bf16)
-    logits[...] = mxu(d_attn[:, :, width:].reshape(length, 128), select).astype(bf16)
-    for q in range(4):
-        await_bytes(own, gs.at[q])
-    for there, slot in ((p.high, 0), (p.low, 1)):
-
-        @pl.when(jnp.logical_not(there))
-        def _():
-            await_bytes(own, gz.at[p.z, slot])
-
-    for k in range(1, 4):
-
-        @pl.when(p.inner)
-        def _():
-            await_bytes(own, gz.at[p.near(k), 0])
-
-    loads[1].start()
-    loads[1].wait()
-    column_grads(logits, proj_cols + head_cols, 128)
+    router_grads()
     cols_start()
     gains_take(1)
     gains_z_pass()
@@ -1653,6 +1663,20 @@
     gains_out[...] = g_send[3] + g_in[6]
     for t in range(6):
         await_bytes(g_in.at[0], ts.at[t])
+    for q in range(4):
+        await_bytes(own, gs.at[q])
+    for there, slot in ((p.high, 0), (p.low, 1)):
+
+        @pl.when(jnp.logical_not(there))
+        def _():
+            await_bytes(own, gz.at[p.z, slot])
+
+    for k in range(1, 4):
+
+        @pl.when(p.inner)
+        def _():
+            await_bytes(own, gz.at[p.near(k), 0])
+
     piece = x_in.at[0]
     for i in range(8):
         await_bytes(piece, ys.at[i])
@@ -1679,7 +1703,7 @@
             s, :, proj_cols : proj_cols + head_cols
         ].astype(f32)
         part = cols_out[s, :, proj_cols + head_cols :].astype(f32)
-        router_total = router_total + (pltpu.roll(part, s * router_cols, 1) if s else part)
+        router_total = router_total + part
     d_router[...] = router_total
     for g in range(KEY_VALUE_HEADS):
         for j in range(2):
@@ -1692,10 +1716,13 @@
 
 
 def back(
-    own, pair, rows_all, columns, normed, queries, keys, values, attended,
+    own, pair, columns, normed, queries, keys, values, attended,
     q_raw, k_raw, cosine, sine, q_gain, k_gain, attn_gain, gains, tokens, d_hidden,
-    collective_id,
+    routed, d_logits, collective_id,
 ):
+    inputs = (
+        queries, keys, values, attended, q_raw, k_raw, cosine, sine, tokens, d_hidden, routed, d_logits,
+    )
     rows, wide = own.shape
     length, head_cols = queries.shape
     width = normed.shape[1]
@@ -1714,9 +1741,11 @@
             jax.ShapeDtypeStruct(gains.shape, f32),
             jax.ShapeDtypeStruct((rows, width), bf16),
         ],
-        in_specs=[anywhere] * 5 + [vmem] * 14,
+        in_specs=[anywhere] * 16 + [vmem] * 4,
         out_specs=[vmem] * 6,
         scratch_shapes=[
+            *[pltpu.VMEM(array.shape, array.dtype) for array in inputs],
+            dma((len(inputs),)),
             pltpu.VMEM((8, piece_rows, piece_width), bf16),
             pltpu.VMEM((8, rows, wide), bf16),
             pltpu.VMEM(columns.shape, bf16),
@@ -1727,7 +1756,6 @@
             pltpu.VMEM((length, HEAD_DIMENSION), f32),
             pltpu.VMEM((length, HEAD_DIMENSION), f32),
             pltpu.VMEM((length, proj_cols), bf16),
-            pltpu.VMEM((length, 128), bf16),
             pltpu.VMEM((8, HEAD_DIMENSION), f32),
             pltpu.VMEM((8, HEAD_DIMENSION), f32),
             pltpu.VMEM((8, rows, width), bf16),
@@ -1772,8 +1800,7 @@
         ),
         name="back",
     )(
-        own, pair, rows_all, columns, normed, queries, keys, values, attended,
-        q_raw, k_raw, cosine, sine, q_gain, k_gain, attn_gain, gains, tokens, d_hidden,
+        own, pair, columns, normed, *inputs, q_gain, k_gain, attn_gain, gains,
     )
 
 
@@ -1781,8 +1808,10 @@
 
 
 def front_kernel(
-    tokens, pieces, cot, cosine, sine, q_gain, k_gain, attn_gain, ffn_gain, routes,
-    normed_out, columns_out, cot_all, queries, keys, values, attended, q_raw, k_raw, hidden, gates, routed,
+    tokens, pieces, cot, cosine_hbm, sine_hbm, q_gain, k_gain, attn_gain, ffn_gain, routes,
+    normed_out, columns_out, cot_all, queries_out, keys_out, values_out, attended_out, q_raw_out, k_raw_out,
+    hidden, gates, routed,
+    queries, keys, values, attended, q_raw, k_raw, cosine, sine, result_sems, table_sems,
     own, normed, columns, part, x_in, z_in,
     ss, rs, zs, cs, cr, ys, yr, ks, kr, local_sems, gs, gr, gz, xs, xr, us, ur,
 ):
@@ -2014,7 +2043,26 @@
 
         send(part.at[q * 2 + 1 - p.x], x_in.at[q], xs.at[q], xr.at[q], p.by_x)
 
+    tables = [
+        pltpu.make_async_copy(cosine_hbm, cosine, table_sems.at[0]),
+        pltpu.make_async_copy(sine_hbm, sine, table_sems.at[1]),
+    ]
+    results = [
+        pltpu.make_async_copy(source, target, result_sems.at[i])
+        for i, (source, target) in enumerate(
+            (
+                (queries, queries_out),
+                (keys, keys_out),
+                (values, values_out),
+                (q_raw, q_raw_out),
+                (k_raw, k_raw_out),
+                (attended, attended_out),
+            )
+        )
+    ]
     rows_move(0)
+    for copy in tables:
+        copy.start()
     for d in range(1, 8):
         send(pieces.at[(place + d) % 8], columns.at[mine], cs.at[d], cr.at[d], seq_peer(p, d))
     pltpu.make_async_copy(pieces.at[place], columns.at[mine], local_sems.at[1]).start()
@@ -2050,7 +2098,11 @@
         project(n)
     cot_hop(2)
     cot_move(2)
+    for copy in tables:
+        copy.wait()
     prepare()
+    for copy in results[:5]:
+        copy.start()
     cot_turn(1)
     attention(0)
     cot_end(0)
@@ -2063,12 +2115,15 @@
     cot_end(1)
     sum_end(1)
     attention(3)
+    results[5].start()
     cot_turn(3)
     sum_end(2)
     cot_end(2)
     sum_end(3)
     cot_end(3)
     route()
+    for copy in results:
+        copy.wait()
     for q in range(4):
         for j in range(4):
             await_bytes(cot, gr.at[q, C_C + j])
@@ -2129,9 +2184,19 @@
             jax.ShapeDtypeStruct((rows, 128), f32),
             jax.ShapeDtypeStruct((rows, width + 128), bf16),
         ],
-        in_specs=[vmem] + [anywhere] * 2 + [vmem] * 7,
-        out_specs=[anywhere] * 3 + [vmem] * 9,
+        in_specs=[vmem] + [anywhere] * 4 + [vmem] * 5,
+        out_specs=[anywhere] * 9 + [vmem] * 3,
         scratch_shapes=[
+            pltpu.VMEM((length, head_cols), bf16),
+            pltpu.VMEM((length, HEAD_DIMENSION), bf16),
+            pltpu.VMEM((length, HEAD_DIMENSION), bf16),
+            pltpu.VMEM((length, head_cols), bf16),
+            pltpu.VMEM((length, head_cols), f32),
+            pltpu.VMEM((length, HEAD_DIMENSION), f32),
+            pltpu.VMEM(cosine.shape, f32),
+            pltpu.VMEM(sine.shape, f32),
+            dma((6,)),
+            dma((2,)),
             pltpu.VMEM((rows, width), bf16),
             pltpu.VMEM((count, rows, width), bf16),
             pltpu.VMEM((count * 4, piece_rows, piece_width), bf16),
@@ -2256,7 +2321,7 @@
 
     gate_weight = w_in[0]
     down_weight = w_down[0]
-    rows_all, out_part, d_part, rows_in, d_expert, inner_act, d_gate_up = experts_gathered(
+    unused_rows, out_part, d_part, rows_in, d_expert, inner_act, d_gate_up = experts_gathered(
         routed,
         cot_all,
         gate_weight,
@@ -2264,7 +2329,7 @@
         capacity,
         3,
     )
-    d_send, d_hidden, gains, out_pair, d_w_in, d_w_down = sum_all(
+    d_attn, d_logits, d_hidden, gains, out_pair, d_w_in, d_w_down = sum_all(
         d_part,
         out_part,
         rows_in,
@@ -2281,9 +2346,8 @@
     d_w_in, d_w_down = d_w_in.astype(f32)[None], d_w_down.astype(f32)[None]
 
     d_tokens, d_w_qkv, d_w_out_t, d_w_router, gains, mixture = back(
-        d_send,
+        d_attn,
         out_pair.reshape(2 * seq_size, rows, width),
-        rows_all.reshape(seq_size, shard_size, rows, -1),
         columns.reshape(seq_size, 2, shard_size // 2, weight_rows, all_cols + spare_cols),
         normed_all,
         queries,
@@ -2300,6 +2364,8 @@
         gains,
         tokens[0],
         d_hidden,
+        routed,
+        d_logits,
         6,
     )
     output = (hidden + mixture.astype(f32)).astype(bf16)

time: 603 us -> 595 us (0.987)
  Pallas kernels: 568 us -> 560 us
where the time goes in v8:
time: 595 us; the launch traced here: 587 us
  Pallas kernels  560 us (94%)
  other arithmetic  14.2 us (2%)
  local copies, waits for them, and re-layouts  11 us (2%)
    pallas_call x1, Pallas kernels, back(): pl.pallas_call(back_kernel, out_shape=[jax.ShapeDtypeStruct((rows, width)...  176 us
    pallas_call x1, Pallas kernels, front(): pl.pallas_call(front_kernel, out_shape=[jax.ShapeDtypeStruct((count, rows...  170 us
    pallas_call x1, Pallas kernels, experts_gathered(): pl.pallas_call(experts_kernel, out_shape=[array(experts, tokens, wide), a...  129 us
    pallas_call x1, Pallas kernels, sum_all(): pl.pallas_call(sum_all_kernel, out_shape=[jax.ShapeDtypeStruct(hidden.sha...  84.9 us
    broadcast_in_dim x2, other arithmetic, gathered_body(): d_w_in, d_w_down = (d_w_in.astype(f32)[None], d_w_down.astype(f32)[None])  12.1 us

profile of v8, /device:TPU:16, one launch (start us, length us, event | category | flops | bytes accessed | tf_op | source)
XLA Modules:
  0.0 586.7 jit_solution(18326380439361847947)
XLA Ops:
  0.6 0.0 slice-start.2
  0.7 0.8 copy.47
  1.5 0.9 fusion.3
  2.5 0.1 fusion.6
  2.6 0.1 fusion.5
  2.7 0.0 copy-start.4
  2.7 0.0 slice-done.2
  3.0 0.7 copy-done.4
  3.8 0.0 copy-start.1
  3.8 1.1 copy-done.1
  4.9 170.1 %front.1 = (bf16[8,128,2048]{2,1,0:T(8,128)(2,1)}, bf16[32,64,1408]{2,1,0:T(8,128)(2,1)}, bf16[32,128,2048]{2,1,0:T(8,128)(2,1)}, bf16[1024,512]{1,0:T(8,128)(2,...) custom-call(bf16[128,2048]{1,0:T(8,128)(2,1)} %bitcast.109, ...), custom_call_target="tpu_custom_call" | custom-call | tf_op jit(solution)/shard_map/front/pallas_call | solution.py:2171
  175.0 129.5 %experts.1 = (bf16[32,128,2176]{2,1,0:T(8,128)(2,1)}, bf16[32,128,2048]{2,1,0:T(8,128)(2,1)}, bf16[32,128,2176]{2,1,0:T(8,128)(2,1)}, bf16[2048,2048]{1,0:T(8,12...) custom-call(bf16[128,2176]{1,0:T(8,128)(2,1)} %get-tuple-element.43.own.routed_hbm, ...), custom_call_target="tpu_custom_call" | custom-call | tf_op jit(solution)/shard_map/experts/pallas_call | solution.py:1224
  304.5 84.9 %sum_all.1 = (bf16[128,2048]{1,0:T(8,128)(2,1)}, bf16[128,128]{1,0:T(8,128)(2,1)}, f32[128,2048]{1,0:T(8,128)}, f32[8,2048]{1,0:T(8,128)}, bf16[8,2,128,2048]{3,...) custom-call(bf16[32,128,2176]{2,1,0:T(8,128)(2,1)} %get-tuple-element.45.part, ...), custom_call_target="tpu_custom_call" | custom-call | tf_op jit(solution)/shard_map/sum_all/pallas_call | solution.py:853
  389.4 0.0 copy-start
  389.4 175.7 %back.1 = (bf16[128,2048]{1,0:T(8,128)(2,1)}, f32[64,5120]{1,0:T(8,128)}, f32[64,4096]{1,0:T(8,128)}, f32[64,128]{1,0:T(8,128)}, f32[8,2048]{1,0:T(8,128)}, /*index=5*/bf16[128,2048]{1,0:T(8,128)(2,1)}) custom-call(bf16[128,2048]{1,0:T(8,128)(2,1)} %get-tuple-element.53.own, bf16[16,128,2048]{2,1,0:T(8,128)(2,1)} %bitcast.101, ...), custom_call_target="tpu_custom_call" | custom-call | tf_op jit(solution)/shard_map/back/pallas_call | solution.py:1734
  565.1 0.0 copy-start.6
  565.1 0.0 copy-done
  565.1 0.0 slice-start
  565.1 2.1 fusion
  567.2 1.2 slice_bitcast_fusion
  568.4 1.5 fusion.4
  570.0 0.0 copy-done.6
  570.0 0.7 copy.38
  570.6 0.0 slice-start.1
  570.6 5.6 bitcast_convert_fusion.1
  576.2 0.0 slice-done
  576.2 0.0 slice-done.1
  576.2 0.0 copy-start.5
  576.2 0.0 copy-start.2
  576.2 6.6 %bitcast_convert_fusion = f32[1,2048,1536]{2,1,0:T(8,128)} fusion(bf16[2048,1536]{1,0:T(8,128)(2,1)S(1)} %bitcast.105), kind=kLoop, calls=%fused_computation | loop fusion | flops 3145728 | bytes 18874368 | tf_op jit(solution)/shard_map/broadcast_in_dim | solution.py:2346
  582.8 0.0 copy-done.5
  582.8 0.8 copy.113
  583.6 0.0 copy-done.2
  583.6 0.0 copy-start.3
  583.6 1.1 copy.114
  584.7 0.6 copy-done.3
  585.3 1.0 copy.115
  (23 shorter events, 0.4 us)
Async XLA Ops:
  0.6 2.0 slice-start.2
  2.7 1.0 copy-start.4
  3.8 1.1 copy-start.1
  389.4 175.7 %copy-start = (f32[128,2048]{1,0:T(8,128)S(1)}, f32[128,2048]{1,0:T(8,128)}, u32[]{:S(2)}) copy-start(f32[128,2048]{1,0:T(8,128)} %get-tuple-element.42.hidden) | copy-start | bytes 3145732
  565.1 4.9 copy-start.6
  565.1 11.1 %slice-start = ((s8[6291456]{0:T(1024)(128)(4,1)}), s8[2097152]{0:T(1024)(128)(4,1)S(1)}, s32[]{:S(2)}) async-start(s8[6291456]{0:T(1024)(128)(4,1)} %bitcast.104), calls=%async_computation | async-start | bytes 4194304
  570.6 5.6 slice-start.1
  576.2 6.6 %copy-start.5 = (bf16[128,2048]{1,0:T(8,128)(2,1)S(1)}, bf16[128,2048]{1,0:T(8,128)(2,1)}, u32[]{:S(2)}) copy-start(bf16[128,2048]{1,0:T(8,128)(2,1)} %get-tuple-element.66) | copy-start | bytes 1572868
  576.2 7.4 %copy-start.2 = (f32[64,5120]{1,0:T(8,128)S(1)}, f32[64,5120]{1,0:T(8,128)}, u32[]{:S(2)}) copy-start(f32[64,5120]{1,0:T(8,128)} %get-tuple-element.122) | copy-start | bytes 3932164
  583.6 1.7 copy-start.3

commit v9 on v8

--- a/solution.py
+++ b/solution.py
@@ -919,7 +919,8 @@
 
 NT = (((1,), (1,)), ((), ()))
 TILE = 256
-WIDE = 512
+WIDE = 1024
+TALL = 512
 
 
 def mxu(a, b, dims=(((1,), (0,)), ((), ()))):
@@ -1088,16 +1089,16 @@
         at = slots_at(g)
         d_gates[at, :] = jnp.zeros_like(d_gates[at, :])
 
-        @pl.loop(0, width // TILE)
+        @pl.loop(0, width // TALL)
         def _(n):
-            cols = pl.ds(pl.multiple_of(n * TILE, TILE), TILE)
+            cols = pl.ds(pl.multiple_of(n * TALL, TALL), TALL)
             result = mxu(inner[at, :], w_down[:, cols]).astype(bf16).astype(f32)
             product = result * cot[at, cols].astype(f32)
             total = product[:, :128]
-            for j in range(1, TILE // 128):
+            for j in range(1, TALL // 128):
                 total = total + product[:, j * 128 : (j + 1) * 128]
             d_gates[at, :] += total
-            scale = jnp.concatenate([gates[at, :]] * (TILE // 128), axis=1)
+            scale = jnp.concatenate([gates[at, :]] * (TALL // 128), axis=1)
             held[at, cols] = (scale * result).astype(bf16)
 
     def d_down(g=None, sides_done=(0, 1)):
@@ -1113,9 +1114,9 @@
             d_stage[pl.ds(side * group, group), :, width:] = result.reshape(group, tokens, 128)
         at = slots_at(g)
 
-        @pl.loop(0, width // TILE)
+        @pl.loop(0, width // TALL)
         def _(n):
-            cols = pl.ds(pl.multiple_of(n * TILE, TILE), TILE)
+            cols = pl.ds(pl.multiple_of(n * TALL, TALL), TALL)
             held[at, cols] = mxu(d_gate_up[at, :], w_in[cols, :], NT).astype(bf16)
 
     plane_out(0)

time: 595 us -> 585 us (0.983)
  Pallas kernels: 560 us -> 549 us
    pallas_call x1, Pallas kernels: 129 us -> 119 us  [experts_gathered(): pl.pallas_call(experts_kernel, out_shape=[array(experts, tokens, wide), a...]
where the time goes in v9:
time: 585 us; the launch traced here: 576 us
  Pallas kernels  549 us (94%)
  other arithmetic  14.2 us (2%)
  local copies, waits for them, and re-layouts  11 us (2%)
    pallas_call x1, Pallas kernels, back(): pl.pallas_call(back_kernel, out_shape=[jax.ShapeDtypeStruct((rows, width)...  175 us
    pallas_call x1, Pallas kernels, front(): pl.pallas_call(front_kernel, out_shape=[jax.ShapeDtypeStruct((count, rows...  170 us
    pallas_call x1, Pallas kernels, experts_gathered(): pl.pallas_call(experts_kernel, out_shape=[array(experts, tokens, wide), a...  119 us
    pallas_call x1, Pallas kernels, sum_all(): pl.pallas_call(sum_all_kernel, out_shape=[jax.ShapeDtypeStruct(hidden.sha...  84.9 us
    broadcast_in_dim x2, other arithmetic, gathered_body(): d_w_in, d_w_down = (d_w_in.astype(f32)[None], d_w_down.astype(f32)[None])  12.1 us

profile of v9, /device:TPU:16, one launch (start us, length us, event | category | flops | bytes accessed | tf_op | source)
XLA Modules:
  0.0 575.8 jit_solution(9242375353467442141)
XLA Ops:
  0.6 0.0 slice-start.2
  0.7 0.8 copy.47
  1.5 0.9 fusion.3
  2.5 0.1 fusion.6
  2.6 0.1 fusion.5
  2.7 0.0 copy-start.4
  2.7 0.0 slice-done.2
  3.0 0.7 copy-done.4
  3.8 0.0 copy-start.1
  3.8 1.1 copy-done.1
  4.9 170.1 %front.1 = (bf16[8,128,2048]{2,1,0:T(8,128)(2,1)}, bf16[32,64,1408]{2,1,0:T(8,128)(2,1)}, bf16[32,128,2048]{2,1,0:T(8,128)(2,1)}, bf16[1024,512]{1,0:T(8,128)(2,...) custom-call(bf16[128,2048]{1,0:T(8,128)(2,1)} %bitcast.109, ...), custom_call_target="tpu_custom_call" | custom-call | tf_op jit(solution)/shard_map/front/pallas_call | solution.py:2172
  175.0 119.1 %experts.1 = (bf16[32,128,2176]{2,1,0:T(8,128)(2,1)}, bf16[32,128,2048]{2,1,0:T(8,128)(2,1)}, bf16[32,128,2176]{2,1,0:T(8,128)(2,1)}, bf16[2048,2048]{1,0:T(8,12...) custom-call(bf16[128,2176]{1,0:T(8,128)(2,1)} %get-tuple-element.43.own.routed_hbm, ...), custom_call_target="tpu_custom_call" | custom-call | tf_op jit(solution)/shard_map/experts/pallas_call | solution.py:1225
  294.1 84.9 %sum_all.1 = (bf16[128,2048]{1,0:T(8,128)(2,1)}, bf16[128,128]{1,0:T(8,128)(2,1)}, f32[128,2048]{1,0:T(8,128)}, f32[8,2048]{1,0:T(8,128)}, bf16[8,2,128,2048]{3,...) custom-call(bf16[32,128,2176]{2,1,0:T(8,128)(2,1)} %get-tuple-element.45.part, ...), custom_call_target="tpu_custom_call" | custom-call | tf_op jit(solution)/shard_map/sum_all/pallas_call | solution.py:853
  379.0 0.0 copy-start
  379.0 175.4 %back.1 = (bf16[128,2048]{1,0:T(8,128)(2,1)}, f32[64,5120]{1,0:T(8,128)}, f32[64,4096]{1,0:T(8,128)}, f32[64,128]{1,0:T(8,128)}, f32[8,2048]{1,0:T(8,128)}, /*index=5*/bf16[128,2048]{1,0:T(8,128)(2,1)}) custom-call(bf16[128,2048]{1,0:T(8,128)(2,1)} %get-tuple-element.53.own, bf16[16,128,2048]{2,1,0:T(8,128)(2,1)} %bitcast.101, ...), custom_call_target="tpu_custom_call" | custom-call | tf_op jit(solution)/shard_map/back/pallas_call | solution.py:1735
  554.4 0.0 copy-start.6
  554.4 0.0 copy-done
  554.5 0.0 slice-start
  554.5 2.1 fusion
  556.6 1.2 slice_bitcast_fusion
  557.8 1.5 fusion.4
  559.3 0.0 copy-done.6
  559.3 0.7 copy.38
  560.0 0.0 slice-start.1
  560.0 5.6 bitcast_convert_fusion.1
  565.6 0.0 slice-done
  565.6 0.0 slice-done.1
  565.6 0.0 copy-start.5
  565.6 0.0 copy-start.2
  565.6 6.6 %bitcast_convert_fusion = f32[1,2048,1536]{2,1,0:T(8,128)} fusion(bf16[2048,1536]{1,0:T(8,128)(2,1)S(1)} %bitcast.105), kind=kLoop, calls=%fused_computation | loop fusion | flops 3145728 | bytes 18874368 | tf_op jit(solution)/shard_map/broadcast_in_dim | solution.py:2347
  572.1 0.0 copy-done.5
  572.1 0.8 copy.113
  572.9 0.0 copy-done.2
  572.9 0.0 copy-start.3
  572.9 1.1 copy.114
  574.0 0.6 copy-done.3
  574.6 1.0 copy.115
  (23 shorter events, 0.4 us)
Async XLA Ops:
  0.6 2.0 slice-start.2
  2.7 1.0 copy-start.4
  3.8 1.1 copy-start.1
  379.0 175.4 %copy-start = (f32[128,2048]{1,0:T(8,128)S(1)}, f32[128,2048]{1,0:T(8,128)}, u32[]{:S(2)}) copy-start(f32[128,2048]{1,0:T(8,128)} %get-tuple-element.42.hidden) | copy-start | bytes 3145732
  554.4 4.9 copy-start.6
  554.5 11.1 %slice-start = ((s8[6291456]{0:T(1024)(128)(4,1)}), s8[2097152]{0:T(1024)(128)(4,1)S(1)}, s32[]{:S(2)}) async-start(s8[6291456]{0:T(1024)(128)(4,1)} %bitcast.104), calls=%async_computation | async-start | bytes 4194304
  560.0 5.6 slice-start.1
  565.6 6.6 %copy-start.5 = (bf16[128,2048]{1,0:T(8,128)(2,1)S(1)}, bf16[128,2048]{1,0:T(8,128)(2,1)}, u32[]{:S(2)}) copy-start(bf16[128,2048]{1,0:T(8,128)(2,1)} %get-tuple-element.66) | copy-start | bytes 1572868
  565.6 7.4 %copy-start.2 = (f32[64,5120]{1,0:T(8,128)S(1)}, f32[64,5120]{1,0:T(8,128)}, u32[]{:S(2)}) copy-start(f32[64,5120]{1,0:T(8,128)} %get-tuple-element.122) | copy-start | bytes 3932164
  572.9 1.7 copy-start.3

commit v10 on v9

--- a/solution.py
+++ b/solution.py
@@ -920,7 +920,7 @@
 NT = (((1,), (1,)), ((), ()))
 TILE = 256
 WIDE = 1024
-TALL = 512
+TALL = 1024
 
 
 def mxu(a, b, dims=(((1,), (0,)), ((), ()))):

time: 585 us -> 583 us (level)
  no operation moved by 1% of the time
where the time goes in v10:
time: 583 us; the launch traced here: 574 us
  Pallas kernels  547 us (94%)
  other arithmetic  14.2 us (2%)
  local copies, waits for them, and re-layouts  11 us (2%)
    pallas_call x1, Pallas kernels, back(): pl.pallas_call(back_kernel, out_shape=[jax.ShapeDtypeStruct((rows, width)...  176 us
    pallas_call x1, Pallas kernels, front(): pl.pallas_call(front_kernel, out_shape=[jax.ShapeDtypeStruct((count, rows...  170 us
    pallas_call x1, Pallas kernels, experts_gathered(): pl.pallas_call(experts_kernel, out_shape=[array(experts, tokens, wide), a...  117 us
    pallas_call x1, Pallas kernels, sum_all(): pl.pallas_call(sum_all_kernel, out_shape=[jax.ShapeDtypeStruct(hidden.sha...  85.1 us
    broadcast_in_dim x2, other arithmetic, gathered_body(): d_w_in, d_w_down = (d_w_in.astype(f32)[None], d_w_down.astype(f32)[None])  12.1 us

profile of v10, /device:TPU:16, one launch (start us, length us, event | category | flops | bytes accessed | tf_op | source)
XLA Modules:
  0.0 574.0 jit_solution(12249982376509827047)
XLA Ops:
  0.6 0.0 slice-start.2
  0.7 0.8 copy.47
  1.5 0.9 fusion.3
  2.5 0.1 fusion.6
  2.6 0.1 fusion.5
  2.7 0.0 copy-start.4
  2.7 0.0 slice-done.2
  3.0 0.7 copy-done.4
  3.8 0.0 copy-start.1
  3.8 1.1 copy-done.1
  4.9 170.1 %front.1 = (bf16[8,128,2048]{2,1,0:T(8,128)(2,1)}, bf16[32,64,1408]{2,1,0:T(8,128)(2,1)}, bf16[32,128,2048]{2,1,0:T(8,128)(2,1)}, bf16[1024,512]{1,0:T(8,128)(2,...) custom-call(bf16[128,2048]{1,0:T(8,128)(2,1)} %bitcast.109, ...), custom_call_target="tpu_custom_call" | custom-call | tf_op jit(solution)/shard_map/front/pallas_call | solution.py:2172
  175.0 116.5 %experts.1 = (bf16[32,128,2176]{2,1,0:T(8,128)(2,1)}, bf16[32,128,2048]{2,1,0:T(8,128)(2,1)}, bf16[32,128,2176]{2,1,0:T(8,128)(2,1)}, bf16[2048,2048]{1,0:T(8,12...) custom-call(bf16[128,2176]{1,0:T(8,128)(2,1)} %get-tuple-element.43.own.routed_hbm, ...), custom_call_target="tpu_custom_call" | custom-call | tf_op jit(solution)/shard_map/experts/pallas_call | solution.py:1225
  291.6 85.1 %sum_all.1 = (bf16[128,2048]{1,0:T(8,128)(2,1)}, bf16[128,128]{1,0:T(8,128)(2,1)}, f32[128,2048]{1,0:T(8,128)}, f32[8,2048]{1,0:T(8,128)}, bf16[8,2,128,2048]{3,...) custom-call(bf16[32,128,2176]{2,1,0:T(8,128)(2,1)} %get-tuple-element.45.part, ...), custom_call_target="tpu_custom_call" | custom-call | tf_op jit(solution)/shard_map/sum_all/pallas_call | solution.py:853
  376.7 0.0 copy-start
  376.7 175.6 %back.1 = (bf16[128,2048]{1,0:T(8,128)(2,1)}, f32[64,5120]{1,0:T(8,128)}, f32[64,4096]{1,0:T(8,128)}, f32[64,128]{1,0:T(8,128)}, f32[8,2048]{1,0:T(8,128)}, /*index=5*/bf16[128,2048]{1,0:T(8,128)(2,1)}) custom-call(bf16[128,2048]{1,0:T(8,128)(2,1)} %get-tuple-element.53.own, bf16[16,128,2048]{2,1,0:T(8,128)(2,1)} %bitcast.101, ...), custom_call_target="tpu_custom_call" | custom-call | tf_op jit(solution)/shard_map/back/pallas_call | solution.py:1735
  552.3 0.0 copy-start.6
  552.3 0.0 copy-done
  552.4 0.0 slice-start
  552.4 2.1 fusion
  554.5 1.2 slice_bitcast_fusion
  555.7 1.5 fusion.4
  557.2 0.0 copy-done.6
  557.2 0.7 copy.38
  557.9 0.0 slice-start.1
  557.9 5.6 bitcast_convert_fusion.1
  563.5 0.0 slice-done
  563.5 0.0 slice-done.1
  563.5 0.0 copy-start.5
  563.5 0.0 copy-start.2
  563.5 6.6 %bitcast_convert_fusion = f32[1,2048,1536]{2,1,0:T(8,128)} fusion(bf16[2048,1536]{1,0:T(8,128)(2,1)S(1)} %bitcast.105), kind=kLoop, calls=%fused_computation | loop fusion | flops 3145728 | bytes 18874368 | tf_op jit(solution)/shard_map/broadcast_in_dim | solution.py:2347
  570.0 0.0 copy-done.5
  570.0 0.8 copy.113
  570.8 0.0 copy-done.2
  570.8 0.0 copy-start.3
  570.8 1.1 copy.114
  571.9 0.6 copy-done.3
  572.5 1.0 copy.115
  (23 shorter events, 0.4 us)
Async XLA Ops:
  0.6 2.0 slice-start.2
  2.7 1.0 copy-start.4
  3.8 1.1 copy-start.1
  376.7 175.7 %copy-start = (f32[128,2048]{1,0:T(8,128)S(1)}, f32[128,2048]{1,0:T(8,128)}, u32[]{:S(2)}) copy-start(f32[128,2048]{1,0:T(8,128)} %get-tuple-element.42.hidden) | copy-start | bytes 3145732
  552.3 4.9 copy-start.6
  552.4 11.1 %slice-start = ((s8[6291456]{0:T(1024)(128)(4,1)}), s8[2097152]{0:T(1024)(128)(4,1)S(1)}, s32[]{:S(2)}) async-start(s8[6291456]{0:T(1024)(128)(4,1)} %bitcast.104), calls=%async_computation | async-start | bytes 4194304
  557.9 5.6 slice-start.1
  563.5 6.6 %copy-start.5 = (bf16[128,2048]{1,0:T(8,128)(2,1)S(1)}, bf16[128,2048]{1,0:T(8,128)(2,1)}, u32[]{:S(2)}) copy-start(bf16[128,2048]{1,0:T(8,128)(2,1)} %get-tuple-element.66) | copy-start | bytes 1572868
  563.5 7.4 %copy-start.2 = (f32[64,5120]{1,0:T(8,128)S(1)}, f32[64,5120]{1,0:T(8,128)}, u32[]{:S(2)}) copy-start(f32[64,5120]{1,0:T(8,128)} %get-tuple-element.122) | copy-start | bytes 3932164
  570.8 1.7 copy-start.3
